TPU v7x, 256 devices: a whole 4x4x8 slice. The times are simulated.
256 devices in a mesh: section: 4 (over x), blk: 32 (over y_lo, z, core), tp: 2 (over y_hi).
Axes of the slice: x: 4, y: 4 (y_hi: 2, y_lo: 2; y = y_hi * 2 + y_lo), z: 8, core: 2. Of those that a mesh axis runs over, the one named last changes fastest.
Arguments:
- patches: bfloat16 [4, 8192, 1280], P('section', 'blk'), may hold values from -8 to 8
- frame_ids: int32 [4, 8192], P('section'), may hold values from 0 to 3, never falling along the last dimension, each value on 1 to 4096 neighbouring positions
- groups: int32 [4, 2048, 4], P('section', 'blk'), may hold values from 0 to 255, as said below
- norm_gain: float32 [1280], replicated, may hold values from 0.25 to 1.75
- qkv_weight: bfloat16 [3, 1280, 1280], P(None, 'section', 'tp'), may hold values from -1 to 1
- out_weight: bfloat16 [1280, 1280], P('tp', 'section'), may hold values from -0.47851562 to 0.47851562
- merge_gain: float32 [1280], replicated, may hold values from 0.25 to 1.75
- merger_up: bfloat16 [5120, 2560], P(None, ('section', 'tp')), may hold values from -0.078125 to 0.078125
- merger_down: bfloat16 [2560, 3584], P(('section', 'tp')), may hold values from -0.125 to 0.125
Outputs:
- llm_input: bfloat16 [4, 2048, 3584], P('section', ('blk', 'tp'))
Inputs may be any that keep to these rules, and one draw needn't show every extreme that they name: `groups`: each aligned block of 64 rows of a video names every patch of its device block of 256 patches exactly once. `frame_ids`: frame blocks are runs of consecutive patches, numbered upward.
All inputs are finite; a program needn't handle non-finite values.
Results may differ from a plain program's by a relative error of at most 0.024.
Values may be sent and summed in bfloat16 or wider, within the bound.
No kernel may reach another device: no remote copies, remote signals or barrier semaphores. Data moves between devices by JAX's collectives and lax.ppermute only.
A program may use at most 128 MiB of HBM per device.

v0:
```python
import jax
import jax.numpy as jnp
from jax import lax
from jax.sharding import PartitionSpec as P

HD = 80


def passed_along(block, axis, distance):
    devices = range(lax.axis_size(axis))
    route = [((i - distance) % len(devices), i) for i in devices]
    return lax.ppermute(block, axis, route)


def rms_norm(value, gain):
    return value * lax.rsqrt(jnp.mean(value * value, axis=-1, keepdims=True) + 1e-06) * gain


def attend_block(carry, queries, key_rows, value_rows, my_frames, key_frames):
    run_max, run_total, accum = carry
    count = key_rows.shape[0]
    local_heads = queries.shape[1]
    keys = key_rows.reshape(count, local_heads, HD)
    values = value_rows.reshape(count, local_heads, HD)
    scores = jnp.einsum("qhd,khd->hqk", queries, keys, preferred_element_type=jnp.float32) * HD ** (
        -0.5
    )
    visible = (my_frames[:, None] == key_frames[None, :])[None]
    scores = jnp.where(visible, scores, -1e30)
    new_max = jnp.maximum(run_max, jnp.max(scores, axis=-1))
    weights = jnp.where(visible, jnp.exp(scores - new_max[..., None]), 0.0)
    factor = jnp.exp(run_max - new_max)
    new_total = run_total * factor + jnp.sum(weights, axis=-1)
    new_accum = accum * factor[..., None] + jnp.einsum(
        "hqk,khd->hqd", weights.astype(jnp.bfloat16), values, preferred_element_type=jnp.float32
    )
    return (new_max, new_total, new_accum)


def on_device(
    patches,
    frame_ids,
    groups,
    norm_gain,
    qkv_weight,
    out_weight,
    merge_gain,
    merger_up,
    merger_down,
):
    xfloat = patches[0].astype(jnp.float32)
    rows = xfloat.shape[0]
    normed = rms_norm(xfloat, norm_gain).astype(jnp.bfloat16)
    half_width = qkv_weight.shape[2]
    projected = jnp.einsum(
        "pd,ade->ape",
        normed,
        lax.all_gather(qkv_weight, "section", axis=1, tiled=True),
        preferred_element_type=jnp.float32,
    )
    projected = projected.astype(jnp.bfloat16)
    local_heads = half_width // HD
    queries = projected[0].reshape(rows, local_heads, HD)
    all_frames = frame_ids[0]
    my_frames = lax.dynamic_slice_in_dim(all_frames, lax.axis_index("blk") * rows, rows)
    start_carry = (
        jnp.full((local_heads, rows), -1e30, jnp.float32),
        jnp.zeros((local_heads, rows), jnp.float32),
        jnp.zeros((local_heads, rows, HD), jnp.float32),
    )
    piece = lax.all_gather(projected[1:], "blk", axis=1, tiled=True)
    count = piece.shape[1]
    steps_count = count // 1024
    key_blocks = piece[0].reshape(steps_count, 1024, half_width)
    value_blocks = piece[1].reshape(steps_count, 1024, half_width)
    frame_blocks = all_frames.reshape(steps_count, 1024)

    def inner(state, block):
        return (attend_block(state, queries, block[0], block[1], my_frames, block[2]), None)

    result, unused = lax.scan(inner, start_carry, (key_blocks, value_blocks, frame_blocks))
    run_max, run_total, accum = result
    attn = (
        (accum / run_total[..., None])
        .transpose(1, 0, 2)
        .reshape(rows, half_width)
        .astype(jnp.bfloat16)
    )
    partial_out = jnp.dot(
        attn,
        lax.all_gather(out_weight, "section", axis=1, tiled=True),
        preferred_element_type=jnp.float32,
    )
    summed = lax.psum(partial_out.astype(jnp.bfloat16), "tp").astype(jnp.float32)
    merged_normed = rms_norm(xfloat + summed, merge_gain).astype(jnp.bfloat16)
    tokens = merged_normed[groups[0]].reshape(rows // 4, 4 * merged_normed.shape[1])
    video_rows = lax.all_gather(tokens, "section", axis=0, tiled=True)
    piece = video_rows
    hidden = jax.nn.gelu(
        jnp.dot(piece, merger_up, preferred_element_type=jnp.float32), approximate=False
    ).astype(jnp.bfloat16)
    merged_out = lax.psum_scatter(
        jnp.dot(hidden, merger_down, preferred_element_type=jnp.float32).astype(jnp.bfloat16),
        ("section", "tp"),
        scatter_dimension=0,
        tiled=True,
    )
    merged_out = passed_along(merged_out, "section", 1)
    return merged_out[None]


def solution(mesh):
    in_specs = (
        P("section", "blk", None),
        P("section", None),
        P("section", "blk", None),
        P(),
        P(None, "section", "tp"),
        P("tp", "section"),
        P(),
        P(None, ("section", "tp")),
        P(("section", "tp"), None),
    )
    out_specs = P("section", ("blk", "tp"), None)
    return jax.shard_map(
        on_device, mesh=mesh, in_specs=in_specs, out_specs=out_specs, check_vma=False
    )
```

profile of v0, /device:TPU:32, one launch (start us, length us, event | category | flops | bytes accessed | tf_op | source)
XLA Modules:
  0.0 653.7 jit_solution(1634282347257062807)
XLA Ops:
  8.8 59.8 %all-gather.5.cloned.1.call-done = bf16[3,1280,640]{2,1,0:T(8,128)(2,1)} async-done(((bf16[3,320,640]{2,1,0:T(8,128)(2,1)}), bf16[3,1280,640]{2,1,0:T(8,128)(2,1)}) %all-gather.5.cloned.1.call-update) | async-done | bytes 4915216 | tf_op jit(solution)/shard_map/all_gather | solution.py:58
  68.6 4.2 fusion.13
  81.6 114.6 %all-gather.7.cloned.1.call-done = bf16[2,8192,640]{2,1,0:T(8,128)(2,1)} async-done(((bf16[2,256,640]{2,1,0:T(8,128)(2,1)}), bf16[2,8192,640]{2,1,0:T(8,128)(2,1)}) %all-gather.7.cloned.1.call-update) | async-done | bytes 20971536 | tf_op jit(solution)/shard_map/all_gather | solution.py:71
  196.2 16.0 %fusion.93 = (bf16[1,8192,640]{2,1,0:T(8,128)(2,1)}, bf16[1,8192,640]{2,1,0:T(8,128)(2,1)}) fusion(bf16[2,8192,640]{2,1,0:T(8,128)(2,1)} %all-gather.7.cloned.1.call-done), kind=kLoop, calls=%fused_computation.122 | loop fusion | bytes 41943040 | tf_op jit(solution)/shard_map/slice | solution.py:75
  212.2 240.4 %while.15 = (s32[]{:T(128)}, f32[8,256]{1,0:T(8,128)S(1)}, f32[8,256]{1,0:T(8,128)}, f32[8,256,80]{1,2,0:T(8,128)}, s32[256]{0:T(256)}, /*index=5*/s32[8,1024]{1...) while((s32[]{:T(128)}, f32[8,256]{1,0:T(8,128)S(1)}, ...), condition=%wide.region_4.5_spmd.clone, body=%wide.region_1.4_spmd.clone.sunk | while | flops 699115520 | bytes 41202896 | solution.py:81
  213.8 3.5 constant_dynamic-slice_fusion.7
  219.8 6.8 %fusion.117 = (f32[8,256]{1,0:T(8,128)}, f32[8,1024,256]{2,1,0:T(8,128)}) fusion(pred[256,1024]{0,1:T(8,128)(4,1)S(1)} %broadcast_compare_fusion.2, bf16[1024,8,80]{0,2,1:T(8,128)(2,1)} %bitcast.69, bf16[256,8,80]{0,2,1:T(8,128)(2,1)} %get-tuple-element.225), kind=kOutput, calls=%fused_computation.3.clone.1 | convolution fusion | flops 341833728 | bytes 10297344 | tf_op jit(solution)/shard_map/while/body/eval_jaxpr/qhd,khd->hqk/dot_general | solution.py:25
  227.3 4.5 fusion.118
  233.0 2.5 copy.25
  235.5 6.8 %fusion.120 = f32[8,256,80]{1,2,0:T(8,128)} fusion(bf16[1024,8,80]{0,2,1:T(8,128)(2,1)} %bitcast.70, f32[8,1024,256]{2,1,0:T(8,128)} %get-tuple-element.192, f32[8,256]{1,0:T(8,128)S(1)} %select_maximum_fusion.2, pred[256,1024]{0,1:T(8,128)(4,1)S(1)} %broadcast_compare_fusion.2, f32[8,256,80]{1,2,0:T(8,128)} %get-tuple-element.210, ...), kind=kOutput, calls=%fused_computation.8.clone.1 | convolution fusion | flops 346521600 | bytes 11288577 | tf_op jit(solution)/shard_map/while/body/eval_jaxpr/hqk,khd->hqd/dot_general | solution.py:34
  243.9 3.4 constant_dynamic-slice_fusion.7
  249.8 6.8 %fusion.117 = (f32[8,256]{1,0:T(8,128)}, f32[8,1024,256]{2,1,0:T(8,128)}) fusion(pred[256,1024]{0,1:T(8,128)(4,1)S(1)} %broadcast_compare_fusion.2, bf16[1024,8,80]{0,2,1:T(8,128)(2,1)} %bitcast.69, bf16[256,8,80]{0,2,1:T(8,128)(2,1)} %get-tuple-element.225), kind=kOutput, calls=%fused_computation.3.clone.1 | convolution fusion | flops 341833728 | bytes 10297344 | tf_op jit(solution)/shard_map/while/body/eval_jaxpr/qhd,khd->hqk/dot_general | solution.py:25
  257.2 4.5 fusion.118
  265.4 6.9 %fusion.120 = f32[8,256,80]{1,2,0:T(8,128)} fusion(bf16[1024,8,80]{0,2,1:T(8,128)(2,1)} %bitcast.70, f32[8,1024,256]{2,1,0:T(8,128)} %get-tuple-element.192, f32[8,256]{1,0:T(8,128)S(1)} %select_maximum_fusion.2, pred[256,1024]{0,1:T(8,128)(4,1)S(1)} %broadcast_compare_fusion.2, f32[8,256,80]{1,2,0:T(8,128)} %get-tuple-element.210, ...), kind=kOutput, calls=%fused_computation.8.clone.1 | convolution fusion | flops 346521600 | bytes 11288577 | tf_op jit(solution)/shard_map/while/body/eval_jaxpr/hqk,khd->hqd/dot_general | solution.py:34
  273.9 3.4 constant_dynamic-slice_fusion.7
  279.8 6.8 %fusion.117 = (f32[8,256]{1,0:T(8,128)}, f32[8,1024,256]{2,1,0:T(8,128)}) fusion(pred[256,1024]{0,1:T(8,128)(4,1)S(1)} %broadcast_compare_fusion.2, bf16[1024,8,80]{0,2,1:T(8,128)(2,1)} %bitcast.69, bf16[256,8,80]{0,2,1:T(8,128)(2,1)} %get-tuple-element.225), kind=kOutput, calls=%fused_computation.3.clone.1 | convolution fusion | flops 341833728 | bytes 10297344 | tf_op jit(solution)/shard_map/while/body/eval_jaxpr/qhd,khd->hqk/dot_general | solution.py:25
  287.3 4.5 fusion.118
  295.5 6.9 %fusion.120 = f32[8,256,80]{1,2,0:T(8,128)} fusion(bf16[1024,8,80]{0,2,1:T(8,128)(2,1)} %bitcast.70, f32[8,1024,256]{2,1,0:T(8,128)} %get-tuple-element.192, f32[8,256]{1,0:T(8,128)S(1)} %select_maximum_fusion.2, pred[256,1024]{0,1:T(8,128)(4,1)S(1)} %broadcast_compare_fusion.2, f32[8,256,80]{1,2,0:T(8,128)} %get-tuple-element.210, ...), kind=kOutput, calls=%fused_computation.8.clone.1 | convolution fusion | flops 346521600 | bytes 11288577 | tf_op jit(solution)/shard_map/while/body/eval_jaxpr/hqk,khd->hqd/dot_general | solution.py:34
  304.0 3.4 constant_dynamic-slice_fusion.7
  309.9 6.8 %fusion.117 = (f32[8,256]{1,0:T(8,128)}, f32[8,1024,256]{2,1,0:T(8,128)}) fusion(pred[256,1024]{0,1:T(8,128)(4,1)S(1)} %broadcast_compare_fusion.2, bf16[1024,8,80]{0,2,1:T(8,128)(2,1)} %bitcast.69, bf16[256,8,80]{0,2,1:T(8,128)(2,1)} %get-tuple-element.225), kind=kOutput, calls=%fused_computation.3.clone.1 | convolution fusion | flops 341833728 | bytes 10297344 | tf_op jit(solution)/shard_map/while/body/eval_jaxpr/qhd,khd->hqk/dot_general | solution.py:25
  317.3 4.5 fusion.118
  323.0 2.5 copy.25
  325.5 6.9 %fusion.120 = f32[8,256,80]{1,2,0:T(8,128)} fusion(bf16[1024,8,80]{0,2,1:T(8,128)(2,1)} %bitcast.70, f32[8,1024,256]{2,1,0:T(8,128)} %get-tuple-element.192, f32[8,256]{1,0:T(8,128)S(1)} %select_maximum_fusion.2, pred[256,1024]{0,1:T(8,128)(4,1)S(1)} %broadcast_compare_fusion.2, f32[8,256,80]{1,2,0:T(8,128)} %get-tuple-element.210, ...), kind=kOutput, calls=%fused_computation.8.clone.1 | convolution fusion | flops 346521600 | bytes 11288577 | tf_op jit(solution)/shard_map/while/body/eval_jaxpr/hqk,khd->hqd/dot_general | solution.py:34
  334.0 3.4 constant_dynamic-slice_fusion.7
  339.9 6.8 %fusion.117 = (f32[8,256]{1,0:T(8,128)}, f32[8,1024,256]{2,1,0:T(8,128)}) fusion(pred[256,1024]{0,1:T(8,128)(4,1)S(1)} %broadcast_compare_fusion.2, bf16[1024,8,80]{0,2,1:T(8,128)(2,1)} %bitcast.69, bf16[256,8,80]{0,2,1:T(8,128)(2,1)} %get-tuple-element.225), kind=kOutput, calls=%fused_computation.3.clone.1 | convolution fusion | flops 341833728 | bytes 10297344 | tf_op jit(solution)/shard_map/while/body/eval_jaxpr/qhd,khd->hqk/dot_general | solution.py:25
  347.4 4.5 fusion.118
  353.1 2.5 copy.25
  355.6 6.9 %fusion.120 = f32[8,256,80]{1,2,0:T(8,128)} fusion(bf16[1024,8,80]{0,2,1:T(8,128)(2,1)} %bitcast.70, f32[8,1024,256]{2,1,0:T(8,128)} %get-tuple-element.192, f32[8,256]{1,0:T(8,128)S(1)} %select_maximum_fusion.2, pred[256,1024]{0,1:T(8,128)(4,1)S(1)} %broadcast_compare_fusion.2, f32[8,256,80]{1,2,0:T(8,128)} %get-tuple-element.210, ...), kind=kOutput, calls=%fused_computation.8.clone.1 | convolution fusion | flops 346521600 | bytes 11288577 | tf_op jit(solution)/shard_map/while/body/eval_jaxpr/hqk,khd->hqd/dot_general | solution.py:34
  364.1 3.4 constant_dynamic-slice_fusion.7
  370.0 6.8 %fusion.117 = (f32[8,256]{1,0:T(8,128)}, f32[8,1024,256]{2,1,0:T(8,128)}) fusion(pred[256,1024]{0,1:T(8,128)(4,1)S(1)} %broadcast_compare_fusion.2, bf16[1024,8,80]{0,2,1:T(8,128)(2,1)} %bitcast.69, bf16[256,8,80]{0,2,1:T(8,128)(2,1)} %get-tuple-element.225), kind=kOutput, calls=%fused_computation.3.clone.1 | convolution fusion | flops 341833728 | bytes 10297344 | tf_op jit(solution)/shard_map/while/body/eval_jaxpr/qhd,khd->hqk/dot_general | solution.py:25
  377.4 4.5 fusion.118
  383.1 2.5 copy.25
  385.6 6.9 %fusion.120 = f32[8,256,80]{1,2,0:T(8,128)} fusion(bf16[1024,8,80]{0,2,1:T(8,128)(2,1)} %bitcast.70, f32[8,1024,256]{2,1,0:T(8,128)} %get-tuple-element.192, f32[8,256]{1,0:T(8,128)S(1)} %select_maximum_fusion.2, pred[256,1024]{0,1:T(8,128)(4,1)S(1)} %broadcast_compare_fusion.2, f32[8,256,80]{1,2,0:T(8,128)} %get-tuple-element.210, ...), kind=kOutput, calls=%fused_computation.8.clone.1 | convolution fusion | flops 346521600 | bytes 11288577 | tf_op jit(solution)/shard_map/while/body/eval_jaxpr/hqk,khd->hqd/dot_general | solution.py:34
  394.1 3.4 constant_dynamic-slice_fusion.7
  400.0 6.8 %fusion.117 = (f32[8,256]{1,0:T(8,128)}, f32[8,1024,256]{2,1,0:T(8,128)}) fusion(pred[256,1024]{0,1:T(8,128)(4,1)S(1)} %broadcast_compare_fusion.2, bf16[1024,8,80]{0,2,1:T(8,128)(2,1)} %bitcast.69, bf16[256,8,80]{0,2,1:T(8,128)(2,1)} %get-tuple-element.225), kind=kOutput, calls=%fused_computation.3.clone.1 | convolution fusion | flops 341833728 | bytes 10297344 | tf_op jit(solution)/shard_map/while/body/eval_jaxpr/qhd,khd->hqk/dot_general | solution.py:25
  407.5 4.5 fusion.118
  415.7 6.9 %fusion.120 = f32[8,256,80]{1,2,0:T(8,128)} fusion(bf16[1024,8,80]{0,2,1:T(8,128)(2,1)} %bitcast.70, f32[8,1024,256]{2,1,0:T(8,128)} %get-tuple-element.192, f32[8,256]{1,0:T(8,128)S(1)} %select_maximum_fusion.2, pred[256,1024]{0,1:T(8,128)(4,1)S(1)} %broadcast_compare_fusion.2, f32[8,256,80]{1,2,0:T(8,128)} %get-tuple-element.210, ...), kind=kOutput, calls=%fused_computation.8.clone.1 | convolution fusion | flops 346521600 | bytes 11288577 | tf_op jit(solution)/shard_map/while/body/eval_jaxpr/hqk,khd->hqd/dot_general | solution.py:34
  424.2 3.4 constant_dynamic-slice_fusion.7
  430.1 6.8 %fusion.117 = (f32[8,256]{1,0:T(8,128)}, f32[8,1024,256]{2,1,0:T(8,128)}) fusion(pred[256,1024]{0,1:T(8,128)(4,1)S(1)} %broadcast_compare_fusion.2, bf16[1024,8,80]{0,2,1:T(8,128)(2,1)} %bitcast.69, bf16[256,8,80]{0,2,1:T(8,128)(2,1)} %get-tuple-element.225), kind=kOutput, calls=%fused_computation.3.clone.1 | convolution fusion | flops 341833728 | bytes 10297344 | tf_op jit(solution)/shard_map/while/body/eval_jaxpr/qhd,khd->hqk/dot_general | solution.py:25
  437.6 4.5 fusion.118
  445.7 6.9 %fusion.120 = f32[8,256,80]{1,2,0:T(8,128)} fusion(bf16[1024,8,80]{0,2,1:T(8,128)(2,1)} %bitcast.70, f32[8,1024,256]{2,1,0:T(8,128)} %get-tuple-element.192, f32[8,256]{1,0:T(8,128)S(1)} %select_maximum_fusion.2, pred[256,1024]{0,1:T(8,128)(4,1)S(1)} %broadcast_compare_fusion.2, f32[8,256,80]{1,2,0:T(8,128)} %get-tuple-element.210, ...), kind=kOutput, calls=%fused_computation.8.clone.1 | convolution fusion | flops 346521600 | bytes 11288577 | tf_op jit(solution)/shard_map/while/body/eval_jaxpr/hqk,khd->hqd/dot_general | solution.py:34
  454.5 3.1 convolution_convert_fusion.1
  457.9 45.0 %all-reduce.2.cloned.1.call-done = bf16[256,1280]{1,0:T(8,128)(2,1)} async-done(((bf16[256,1280]{1,0:T(8,128)(2,1)}), bf16[256,1280]{1,0:T(8,128)(2,1)}) %all-reduce.2.cloned.1.call-update) | async-done | bytes 655376 | tf_op jit(solution)/shard_map/psum | solution.py:94
  506.8 3.8 gather_fusion
  513.1 37.1 %all-gather.11.cloned.1.call-done = bf16[256,5120]{1,0:T(8,128)(2,1)} async-done(((bf16[64,5120]{1,0:T(8,128)(2,1)}), bf16[256,5120]{1,0:T(8,128)(2,1)}) %all-gather.11.cloned.1.call-update) | async-done | bytes 2621456 | tf_op jit(solution)/shard_map/all_gather | solution.py:97
  550.2 8.1 %convolution_convert_fusion = bf16[256,3584]{1,0:T(8,128)(2,1)} fusion(bf16[320,3584]{1,0:T(8,128)(2,1)} %param.19, bf16[256,5120]{1,0:T(8,128)(2,1)} %all-gather.11.cloned.1.call-done, bf16[5120,320]{0,1:T(8,128)(2,1)S(1)} %copy-done), kind=kOutput, calls=%fused_computation.21 | convolution fusion | flops 1432305664 | bytes 10027008 | tf_op jit(solution)/shard_map/dot_general | solution.py:103
  558.4 80.4 %reduce-scatter.2.cloned.1.call-done = bf16[32,3584]{1,0:T(8,128)(2,1)} async-done(((bf16[256,3584]{1,0:T(8,128)(2,1)}), bf16[32,3584]{1,0:T(8,128)(2,1)}) %reduce-scatter.2.cloned.1.call-update) | async-done | bytes 229392 | tf_op jit(solution)/shard_map/reduce_scatter | solution.py:102
  639.9 6.3 collective-permute-done
  (146 shorter events, 79.6 us)
Async XLA Ops:
  6.5 543.7 %copy-start = (bf16[5120,320]{0,1:T(8,128)(2,1)S(1)}, bf16[5120,320]{0,1:T(8,128)(2,1)}, u32[]{:S(2)}) copy-start(bf16[5120,320]{0,1:T(8,128)(2,1)} %param.18) | copy-start | bytes 9830404
  6.5 62.1 %all-gather.5.cloned.1.call-start = ((), (), s32[]{:S(2)}) async-start(), calls=%async_computation.1 | async-start | bytes 6144000 | tf_op jit(solution)/shard_map/all_gather | solution.py:58
  7.3 189.0 %all-gather.7.cloned.1.call-start = ((), (), s32[]{:S(2)}) async-start(), calls=%async_computation.2 | async-start | bytes 21626880 | tf_op jit(solution)/shard_map/all_gather | solution.py:71
  8.8 66.7 %copy-start.5 = (s32[1,8192]{1,0:T(1,128)S(1)}, s32[1,8192]{1,0:T(1,128)}, u32[]{:S(2)}) copy-start(s32[1,8192]{1,0:T(1,128)} %param.12) | copy-start | bytes 98308
  72.8 0.9 copy-start.1
  74.7 379.8 %all-gather.9.cloned.1.call-start = ((), (), s32[]{:S(2)}) async-start(), calls=%async_computation.3 | async-start | bytes 2048000 | tf_op jit(solution)/shard_map/all_gather | solution.py:91
  75.5 427.4 %all-reduce.2.cloned.1.call-start = ((), (), s32[]{:S(2)}) async-start(), calls=%async_computation.4 | async-start | bytes 1310720 | tf_op jit(solution)/shard_map/psum | solution.py:94
  227.3 4.5 copy-start.2
  232.4 0.6 copy-start.3
  233.0 2.5 copy-start.4
  257.2 4.5 copy-start.2
  262.3 0.6 copy-start.3
  262.9 2.5 copy-start.4
  287.3 4.5 copy-start.2
  292.4 0.6 copy-start.3
  293.0 2.5 copy-start.4
  317.3 4.5 copy-start.2
  322.4 0.6 copy-start.3
  323.0 2.5 copy-start.4
  347.4 4.5 copy-start.2
  352.5 0.6 copy-start.3
  353.1 2.5 copy-start.4
  377.4 4.5 copy-start.2
  382.6 0.6 copy-start.3
  383.1 2.5 copy-start.4
  407.5 4.5 copy-start.2
  412.6 0.6 copy-start.3
  413.2 2.5 copy-start.4
  437.6 4.5 copy-start.2
  442.7 0.6 copy-start.3
  443.3 2.5 copy-start.4
  452.6 5.1 copy-start.7
  452.6 51.8 %copy-start.6 = (f32[1280]{0:T(1024)S(1)}, f32[1280]{0:T(1024)}, u32[]{:S(2)}) copy-start(f32[1280]{0:T(1024)} %param.17) | copy-start | bytes 15364
  457.6 92.6 %all-gather.11.cloned.1.call-start = ((), (), s32[]{:S(2)}) async-start(), calls=%async_computation.5 | async-start | bytes 3276800 | tf_op jit(solution)/shard_map/all_gather | solution.py:97
  512.9 125.9 %reduce-scatter.2.cloned.1.call-start = ((), (), s32[]{:S(2)}) async-start(), calls=%async_computation.6 | async-start | bytes 2064384 | tf_op jit(solution)/shard_map/reduce_scatter | solution.py:102
  638.8 7.4 %collective-permute-start = (bf16[32,3584]{1,0:T(8,128)(2,1)}, bf16[32,3584]{1,0:T(8,128)(2,1)S(1)}, u32[]{:S(2)}, u32[]{:S(2)}) collective-permute-start(bf16[32,3584]{1,0:T(8,128)(2,1)} %reduce-scatter.2.cloned.1.call-done), channel_id=1, source_target_pairs={{192,0},{0,64},{64,128},{128,192},{193,1},{1,65},{65,129},{129,193... | collective-permute-start | bytes 688136 | tf_op jit(solution)/shard_map/ppermute | solution.py:12
Sparse Core Ops, SparseCore 0:
  9.2 59.3 all-gather.4
  74.9 121.3 all-gather.6
  198.1 29.9 all-gather.8
  457.7 45.0 all-reduce.1
  513.0 37.1 all-gather.10
  558.5 80.2 reduce-scatter.1
where the time goes:
time: 656 us; the launch traced here: 654 us
  waiting for transfers between devices  345 us (53%)
  matrix products  124 us (19%)
  local copies, waits for them, and re-layouts  108 us (16%)
  other arithmetic  61.3 us (9%)
  between operations  13.6 us (2%)
    all_gather x1, waiting for transfers between devices, on_device(): piece = lax.all_gather(projected[1:], 'blk', axis=1, tiled=True)  115 us
    reduce_scatter x1, waiting for transfers between devices, on_device(): lax.psum_scatter(jnp.dot(hidden, merger_down, preferred_element_type=jnp....  80.4 us
    dynamic_slice x32, local copies, waits for them, and re-layouts, on_device(): lax.scan(inner, start_carry, (key_blocks, value_blocks, frame_blocks))  73.3 us
    all_gather x1, waiting for transfers between devices, on_device(): lax.all_gather(qkv_weight, 'section', axis=1, tiled=True)  59.8 us
    dot_general x8, matrix products, attend_block(): jnp.einsum('hqk,khd->hqd', weights.astype(jnp.bfloat16), values, preferre...  54.8 us
    dot_general x8, matrix products, attend_block(): jnp.einsum('qhd,khd->hqk', queries, keys, preferred_element_type=jnp.floa...  54.1 us
    psum x1, waiting for transfers between devices, on_device(): lax.psum(partial_out.astype(jnp.bfloat16), 'tp').astype(jnp.float32)  45 us
    all_gather x1, waiting for transfers between devices, on_device(): video_rows = lax.all_gather(tokens, 'section', axis=0, tiled=True)  37.1 us
  transfers between devices with their start and end apart: 7, of which 6 were waited for; matrix products, arithmetic and copies ran while one was open for 40% of the time, Pallas kernels for 0%

commit v1 on v0

v1 whole, which is shorter than its diff:
```python
import functools
import math

import jax
import jax.numpy as jnp
from jax import lax
from jax.experimental import pallas as pl
from jax.experimental.pallas import tpu as pltpu
from jax.sharding import PartitionSpec as P

HD = 80
ZN = 8
KB = 512
SECTIONS = 4
VMEM = pl.BlockSpec(memory_space=pltpu.VMEM)
SMEM = pl.BlockSpec(memory_space=pltpu.SMEM)
LIMIT = 56 * 1024 * 1024
bf16, f32 = jnp.bfloat16, jnp.float32

Z_GROUPS = [[y * 16 + z * 2 + c for z in range(ZN)] for y in range(2) for c in range(2)]


def call(kernel, out_shape, specs, scratch=(), flops=0, moved=0, name=None):
    return pl.pallas_call(
        kernel,
        out_shape=out_shape,
        in_specs=specs,
        out_specs=jax.tree.map(lambda _: VMEM, out_shape),
        scratch_shapes=list(scratch),
        compiler_params=pltpu.CompilerParams(vmem_limit_bytes=LIMIT),
        cost_estimate=pl.CostEstimate(flops=flops, bytes_accessed=moved, transcendentals=0),
        name=name,
    )


def section_shift(value, distance):
    route = [(i, (i + distance) % SECTIONS) for i in range(SECTIONS)]
    return lax.ppermute(value, "section", route)


def blk_swap(value, bit):
    return lax.ppermute(value, "blk", [(i, i ^ bit) for i in range(32)])


def tp_swap(value):
    return lax.ppermute(value, "tp", [(0, 1), (1, 0)])


def z_exchange(value):
    return lax.all_to_all(value, "blk", 0, 0, axis_index_groups=Z_GROUPS, tiled=True)


def rms_norm(value, gain):
    return value * lax.rsqrt(jnp.mean(value * value, axis=-1, keepdims=True) + 1e-06) * gain


def ring_halves(own):
    half = own.shape[-2] // 2
    right = section_shift(own, -1)
    left = section_shift(own, 1)
    opposite_a = section_shift(right[..., :half, :], -1)
    opposite_b = section_shift(left[..., half:, :], 1)
    return right, left, opposite_a, opposite_b


def project_kernel(count, place_ref, normed_ref, own_ref, mine_ref, other_ref, out_ref, weight):
    me, core = place_ref[0], place_ref[1]
    row = lambda section, half: pl.ds(pl.multiple_of(section * 320 + half * 160, 16), 160)
    for t in range(count):
        weight[t, pl.ds(pl.multiple_of(me * 320, 16), 320), :] = own_ref[t]
        for source, half in ((mine_ref, core), (other_ref, 1 - core)):
            for k in range(3):
                section = lax.rem(me + k + 1, SECTIONS)
                weight[t, row(section, half), :] = source[k, t]
        made = jnp.dot(normed_ref[...], weight[t], preferred_element_type=f32)
        turned = made.T.astype(bf16)
        for h in range(ZN):
            out_ref[h, t * HD : (t + 1) * HD, :] = turned[h * HD : (h + 1) * HD, :]


def project(place, normed, own, core):
    count = own.shape[0]
    half = lax.dynamic_slice_in_dim(own, core * 160, 160, axis=1)
    right, left, opp_a, opp_b = ring_halves(half)
    mine = jnp.stack([right, jnp.concatenate([opp_a, opp_b], axis=1), left])
    other = blk_swap(mine, 1)
    return call(
        functools.partial(project_kernel, count),
        jax.ShapeDtypeStruct((ZN, count * HD, 256), bf16),
        [SMEM] + [VMEM] * 4,
        [pltpu.VMEM((count, 1280, 640), bf16)],
        flops=2 * 256 * 1280 * 640 * count,
        moved=count * 2 * 1280 * 640,
        name="project",
    )(place, normed, own, mine, other)


def attention_kernel(bounds_ref, place_ref, qframe_ref, kframe_ref, q_ref, kv_ref, out_ref, keys, values):
    y, core = place_ref[2], place_ref[1]
    scale = HD ** (-0.5) * math.log2(math.e)
    filler = (lax.broadcasted_iota(jnp.int32, (48, 256), 0) == 0).astype(f32).astype(bf16)

    def arrange(step, carry):
        which, z = step // ZN, lax.rem(step, ZN)
        y_of = jnp.bitwise_xor(y, which // 2)
        core_of = jnp.bitwise_xor(core, lax.rem(which, 2))
        place = pl.multiple_of((y_of * 16 + z * 2 + core_of) * 256, 256)
        keys[:, pl.ds(place, 256)] = kv_ref[which, z, :HD, :]
        padded = jnp.concatenate([kv_ref[which, z, HD:, :], filler], axis=0)
        values[pl.ds(place, 256), :] = padded.T
        return carry

    lax.fori_loop(0, 4 * ZN, arrange, 0)

    def one_block(block, unused):
        query = q_ref[block].T
        qframe = qframe_ref[block]

        def step(masked, index, carry):
            top, accum = carry
            start = pl.multiple_of(index * KB, KB)
            scores = jnp.dot(query, keys[:, pl.ds(start, KB)], preferred_element_type=f32)
            if masked:
                scores = jnp.where(qframe == kframe_ref[:, pl.ds(start, KB)], scores, -1e30)
            new_top = jnp.maximum(top, jnp.max(scores, axis=1, keepdims=True))
            weights = jnp.exp2((scores - new_top) * scale)
            factor = jnp.exp2((top - new_top) * scale)
            product = jnp.dot(weights.astype(bf16), values[pl.ds(start, KB), :], preferred_element_type=f32)
            return new_top, accum * factor + product

        first, inner, outer, last = (bounds_ref[k, block] for k in range(4))
        carry = (jnp.full((256, 1), -1e30, f32), jnp.zeros((256, 128), f32))
        carry = lax.fori_loop(first, inner, functools.partial(step, True), carry)
        carry = lax.fori_loop(inner, outer, functools.partial(step, False), carry)
        carry = lax.fori_loop(outer, last, functools.partial(step, True), carry)
        accum = carry[1]
        result = accum / accum[:, HD : HD + 1]
        out_ref[block] = result.T[:HD, :].astype(bf16)
        return unused

    lax.fori_loop(0, ZN, one_block, 0)


def attention(place, frames, q, kv, y, core):
    ends = jnp.sum((frames[None, :] <= jnp.arange(-1, 4)[:, None]).astype(jnp.int32), axis=1)
    grid = frames.reshape(2, ZN, 2, 256)
    mine = lax.dynamic_index_in_dim(lax.dynamic_index_in_dim(grid, y, 0, False), core, 1, False)
    low, high = mine[:, 0], mine[:, -1]
    start, stop = ends[low], ends[high + 1]
    single = low == high
    first, last = start // KB, (stop + KB - 1) // KB
    inner = jnp.where(single, (start + KB - 1) // KB, last)
    outer = jnp.where(single, stop // KB, last)
    inner = jnp.minimum(inner, last)
    outer = jnp.maximum(outer, inner)
    bounds = jnp.stack([first, inner, outer, last]).astype(jnp.int32)
    return call(
        attention_kernel,
        jax.ShapeDtypeStruct((ZN, HD, 256), bf16),
        [SMEM, SMEM] + [VMEM] * 4,
        [pltpu.VMEM((HD, 8192), bf16), pltpu.VMEM((8192, 128), bf16)],
        flops=4 * 2048 * 4096 * 256,
        moved=4 * 8192 * HD,
        name="attention",
    )(bounds, place, mine[:, :, None], frames[None, :], q, kv)


def output_kernel(place_ref, order_ref, patch_ref, attn_ref, weight_ref, base_ref, send_ref):
    tp = place_ref[3]
    pick = (order_ref[...] == lax.broadcasted_iota(jnp.int32, (256, 256), 1)).astype(f32).astype(bf16)
    attn = attn_ref[...].reshape(ZN * HD, 256)
    picked = lax.dot_general(pick, attn, (((1,), (1,)), ((), ())), preferred_element_type=f32).astype(bf16)
    partial = jnp.dot(picked, weight_ref[...], preferred_element_type=f32)
    patch = jnp.dot(pick, patch_ref[...], preferred_element_type=f32)

    @pl.when(tp == 0)
    def _():
        base_ref[...] = partial[:128] + patch[:128]
        send_ref[...] = partial[128:].astype(bf16)

    @pl.when(tp == 1)
    def _():
        base_ref[...] = partial[128:] + patch[128:]
        send_ref[...] = partial[:128].astype(bf16)


def merger_kernel(place_ref, *refs):
    pieces, (up_ref, down_ref, out_ref, tokens) = refs[:10], refs[10:]
    me, tp = place_ref[0], place_ref[3]
    own, own_t, right, left, opp_a, opp_b, right_t, left_t, opp_at, opp_bt = pieces

    def put(distance, flip, source, low):
        slot = lax.rem(me + distance + 1, SECTIONS) * 2 + (1 - tp if flip else tp)
        rows = pl.ds(pl.multiple_of(slot * 32, 32), 32)
        for j in range(source.shape[0] // 32):
            tokens[low // 32 + j, rows, :] = source[j * 32 : (j + 1) * 32, :]

    put(0, False, own, 0)
    put(0, True, own_t, 0)
    put(1, False, right, 0)
    put(1, True, right_t, 0)
    put(3, False, left, 0)
    put(3, True, left_t, 0)
    put(2, False, opp_a, 0)
    put(2, False, opp_b, 64)
    put(2, True, opp_at, 0)
    put(2, True, opp_bt, 64)
    hidden = jnp.zeros((256, 320), f32)
    for j in range(4):
        hidden += jnp.dot(tokens[j], up_ref[j * 1280 : (j + 1) * 1280, :], preferred_element_type=f32)
    hidden = (0.5 * hidden * (1.0 + lax.erf(hidden * (0.5**0.5)))).astype(bf16)
    for k in range(7):
        columns = slice(k * 512, (k + 1) * 512)
        out_ref[:, columns] = jnp.dot(hidden, down_ref[:, columns], preferred_element_type=f32).astype(bf16)


def on_device(patches, frame_ids, groups, norm_gain, qkv_weight, out_weight, merge_gain, merger_up, merger_down):
    me, blk, tp = lax.axis_index("section"), lax.axis_index("blk"), lax.axis_index("tp")
    core, y = blk % 2, blk // 16
    place = jnp.stack([me, core, y, tp]).astype(jnp.int32)
    patch = patches[0]
    normed = rms_norm(patch.astype(f32), norm_gain).astype(bf16)

    kv = z_exchange(project(place, normed, qkv_weight[1:3], core))
    q = z_exchange(project(place, normed, qkv_weight[0:1], core))

    far = blk_swap(kv, 16)
    pair = jnp.stack([kv, far])
    across = blk_swap(pair, 1)
    kv_all = jnp.stack([kv, across[0], far, across[1]])

    attn = z_exchange(attention(place, frame_ids[0], q, kv_all, y, core))

    pieces = jnp.stack([out_weight] + [section_shift(out_weight, -d) for d in (1, 2, 3)])
    turned = jnp.roll(pieces, me, axis=0)
    whole = turned.transpose(1, 0, 2).reshape(640, 1280)
    order = groups[0].reshape(2, 32, 4).transpose(0, 2, 1).reshape(256, 1)
    base, send = call(
        output_kernel,
        (jax.ShapeDtypeStruct((128, 1280), f32), jax.ShapeDtypeStruct((128, 1280), bf16)),
        [SMEM] + [VMEM] * 4,
        flops=2 * 256 * 1280 * 900,
        moved=4000000,
        name="output",
    )(place, order, patch, attn, whole)
    resid = base + tp_swap(send).astype(f32)
    own = rms_norm(resid, merge_gain).astype(bf16)

    own_t = tp_swap(own)
    right, left, opp_a, opp_b = ring_halves(own)
    right_t, left_t, opp_at, opp_bt = ring_halves(own_t)
    partial = call(
        merger_kernel,
        jax.ShapeDtypeStruct((256, 3584), bf16),
        [SMEM] + [VMEM] * 12,
        [pltpu.VMEM((4, 256, 1280), bf16)],
        flops=2 * 256 * 320 * (5120 + 3584),
        moved=9000000,
        name="merger",
    )(place, own, own_t, right, left, opp_a, opp_b, right_t, left_t, opp_at, opp_bt, merger_up, merger_down)
    parts = lax.all_to_all(partial.reshape(8, 32, 3584), ("section", "tp"), 0, 0, tiled=True)
    return jnp.sum(parts.astype(f32), axis=0).astype(bf16)[None]


def solution(mesh):
    in_specs = (
        P("section", "blk", None),
        P("section", None),
        P("section", "blk", None),
        P(),
        P(None, "section", "tp"),
        P("tp", "section"),
        P(),
        P(None, ("section", "tp")),
        P(("section", "tp"), None),
    )
    out_specs = P("section", ("blk", "tp"), None)
    return jax.shard_map(on_device, mesh=mesh, in_specs=in_specs, out_specs=out_specs, check_vma=False)
```

time: 656 us -> 240 us (0.37)
  the two profiles are of different devices: /device:TPU:32 before, /device:TPU:8 now
where the time goes in v1:
time: 240 us; the launch traced here: 236 us
  starting transfers between devices  69.3 us (29%)
  waiting for transfers between devices  55.4 us (23%)
  Pallas kernels  44.4 us (18%)
  local copies, waits for them, and re-layouts  30.5 us (13%)
  blocking collectives  24.6 us (10%)
  other arithmetic  11.6 us (5%)
    ppermute x19, starting transfers between devices, section_shift(): return lax.ppermute(value, 'section', route)  47.4 us
    pallas_call x1, Pallas kernels, attention(): call(attention_kernel, jax.ShapeDtypeStruct((ZN, HD, 256), bf16), [SMEM,...  25.2 us
    all_to_all x1, blocking collectives, on_device(): lax.all_to_all(partial.reshape(8, 32, 3584), ('section', 'tp'), 0, 0, til...  24.6 us
    all_to_all x3, waiting for transfers between devices, z_exchange(): lax.all_to_all(value, 'blk', 0, 0, axis_index_groups=Z_GROUPS, tiled=True)  24.3 us
    ppermute x19, waiting for transfers between devices, section_shift(): return lax.ppermute(value, 'section', route)  18.6 us
    all_to_all x3, starting transfers between devices, z_exchange(): lax.all_to_all(value, 'blk', 0, 0, axis_index_groups=Z_GROUPS, tiled=True)  15.5 us
    unnamed x58, local copies, waits for them, and re-layouts  14.3 us
    pallas_call x1, Pallas kernels, on_device(): call(merger_kernel, jax.ShapeDtypeStruct((256, 3584), bf16), [SMEM] + [VM...  7.61 us
  transfers between devices with their start and end apart: 28, of which 10 were waited for; matrix products, arithmetic and copies ran while one was open for 14% of the time, Pallas kernels for 1%

profile of v1, /device:TPU:8, one launch (start us, length us, event | category | flops | bytes accessed | tf_op | source)
XLA Modules:
  0.0 236.2 jit_solution(17074534444092994261)
XLA Ops:
  0.0 1.2 slice.47.own_ref
  1.3 1.6 collective-permute-start.7
  2.9 1.7 collective-permute-start.5
  4.6 9.2 %collective-permute-done.7 = bf16[2,160,640]{2,1,0:T(8,128)(2,1)S(1)} collective-permute-done((bf16[2,160,640]{2,1,0:T(8,128)(2,1)S(1)}, bf16[2,160,640]{2,1,0:T(8,128)(2,1)S(1)}, u32[]{:S(2)}, u32[]{:S(2)}) %collective-permute-start.7) | collective-permute-done | bytes 409632 | tf_op jit(solution)/shard_map/ppermute | solution.py:38
  14.2 3.0 %collective-permute-start.6 = (bf16[2,80,640]{2,1,0:T(8,128)(2,1)S(1)}, bf16[2,80,640]{2,1,0:T(8,128)(2,1)S(1)}, u32[]{:S(2)}, u32[]{:S(2)}) collective-permute-start(bf16[2,80,640]{2,1,0:T(8,128)(2,1)S(1)} %slice.64), channel_id=1, source_target_pairs={{0,192},{64,0},{128,64},{192,128},{1,193},{65,1},{129,65},{193,129... | collective-permute-start | bytes 614408 | tf_op jit(solution)/shard_map/ppermute | solution.py:38
  17.2 3.8 %collective-permute-done.8 = bf16[2,80,640]{2,1,0:T(8,128)(2,1)S(1)} collective-permute-done((bf16[2,80,640]{2,1,0:T(8,128)(2,1)S(1)}, bf16[2,80,640]{2,1,0:T(8,128)(2,1)S(1)}, u32[]{:S(2)}, u32[]{:S(2)}) %collective-permute-start.8) | collective-permute-done | bytes 204832 | tf_op jit(solution)/shard_map/ppermute | solution.py:38
  22.4 1.1 fusion.2.normed_ref
  23.5 1.0 collective-permute-done.9.other_ref
  24.4 4.4 %project.3 = bf16[8,160,256]{2,1,0:T(8,128)(2,1)} custom-call(s32[4]{0:T(128)} %pad_add_fusion.1.place_ref, bf16[256,1280]{1,0:T(8,128)(2,1)} %fusion.2.normed_ref, bf16[2,320,640]{2,1,0:T(8,128)(2,1)} %copy-done.1, bf16[3,2,160,640]{3,2,1,0:T(8,128)(2,1)} %copy-done.2, bf16[3,2,160,640]{3,2,1,0:T(8,128)(2,1)} %collective-permute-done.9.other_ref), custom_call_target="tpu_custom_call" | custom-call | flops 838860800 | bytes 3276800 | tf_op jit(solution)/shard_map/project/pallas_call | solution.py:87
  28.8 8.6 %all-to-all-start.1 = ((bf16[8,160,256]{2,1,0:T(8,128)(2,1)}), bf16[8,160,256]{2,1,0:T(8,128)(2,1)S(1)}, u32[]{:S(2)}, u32[]{:S(2)}) async-start(bf16[8,160,256]{2,1,0:T(8,128)(2,1)} %project.3), calls=%async_computation.1 | async-start | bytes 1310720 | tf_op jit(solution)/shard_map/all_to_all | solution.py:50
  37.4 1.0 slice.44.own_ref
  39.7 2.8 %collective-permute-start = (bf16[1,160,640]{2,1,0:T(8,128)(2,1)}, bf16[1,160,640]{2,1,0:T(8,128)(2,1)S(1)}, u32[]{:S(2)}, u32[]{:S(2)}) collective-permute-start(bf16[1,160,640]{2,1,0:T(8,128)(2,1)} %constant_dynamic-slice_fusion.2), channel_id=1, source_target_pairs={{0,192},{64,0},{128,64},{192,128},{1,193},{65,1},{129,65},{193,129... | collective-permute-start | bytes 614408 | tf_op jit(solution)/shard_map/ppermute | solution.py:38
  42.5 1.9 collective-permute-start.12
  47.7 10.3 %all-to-all-done.1 = bf16[8,160,256]{2,1,0:T(8,128)(2,1)S(1)} async-done(((bf16[8,160,256]{2,1,0:T(8,128)(2,1)}), bf16[8,160,256]{2,1,0:T(8,128)(2,1)S(1)}, u32[]{:S(2)}, u32[]{:S(2)}) %all-to-all-start.1) | async-done | bytes 655392 | tf_op jit(solution)/shard_map/all_to_all | solution.py:50
  61.2 2.8 %collective-permute-start.1 = (bf16[1,80,640]{2,1,0:T(8,128)(2,1)}, bf16[1,80,640]{2,1,0:T(8,128)(2,1)}, u32[]{:S(2)}, u32[]{:S(2)}) collective-permute-start(bf16[1,80,640]{2,1,0:T(8,128)(2,1)} %slice.62), channel_id=1, source_target_pairs={{0,192},{64,0},{128,64},{192,128},{1,193},{65,1},{129,65},{193,129... | collective-permute-start | bytes 307208 | tf_op jit(solution)/shard_map/ppermute | solution.py:38
  65.4 1.3 broadcast_in_dim.6.qframe_ref
  66.8 1.6 collective-permute-start.13
  68.4 0.9 maximum_bitcast_fusion.1
  69.4 5.3 %collective-permute-done.10 = bf16[8,160,256]{2,1,0:T(8,128)(2,1)S(1)} collective-permute-done((bf16[8,160,256]{2,1,0:T(8,128)(2,1)S(1)}, bf16[8,160,256]{2,1,0:T(8,128)(2,1)S(1)}, u32[]{:S(2)}, u32[]{:S(2)}) %collective-permute-start.10) | collective-permute-done | bytes 655392 | tf_op jit(solution)/shard_map/ppermute | solution.py:42
  74.7 1.2 pad_maximum_fusion.1
  77.4 2.0 collective-permute-done.13
  81.7 0.9 copy-done.13
  82.6 3.2 %project.2 = bf16[8,80,256]{2,1,0:T(8,128)(2,1)} custom-call(s32[4]{0:T(128)} %pad_add_fusion.1.place_ref, bf16[256,1280]{1,0:T(8,128)(2,1)} %fusion.2.normed_ref, bf16[1,320,640]{2,1,0:T(8,128)(2,1)} %copy-done.4, bf16[3,1,160,640]{3,2,1,0:T(8,128)(2,1)} %copy-done.5, bf16[3,1,160,640]{3,2,1,0:T(8,128)(2,1)} %copy-done.13), custom_call_target="tpu_custom_call" | custom-call | flops 419430400 | bytes 1638400 | tf_op jit(solution)/shard_map/project/pallas_call | solution.py:87
  85.8 3.4 %all-to-all-start = ((bf16[8,80,256]{2,1,0:T(8,128)(2,1)}), bf16[8,80,256]{2,1,0:T(8,128)(2,1)S(1)}, u32[]{:S(2)}, u32[]{:S(2)}) async-start(bf16[8,80,256]{2,1,0:T(8,128)(2,1)} %project.2), calls=%async_computation | async-start | bytes 655360 | tf_op jit(solution)/shard_map/all_to_all | solution.py:50
  90.0 1.4 fusion.8
  91.4 1.8 pad_maximum_fusion.kv_ref
  93.2 8.1 %all-to-all-done.q_ref = bf16[8,80,256]{2,1,0:T(8,128)(2,1)S(1)} async-done(((bf16[8,80,256]{2,1,0:T(8,128)(2,1)}), bf16[8,80,256]{2,1,0:T(8,128)(2,1)S(1)}, u32[]{:S(2)}, u32[]{:S(2)}) %all-to-all-start) | async-done | bytes 327712 | tf_op jit(solution)/shard_map/all_to_all | solution.py:50
  102.1 25.2 %attention.1 = bf16[8,80,256]{2,1,0:T(8,128)(2,1)} custom-call(s32[4,8]{1,0:T(4,128)} %pad_add_fusion.bounds_ref, s32[4]{0:T(128)} %pad_add_fusion.1.place_ref, s32[8,256,1]{2,1,0:T(8,128)} %broadcast_in_dim.6.qframe_ref, s32[1,8192]{1,0:T(1,128)} %kframe_ref.1, bf16[8,80,256]{2,1,0:T(8,128)(2,1)} %copy-done.19, bf16[4,8,160,256]{3,2,1,0:T(8,128)(2,1)} %pad_maximum_fusion.kv_ref), custom_call_target="tpu_custom_call" | custom-call | flops 8589934592 | bytes 2621440 | tf_op jit(solution)/shard_map/attention/pallas_call | solution.py:157
  127.3 3.4 %all-to-all-start.2 = ((bf16[8,80,256]{2,1,0:T(8,128)(2,1)}), bf16[8,80,256]{2,1,0:T(8,128)(2,1)S(1)}, u32[]{:S(2)}, u32[]{:S(2)}) async-start(bf16[8,80,256]{2,1,0:T(8,128)(2,1)} %attention.1), calls=%async_computation.2 | async-start | bytes 655360 | tf_op jit(solution)/shard_map/all_to_all | solution.py:50
  132.3 1.6 constant_dynamic-slice_fusion
  133.9 2.2 copy.33.weight_ref
  136.1 5.9 %all-to-all-done.2.attn_ref = bf16[8,80,256]{2,1,0:T(8,128)(2,1)S(1)} async-done(((bf16[8,80,256]{2,1,0:T(8,128)(2,1)}), bf16[8,80,256]{2,1,0:T(8,128)(2,1)S(1)}, u32[]{:S(2)}, u32[]{:S(2)}) %all-to-all-start.2) | async-done | bytes 327712 | tf_op jit(solution)/shard_map/all_to_all | solution.py:50
  142.8 4.0 %output.1 = (f32[128,1280]{1,0:T(8,128)}, bf16[128,1280]{1,0:T(8,128)(2,1)}) custom-call(s32[4]{0:T(128)} %pad_add_fusion.1.place_ref, s32[256,1]{1,0:T(8,128)} %reshape.301.order_ref, bf16[256,1280]{1,0:T(8,128)(2,1)} %bitcast.88, bf16[8,80,256]{2,1,0:T(8,128)(2,1)} %copy-done.8, bf16[640,1280]{1,0:T(8,128)(2,1)} %copy.33.weight_ref), custom_call_target="tpu_custom_call" | custom-call | flops 589824000 | bytes 4000000 | tf_op jit(solution)/shard_map/output/pallas_call | solution.py:238
  146.8 2.6 %collective-permute-start.15 = (bf16[128,1280]{1,0:T(8,128)(2,1)}, bf16[128,1280]{1,0:T(8,128)(2,1)S(1)}, u32[]{:S(2)}, u32[]{:S(2)}) collective-permute-start(bf16[128,1280]{1,0:T(8,128)(2,1)} %get-tuple-element.8), channel_id=1, source_target_pairs={{0,1},{1,0},{2,3},{3,2},{4,5},{5,4},{6,7},{7,6},{8,9},{9,8},{10,11... | collective-permute-start | bytes 983048 | tf_op jit(solution)/shard_map/ppermute | solution.py:46
  149.4 6.2 %collective-permute-done.15 = bf16[128,1280]{1,0:T(8,128)(2,1)S(1)} collective-permute-done((bf16[128,1280]{1,0:T(8,128)(2,1)}, bf16[128,1280]{1,0:T(8,128)(2,1)S(1)}, u32[]{:S(2)}, u32[]{:S(2)}) %collective-permute-start.15) | collective-permute-done | bytes 327712 | tf_op jit(solution)/shard_map/ppermute | solution.py:46
  155.6 1.3 multiply_reduce_fusion
  156.8 1.2 multiply_convert_fusion.refs_0_
  158.1 2.7 %collective-permute-start.16 = (bf16[128,1280]{1,0:T(8,128)(2,1)S(1)}, bf16[128,1280]{1,0:T(8,128)(2,1)S(1)}, u32[]{:S(2)}, u32[]{:S(2)}) collective-permute-start(bf16[128,1280]{1,0:T(8,128)(2,1)S(1)} %multiply_convert_fusion.refs_0_), channel_id=1, source_target_pairs={{0,1},{1,0},{2,3},{3,2},{4,5},{5,4},{6,7},{7,6},{8,9},{9,8},{10,11... | collective-permute-start | bytes 983048 | tf_op jit(solution)/shard_map/ppermute | solution.py:46
  160.8 10.9 %collective-permute-start.18 = (bf16[128,1280]{1,0:T(8,128)(2,1)S(1)}, bf16[128,1280]{1,0:T(8,128)(2,1)S(1)}, u32[]{:S(2)}, u32[]{:S(2)}) collective-permute-start(bf16[128,1280]{1,0:T(8,128)(2,1)S(1)} %multiply_convert_fusion.refs_0_), channel_id=1, source_target_pairs={{0,64},{64,128},{128,192},{192,0},{1,65},{65,129},{129,193},{193,1... | collective-permute-start | bytes 983048 | tf_op jit(solution)/shard_map/ppermute | solution.py:38
  171.7 7.0 %collective-permute-start.17 = (bf16[128,1280]{1,0:T(8,128)(2,1)S(1)}, bf16[128,1280]{1,0:T(8,128)(2,1)S(1)}, u32[]{:S(2)}, u32[]{:S(2)}) collective-permute-start(bf16[128,1280]{1,0:T(8,128)(2,1)S(1)} %multiply_convert_fusion.refs_0_), channel_id=1, source_target_pairs={{0,192},{64,0},{128,64},{192,128},{1,193},{65,1},{129,65},{193,129... | collective-permute-start | bytes 983048 | tf_op jit(solution)/shard_map/ppermute | solution.py:38
  178.7 6.7 %collective-permute-start.21 = (bf16[128,1280]{1,0:T(8,128)(2,1)S(1)}, bf16[128,1280]{1,0:T(8,128)(2,1)S(1)}, u32[]{:S(2)}, u32[]{:S(2)}) collective-permute-start(bf16[128,1280]{1,0:T(8,128)(2,1)S(1)} %collective-permute-done.16.refs_1_), channel_id=1, source_target_pairs={{0,192},{64,0},{128,64},{192,128},{1,193},{65,1},{129,65},{193,129... | collective-permute-start | bytes 983048 | tf_op jit(solution)/shard_map/ppermute | solution.py:38
  186.9 2.6 %collective-permute-start.19 = (bf16[64,1280]{1,0:T(8,128)(2,1)}, bf16[64,1280]{1,0:T(8,128)(2,1)}, u32[]{:S(2)}, u32[]{:S(2)}) collective-permute-start(bf16[64,1280]{1,0:T(8,128)(2,1)} %slice.68), channel_id=1, source_target_pairs={{0,192},{64,0},{128,64},{192,128},{1,193},{65,1},{129,65},{193,129... | collective-permute-start | bytes 491528 | tf_op jit(solution)/shard_map/ppermute | solution.py:38
  189.6 3.7 %collective-permute-done.22.refs_7_ = bf16[128,1280]{1,0:T(8,128)(2,1)S(1)} collective-permute-done((bf16[128,1280]{1,0:T(8,128)(2,1)S(1)}, bf16[128,1280]{1,0:T(8,128)(2,1)S(1)}, u32[]{:S(2)}, u32[]{:S(2)}) %collective-permute-start.22) | collective-permute-done | bytes 327712 | tf_op jit(solution)/shard_map/ppermute | solution.py:38
  196.0 3.2 %collective-permute-start.23 = (bf16[64,1280]{1,0:T(8,128)(2,1)}, bf16[64,1280]{1,0:T(8,128)(2,1)}, u32[]{:S(2)}, u32[]{:S(2)}) collective-permute-start(bf16[64,1280]{1,0:T(8,128)(2,1)} %slice.70), channel_id=1, source_target_pairs={{0,192},{64,0},{128,64},{192,128},{1,193},{65,1},{129,65},{193,129... | collective-permute-start | bytes 491528 | tf_op jit(solution)/shard_map/ppermute | solution.py:38
  199.3 3.7 %copy.34.refs_10_ = bf16[5120,320]{1,0:T(8,128)(2,1)} copy(bf16[5120,320]{0,1:T(8,128)(2,1)S(1)} %copy-done.3) | data formatting | bytes 6553600 | tf_op args[7]
  203.0 7.6 %merger.1 = bf16[256,3584]{1,0:T(8,128)(2,1)} custom-call(s32[4]{0:T(128)} %pad_add_fusion.1.place_ref, bf16[128,1280]{1,0:T(8,128)(2,1)} %copy-done.7, bf16[128,1280]{1,0:T(8,128)(2,1)} %copy-done.18, bf16[128,1280]{1,0:T(8,128)(2,1)} %copy-done.10, bf16[128,1280]{1,0:T(8,128)(2,1)} %copy-done.9, bf16[64,1280]{1,0:T(8,128)(2,1)} %collective-permute-done.19.refs_4_, ...), custom_call_target="tpu_custom_call" | custom-call | flops 1426063360 | bytes 9000000 | tf_op jit(solution)/shard_map/merger/pallas_call | solution.py:252
  210.6 24.6 %all_to_all.20 = bf16[8,32,3584]{2,1,0:T(8,128)(2,1)S(1)} all-to-all(bf16[8,32,3584]{2,1,0:T(8,128)(2,1)} %bitcast.84), channel_id=1, replica_groups=mesh['section'=4,'blk'=32,'tp'=2] {'section','tp'}, dimensions={0} | all-to-all | bytes 3670016 | tf_op jit(solution)/shard_map/all_to_all | solution.py:261
  235.2 1.0 reduce_sum.42
  (118 shorter events, 23.0 us)
Async XLA Ops:
  1.2 21.1 %copy-start.1 = (bf16[2,320,640]{2,1,0:T(8,128)(2,1)}, bf16[2,320,640]{2,1,0:T(8,128)(2,1)S(1)}, u32[]{:S(2)}) copy-start(bf16[2,320,640]{2,1,0:T(8,128)(2,1)S(1)} %slice.47.own_ref) | copy-start | bytes 2457604
  1.2 20.9 %copy-start = (bf16[1,256,1280]{2,1,0:T(8,128)(2,1)S(1)}, bf16[1,256,1280]{2,1,0:T(8,128)(2,1)}, u32[]{:S(2)}) copy-start(bf16[1,256,1280]{2,1,0:T(8,128)(2,1)} %param.9) | copy-start | bytes 1966084
  1.2 21.1 %copy-start.21 = (f32[1280]{0:T(1024)S(1)}, f32[1280]{0:T(1024)}, u32[]{:S(2)}) copy-start(f32[1280]{0:T(1024)} %param.12) | copy-start | bytes 15364
  1.3 12.5 %collective-permute-start.7 = (bf16[2,160,640]{2,1,0:T(8,128)(2,1)S(1)}, bf16[2,160,640]{2,1,0:T(8,128)(2,1)S(1)}, u32[]{:S(2)}, u32[]{:S(2)}) collective-permute-start(bf16[2,160,640]{2,1,0:T(8,128)(2,1)S(1)} %constant_dynamic-slice_fusion.1), channel_id=1, source_target_pairs={{0,64},{64,128},{128,192},{192,0},{1,65},{65,129},{129,193},{193,1... | collective-permute-start | bytes 1228808 | tf_op jit(solution)/shard_map/ppermute | solution.py:38
  2.9 11.3 %collective-permute-start.5 = (bf16[2,160,640]{2,1,0:T(8,128)(2,1)S(1)}, bf16[2,160,640]{2,1,0:T(8,128)(2,1)S(1)}, u32[]{:S(2)}, u32[]{:S(2)}) collective-permute-start(bf16[2,160,640]{2,1,0:T(8,128)(2,1)S(1)} %constant_dynamic-slice_fusion.1), channel_id=1, source_target_pairs={{0,192},{64,0},{128,64},{192,128},{1,193},{65,1},{129,65},{193,129... | collective-permute-start | bytes 1228808 | tf_op jit(solution)/shard_map/ppermute | solution.py:38
  13.8 7.2 %collective-permute-start.8 = (bf16[2,80,640]{2,1,0:T(8,128)(2,1)S(1)}, bf16[2,80,640]{2,1,0:T(8,128)(2,1)S(1)}, u32[]{:S(2)}, u32[]{:S(2)}) collective-permute-start(bf16[2,80,640]{2,1,0:T(8,128)(2,1)S(1)} %slice.65), channel_id=1, source_target_pairs={{0,64},{64,128},{128,192},{192,0},{1,65},{65,129},{129,193},{193,1... | collective-permute-start | bytes 614408 | tf_op jit(solution)/shard_map/ppermute | solution.py:38
  14.2 6.9 %collective-permute-start.6 = (bf16[2,80,640]{2,1,0:T(8,128)(2,1)S(1)}, bf16[2,80,640]{2,1,0:T(8,128)(2,1)S(1)}, u32[]{:S(2)}, u32[]{:S(2)}) collective-permute-start(bf16[2,80,640]{2,1,0:T(8,128)(2,1)S(1)} %slice.64), channel_id=1, source_target_pairs={{0,192},{64,0},{128,64},{192,128},{1,193},{65,1},{129,65},{193,129... | collective-permute-start | bytes 614408 | tf_op jit(solution)/shard_map/ppermute | solution.py:38
  21.3 3.1 %copy-start.2 = (bf16[3,2,160,640]{3,2,1,0:T(8,128)(2,1)}, bf16[3,2,160,640]{3,2,1,0:T(8,128)(2,1)S(1)}, u32[]{:S(2)}) copy-start(bf16[3,2,160,640]{3,2,1,0:T(8,128)(2,1)S(1)} %pad_maximum_fusion.2.mine_ref) | copy-start | bytes 3686404
  21.3 3.1 %collective-permute-start.9 = (bf16[3,2,160,640]{3,2,1,0:T(8,128)(2,1)S(1)}, bf16[3,2,160,640]{3,2,1,0:T(8,128)(2,1)}, u32[]{:S(2)}, u32[]{:S(2)}) collective-permute-start(bf16[3,2,160,640]{3,2,1,0:T(8,128)(2,1)S(1)} %pad_maximum_fusion.2.mine_ref), channel_id=1, source_target_pairs={{0,2},{2,0},{4,6},{6,4},{8,10},{10,8},{12,14},{14,12},{16,18},{18,... | collective-permute-start | bytes 3686408 | tf_op jit(solution)/shard_map/ppermute | solution.py:42
  23.5 19.0 %copy-start.6 = (bf16[640,320]{0,1:T(8,128)(2,1)S(1)}, bf16[640,320]{0,1:T(8,128)(2,1)}, u32[]{:S(2)}) copy-start(bf16[640,320]{0,1:T(8,128)(2,1)} %param.14) | copy-start | bytes 1228804
  23.5 21.6 %copy-start.20 = (s32[1,8192]{1,0:T(1,128)S(1)}, s32[1,8192]{1,0:T(1,128)}, u32[]{:S(2)}) copy-start(s32[1,8192]{1,0:T(1,128)} %kframe_ref.1) | copy-start | bytes 98308
  28.8 35.7 %copy-start.23 = (s32[1,64,4]{1,2,0:T(4,128)S(1)}, s32[1,64,4]{1,2,0:T(4,128)}, u32[]{:S(2)}) copy-start(s32[1,64,4]{1,2,0:T(4,128)} %param.11) | copy-start | bytes 3076
  28.8 29.2 %all-to-all-start.1 = ((bf16[8,160,256]{2,1,0:T(8,128)(2,1)}), bf16[8,160,256]{2,1,0:T(8,128)(2,1)S(1)}, u32[]{:S(2)}, u32[]{:S(2)}) async-start(bf16[8,160,256]{2,1,0:T(8,128)(2,1)} %project.3), calls=%async_computation.1 | async-start | bytes 1310720 | tf_op jit(solution)/shard_map/all_to_all | solution.py:50
  38.4 37.4 %copy-start.4 = (bf16[1,320,640]{2,1,0:T(8,128)(2,1)}, bf16[1,320,640]{2,1,0:T(8,128)(2,1)S(1)}, u32[]{:S(2)}) copy-start(bf16[1,320,640]{2,1,0:T(8,128)(2,1)S(1)} %slice.44.own_ref) | copy-start | bytes 1228804
  39.2 20.0 %collective-permute-start.2 = (bf16[1,160,640]{2,1,0:T(8,128)(2,1)}, bf16[1,160,640]{2,1,0:T(8,128)(2,1)S(1)}, u32[]{:S(2)}, u32[]{:S(2)}) collective-permute-start(bf16[1,160,640]{2,1,0:T(8,128)(2,1)} %constant_dynamic-slice_fusion.2), channel_id=1, source_target_pairs={{0,64},{64,128},{128,192},{192,0},{1,65},{65,129},{129,193},{193,1... | collective-permute-start | bytes 614408 | tf_op jit(solution)/shard_map/ppermute | solution.py:38
  39.7 20.8 %collective-permute-start = (bf16[1,160,640]{2,1,0:T(8,128)(2,1)}, bf16[1,160,640]{2,1,0:T(8,128)(2,1)S(1)}, u32[]{:S(2)}, u32[]{:S(2)}) collective-permute-start(bf16[1,160,640]{2,1,0:T(8,128)(2,1)} %constant_dynamic-slice_fusion.2), channel_id=1, source_target_pairs={{0,192},{64,0},{128,64},{192,128},{1,193},{65,1},{129,65},{193,129... | collective-permute-start | bytes 614408 | tf_op jit(solution)/shard_map/ppermute | solution.py:38
  42.5 34.1 %collective-permute-start.12 = (bf16[640,320]{0,1:T(8,128)(2,1)S(1)}, bf16[640,320]{0,1:T(8,128)(2,1)S(1)}, u32[]{:S(2)}, u32[]{:S(2)}) collective-permute-start(bf16[640,320]{0,1:T(8,128)(2,1)S(1)} %copy-done.6), channel_id=1, source_target_pairs={{0,192},{64,0},{128,64},{192,128},{1,193},{65,1},{129,65},{193,129... | collective-permute-start | bytes 1228808 | tf_op jit(solution)/shard_map/ppermute | solution.py:38
  44.4 35.7 %collective-permute-start.14 = (bf16[640,320]{0,1:T(8,128)(2,1)S(1)}, bf16[640,320]{0,1:T(8,128)(2,1)S(1)}, u32[]{:S(2)}, u32[]{:S(2)}) collective-permute-start(bf16[640,320]{0,1:T(8,128)(2,1)S(1)} %copy-done.6), channel_id=1, source_target_pairs={{0,64},{64,128},{128,192},{192,0},{1,65},{65,129},{129,193},{193,1... | collective-permute-start | bytes 1228808 | tf_op jit(solution)/shard_map/ppermute | solution.py:38
  58.0 16.7 %collective-permute-start.10 = (bf16[8,160,256]{2,1,0:T(8,128)(2,1)S(1)}, bf16[8,160,256]{2,1,0:T(8,128)(2,1)S(1)}, u32[]{:S(2)}, u32[]{:S(2)}) collective-permute-start(bf16[8,160,256]{2,1,0:T(8,128)(2,1)S(1)} %all-to-all-done.1), channel_id=1, source_target_pairs={{0,32},{2,34},{4,36},{6,38},{8,40},{10,42},{12,44},{14,46},{16,48}... | collective-permute-start | bytes 1966088 | tf_op jit(solution)/shard_map/ppermute | solution.py:42
  59.3 7.5 %copy-start.14 = (bf16[1,160,640]{2,1,0:T(8,128)(2,1)}, bf16[1,160,640]{2,1,0:T(8,128)(2,1)S(1)}, u32[]{:S(2)}) copy-start(bf16[1,160,640]{2,1,0:T(8,128)(2,1)S(1)} %collective-permute-done.2) | copy-start | bytes 614404
  60.0 6.8 %collective-permute-start.3 = (bf16[1,80,640]{2,1,0:T(8,128)(2,1)}, bf16[1,80,640]{2,1,0:T(8,128)(2,1)S(1)}, u32[]{:S(2)}, u32[]{:S(2)}) collective-permute-start(bf16[1,80,640]{2,1,0:T(8,128)(2,1)} %slice.63), channel_id=1, source_target_pairs={{0,64},{64,128},{128,192},{192,0},{1,65},{65,129},{129,193},{193,1... | collective-permute-start | bytes 307208 | tf_op jit(solution)/shard_map/ppermute | solution.py:38
  60.5 6.3 %copy-start.16 = (bf16[1,160,640]{2,1,0:T(8,128)(2,1)}, bf16[1,160,640]{2,1,0:T(8,128)(2,1)S(1)}, u32[]{:S(2)}) copy-start(bf16[1,160,640]{2,1,0:T(8,128)(2,1)S(1)} %collective-permute-done) | copy-start | bytes 614404
  61.2 7.2 %collective-permute-start.1 = (bf16[1,80,640]{2,1,0:T(8,128)(2,1)}, bf16[1,80,640]{2,1,0:T(8,128)(2,1)}, u32[]{:S(2)}, u32[]{:S(2)}) collective-permute-start(bf16[1,80,640]{2,1,0:T(8,128)(2,1)} %slice.62), channel_id=1, source_target_pairs={{0,192},{64,0},{128,64},{192,128},{1,193},{65,1},{129,65},{193,129... | collective-permute-start | bytes 307208 | tf_op jit(solution)/shard_map/ppermute | solution.py:38
  66.8 9.1 %copy-start.15 = (bf16[1,160,640]{2,1,0:T(8,128)(2,1)S(1)}, bf16[1,160,640]{2,1,0:T(8,128)(2,1)}, u32[]{:S(2)}) copy-start(bf16[1,160,640]{2,1,0:T(8,128)(2,1)} %copy-done.14) | copy-start | bytes 614404
  66.8 9.1 %copy-start.17 = (bf16[1,160,640]{2,1,0:T(8,128)(2,1)S(1)}, bf16[1,160,640]{2,1,0:T(8,128)(2,1)}, u32[]{:S(2)}) copy-start(bf16[1,160,640]{2,1,0:T(8,128)(2,1)} %copy-done.16) | copy-start | bytes 614404
  66.8 12.5 %collective-permute-start.13 = (bf16[640,320]{0,1:T(8,128)(2,1)S(1)}, bf16[640,320]{0,1:T(8,128)(2,1)S(1)}, u32[]{:S(2)}, u32[]{:S(2)}) collective-permute-start(bf16[640,320]{0,1:T(8,128)(2,1)S(1)} %copy-done.6), channel_id=1, source_target_pairs={{0,128},{64,192},{128,0},{192,64},{1,129},{65,193},{129,1},{193,65... | collective-permute-start | bytes 1228808 | tf_op jit(solution)/shard_map/ppermute | solution.py:38
  75.9 14.2 %collective-permute-start.11 = (bf16[2,8,160,256]{3,2,1,0:T(8,128)(2,1)}, bf16[2,8,160,256]{3,2,1,0:T(8,128)(2,1)}, u32[]{:S(2)}, u32[]{:S(2)}) collective-permute-start(bf16[2,8,160,256]{3,2,1,0:T(8,128)(2,1)} %pad_maximum_fusion.1), channel_id=1, source_target_pairs={{0,2},{2,0},{4,6},{6,4},{8,10},{10,8},{12,14},{14,12},{16,18},{18,... | collective-permute-start | bytes 3932168 | tf_op jit(solution)/shard_map/ppermute | solution.py:42
  76.0 5.7 %copy-start.5 = (bf16[3,1,160,640]{3,2,1,0:T(8,128)(2,1)}, bf16[3,1,160,640]{3,2,1,0:T(8,128)(2,1)S(1)}, u32[]{:S(2)}) copy-start(bf16[3,1,160,640]{3,2,1,0:T(8,128)(2,1)S(1)} %pad_maximum_fusion.3.mine_ref) | copy-start | bytes 1843204
  76.0 5.7 %collective-permute-start.4 = (bf16[3,1,160,640]{3,2,1,0:T(8,128)(2,1)S(1)}, bf16[3,1,160,640]{3,2,1,0:T(8,128)(2,1)S(1)}, u32[]{:S(2)}, u32[]{:S(2)}) collective-permute-start(bf16[3,1,160,640]{3,2,1,0:T(8,128)(2,1)S(1)} %pad_maximum_fusion.3.mine_ref), channel_id=1, source_target_pairs={{0,2},{2,0},{4,6},{6,4},{8,10},{10,8},{12,14},{14,12},{16,18},{18,... | collective-permute-start | bytes 1843208 | tf_op jit(solution)/shard_map/ppermute | solution.py:42
  81.7 0.9 copy-start.13
  85.8 15.5 %all-to-all-start = ((bf16[8,80,256]{2,1,0:T(8,128)(2,1)}), bf16[8,80,256]{2,1,0:T(8,128)(2,1)S(1)}, u32[]{:S(2)}, u32[]{:S(2)}) async-start(bf16[8,80,256]{2,1,0:T(8,128)(2,1)} %project.2), calls=%async_computation | async-start | bytes 655360 | tf_op jit(solution)/shard_map/all_to_all | solution.py:50
  127.3 14.8 %all-to-all-start.2 = ((bf16[8,80,256]{2,1,0:T(8,128)(2,1)}), bf16[8,80,256]{2,1,0:T(8,128)(2,1)S(1)}, u32[]{:S(2)}, u32[]{:S(2)}) async-start(bf16[8,80,256]{2,1,0:T(8,128)(2,1)} %attention.1), calls=%async_computation.2 | async-start | bytes 655360 | tf_op jit(solution)/shard_map/all_to_all | solution.py:50
  136.1 20.7 %copy-start.22 = (f32[1280]{0:T(1024)S(1)}, f32[1280]{0:T(1024)}, u32[]{:S(2)}) copy-start(f32[1280]{0:T(1024)} %param.15) | copy-start | bytes 15364
  142.1 0.7 copy-start.8
  142.8 56.5 %copy-start.3 = (bf16[5120,320]{0,1:T(8,128)(2,1)S(1)}, bf16[5120,320]{0,1:T(8,128)(2,1)}, u32[]{:S(2)}) copy-start(bf16[5120,320]{0,1:T(8,128)(2,1)} %param.16) | copy-start | bytes 9830404
  146.8 8.8 %collective-permute-start.15 = (bf16[128,1280]{1,0:T(8,128)(2,1)}, bf16[128,1280]{1,0:T(8,128)(2,1)S(1)}, u32[]{:S(2)}, u32[]{:S(2)}) collective-permute-start(bf16[128,1280]{1,0:T(8,128)(2,1)} %get-tuple-element.8), channel_id=1, source_target_pairs={{0,1},{1,0},{2,3},{3,2},{4,5},{5,4},{6,7},{7,6},{8,9},{9,8},{10,11... | collective-permute-start | bytes 983048 | tf_op jit(solution)/shard_map/ppermute | solution.py:46
  158.1 13.6 %copy-start.7 = (bf16[128,1280]{1,0:T(8,128)(2,1)}, bf16[128,1280]{1,0:T(8,128)(2,1)S(1)}, u32[]{:S(2)}) copy-start(bf16[128,1280]{1,0:T(8,128)(2,1)S(1)} %multiply_convert_fusion.refs_0_) | copy-start | bytes 983044
  158.1 20.6 %collective-permute-start.16 = (bf16[128,1280]{1,0:T(8,128)(2,1)S(1)}, bf16[128,1280]{1,0:T(8,128)(2,1)S(1)}, u32[]{:S(2)}, u32[]{:S(2)}) collective-permute-start(bf16[128,1280]{1,0:T(8,128)(2,1)S(1)} %multiply_convert_fusion.refs_0_), channel_id=1, source_target_pairs={{0,1},{1,0},{2,3},{3,2},{4,5},{5,4},{6,7},{7,6},{8,9},{9,8},{10,11... | collective-permute-start | bytes 983048 | tf_op jit(solution)/shard_map/ppermute | solution.py:46
  160.8 24.6 %collective-permute-start.18 = (bf16[128,1280]{1,0:T(8,128)(2,1)S(1)}, bf16[128,1280]{1,0:T(8,128)(2,1)S(1)}, u32[]{:S(2)}, u32[]{:S(2)}) collective-permute-start(bf16[128,1280]{1,0:T(8,128)(2,1)S(1)} %multiply_convert_fusion.refs_0_), channel_id=1, source_target_pairs={{0,64},{64,128},{128,192},{192,0},{1,65},{65,129},{129,193},{193,1... | collective-permute-start | bytes 983048 | tf_op jit(solution)/shard_map/ppermute | solution.py:38
  171.7 13.8 %collective-permute-start.17 = (bf16[128,1280]{1,0:T(8,128)(2,1)S(1)}, bf16[128,1280]{1,0:T(8,128)(2,1)S(1)}, u32[]{:S(2)}, u32[]{:S(2)}) collective-permute-start(bf16[128,1280]{1,0:T(8,128)(2,1)S(1)} %multiply_convert_fusion.refs_0_), channel_id=1, source_target_pairs={{0,192},{64,0},{128,64},{192,128},{1,193},{65,1},{129,65},{193,129... | collective-permute-start | bytes 983048 | tf_op jit(solution)/shard_map/ppermute | solution.py:38
  178.7 17.3 %copy-start.18 = (bf16[128,1280]{1,0:T(8,128)(2,1)}, bf16[128,1280]{1,0:T(8,128)(2,1)S(1)}, u32[]{:S(2)}) copy-start(bf16[128,1280]{1,0:T(8,128)(2,1)S(1)} %collective-permute-done.16.refs_1_) | copy-start | bytes 983044
  178.7 14.5 %collective-permute-start.22 = (bf16[128,1280]{1,0:T(8,128)(2,1)S(1)}, bf16[128,1280]{1,0:T(8,128)(2,1)S(1)}, u32[]{:S(2)}, u32[]{:S(2)}) collective-permute-start(bf16[128,1280]{1,0:T(8,128)(2,1)S(1)} %collective-permute-done.16.refs_1_), channel_id=1, source_target_pairs={{0,64},{64,128},{128,192},{192,0},{1,65},{65,129},{129,193},{193,1... | collective-permute-start | bytes 983048 | tf_op jit(solution)/shard_map/ppermute | solution.py:38
  178.7 15.9 %collective-permute-start.21 = (bf16[128,1280]{1,0:T(8,128)(2,1)S(1)}, bf16[128,1280]{1,0:T(8,128)(2,1)S(1)}, u32[]{:S(2)}, u32[]{:S(2)}) collective-permute-start(bf16[128,1280]{1,0:T(8,128)(2,1)S(1)} %collective-permute-done.16.refs_1_), channel_id=1, source_target_pairs={{0,192},{64,0},{128,64},{192,128},{1,193},{65,1},{129,65},{193,129... | collective-permute-start | bytes 983048 | tf_op jit(solution)/shard_map/ppermute | solution.py:38
  185.4 17.5 %collective-permute-start.20 = (bf16[64,1280]{1,0:T(8,128)(2,1)S(1)}, bf16[64,1280]{1,0:T(8,128)(2,1)}, u32[]{:S(2)}, u32[]{:S(2)}) collective-permute-start(bf16[64,1280]{1,0:T(8,128)(2,1)S(1)} %slice.69), channel_id=1, source_target_pairs={{0,64},{64,128},{128,192},{192,0},{1,65},{65,129},{129,193},{193,1... | collective-permute-start | bytes 491528 | tf_op jit(solution)/shard_map/ppermute | solution.py:38
  186.1 0.8 copy-start.10
  186.9 16.0 %collective-permute-start.19 = (bf16[64,1280]{1,0:T(8,128)(2,1)}, bf16[64,1280]{1,0:T(8,128)(2,1)}, u32[]{:S(2)}, u32[]{:S(2)}) collective-permute-start(bf16[64,1280]{1,0:T(8,128)(2,1)} %slice.68), channel_id=1, source_target_pairs={{0,192},{64,0},{128,64},{192,128},{1,193},{65,1},{129,65},{193,129... | collective-permute-start | bytes 491528 | tf_op jit(solution)/shard_map/ppermute | solution.py:38
  194.6 8.3 %collective-permute-start.24 = (bf16[64,1280]{1,0:T(8,128)(2,1)}, bf16[64,1280]{1,0:T(8,128)(2,1)}, u32[]{:S(2)}, u32[]{:S(2)}) collective-permute-start(bf16[64,1280]{1,0:T(8,128)(2,1)} %slice.71), channel_id=1, source_target_pairs={{0,64},{64,128},{128,192},{192,0},{1,65},{65,129},{129,193},{193,1... | collective-permute-start | bytes 491528 | tf_op jit(solution)/shard_map/ppermute | solution.py:38
  196.0 6.9 %collective-permute-start.23 = (bf16[64,1280]{1,0:T(8,128)(2,1)}, bf16[64,1280]{1,0:T(8,128)(2,1)}, u32[]{:S(2)}, u32[]{:S(2)}) collective-permute-start(bf16[64,1280]{1,0:T(8,128)(2,1)} %slice.70), channel_id=1, source_target_pairs={{0,192},{64,0},{128,64},{192,128},{1,193},{65,1},{129,65},{193,129... | collective-permute-start | bytes 491528 | tf_op jit(solution)/shard_map/ppermute | solution.py:38
  (4 other events, 2.9 us)

commit v2 on v1

--- a/solution.py
+++ b/solution.py
@@ -63,7 +63,7 @@
     return right, left, opposite_a, opposite_b
 
 
-def project_kernel(count, place_ref, normed_ref, own_ref, mine_ref, other_ref, out_ref, weight):
+def project_kernel(scale, count, place_ref, normed_ref, own_ref, mine_ref, other_ref, out_ref, weight):
     me, core = place_ref[0], place_ref[1]
     row = lambda section, half: pl.ds(pl.multiple_of(section * 320 + half * 160, 16), 160)
     for t in range(count):
@@ -73,19 +73,19 @@
                 section = lax.rem(me + k + 1, SECTIONS)
                 weight[t, row(section, half), :] = source[k, t]
         made = jnp.dot(normed_ref[...], weight[t], preferred_element_type=f32)
-        turned = made.T.astype(bf16)
+        turned = (made * scale).T.astype(bf16)
         for h in range(ZN):
             out_ref[h, t * HD : (t + 1) * HD, :] = turned[h * HD : (h + 1) * HD, :]
 
 
-def project(place, normed, own, core):
+def project(place, normed, own, core, scale):
     count = own.shape[0]
     half = lax.dynamic_slice_in_dim(own, core * 160, 160, axis=1)
     right, left, opp_a, opp_b = ring_halves(half)
     mine = jnp.stack([right, jnp.concatenate([opp_a, opp_b], axis=1), left])
     other = blk_swap(mine, 1)
     return call(
-        functools.partial(project_kernel, count),
+        functools.partial(project_kernel, scale, count),
         jax.ShapeDtypeStruct((ZN, count * HD, 256), bf16),
         [SMEM] + [VMEM] * 4,
         [pltpu.VMEM((count, 1280, 640), bf16)],
@@ -95,44 +95,61 @@
     )(place, normed, own, mine, other)
 
 
-def attention_kernel(bounds_ref, place_ref, qframe_ref, kframe_ref, q_ref, kv_ref, out_ref, keys, values):
+def attention_kernel(bounds_ref, place_ref, qframe_ref, kframe_ref, q_ref, own, near, far, across, out_ref, keys, values, held):
     y, core = place_ref[2], place_ref[1]
-    scale = HD ** (-0.5) * math.log2(math.e)
     filler = (lax.broadcasted_iota(jnp.int32, (48, 256), 0) == 0).astype(f32).astype(bf16)
-
-    def arrange(step, carry):
-        which, z = step // ZN, lax.rem(step, ZN)
-        y_of = jnp.bitwise_xor(y, which // 2)
-        core_of = jnp.bitwise_xor(core, lax.rem(which, 2))
-        place = pl.multiple_of((y_of * 16 + z * 2 + core_of) * 256, 256)
-        keys[:, pl.ds(place, 256)] = kv_ref[which, z, :HD, :]
-        padded = jnp.concatenate([kv_ref[which, z, HD:, :], filler], axis=0)
-        values[pl.ds(place, 256), :] = padded.T
-        return carry
-
-    lax.fori_loop(0, 4 * ZN, arrange, 0)
+    frame = lax.broadcasted_iota(jnp.int32, (16, 256), 0)
+
+    def arrange(z, unused):
+        for which, source in enumerate((own, near, far, across)):
+            y_of = jnp.bitwise_xor(y, which // 2)
+            core_of = jnp.bitwise_xor(core, which % 2)
+            place = pl.ds(pl.multiple_of((y_of * 16 + z * 2 + core_of) * 256, 256), 256)
+            keys[:HD, place] = source[z, :HD, :]
+            other = (frame < 4) & (frame != kframe_ref[:, place])
+            keys[HD:, place] = jnp.where(other, -1e30, 0.0).astype(bf16)
+            values[place, :] = jnp.concatenate([source[z, HD:, :], filler], axis=0).T
+        return unused
+
+    lax.fori_loop(0, ZN, arrange, 0)
 
     def one_block(block, unused):
-        query = q_ref[block].T
-        qframe = qframe_ref[block]
-
-        def step(masked, index, carry):
+        tag = (frame == qframe_ref[pl.ds(block, 1), :]).astype(f32).astype(bf16)
+        query = jnp.concatenate([q_ref[block], tag], axis=0).T
+        first, last = bounds_ref[0, block], bounds_ref[1, block]
+
+        def part(index):
+            return pl.ds(pl.multiple_of(index * KB, KB), KB)
+
+        def scores_of(index):
+            return jnp.dot(query, keys[:, part(index)], preferred_element_type=f32)
+
+        def absorb(scores, index, carry):
             top, accum = carry
-            start = pl.multiple_of(index * KB, KB)
-            scores = jnp.dot(query, keys[:, pl.ds(start, KB)], preferred_element_type=f32)
-            if masked:
-                scores = jnp.where(qframe == kframe_ref[:, pl.ds(start, KB)], scores, -1e30)
             new_top = jnp.maximum(top, jnp.max(scores, axis=1, keepdims=True))
-            weights = jnp.exp2((scores - new_top) * scale)
-            factor = jnp.exp2((top - new_top) * scale)
-            product = jnp.dot(weights.astype(bf16), values[pl.ds(start, KB), :], preferred_element_type=f32)
-            return new_top, accum * factor + product
-
-        first, inner, outer, last = (bounds_ref[k, block] for k in range(4))
+            weights = jnp.exp2(scores - new_top).astype(bf16)
+            product = jnp.dot(weights, values[part(index), :], preferred_element_type=f32)
+            return new_top, accum * jnp.exp2(top - new_top) + product
+
+        def run(length, start, count, carry):
+            def body(step, carry):
+                index = start + length * step
+                for k in range(length):
+                    scores = held[k % 2]
+                    held[(k + 1) % 2] = scores_of(jnp.minimum(index + k + 1, last - 1))
+                    carry = absorb(scores, index + k, carry)
+                return carry
+
+            return lax.fori_loop(0, count, body, carry)
+
+        held[0] = scores_of(first)
         carry = (jnp.full((256, 1), -1e30, f32), jnp.zeros((256, 128), f32))
-        carry = lax.fori_loop(first, inner, functools.partial(step, True), carry)
-        carry = lax.fori_loop(inner, outer, functools.partial(step, False), carry)
-        carry = lax.fori_loop(outer, last, functools.partial(step, True), carry)
+        fours = (last - first) // 4
+        carry = run(4, first, fours, carry)
+        rest = first + 4 * fours
+        twos = (last - rest) // 2
+        carry = run(2, rest, twos, carry)
+        carry = lax.fori_loop(rest + 2 * twos, last, lambda index, c: absorb(held[0], index, c), carry)
         accum = carry[1]
         result = accum / accum[:, HD : HD + 1]
         out_ref[block] = result.T[:HD, :].astype(bf16)
@@ -141,28 +158,21 @@
     lax.fori_loop(0, ZN, one_block, 0)
 
 
-def attention(place, frames, q, kv, y, core):
+def attention(place, frames, q, sources, y, core):
     ends = jnp.sum((frames[None, :] <= jnp.arange(-1, 4)[:, None]).astype(jnp.int32), axis=1)
     grid = frames.reshape(2, ZN, 2, 256)
     mine = lax.dynamic_index_in_dim(lax.dynamic_index_in_dim(grid, y, 0, False), core, 1, False)
-    low, high = mine[:, 0], mine[:, -1]
-    start, stop = ends[low], ends[high + 1]
-    single = low == high
-    first, last = start // KB, (stop + KB - 1) // KB
-    inner = jnp.where(single, (start + KB - 1) // KB, last)
-    outer = jnp.where(single, stop // KB, last)
-    inner = jnp.minimum(inner, last)
-    outer = jnp.maximum(outer, inner)
-    bounds = jnp.stack([first, inner, outer, last]).astype(jnp.int32)
+    start, stop = ends[mine[:, 0]], ends[mine[:, -1] + 1]
+    bounds = jnp.stack([start // KB, (stop + KB - 1) // KB]).astype(jnp.int32)
     return call(
         attention_kernel,
         jax.ShapeDtypeStruct((ZN, HD, 256), bf16),
-        [SMEM, SMEM] + [VMEM] * 4,
-        [pltpu.VMEM((HD, 8192), bf16), pltpu.VMEM((8192, 128), bf16)],
+        [SMEM, SMEM] + [VMEM] * 7,
+        [pltpu.VMEM((HD + 16, 8192), bf16), pltpu.VMEM((8192, 128), bf16), pltpu.VMEM((2, 256, KB), f32)],
         flops=4 * 2048 * 4096 * 256,
         moved=4 * 8192 * HD,
         name="attention",
-    )(bounds, place, mine[:, :, None], frames[None, :], q, kv)
+    )(bounds, place, mine, frames[None, :], q, *sources)
 
 
 def output_kernel(place_ref, order_ref, patch_ref, attn_ref, weight_ref, base_ref, send_ref):
@@ -221,19 +231,21 @@
     patch = patches[0]
     normed = rms_norm(patch.astype(f32), norm_gain).astype(bf16)
 
-    kv = z_exchange(project(place, normed, qkv_weight[1:3], core))
-    q = z_exchange(project(place, normed, qkv_weight[0:1], core))
-
+    kv = z_exchange(project(place, normed, qkv_weight[1:3], core, 1.0))
+    q = project(place, normed, qkv_weight[0:1], core, HD ** (-0.5) * math.log2(math.e))
+    kv, q = lax.optimization_barrier((kv, q))
     far = blk_swap(kv, 16)
-    pair = jnp.stack([kv, far])
-    across = blk_swap(pair, 1)
-    kv_all = jnp.stack([kv, across[0], far, across[1]])
-
-    attn = z_exchange(attention(place, frame_ids[0], q, kv_all, y, core))
+    near = blk_swap(kv, 1)
+    q = z_exchange(q)
+    across = blk_swap(far, 1)
 
     pieces = jnp.stack([out_weight] + [section_shift(out_weight, -d) for d in (1, 2, 3)])
     turned = jnp.roll(pieces, me, axis=0)
     whole = turned.transpose(1, 0, 2).reshape(640, 1280)
+    across, whole = lax.optimization_barrier((across, whole))
+
+    attn = z_exchange(attention(place, frame_ids[0], q, (kv, near, far, across), y, core))
+
     order = groups[0].reshape(2, 32, 4).transpose(0, 2, 1).reshape(256, 1)
     base, send = call(
         output_kernel,

time: 240 us -> 239 us (level)
  the two profiles are of different devices: /device:TPU:8 before, /device:TPU:32 now
where the time goes in v2:
time: 239 us; the launch traced here: 238 us
  waiting for transfers between devices  79.2 us (33%)
  starting transfers between devices  53.4 us (22%)
  Pallas kernels  38.1 us (16%)
  local copies, waits for them, and re-layouts  30.4 us (13%)
  blocking collectives  24.9 us (10%)
  other arithmetic  11.5 us (5%)
    ppermute x19, waiting for transfers between devices, section_shift(): return lax.ppermute(value, 'section', route)  32.6 us
    all_to_all x1, blocking collectives, on_device(): lax.all_to_all(partial.reshape(8, 32, 3584), ('section', 'tp'), 0, 0, til...  24.9 us
    ppermute x19, starting transfers between devices, section_shift(): return lax.ppermute(value, 'section', route)  23.7 us
    all_to_all x3, starting transfers between devices, z_exchange(): lax.all_to_all(value, 'blk', 0, 0, axis_index_groups=Z_GROUPS, tiled=True)  21.2 us
    all_to_all x3, waiting for transfers between devices, z_exchange(): lax.all_to_all(value, 'blk', 0, 0, axis_index_groups=Z_GROUPS, tiled=True)  20 us
    pallas_call x1, Pallas kernels, attention(): call(attention_kernel, jax.ShapeDtypeStruct((ZN, HD, 256), bf16), [SMEM,...  19 us
    ppermute x2, waiting for transfers between devices, tp_swap(): return lax.ppermute(value, 'tp', [(0, 1), (1, 0)])  13.9 us
    unnamed x50, local copies, waits for them, and re-layouts  12.9 us
  transfers between devices with their start and end apart: 29, of which 13 were waited for; matrix products, arithmetic and copies ran while one was open for 14% of the time, Pallas kernels for 3%

profile of v2, /device:TPU:32, one launch (start us, length us, event | category | flops | bytes accessed | tf_op | source)
XLA Modules:
  0.0 237.9 jit_solution(5104064420318942717)
XLA Ops:
  0.0 1.2 slice.38.own_ref
  2.0 2.8 %collective-permute-start = (bf16[2,160,640]{2,1,0:T(8,128)(2,1)}, bf16[2,160,640]{2,1,0:T(8,128)(2,1)S(1)}, u32[]{:S(2)}, u32[]{:S(2)}) collective-permute-start(bf16[2,160,640]{2,1,0:T(8,128)(2,1)} %constant_dynamic-slice_fusion.2), channel_id=1, source_target_pairs={{0,192},{64,0},{128,64},{192,128},{1,193},{65,1},{129,65},{193,129... | collective-permute-start | bytes 1228808 | tf_op jit(solution)/shard_map/ppermute | solution.py:38
  4.8 3.2 %collective-permute-start.13 = (bf16[640,320]{0,1:T(8,128)(2,1)}, bf16[640,320]{0,1:T(8,128)(2,1)S(1)}, u32[]{:S(2)}, u32[]{:S(2)}) collective-permute-start(bf16[640,320]{0,1:T(8,128)(2,1)} %param.14), channel_id=1, source_target_pairs={{0,192},{64,0},{128,64},{192,128},{1,193},{65,1},{129,65},{193,129... | collective-permute-start | bytes 1228808 | tf_op jit(solution)/shard_map/ppermute | solution.py:38
  8.0 1.0 slice.41.own_ref
  9.8 1.5 collective-permute-start.5
  11.8 2.0 reduce.8
  13.9 1.4 reshape_squeeze.7
  16.0 2.7 %collective-permute-start.1 = (bf16[2,80,640]{2,1,0:T(8,128)(2,1)S(1)}, bf16[2,80,640]{2,1,0:T(8,128)(2,1)S(1)}, u32[]{:S(2)}, u32[]{:S(2)}) collective-permute-start(bf16[2,80,640]{2,1,0:T(8,128)(2,1)S(1)} %slice.54), channel_id=1, source_target_pairs={{0,192},{64,0},{128,64},{192,128},{1,193},{65,1},{129,65},{193,129... | collective-permute-start | bytes 614408 | tf_op jit(solution)/shard_map/ppermute | solution.py:38
  18.7 8.1 %collective-permute-done.2 = bf16[2,160,640]{2,1,0:T(8,128)(2,1)} collective-permute-done((bf16[2,160,640]{2,1,0:T(8,128)(2,1)}, bf16[2,160,640]{2,1,0:T(8,128)(2,1)}, u32[]{:S(2)}, u32[]{:S(2)}) %collective-permute-start.2) | collective-permute-done | bytes 409632 | tf_op jit(solution)/shard_map/ppermute | solution.py:38
  27.9 1.0 convert_reduce_fusion
  28.9 11.2 %collective-permute-done.1 = bf16[2,80,640]{2,1,0:T(8,128)(2,1)S(1)} collective-permute-done((bf16[2,80,640]{2,1,0:T(8,128)(2,1)S(1)}, bf16[2,80,640]{2,1,0:T(8,128)(2,1)S(1)}, u32[]{:S(2)}, u32[]{:S(2)}) %collective-permute-start.1) | collective-permute-done | bytes 204832 | tf_op jit(solution)/shard_map/ppermute | solution.py:38
  40.1 1.2 collective-permute-start.7
  41.3 1.2 pad_maximum_fusion.mine_ref
  43.6 1.1 fusion.2.normed_ref
  45.5 1.6 collective-permute-start.15
  47.1 4.4 %project.2 = bf16[8,160,256]{2,1,0:T(8,128)(2,1)} custom-call(s32[4]{0:T(128)} %pad_add_fusion.1.place_ref, bf16[256,1280]{1,0:T(8,128)(2,1)} %fusion.2.normed_ref, bf16[2,320,640]{2,1,0:T(8,128)(2,1)} %copy-done.1, bf16[3,2,160,640]{3,2,1,0:T(8,128)(2,1)} %copy-done.2, bf16[3,2,160,640]{3,2,1,0:T(8,128)(2,1)} %copy-done.8), custom_call_target="tpu_custom_call" | custom-call | flops 838860800 | bytes 3276800 | tf_op jit(solution)/shard_map/project/pallas_call | solution.py:87
  51.5 8.6 %all-to-all-start = ((bf16[8,160,256]{2,1,0:T(8,128)(2,1)}), bf16[8,160,256]{2,1,0:T(8,128)(2,1)}, u32[]{:S(2)}, u32[]{:S(2)}) async-start(bf16[8,160,256]{2,1,0:T(8,128)(2,1)} %project.2), calls=%async_computation | async-start | bytes 1310720 | tf_op jit(solution)/shard_map/all_to_all | solution.py:50
  61.2 2.0 collective-permute-start.6
  64.6 1.6 collective-permute-done.6
  66.2 3.8 %collective-permute-done.8 = bf16[1,80,640]{2,1,0:T(8,128)(2,1)S(1)} collective-permute-done((bf16[1,80,640]{2,1,0:T(8,128)(2,1)S(1)}, bf16[1,80,640]{2,1,0:T(8,128)(2,1)S(1)}, u32[]{:S(2)}, u32[]{:S(2)}) %collective-permute-start.8) | collective-permute-done | bytes 102432 | tf_op jit(solution)/shard_map/ppermute | solution.py:38
  70.1 1.1 pad_maximum_fusion.1.mine_ref
  75.0 3.2 %project.3 = bf16[8,80,256]{2,1,0:T(8,128)(2,1)} custom-call(s32[4]{0:T(128)} %pad_add_fusion.1.place_ref, bf16[256,1280]{1,0:T(8,128)(2,1)} %fusion.2.normed_ref, bf16[1,320,640]{2,1,0:T(8,128)(2,1)} %copy-done.4, bf16[3,1,160,640]{3,2,1,0:T(8,128)(2,1)} %copy-done.5, bf16[3,1,160,640]{3,2,1,0:T(8,128)(2,1)} %copy-done.13), custom_call_target="tpu_custom_call" | custom-call | flops 419430400 | bytes 1638400 | tf_op jit(solution)/shard_map/project/pallas_call | solution.py:87
  78.2 1.0 all-to-all-done.own
  79.3 1.6 collective-permute-start.11
  83.2 12.5 %collective-permute-done.11.far = bf16[8,160,256]{2,1,0:T(8,128)(2,1)} collective-permute-done((bf16[8,160,256]{2,1,0:T(8,128)(2,1)}, bf16[8,160,256]{2,1,0:T(8,128)(2,1)}, u32[]{:S(2)}, u32[]{:S(2)}) %collective-permute-start.11) | collective-permute-done | bytes 655392 | tf_op jit(solution)/shard_map/ppermute | solution.py:42
  96.5 7.2 %all-to-all-start.1 = ((bf16[8,80,256]{2,1,0:T(8,128)(2,1)}), bf16[8,80,256]{2,1,0:T(8,128)(2,1)S(1)}, u32[]{:S(2)}, u32[]{:S(2)}) async-start(bf16[8,80,256]{2,1,0:T(8,128)(2,1)} %project.3), calls=%async_computation.1 | async-start | bytes 655360 | tf_op jit(solution)/shard_map/all_to_all | solution.py:50
  105.3 1.6 constant_dynamic-slice_fusion
  106.9 9.3 %all-to-all-done.1.q_ref = bf16[8,80,256]{2,1,0:T(8,128)(2,1)S(1)} async-done(((bf16[8,80,256]{2,1,0:T(8,128)(2,1)}), bf16[8,80,256]{2,1,0:T(8,128)(2,1)S(1)}, u32[]{:S(2)}, u32[]{:S(2)}) %all-to-all-start.1) | async-done | bytes 327712 | tf_op jit(solution)/shard_map/all_to_all | solution.py:50
  116.9 19.0 %attention.1 = bf16[8,80,256]{2,1,0:T(8,128)(2,1)} custom-call(s32[2,8]{1,0:T(2,128)} %pad_add_fusion.bounds_ref, s32[4]{0:T(128)} %pad_add_fusion.1.place_ref, s32[8,256]{1,0:T(8,128)} %bitcast.63, s32[1,8192]{1,0:T(1,128)} %kframe_ref.1, bf16[8,80,256]{2,1,0:T(8,128)(2,1)} %copy-done.15, bf16[8,160,256]{2,1,0:T(8,128)(2,1)} %all-to-all-done.own, ...), custom_call_target="tpu_custom_call" | custom-call | flops 8589934592 | bytes 2621440 | tf_op jit(solution)/shard_map/attention/pallas_call | solution.py:167
  136.0 5.4 %all-to-all-start.2 = ((bf16[8,80,256]{2,1,0:T(8,128)(2,1)}), bf16[8,80,256]{2,1,0:T(8,128)(2,1)}, u32[]{:S(2)}, u32[]{:S(2)}) async-start(bf16[8,80,256]{2,1,0:T(8,128)(2,1)} %attention.1), calls=%async_computation.2 | async-start | bytes 655360 | tf_op jit(solution)/shard_map/all_to_all | solution.py:50
  142.3 2.2 copy.22.weight_ref
  144.4 9.8 %all-to-all-done.2.attn_ref = bf16[8,80,256]{2,1,0:T(8,128)(2,1)} async-done(((bf16[8,80,256]{2,1,0:T(8,128)(2,1)}), bf16[8,80,256]{2,1,0:T(8,128)(2,1)}, u32[]{:S(2)}, u32[]{:S(2)}) %all-to-all-start.2) | async-done | bytes 327712 | tf_op jit(solution)/shard_map/all_to_all | solution.py:50
  154.2 3.8 %output.1 = (f32[128,1280]{1,0:T(8,128)}, bf16[128,1280]{1,0:T(8,128)(2,1)}) custom-call(s32[4]{0:T(128)} %pad_add_fusion.1.place_ref, s32[256,1]{1,0:T(8,128)} %reshape.155.order_ref, bf16[256,1280]{1,0:T(8,128)(2,1)} %bitcast.59, bf16[8,80,256]{2,1,0:T(8,128)(2,1)} %all-to-all-done.2.attn_ref, bf16[640,1280]{1,0:T(8,128)(2,1)} %copy.22.weight_ref), custom_call_target="tpu_custom_call" | custom-call | flops 589824000 | bytes 4000000 | tf_op jit(solution)/shard_map/output/pallas_call | solution.py:250
  158.0 3.2 %collective-permute-start.16 = (bf16[128,1280]{1,0:T(8,128)(2,1)}, bf16[128,1280]{1,0:T(8,128)(2,1)S(1)}, u32[]{:S(2)}, u32[]{:S(2)}) collective-permute-start(bf16[128,1280]{1,0:T(8,128)(2,1)} %get-tuple-element.16), channel_id=1, source_target_pairs={{0,1},{1,0},{2,3},{3,2},{4,5},{5,4},{6,7},{7,6},{8,9},{9,8},{10,11... | collective-permute-start | bytes 983048 | tf_op jit(solution)/shard_map/ppermute | solution.py:46
  161.3 8.5 %collective-permute-done.16 = bf16[128,1280]{1,0:T(8,128)(2,1)S(1)} collective-permute-done((bf16[128,1280]{1,0:T(8,128)(2,1)}, bf16[128,1280]{1,0:T(8,128)(2,1)S(1)}, u32[]{:S(2)}, u32[]{:S(2)}) %collective-permute-start.16) | collective-permute-done | bytes 327712 | tf_op jit(solution)/shard_map/ppermute | solution.py:46
  169.7 1.3 multiply_reduce_fusion
  171.0 1.2 multiply_convert_fusion.refs_0_
  172.2 3.3 %collective-permute-start.17 = (bf16[128,1280]{1,0:T(8,128)(2,1)S(1)}, bf16[128,1280]{1,0:T(8,128)(2,1)S(1)}, u32[]{:S(2)}, u32[]{:S(2)}) collective-permute-start(bf16[128,1280]{1,0:T(8,128)(2,1)S(1)} %multiply_convert_fusion.refs_0_), channel_id=1, source_target_pairs={{0,1},{1,0},{2,3},{3,2},{4,5},{5,4},{6,7},{7,6},{8,9},{9,8},{10,11... | collective-permute-start | bytes 983048 | tf_op jit(solution)/shard_map/ppermute | solution.py:46
  175.5 2.0 collective-permute-start.19
  177.6 5.4 %collective-permute-done.17.refs_1_ = bf16[128,1280]{1,0:T(8,128)(2,1)S(1)} collective-permute-done((bf16[128,1280]{1,0:T(8,128)(2,1)S(1)}, bf16[128,1280]{1,0:T(8,128)(2,1)S(1)}, u32[]{:S(2)}, u32[]{:S(2)}) %collective-permute-start.17) | collective-permute-done | bytes 327712 | tf_op jit(solution)/shard_map/ppermute | solution.py:46
  183.0 2.0 collective-permute-start.23
  185.0 1.3 collective-permute-start.20
  188.0 5.2 %collective-permute-done.22.refs_6_ = bf16[128,1280]{1,0:T(8,128)(2,1)S(1)} collective-permute-done((bf16[128,1280]{1,0:T(8,128)(2,1)S(1)}, bf16[128,1280]{1,0:T(8,128)(2,1)S(1)}, u32[]{:S(2)}, u32[]{:S(2)}) %collective-permute-start.22) | collective-permute-done | bytes 327712 | tf_op jit(solution)/shard_map/ppermute | solution.py:38
  194.6 1.5 collective-permute-start.24
  198.0 3.7 %copy.23.refs_10_ = bf16[5120,320]{1,0:T(8,128)(2,1)} copy(bf16[5120,320]{0,1:T(8,128)(2,1)S(1)} %copy-done.3) | data formatting | bytes 6553600 | tf_op args[7]
  201.7 2.6 %collective-permute-done.25.refs_9_ = bf16[64,1280]{1,0:T(8,128)(2,1)} collective-permute-done((bf16[64,1280]{1,0:T(8,128)(2,1)}, bf16[64,1280]{1,0:T(8,128)(2,1)}, u32[]{:S(2)}, u32[]{:S(2)}) %collective-permute-start.25) | collective-permute-done | bytes 163872 | tf_op jit(solution)/shard_map/ppermute | solution.py:38
  204.3 7.6 %merger.1 = bf16[256,3584]{1,0:T(8,128)(2,1)} custom-call(s32[4]{0:T(128)} %pad_add_fusion.1.place_ref, bf16[128,1280]{1,0:T(8,128)(2,1)} %copy-done.7, bf16[128,1280]{1,0:T(8,128)(2,1)} %copy-done.14, bf16[128,1280]{1,0:T(8,128)(2,1)} %copy-done.9, bf16[128,1280]{1,0:T(8,128)(2,1)} %copy-done.10, bf16[64,1280]{1,0:T(8,128)(2,1)} %collective-permute-done.20.refs_4_, ...), custom_call_target="tpu_custom_call" | custom-call | flops 1426063360 | bytes 9000000 | tf_op jit(solution)/shard_map/merger/pallas_call | solution.py:264
  212.0 24.9 %all_to_all.20 = bf16[8,32,3584]{2,1,0:T(8,128)(2,1)S(1)} all-to-all(bf16[8,32,3584]{2,1,0:T(8,128)(2,1)} %bitcast.57), channel_id=1, replica_groups=mesh['section'=4,'blk'=32,'tp'=2] {'section','tp'}, dimensions={0} | all-to-all | bytes 3670016 | tf_op jit(solution)/shard_map/all_to_all | solution.py:273
  (108 shorter events, 24.5 us)
Async XLA Ops:
  1.2 41.6 %copy-start.1 = (bf16[2,320,640]{2,1,0:T(8,128)(2,1)}, bf16[2,320,640]{2,1,0:T(8,128)(2,1)S(1)}, u32[]{:S(2)}) copy-start(bf16[2,320,640]{2,1,0:T(8,128)(2,1)S(1)} %slice.38.own_ref) | copy-start | bytes 2457604
  1.2 41.4 %copy-start = (bf16[1,256,1280]{2,1,0:T(8,128)(2,1)S(1)}, bf16[1,256,1280]{2,1,0:T(8,128)(2,1)}, u32[]{:S(2)}) copy-start(bf16[1,256,1280]{2,1,0:T(8,128)(2,1)} %param.9) | copy-start | bytes 1966084
  2.0 40.8 %copy-start.6 = (bf16[640,320]{0,1:T(8,128)(2,1)S(1)}, bf16[640,320]{0,1:T(8,128)(2,1)}, u32[]{:S(2)}) copy-start(bf16[640,320]{0,1:T(8,128)(2,1)} %param.14) | copy-start | bytes 1228804
  2.0 13.9 %collective-permute-start = (bf16[2,160,640]{2,1,0:T(8,128)(2,1)}, bf16[2,160,640]{2,1,0:T(8,128)(2,1)S(1)}, u32[]{:S(2)}, u32[]{:S(2)}) collective-permute-start(bf16[2,160,640]{2,1,0:T(8,128)(2,1)} %constant_dynamic-slice_fusion.2), channel_id=1, source_target_pairs={{0,192},{64,0},{128,64},{192,128},{1,193},{65,1},{129,65},{193,129... | collective-permute-start | bytes 1228808 | tf_op jit(solution)/shard_map/ppermute | solution.py:38
  4.8 22.0 %collective-permute-start.2 = (bf16[2,160,640]{2,1,0:T(8,128)(2,1)}, bf16[2,160,640]{2,1,0:T(8,128)(2,1)}, u32[]{:S(2)}, u32[]{:S(2)}) collective-permute-start(bf16[2,160,640]{2,1,0:T(8,128)(2,1)} %constant_dynamic-slice_fusion.2), channel_id=1, source_target_pairs={{0,64},{64,128},{128,192},{192,0},{1,65},{65,129},{129,193},{193,1... | collective-permute-start | bytes 1228808 | tf_op jit(solution)/shard_map/ppermute | solution.py:38
  4.8 68.6 %collective-permute-start.13 = (bf16[640,320]{0,1:T(8,128)(2,1)}, bf16[640,320]{0,1:T(8,128)(2,1)S(1)}, u32[]{:S(2)}, u32[]{:S(2)}) collective-permute-start(bf16[640,320]{0,1:T(8,128)(2,1)} %param.14), channel_id=1, source_target_pairs={{0,192},{64,0},{128,64},{192,128},{1,193},{65,1},{129,65},{193,129... | collective-permute-start | bytes 1228808 | tf_op jit(solution)/shard_map/ppermute | solution.py:38
  8.0 72.8 %collective-permute-start.14 = (bf16[640,320]{0,1:T(8,128)(2,1)}, bf16[640,320]{0,1:T(8,128)(2,1)S(1)}, u32[]{:S(2)}, u32[]{:S(2)}) collective-permute-start(bf16[640,320]{0,1:T(8,128)(2,1)} %param.14), channel_id=1, source_target_pairs={{0,128},{64,192},{128,0},{192,64},{1,129},{65,193},{129,1},{193,65... | collective-permute-start | bytes 1228808 | tf_op jit(solution)/shard_map/ppermute | solution.py:38
  9.1 35.6 %copy-start.4 = (bf16[1,320,640]{2,1,0:T(8,128)(2,1)}, bf16[1,320,640]{2,1,0:T(8,128)(2,1)S(1)}, u32[]{:S(2)}) copy-start(bf16[1,320,640]{2,1,0:T(8,128)(2,1)S(1)} %slice.41.own_ref) | copy-start | bytes 1228804
  9.1 34.6 %copy-start.17 = (f32[1280]{0:T(1024)S(1)}, f32[1280]{0:T(1024)}, u32[]{:S(2)}) copy-start(f32[1280]{0:T(1024)} %param.12) | copy-start | bytes 15364
  9.8 50.4 %collective-permute-start.5 = (bf16[1,160,640]{2,1,0:T(8,128)(2,1)}, bf16[1,160,640]{2,1,0:T(8,128)(2,1)}, u32[]{:S(2)}, u32[]{:S(2)}) collective-permute-start(bf16[1,160,640]{2,1,0:T(8,128)(2,1)} %constant_dynamic-slice_fusion.1), channel_id=1, source_target_pairs={{0,192},{64,0},{128,64},{192,128},{1,193},{65,1},{129,65},{193,129... | collective-permute-start | bytes 614408 | tf_op jit(solution)/shard_map/ppermute | solution.py:38
  16.0 24.1 %collective-permute-start.1 = (bf16[2,80,640]{2,1,0:T(8,128)(2,1)S(1)}, bf16[2,80,640]{2,1,0:T(8,128)(2,1)S(1)}, u32[]{:S(2)}, u32[]{:S(2)}) collective-permute-start(bf16[2,80,640]{2,1,0:T(8,128)(2,1)S(1)} %slice.54), channel_id=1, source_target_pairs={{0,192},{64,0},{128,64},{192,128},{1,193},{65,1},{129,65},{193,129... | collective-permute-start | bytes 614408 | tf_op jit(solution)/shard_map/ppermute | solution.py:38
  27.8 13.5 %collective-permute-start.3 = (bf16[2,80,640]{2,1,0:T(8,128)(2,1)S(1)}, bf16[2,80,640]{2,1,0:T(8,128)(2,1)S(1)}, u32[]{:S(2)}, u32[]{:S(2)}) collective-permute-start(bf16[2,80,640]{2,1,0:T(8,128)(2,1)S(1)} %slice.55), channel_id=1, source_target_pairs={{0,64},{64,128},{128,192},{192,0},{1,65},{65,129},{129,193},{193,1... | collective-permute-start | bytes 614408 | tf_op jit(solution)/shard_map/ppermute | solution.py:38
  40.1 23.1 %collective-permute-start.7 = (bf16[1,160,640]{2,1,0:T(8,128)(2,1)}, bf16[1,160,640]{2,1,0:T(8,128)(2,1)}, u32[]{:S(2)}, u32[]{:S(2)}) collective-permute-start(bf16[1,160,640]{2,1,0:T(8,128)(2,1)} %constant_dynamic-slice_fusion.1), channel_id=1, source_target_pairs={{0,64},{64,128},{128,192},{192,0},{1,65},{65,129},{129,193},{193,1... | collective-permute-start | bytes 614408 | tf_op jit(solution)/shard_map/ppermute | solution.py:38
  42.5 4.6 %copy-start.2 = (bf16[3,2,160,640]{3,2,1,0:T(8,128)(2,1)}, bf16[3,2,160,640]{3,2,1,0:T(8,128)(2,1)S(1)}, u32[]{:S(2)}) copy-start(bf16[3,2,160,640]{3,2,1,0:T(8,128)(2,1)S(1)} %pad_maximum_fusion.mine_ref) | copy-start | bytes 3686404
  42.5 3.0 %collective-permute-start.4 = (bf16[3,2,160,640]{3,2,1,0:T(8,128)(2,1)S(1)}, bf16[3,2,160,640]{3,2,1,0:T(8,128)(2,1)S(1)}, u32[]{:S(2)}, u32[]{:S(2)}) collective-permute-start(bf16[3,2,160,640]{3,2,1,0:T(8,128)(2,1)S(1)} %pad_maximum_fusion.mine_ref), channel_id=1, source_target_pairs={{0,2},{2,0},{4,6},{6,4},{8,10},{10,8},{12,14},{14,12},{16,18},{18,... | collective-permute-start | bytes 3686408 | tf_op jit(solution)/shard_map/ppermute | solution.py:42
  45.3 61.6 %copy-start.16 = (s32[1,8,1,256]{3,1,2,0:T(8,128)}, s32[1,8,1,256]{3,1,2,0:T(8,128)S(1)}, u32[]{:S(2)}) copy-start(s32[1,8,1,256]{3,1,2,0:T(8,128)S(1)} %copy.27) | copy-start | bytes 24580
  45.5 1.6 copy-start.8
  45.5 36.1 %collective-permute-start.15 = (bf16[640,320]{0,1:T(8,128)(2,1)S(1)}, bf16[640,320]{0,1:T(8,128)(2,1)S(1)}, u32[]{:S(2)}, u32[]{:S(2)}) collective-permute-start(bf16[640,320]{0,1:T(8,128)(2,1)S(1)} %copy-done.6), channel_id=1, source_target_pairs={{0,64},{64,128},{128,192},{192,0},{1,65},{65,129},{129,193},{193,1... | collective-permute-start | bytes 1228808 | tf_op jit(solution)/shard_map/ppermute | solution.py:38
  51.5 27.8 %all-to-all-start = ((bf16[8,160,256]{2,1,0:T(8,128)(2,1)}), bf16[8,160,256]{2,1,0:T(8,128)(2,1)}, u32[]{:S(2)}, u32[]{:S(2)}) async-start(bf16[8,160,256]{2,1,0:T(8,128)(2,1)} %project.2), calls=%async_computation | async-start | bytes 1310720 | tf_op jit(solution)/shard_map/all_to_all | solution.py:50
  61.2 5.1 %collective-permute-start.6 = (bf16[1,80,640]{2,1,0:T(8,128)(2,1)S(1)}, bf16[1,80,640]{2,1,0:T(8,128)(2,1)S(1)}, u32[]{:S(2)}, u32[]{:S(2)}) collective-permute-start(bf16[1,80,640]{2,1,0:T(8,128)(2,1)S(1)} %slice.56), channel_id=1, source_target_pairs={{0,192},{64,0},{128,64},{192,128},{1,193},{65,1},{129,65},{193,129... | collective-permute-start | bytes 307208 | tf_op jit(solution)/shard_map/ppermute | solution.py:38
  64.1 5.9 %collective-permute-start.8 = (bf16[1,80,640]{2,1,0:T(8,128)(2,1)S(1)}, bf16[1,80,640]{2,1,0:T(8,128)(2,1)S(1)}, u32[]{:S(2)}, u32[]{:S(2)}) collective-permute-start(bf16[1,80,640]{2,1,0:T(8,128)(2,1)S(1)} %slice.57), channel_id=1, source_target_pairs={{0,64},{64,128},{128,192},{192,0},{1,65},{65,129},{129,193},{193,1... | collective-permute-start | bytes 307208 | tf_op jit(solution)/shard_map/ppermute | solution.py:38
  71.2 3.0 %copy-start.5 = (bf16[3,1,160,640]{3,2,1,0:T(8,128)(2,1)}, bf16[3,1,160,640]{3,2,1,0:T(8,128)(2,1)S(1)}, u32[]{:S(2)}) copy-start(bf16[3,1,160,640]{3,2,1,0:T(8,128)(2,1)S(1)} %pad_maximum_fusion.1.mine_ref) | copy-start | bytes 1843204
  71.2 3.0 %collective-permute-start.9 = (bf16[3,1,160,640]{3,2,1,0:T(8,128)(2,1)S(1)}, bf16[3,1,160,640]{3,2,1,0:T(8,128)(2,1)S(1)}, u32[]{:S(2)}, u32[]{:S(2)}) collective-permute-start(bf16[3,1,160,640]{3,2,1,0:T(8,128)(2,1)S(1)} %pad_maximum_fusion.1.mine_ref), channel_id=1, source_target_pairs={{0,2},{2,0},{4,6},{6,4},{8,10},{10,8},{12,14},{14,12},{16,18},{18,... | collective-permute-start | bytes 1843208 | tf_op jit(solution)/shard_map/ppermute | solution.py:42
  74.2 0.8 copy-start.13
  79.3 16.4 %collective-permute-start.11 = (bf16[8,160,256]{2,1,0:T(8,128)(2,1)}, bf16[8,160,256]{2,1,0:T(8,128)(2,1)}, u32[]{:S(2)}, u32[]{:S(2)}) collective-permute-start(bf16[8,160,256]{2,1,0:T(8,128)(2,1)} %all-to-all-done.own), channel_id=1, source_target_pairs={{0,32},{2,34},{4,36},{6,38},{8,40},{10,42},{12,44},{14,46},{16,48}... | collective-permute-start | bytes 1966088 | tf_op jit(solution)/shard_map/ppermute | solution.py:42
  83.2 33.0 %collective-permute-start.10 = (bf16[8,160,256]{2,1,0:T(8,128)(2,1)}, bf16[8,160,256]{2,1,0:T(8,128)(2,1)}, u32[]{:S(2)}, u32[]{:S(2)}) collective-permute-start(bf16[8,160,256]{2,1,0:T(8,128)(2,1)} %all-to-all-done.own), channel_id=1, source_target_pairs={{0,2},{2,0},{4,6},{6,4},{8,10},{10,8},{12,14},{14,12},{16,18},{18,... | collective-permute-start | bytes 1966088 | tf_op jit(solution)/shard_map/ppermute | solution.py:42
  95.7 11.2 %collective-permute-start.12 = (bf16[8,160,256]{2,1,0:T(8,128)(2,1)}, bf16[8,160,256]{2,1,0:T(8,128)(2,1)}, u32[]{:S(2)}, u32[]{:S(2)}) collective-permute-start(bf16[8,160,256]{2,1,0:T(8,128)(2,1)} %collective-permute-done.11.far), channel_id=1, source_target_pairs={{0,2},{2,0},{4,6},{6,4},{8,10},{10,8},{12,14},{14,12},{16,18},{18,... | collective-permute-start | bytes 1966088 | tf_op jit(solution)/shard_map/ppermute | solution.py:42
  96.5 19.7 %all-to-all-start.1 = ((bf16[8,80,256]{2,1,0:T(8,128)(2,1)}), bf16[8,80,256]{2,1,0:T(8,128)(2,1)S(1)}, u32[]{:S(2)}, u32[]{:S(2)}) async-start(bf16[8,80,256]{2,1,0:T(8,128)(2,1)} %project.3), calls=%async_computation.1 | async-start | bytes 655360 | tf_op jit(solution)/shard_map/all_to_all | solution.py:50
  106.9 34.5 %copy-start.19 = (s32[1,64,4]{1,2,0:T(4,128)S(1)}, s32[1,64,4]{1,2,0:T(4,128)}, u32[]{:S(2)}) copy-start(s32[1,64,4]{1,2,0:T(4,128)} %param.11) | copy-start | bytes 3076
  116.2 0.7 copy-start.15
  136.0 18.2 %all-to-all-start.2 = ((bf16[8,80,256]{2,1,0:T(8,128)(2,1)}), bf16[8,80,256]{2,1,0:T(8,128)(2,1)}, u32[]{:S(2)}, u32[]{:S(2)}) async-start(bf16[8,80,256]{2,1,0:T(8,128)(2,1)} %attention.1), calls=%async_computation.2 | async-start | bytes 655360 | tf_op jit(solution)/shard_map/all_to_all | solution.py:50
  142.3 28.7 %copy-start.18 = (f32[1280]{0:T(1024)S(1)}, f32[1280]{0:T(1024)}, u32[]{:S(2)}) copy-start(f32[1280]{0:T(1024)} %param.15) | copy-start | bytes 15364
  144.4 53.6 %copy-start.3 = (bf16[5120,320]{0,1:T(8,128)(2,1)S(1)}, bf16[5120,320]{0,1:T(8,128)(2,1)}, u32[]{:S(2)}) copy-start(bf16[5120,320]{0,1:T(8,128)(2,1)} %param.16) | copy-start | bytes 9830404
  158.0 11.7 %collective-permute-start.16 = (bf16[128,1280]{1,0:T(8,128)(2,1)}, bf16[128,1280]{1,0:T(8,128)(2,1)S(1)}, u32[]{:S(2)}, u32[]{:S(2)}) collective-permute-start(bf16[128,1280]{1,0:T(8,128)(2,1)} %get-tuple-element.16), channel_id=1, source_target_pairs={{0,1},{1,0},{2,3},{3,2},{4,5},{5,4},{6,7},{7,6},{8,9},{9,8},{10,11... | collective-permute-start | bytes 983048 | tf_op jit(solution)/shard_map/ppermute | solution.py:46
  172.2 3.3 %copy-start.7 = (bf16[128,1280]{1,0:T(8,128)(2,1)}, bf16[128,1280]{1,0:T(8,128)(2,1)S(1)}, u32[]{:S(2)}) copy-start(bf16[128,1280]{1,0:T(8,128)(2,1)S(1)} %multiply_convert_fusion.refs_0_) | copy-start | bytes 983044
  172.2 10.8 %collective-permute-start.17 = (bf16[128,1280]{1,0:T(8,128)(2,1)S(1)}, bf16[128,1280]{1,0:T(8,128)(2,1)S(1)}, u32[]{:S(2)}, u32[]{:S(2)}) collective-permute-start(bf16[128,1280]{1,0:T(8,128)(2,1)S(1)} %multiply_convert_fusion.refs_0_), channel_id=1, source_target_pairs={{0,1},{1,0},{2,3},{3,2},{4,5},{5,4},{6,7},{7,6},{8,9},{9,8},{10,11... | collective-permute-start | bytes 983048 | tf_op jit(solution)/shard_map/ppermute | solution.py:46
  175.5 9.5 %collective-permute-start.18 = (bf16[128,1280]{1,0:T(8,128)(2,1)S(1)}, bf16[128,1280]{1,0:T(8,128)(2,1)S(1)}, u32[]{:S(2)}, u32[]{:S(2)}) collective-permute-start(bf16[128,1280]{1,0:T(8,128)(2,1)S(1)} %multiply_convert_fusion.refs_0_), channel_id=1, source_target_pairs={{0,192},{64,0},{128,64},{192,128},{1,193},{65,1},{129,65},{193,129... | collective-permute-start | bytes 983048 | tf_op jit(solution)/shard_map/ppermute | solution.py:38
  175.5 10.8 %collective-permute-start.19 = (bf16[128,1280]{1,0:T(8,128)(2,1)S(1)}, bf16[128,1280]{1,0:T(8,128)(2,1)S(1)}, u32[]{:S(2)}, u32[]{:S(2)}) collective-permute-start(bf16[128,1280]{1,0:T(8,128)(2,1)S(1)} %multiply_convert_fusion.refs_0_), channel_id=1, source_target_pairs={{0,64},{64,128},{128,192},{192,0},{1,65},{65,129},{129,193},{193,1... | collective-permute-start | bytes 983048 | tf_op jit(solution)/shard_map/ppermute | solution.py:38
  183.0 14.5 %copy-start.14 = (bf16[128,1280]{1,0:T(8,128)(2,1)}, bf16[128,1280]{1,0:T(8,128)(2,1)S(1)}, u32[]{:S(2)}) copy-start(bf16[128,1280]{1,0:T(8,128)(2,1)S(1)} %collective-permute-done.17.refs_1_) | copy-start | bytes 983044
  183.0 10.2 %collective-permute-start.22 = (bf16[128,1280]{1,0:T(8,128)(2,1)S(1)}, bf16[128,1280]{1,0:T(8,128)(2,1)S(1)}, u32[]{:S(2)}, u32[]{:S(2)}) collective-permute-start(bf16[128,1280]{1,0:T(8,128)(2,1)S(1)} %collective-permute-done.17.refs_1_), channel_id=1, source_target_pairs={{0,192},{64,0},{128,64},{192,128},{1,193},{65,1},{129,65},{193,129... | collective-permute-start | bytes 983048 | tf_op jit(solution)/shard_map/ppermute | solution.py:38
  183.0 13.1 %collective-permute-start.23 = (bf16[128,1280]{1,0:T(8,128)(2,1)S(1)}, bf16[128,1280]{1,0:T(8,128)(2,1)S(1)}, u32[]{:S(2)}, u32[]{:S(2)}) collective-permute-start(bf16[128,1280]{1,0:T(8,128)(2,1)S(1)} %collective-permute-done.17.refs_1_), channel_id=1, source_target_pairs={{0,64},{64,128},{128,192},{192,0},{1,65},{65,129},{129,193},{193,1... | collective-permute-start | bytes 983048 | tf_op jit(solution)/shard_map/ppermute | solution.py:38
  185.0 1.3 copy-start.9
  185.0 16.7 %collective-permute-start.20 = (bf16[64,1280]{1,0:T(8,128)(2,1)S(1)}, bf16[64,1280]{1,0:T(8,128)(2,1)}, u32[]{:S(2)}, u32[]{:S(2)}) collective-permute-start(bf16[64,1280]{1,0:T(8,128)(2,1)S(1)} %slice.58), channel_id=1, source_target_pairs={{0,192},{64,0},{128,64},{192,128},{1,193},{65,1},{129,65},{193,129... | collective-permute-start | bytes 491528 | tf_op jit(solution)/shard_map/ppermute | solution.py:38
  186.3 0.8 copy-start.10
  187.1 14.6 %collective-permute-start.21 = (bf16[64,1280]{1,0:T(8,128)(2,1)}, bf16[64,1280]{1,0:T(8,128)(2,1)}, u32[]{:S(2)}, u32[]{:S(2)}) collective-permute-start(bf16[64,1280]{1,0:T(8,128)(2,1)} %slice.59), channel_id=1, source_target_pairs={{0,64},{64,128},{128,192},{192,0},{1,65},{65,129},{129,193},{193,1... | collective-permute-start | bytes 491528 | tf_op jit(solution)/shard_map/ppermute | solution.py:38
  194.6 7.1 %collective-permute-start.24 = (bf16[64,1280]{1,0:T(8,128)(2,1)}, bf16[64,1280]{1,0:T(8,128)(2,1)}, u32[]{:S(2)}, u32[]{:S(2)}) collective-permute-start(bf16[64,1280]{1,0:T(8,128)(2,1)} %slice.60), channel_id=1, source_target_pairs={{0,192},{64,0},{128,64},{192,128},{1,193},{65,1},{129,65},{193,129... | collective-permute-start | bytes 491528 | tf_op jit(solution)/shard_map/ppermute | solution.py:38
  196.1 0.7 copy-start.12
  197.5 6.8 %collective-permute-start.25 = (bf16[64,1280]{1,0:T(8,128)(2,1)}, bf16[64,1280]{1,0:T(8,128)(2,1)}, u32[]{:S(2)}, u32[]{:S(2)}) collective-permute-start(bf16[64,1280]{1,0:T(8,128)(2,1)} %slice.61), channel_id=1, source_target_pairs={{0,64},{64,128},{128,192},{192,0},{1,65},{65,129},{129,193},{193,1... | collective-permute-start | bytes 491528 | tf_op jit(solution)/shard_map/ppermute | solution.py:38
  (1 other events, 0.7 us)

commit v3 on v2

--- a/solution.py
+++ b/solution.py
@@ -78,11 +78,14 @@
             out_ref[h, t * HD : (t + 1) * HD, :] = turned[h * HD : (h + 1) * HD, :]
 
 
-def project(place, normed, own, core, scale):
-    count = own.shape[0]
+def fetch(own, core):
     half = lax.dynamic_slice_in_dim(own, core * 160, 160, axis=1)
     right, left, opp_a, opp_b = ring_halves(half)
-    mine = jnp.stack([right, jnp.concatenate([opp_a, opp_b], axis=1), left])
+    return jnp.stack([right, jnp.concatenate([opp_a, opp_b], axis=1), left])
+
+
+def project(place, normed, own, mine, scale):
+    count = own.shape[0]
     other = blk_swap(mine, 1)
     return call(
         functools.partial(project_kernel, scale, count),
@@ -175,46 +178,45 @@
     )(bounds, place, mine, frames[None, :], q, *sources)
 
 
-def output_kernel(place_ref, order_ref, patch_ref, attn_ref, weight_ref, base_ref, send_ref):
-    tp = place_ref[3]
+def output_kernel(
+    place_ref, order_ref, gain_ref, patch_ref, attn_ref, attn_t_ref, own, right, left, opp_a, opp_b, out_ref, blocks
+):
+    me = place_ref[0]
     pick = (order_ref[...] == lax.broadcasted_iota(jnp.int32, (256, 256), 1)).astype(f32).astype(bf16)
-    attn = attn_ref[...].reshape(ZN * HD, 256)
-    picked = lax.dot_general(pick, attn, (((1,), (1,)), ((), ())), preferred_element_type=f32).astype(bf16)
-    partial = jnp.dot(picked, weight_ref[...], preferred_element_type=f32)
-    patch = jnp.dot(pick, patch_ref[...], preferred_element_type=f32)
-
-    @pl.when(tp == 0)
-    def _():
-        base_ref[...] = partial[:128] + patch[:128]
-        send_ref[...] = partial[128:].astype(bf16)
-
-    @pl.when(tp == 1)
-    def _():
-        base_ref[...] = partial[128:] + patch[128:]
-        send_ref[...] = partial[:128].astype(bf16)
-
-
-def merger_kernel(place_ref, *refs):
-    pieces, (up_ref, down_ref, out_ref, tokens) = refs[:10], refs[10:]
-    me, tp = place_ref[0], place_ref[3]
-    own, own_t, right, left, opp_a, opp_b, right_t, left_t, opp_at, opp_bt = pieces
-
-    def put(distance, flip, source, low):
-        slot = lax.rem(me + distance + 1, SECTIONS) * 2 + (1 - tp if flip else tp)
-        rows = pl.ds(pl.multiple_of(slot * 32, 32), 32)
-        for j in range(source.shape[0] // 32):
-            tokens[low // 32 + j, rows, :] = source[j * 32 : (j + 1) * 32, :]
-
-    put(0, False, own, 0)
-    put(0, True, own_t, 0)
-    put(1, False, right, 0)
-    put(1, True, right_t, 0)
-    put(3, False, left, 0)
-    put(3, True, left_t, 0)
-    put(2, False, opp_a, 0)
-    put(2, False, opp_b, 64)
-    put(2, True, opp_at, 0)
-    put(2, True, opp_bt, 64)
+    picked = []
+    for source in (attn_ref, attn_t_ref):
+        attn = source[...].reshape(ZN * HD, 256)
+        chosen = lax.dot_general(pick, attn, (((1,), (1,)), ((), ())), preferred_element_type=f32)
+        picked.append(chosen.astype(bf16))
+
+    def product(weight, low, high):
+        return sum(jnp.dot(picked[t][:, low:high], weight[t], preferred_element_type=f32) for t in range(2))
+
+    blocks[me] = product(own, 0, 640)
+    blocks[lax.rem(me + 1, SECTIONS)] = product(right, 0, 640)
+    blocks[lax.rem(me + 3, SECTIONS)] = product(left, 0, 640)
+    blocks[lax.rem(me + 2, SECTIONS)] = product(opp_a, 0, 320) + product(opp_b, 320, 640)
+    total = jnp.dot(pick, patch_ref[...], preferred_element_type=f32)
+    total += jnp.concatenate([blocks[section] for section in range(SECTIONS)], axis=1)
+    out_ref[...] = rms_norm(total, gain_ref[...]).astype(bf16)
+
+
+def merger_kernel(place_ref, own, right, left, opp_a, opp_b, up_ref, down_ref, out_ref, tokens):
+    me = place_ref[0]
+
+    def put(distance, source, first_half):
+        for part in range(source.shape[0] // 128):
+            slot = lax.rem(me + distance + 1, SECTIONS) * 2 + first_half + part
+            rows = pl.ds(pl.multiple_of(slot * 32, 32), 32)
+            for j in range(4):
+                low = part * 128 + j * 32
+                tokens[j, rows, :] = source[low : low + 32, :]
+
+    put(0, own, 0)
+    put(1, right, 0)
+    put(3, left, 0)
+    put(2, opp_a, 0)
+    put(2, opp_b, 1)
     hidden = jnp.zeros((256, 320), f32)
     for j in range(4):
         hidden += jnp.dot(tokens[j], up_ref[j * 1280 : (j + 1) * 1280, :], preferred_element_type=f32)
@@ -225,51 +227,52 @@
 
 
 def on_device(patches, frame_ids, groups, norm_gain, qkv_weight, out_weight, merge_gain, merger_up, merger_down):
-    me, blk, tp = lax.axis_index("section"), lax.axis_index("blk"), lax.axis_index("tp")
+    me, blk = lax.axis_index("section"), lax.axis_index("blk")
     core, y = blk % 2, blk // 16
-    place = jnp.stack([me, core, y, tp]).astype(jnp.int32)
+    place = jnp.stack([me, core, y]).astype(jnp.int32)
     patch = patches[0]
     normed = rms_norm(patch.astype(f32), norm_gain).astype(bf16)
 
-    kv = z_exchange(project(place, normed, qkv_weight[1:3], core, 1.0))
-    q = project(place, normed, qkv_weight[0:1], core, HD ** (-0.5) * math.log2(math.e))
+    kv_own, q_own = qkv_weight[1:3], qkv_weight[0:1]
+    kv_mine, out_weight_t = lax.optimization_barrier((fetch(kv_own, core), tp_swap(out_weight)))
+    kv_mine, q_own = lax.optimization_barrier((kv_mine, q_own))
+    kv = z_exchange(project(place, normed, kv_own, kv_mine, 1.0))
+    q = project(place, normed, q_own, fetch(q_own, core), HD ** (-0.5) * math.log2(math.e))
+    out_own = jnp.stack([out_weight, out_weight_t])
+    q, out_own = lax.optimization_barrier((q, out_own))
+    out_right, out_left = section_shift(out_own, -1), section_shift(out_own, 1)
     kv, q = lax.optimization_barrier((kv, q))
     far = blk_swap(kv, 16)
     near = blk_swap(kv, 1)
     q = z_exchange(q)
+    far, q = lax.optimization_barrier((far, q))
     across = blk_swap(far, 1)
 
-    pieces = jnp.stack([out_weight] + [section_shift(out_weight, -d) for d in (1, 2, 3)])
-    turned = jnp.roll(pieces, me, axis=0)
-    whole = turned.transpose(1, 0, 2).reshape(640, 1280)
-    across, whole = lax.optimization_barrier((across, whole))
-
+    out_right, out_left, across = lax.optimization_barrier((out_right, out_left, across))
+    out_a, out_b = section_shift(out_right[:, :320], -1), section_shift(out_left[:, 320:], 1)
     attn = z_exchange(attention(place, frame_ids[0], q, (kv, near, far, across), y, core))
-
+    attn_t = tp_swap(attn)
     order = groups[0].reshape(2, 32, 4).transpose(0, 2, 1).reshape(256, 1)
-    base, send = call(
+    own = call(
         output_kernel,
-        (jax.ShapeDtypeStruct((128, 1280), f32), jax.ShapeDtypeStruct((128, 1280), bf16)),
-        [SMEM] + [VMEM] * 4,
-        flops=2 * 256 * 1280 * 900,
-        moved=4000000,
+        jax.ShapeDtypeStruct((256, 1280), bf16),
+        [SMEM] + [VMEM] * 10,
+        [pltpu.VMEM((SECTIONS, 256, 320), f32)],
+        flops=2 * 256 * 1280 * 1800,
+        moved=5000000,
         name="output",
-    )(place, order, patch, attn, whole)
-    resid = base + tp_swap(send).astype(f32)
-    own = rms_norm(resid, merge_gain).astype(bf16)
-
-    own_t = tp_swap(own)
+    )(place, order, merge_gain[None, :], patch, attn, attn_t, out_own, out_right, out_left, out_a, out_b)
+
     right, left, opp_a, opp_b = ring_halves(own)
-    right_t, left_t, opp_at, opp_bt = ring_halves(own_t)
     partial = call(
         merger_kernel,
         jax.ShapeDtypeStruct((256, 3584), bf16),
-        [SMEM] + [VMEM] * 12,
+        [SMEM] + [VMEM] * 7,
         [pltpu.VMEM((4, 256, 1280), bf16)],
         flops=2 * 256 * 320 * (5120 + 3584),
         moved=9000000,
         name="merger",
-    )(place, own, own_t, right, left, opp_a, opp_b, right_t, left_t, opp_at, opp_bt, merger_up, merger_down)
+    )(place, own, right, left, opp_a, opp_b, merger_up, merger_down)
     parts = lax.all_to_all(partial.reshape(8, 32, 3584), ("section", "tp"), 0, 0, tiled=True)
     return jnp.sum(parts.astype(f32), axis=0).astype(bf16)[None]
 

time: 239 us -> 210 us (0.88); the launches traced: 238 us -> 206 us
  waiting for transfers between devices: 79.2 us -> 62 us
  local copies, waits for them, and re-layouts: 30.4 us -> 18.7 us
  starting transfers between devices: 53.4 us -> 59.6 us
  other arithmetic: 11.5 us -> 6.27 us
  Pallas kernels: 38.1 us -> 35.2 us
    ppermute x5, waiting for transfers between devices: 12.6 us -> 1.81 us  [blk_swap(): return lax.ppermute(value, 'blk', [(i, i ^ bit) for i in range(32)])]
    ppermute x19 -> x16, starting transfers between devices: 23.7 us -> 30.9 us  [section_shift(): return lax.ppermute(value, 'section', route)]
    ppermute x2, waiting for transfers between devices: 13.9 us -> 7.42 us  [tp_swap(): return lax.ppermute(value, 'tp', [(0, 1), (1, 0)])]
    ppermute x19 -> x16, waiting for transfers between devices: 32.6 us -> 37.7 us  [section_shift(): return lax.ppermute(value, 'section', route)]
    pallas_call x1, Pallas kernels: 19 us -> 14.1 us  [attention(): call(attention_kernel, jax.ShapeDtypeStruct((ZN, HD, 256), bf16), [SMEM,...]
    all_to_all x3, waiting for transfers between devices: 20 us -> 15.1 us  [z_exchange(): lax.all_to_all(value, 'blk', 0, 0, axis_index_groups=Z_GROUPS, tiled=True)]
    slice x4 -> x3, local copies, waits for them, and re-layouts: 3.27 us -> 0.05 us  [ring_halves(): opposite_b = section_shift(left[..., half:, :], 1)]
    dynamic_slice x3 -> x2, local copies, waits for them, and re-layouts: 3.06 us -> 0.06 us  [fetch(): half = lax.dynamic_slice_in_dim(own, core * 160, 160, axis=1)]
  transfers between devices with their start and end apart: 29 -> 26, of which waited for: 13 -> 12; matrix products, arithmetic and copies ran while one was open for 14% -> 9% of each run, Pallas kernels for 3% -> 4%
where the time goes in v3:
time: 210 us; the launch traced here: 206 us
  waiting for transfers between devices  62 us (30%)
  starting transfers between devices  59.6 us (28%)
  Pallas kernels  35.2 us (17%)
  blocking collectives  24 us (11%)
  local copies, waits for them, and re-layouts  18.7 us (9%)
  other arithmetic  6.27 us (3%)
    ppermute x16, waiting for transfers between devices, section_shift(): return lax.ppermute(value, 'section', route)  37.7 us
    ppermute x16, starting transfers between devices, section_shift(): return lax.ppermute(value, 'section', route)  30.9 us
    all_to_all x1, blocking collectives, on_device(): lax.all_to_all(partial.reshape(8, 32, 3584), ('section', 'tp'), 0, 0, til...  24 us
    all_to_all x3, starting transfers between devices, z_exchange(): lax.all_to_all(value, 'blk', 0, 0, axis_index_groups=Z_GROUPS, tiled=True)  20.8 us
    all_to_all x3, waiting for transfers between devices, z_exchange(): lax.all_to_all(value, 'blk', 0, 0, axis_index_groups=Z_GROUPS, tiled=True)  15.1 us
    pallas_call x1, Pallas kernels, attention(): call(attention_kernel, jax.ShapeDtypeStruct((ZN, HD, 256), bf16), [SMEM,...  14.1 us
    unnamed x56, local copies, waits for them, and re-layouts  10.6 us
    pallas_call x1, Pallas kernels, on_device(): call(merger_kernel, jax.ShapeDtypeStruct((256, 3584), bf16), [SMEM] + [VM...  7.62 us
  transfers between devices with their start and end apart: 26, of which 12 were waited for; matrix products, arithmetic and copies ran while one was open for 9% of the time, Pallas kernels for 4%

profile of v3, /device:TPU:32, one launch (start us, length us, event | category | flops | bytes accessed | tf_op | source)
XLA Modules:
  0.0 206.4 jit_solution(3621946847668893742)
XLA Ops:
  0.0 1.3 slice.38.own_ref
  1.3 1.6 collective-permute-start.2
  2.9 1.7 collective-permute-start
  4.7 9.2 %collective-permute-done.2 = bf16[2,160,640]{2,1,0:T(8,128)(2,1)S(1)} collective-permute-done((bf16[2,160,640]{2,1,0:T(8,128)(2,1)S(1)}, bf16[2,160,640]{2,1,0:T(8,128)(2,1)S(1)}, u32[]{:S(2)}, u32[]{:S(2)}) %collective-permute-start.2) | collective-permute-done | bytes 409632 | tf_op jit(solution)/shard_map/ppermute | solution.py:38
  14.2 3.0 %collective-permute-start.1 = (bf16[2,80,640]{2,1,0:T(8,128)(2,1)S(1)}, bf16[2,80,640]{2,1,0:T(8,128)(2,1)S(1)}, u32[]{:S(2)}, u32[]{:S(2)}) collective-permute-start(bf16[2,80,640]{2,1,0:T(8,128)(2,1)S(1)} %slice.54), channel_id=1, source_target_pairs={{0,192},{64,0},{128,64},{192,128},{1,193},{65,1},{129,65},{193,129... | collective-permute-start | bytes 614408 | tf_op jit(solution)/shard_map/ppermute | solution.py:38
  17.6 3.3 %collective-permute-start.4 = (bf16[640,320]{1,0:T(8,128)(2,1)S(1)}, bf16[640,320]{1,0:T(8,128)(2,1)S(1)}, u32[]{:S(2)}, u32[]{:S(2)}) collective-permute-start(bf16[640,320]{1,0:T(8,128)(2,1)S(1)} %copy.35), channel_id=1, source_target_pairs={{0,1},{1,0},{2,3},{3,2},{4,5},{5,4},{6,7},{7,6},{8,9},{9,8},{10,11... | collective-permute-start | bytes 1228808 | tf_op jit(solution)/shard_map/ppermute | solution.py:46
  20.8 1.0 slice.41.own_ref
  22.0 1.2 pad_maximum_fusion.mine_ref
  23.3 7.4 %collective-permute-done.4 = bf16[640,320]{1,0:T(8,128)(2,1)S(1)} collective-permute-done((bf16[640,320]{1,0:T(8,128)(2,1)S(1)}, bf16[640,320]{1,0:T(8,128)(2,1)S(1)}, u32[]{:S(2)}, u32[]{:S(2)}) %collective-permute-start.4) | collective-permute-done | bytes 409632 | tf_op jit(solution)/shard_map/ppermute | solution.py:46
  30.7 0.8 copy-done.14
  32.4 1.1 fusion.2.normed_ref
  33.6 3.2 %collective-permute-start.6 = (bf16[1,160,640]{2,1,0:T(8,128)(2,1)S(1)}, bf16[1,160,640]{2,1,0:T(8,128)(2,1)S(1)}, u32[]{:S(2)}, u32[]{:S(2)}) collective-permute-start(bf16[1,160,640]{2,1,0:T(8,128)(2,1)S(1)} %constant_dynamic-slice_fusion), channel_id=1, source_target_pairs={{0,192},{64,0},{128,64},{192,128},{1,193},{65,1},{129,65},{193,129... | collective-permute-start | bytes 614408 | tf_op jit(solution)/shard_map/ppermute | solution.py:38
  36.8 4.4 %project.2 = bf16[8,160,256]{2,1,0:T(8,128)(2,1)} custom-call(s32[3]{0:T(128)} %pad_add_fusion.1.place_ref, bf16[256,1280]{1,0:T(8,128)(2,1)} %fusion.2.normed_ref, bf16[2,320,640]{2,1,0:T(8,128)(2,1)} %copy-done.4, bf16[3,2,160,640]{3,2,1,0:T(8,128)(2,1)} %copy-done.5, bf16[3,2,160,640]{3,2,1,0:T(8,128)(2,1)} %collective-permute-done.5.other_ref), custom_call_target="tpu_custom_call" | custom-call | flops 838860800 | bytes 3276800 | tf_op jit(solution)/shard_map/project/pallas_call | solution.py:90
  41.2 8.6 %all-to-all-start = ((bf16[8,160,256]{2,1,0:T(8,128)(2,1)}), bf16[8,160,256]{2,1,0:T(8,128)(2,1)}, u32[]{:S(2)}, u32[]{:S(2)}) async-start(bf16[8,160,256]{2,1,0:T(8,128)(2,1)} %project.2), calls=%async_computation | async-start | bytes 1310720 | tf_op jit(solution)/shard_map/all_to_all | solution.py:50
  49.9 3.3 %collective-permute-start.7 = (bf16[1,80,640]{2,1,0:T(8,128)(2,1)S(1)}, bf16[1,80,640]{2,1,0:T(8,128)(2,1)S(1)}, u32[]{:S(2)}, u32[]{:S(2)}) collective-permute-start(bf16[1,80,640]{2,1,0:T(8,128)(2,1)S(1)} %slice.56), channel_id=1, source_target_pairs={{0,192},{64,0},{128,64},{192,128},{1,193},{65,1},{129,65},{193,129... | collective-permute-start | bytes 307208 | tf_op jit(solution)/shard_map/ppermute | solution.py:38
  53.2 2.5 %collective-permute-done.9 = bf16[1,80,640]{2,1,0:T(8,128)(2,1)S(1)} collective-permute-done((bf16[1,80,640]{2,1,0:T(8,128)(2,1)S(1)}, bf16[1,80,640]{2,1,0:T(8,128)(2,1)S(1)}, u32[]{:S(2)}, u32[]{:S(2)}) %collective-permute-start.9) | collective-permute-done | bytes 102432 | tf_op jit(solution)/shard_map/ppermute | solution.py:38
  56.2 1.8 collective-permute-done.10.other_ref
  58.0 0.8 copy-done.12
  58.8 3.2 %project.3 = bf16[8,80,256]{2,1,0:T(8,128)(2,1)} custom-call(s32[3]{0:T(128)} %pad_add_fusion.1.place_ref, bf16[256,1280]{1,0:T(8,128)(2,1)} %fusion.2.normed_ref, bf16[1,320,640]{2,1,0:T(8,128)(2,1)} %copy-done.6, bf16[3,1,160,640]{3,2,1,0:T(8,128)(2,1)} %copy-done.7, bf16[3,1,160,640]{3,2,1,0:T(8,128)(2,1)} %copy-done.12), custom_call_target="tpu_custom_call" | custom-call | flops 419430400 | bytes 1638400 | tf_op jit(solution)/shard_map/project/pallas_call | solution.py:90
  62.0 6.8 %all-to-all-done.own = bf16[8,160,256]{2,1,0:T(8,128)(2,1)} async-done(((bf16[8,160,256]{2,1,0:T(8,128)(2,1)}), bf16[8,160,256]{2,1,0:T(8,128)(2,1)}, u32[]{:S(2)}, u32[]{:S(2)}) %all-to-all-start) | async-done | bytes 655392 | tf_op jit(solution)/shard_map/all_to_all | solution.py:50
  68.8 1.6 collective-permute-start.11
  70.4 5.0 %all-to-all-start.1 = ((bf16[8,80,256]{2,1,0:T(8,128)(2,1)}), bf16[8,80,256]{2,1,0:T(8,128)(2,1)S(1)}, u32[]{:S(2)}, u32[]{:S(2)}) async-start(bf16[8,80,256]{2,1,0:T(8,128)(2,1)} %project.3), calls=%async_computation.1 | async-start | bytes 655360 | tf_op jit(solution)/shard_map/all_to_all | solution.py:50
  75.9 0.7 reduce.8
  77.4 3.2 %collective-permute-start.13 = (bf16[2,640,320]{1,2,0:T(8,128)(2,1)S(1)}, bf16[2,640,320]{1,2,0:T(8,128)(2,1)S(1)}, u32[]{:S(2)}, u32[]{:S(2)}) collective-permute-start(bf16[2,640,320]{1,2,0:T(8,128)(2,1)S(1)} %copy.37), channel_id=1, source_target_pairs={{0,192},{64,0},{128,64},{192,128},{1,193},{65,1},{129,65},{193,129... | collective-permute-start | bytes 2457608 | tf_op jit(solution)/shard_map/ppermute | solution.py:38
  80.9 6.5 %all-to-all-done.1.q_ref = bf16[8,80,256]{2,1,0:T(8,128)(2,1)S(1)} async-done(((bf16[8,80,256]{2,1,0:T(8,128)(2,1)}), bf16[8,80,256]{2,1,0:T(8,128)(2,1)S(1)}, u32[]{:S(2)}, u32[]{:S(2)}) %all-to-all-start.1) | async-done | bytes 327712 | tf_op jit(solution)/shard_map/all_to_all | solution.py:50
  89.6 8.6 %collective-permute-done.14 = bf16[2,640,320]{1,2,0:T(8,128)(2,1)S(1)} collective-permute-done((bf16[2,640,320]{1,2,0:T(8,128)(2,1)S(1)}, bf16[2,640,320]{1,2,0:T(8,128)(2,1)S(1)}, u32[]{:S(2)}, u32[]{:S(2)}) %collective-permute-start.14) | collective-permute-done | bytes 819232 | tf_op jit(solution)/shard_map/ppermute | solution.py:38
  98.2 14.1 %attention.1 = bf16[8,80,256]{2,1,0:T(8,128)(2,1)} custom-call(s32[2,8]{1,0:T(2,128)} %pad_add_fusion.bounds_ref, s32[3]{0:T(128)} %pad_add_fusion.1.place_ref, s32[8,256]{1,0:T(8,128)} %bitcast.53, s32[1,8192]{1,0:T(1,128)} %kframe_ref.1, bf16[8,80,256]{2,1,0:T(8,128)(2,1)} %copy-done.20, bf16[8,160,256]{2,1,0:T(8,128)(2,1)} %all-to-all-done.own, ...), custom_call_target="tpu_custom_call" | custom-call | flops 8589934592 | bytes 2621440 | tf_op jit(solution)/shard_map/attention/pallas_call | solution.py:170
  112.3 7.2 %all-to-all-start.2 = ((bf16[8,80,256]{2,1,0:T(8,128)(2,1)}), bf16[8,80,256]{2,1,0:T(8,128)(2,1)S(1)}, u32[]{:S(2)}, u32[]{:S(2)}) async-start(bf16[8,80,256]{2,1,0:T(8,128)(2,1)} %attention.1), calls=%async_computation.2 | async-start | bytes 655360 | tf_op jit(solution)/shard_map/all_to_all | solution.py:50
  120.2 0.9 slice.58
  121.1 6.2 %collective-permute-start.17 = (bf16[2,320,320]{2,1,0:T(8,128)(2,1)}, bf16[2,320,320]{2,1,0:T(8,128)(2,1)}, u32[]{:S(2)}, u32[]{:S(2)}) collective-permute-start(bf16[2,320,320]{2,1,0:T(8,128)(2,1)} %slice.58), channel_id=1, source_target_pairs={{0,192},{64,0},{128,64},{192,128},{1,193},{65,1},{129,65},{193,129... | collective-permute-start | bytes 1228808 | tf_op jit(solution)/shard_map/ppermute | solution.py:38
  128.1 1.8 all-to-all-done.2.attn_ref
  129.9 2.9 %collective-permute-start.16 = (bf16[8,80,256]{2,1,0:T(8,128)(2,1)S(1)}, bf16[8,80,256]{2,1,0:T(8,128)(2,1)S(1)}, u32[]{:S(2)}, u32[]{:S(2)}) collective-permute-start(bf16[8,80,256]{2,1,0:T(8,128)(2,1)S(1)} %all-to-all-done.2.attn_ref), channel_id=1, source_target_pairs={{0,1},{1,0},{2,3},{3,2},{4,5},{5,4},{6,7},{7,6},{8,9},{9,8},{10,11... | collective-permute-start | bytes 983048 | tf_op jit(solution)/shard_map/ppermute | solution.py:46
  133.5 0.8 reshape.142.order_ref
  134.3 1.6 collective-permute-done.17.opp_a
  135.9 3.9 %collective-permute-done.18.opp_b = bf16[2,320,320]{2,1,0:T(8,128)(2,1)S(1)} collective-permute-done((bf16[2,320,320]{2,1,0:T(8,128)(2,1)S(1)}, bf16[2,320,320]{2,1,0:T(8,128)(2,1)S(1)}, u32[]{:S(2)}, u32[]{:S(2)}) %collective-permute-start.18) | collective-permute-done | bytes 409632 | tf_op jit(solution)/shard_map/ppermute | solution.py:38
  139.8 0.8 copy-done.13
  140.7 5.9 %output.1.own = bf16[256,1280]{1,0:T(8,128)(2,1)} custom-call(s32[3]{0:T(128)} %pad_add_fusion.1.place_ref, s32[256,1]{1,0:T(8,128)} %reshape.142.order_ref, f32[1,1280]{1,0:T(1,128)} %broadcast_in_dim.4.gain_ref, bf16[256,1280]{1,0:T(8,128)(2,1)} %bitcast.44, bf16[8,80,256]{2,1,0:T(8,128)(2,1)} %copy-done.10, bf16[8,80,256]{2,1,0:T(8,128)(2,1)} %copy-done.17, ...), custom_call_target="tpu_custom_call" | custom-call | flops 1179648000 | bytes 5000000 | tf_op jit(solution)/shard_map/output/pallas_call | solution.py:256
  146.6 3.7 %collective-permute-start.20 = (bf16[256,1280]{1,0:T(8,128)(2,1)}, bf16[256,1280]{1,0:T(8,128)(2,1)S(1)}, u32[]{:S(2)}, u32[]{:S(2)}) collective-permute-start(bf16[256,1280]{1,0:T(8,128)(2,1)} %output.1.own), channel_id=1, source_target_pairs={{0,64},{64,128},{128,192},{192,0},{1,65},{65,129},{129,193},{193,1... | collective-permute-start | bytes 1966088 | tf_op jit(solution)/shard_map/ppermute | solution.py:38
  150.3 0.9 collective-permute-start.19
  151.2 11.8 %collective-permute-done.20.left = bf16[256,1280]{1,0:T(8,128)(2,1)S(1)} collective-permute-done((bf16[256,1280]{1,0:T(8,128)(2,1)}, bf16[256,1280]{1,0:T(8,128)(2,1)S(1)}, u32[]{:S(2)}, u32[]{:S(2)}) %collective-permute-start.20) | collective-permute-done | bytes 655392 | tf_op jit(solution)/shard_map/ppermute | solution.py:38
  163.0 2.2 %collective-permute-start.22 = (bf16[128,1280]{1,0:T(8,128)(2,1)S(1)}, bf16[128,1280]{1,0:T(8,128)(2,1)S(1)}, u32[]{:S(2)}, u32[]{:S(2)}) collective-permute-start(bf16[128,1280]{1,0:T(8,128)(2,1)S(1)} %slice.61), channel_id=1, source_target_pairs={{0,64},{64,128},{128,192},{192,0},{1,65},{65,129},{129,193},{193,1... | collective-permute-start | bytes 983048 | tf_op jit(solution)/shard_map/ppermute | solution.py:38
  165.2 1.2 collective-permute-start.21
  166.4 5.9 %copy.44.up_ref = bf16[5120,320]{1,0:T(8,128)(2,1)} copy(bf16[5120,320]{0,1:T(8,128)(2,1)} %param.16) | data formatting | bytes 6553600 | tf_op args[7]
  172.4 0.7 copy-done.18
  173.0 0.8 copy-done.19
  173.8 7.6 %merger.1 = bf16[256,3584]{1,0:T(8,128)(2,1)} custom-call(s32[3]{0:T(128)} %pad_add_fusion.1.place_ref, bf16[256,1280]{1,0:T(8,128)(2,1)} %output.1.own, bf16[256,1280]{1,0:T(8,128)(2,1)} %copy-done.9, bf16[256,1280]{1,0:T(8,128)(2,1)} %copy-done.8, bf16[128,1280]{1,0:T(8,128)(2,1)} %copy-done.19, bf16[128,1280]{1,0:T(8,128)(2,1)} %copy-done.18, ...), custom_call_target="tpu_custom_call" | custom-call | flops 1426063360 | bytes 9000000 | tf_op jit(solution)/shard_map/merger/pallas_call | solution.py:267
  181.4 24.0 %all_to_all.20 = bf16[8,32,3584]{2,1,0:T(8,128)(2,1)S(1)} all-to-all(bf16[8,32,3584]{2,1,0:T(8,128)(2,1)} %bitcast.43), channel_id=1, replica_groups=mesh['section'=4,'blk'=32,'tp'=2] {'section','tp'}, dimensions={0} | all-to-all | bytes 3670016 | tf_op jit(solution)/shard_map/all_to_all | solution.py:276
  205.4 1.0 reduce_sum.32
  (107 shorter events, 8.3 us)
Async XLA Ops:
  0.0 17.3 %copy-start.16 = (bf16[640,320]{0,1:T(8,128)(2,1)S(1)}, bf16[640,320]{0,1:T(8,128)(2,1)}, u32[]{:S(2)}) copy-start(bf16[640,320]{0,1:T(8,128)(2,1)} %param.14) | copy-start | bytes 1228804
  1.3 20.6 %copy-start.4 = (bf16[2,320,640]{2,1,0:T(8,128)(2,1)}, bf16[2,320,640]{2,1,0:T(8,128)(2,1)S(1)}, u32[]{:S(2)}) copy-start(bf16[2,320,640]{2,1,0:T(8,128)(2,1)S(1)} %slice.38.own_ref) | copy-start | bytes 2457604
  1.3 12.5 %collective-permute-start.2 = (bf16[2,160,640]{2,1,0:T(8,128)(2,1)S(1)}, bf16[2,160,640]{2,1,0:T(8,128)(2,1)S(1)}, u32[]{:S(2)}, u32[]{:S(2)}) collective-permute-start(bf16[2,160,640]{2,1,0:T(8,128)(2,1)S(1)} %constant_dynamic-slice_fusion.1), channel_id=1, source_target_pairs={{0,64},{64,128},{128,192},{192,0},{1,65},{65,129},{129,193},{193,1... | collective-permute-start | bytes 1228808 | tf_op jit(solution)/shard_map/ppermute | solution.py:38
  2.9 11.3 %collective-permute-start = (bf16[2,160,640]{2,1,0:T(8,128)(2,1)S(1)}, bf16[2,160,640]{2,1,0:T(8,128)(2,1)S(1)}, u32[]{:S(2)}, u32[]{:S(2)}) collective-permute-start(bf16[2,160,640]{2,1,0:T(8,128)(2,1)S(1)} %constant_dynamic-slice_fusion.1), channel_id=1, source_target_pairs={{0,192},{64,0},{128,64},{192,128},{1,193},{65,1},{129,65},{193,129... | collective-permute-start | bytes 1228808 | tf_op jit(solution)/shard_map/ppermute | solution.py:38
  13.9 8.0 %collective-permute-start.3 = (bf16[2,80,640]{2,1,0:T(8,128)(2,1)S(1)}, bf16[2,80,640]{2,1,0:T(8,128)(2,1)S(1)}, u32[]{:S(2)}, u32[]{:S(2)}) collective-permute-start(bf16[2,80,640]{2,1,0:T(8,128)(2,1)S(1)} %slice.55), channel_id=1, source_target_pairs={{0,64},{64,128},{128,192},{192,0},{1,65},{65,129},{129,193},{193,1... | collective-permute-start | bytes 614408 | tf_op jit(solution)/shard_map/ppermute | solution.py:38
  14.2 7.7 %copy-start.11 = (bf16[2,160,640]{2,1,0:T(8,128)(2,1)}, bf16[2,160,640]{2,1,0:T(8,128)(2,1)S(1)}, u32[]{:S(2)}) copy-start(bf16[2,160,640]{2,1,0:T(8,128)(2,1)S(1)} %collective-permute-done) | copy-start | bytes 1228804
  14.2 7.7 %collective-permute-start.1 = (bf16[2,80,640]{2,1,0:T(8,128)(2,1)S(1)}, bf16[2,80,640]{2,1,0:T(8,128)(2,1)S(1)}, u32[]{:S(2)}, u32[]{:S(2)}) collective-permute-start(bf16[2,80,640]{2,1,0:T(8,128)(2,1)S(1)} %slice.54), channel_id=1, source_target_pairs={{0,192},{64,0},{128,64},{192,128},{1,193},{65,1},{129,65},{193,129... | collective-permute-start | bytes 614408 | tf_op jit(solution)/shard_map/ppermute | solution.py:38
  17.6 13.1 %collective-permute-start.4 = (bf16[640,320]{1,0:T(8,128)(2,1)S(1)}, bf16[640,320]{1,0:T(8,128)(2,1)S(1)}, u32[]{:S(2)}, u32[]{:S(2)}) collective-permute-start(bf16[640,320]{1,0:T(8,128)(2,1)S(1)} %copy.35), channel_id=1, source_target_pairs={{0,1},{1,0},{2,3},{3,2},{4,5},{5,4},{6,7},{7,6},{8,9},{9,8},{10,11... | collective-permute-start | bytes 1228808 | tf_op jit(solution)/shard_map/ppermute | solution.py:46
  21.9 11.6 %copy-start.6 = (bf16[1,320,640]{2,1,0:T(8,128)(2,1)}, bf16[1,320,640]{2,1,0:T(8,128)(2,1)S(1)}, u32[]{:S(2)}) copy-start(bf16[1,320,640]{2,1,0:T(8,128)(2,1)S(1)} %slice.41.own_ref) | copy-start | bytes 1228804
  22.0 10.2 %copy-start.3 = (bf16[1,256,1280]{2,1,0:T(8,128)(2,1)S(1)}, bf16[1,256,1280]{2,1,0:T(8,128)(2,1)}, u32[]{:S(2)}) copy-start(bf16[1,256,1280]{2,1,0:T(8,128)(2,1)} %param.9) | copy-start | bytes 1966084
  22.0 10.4 %copy-start.23 = (f32[1280]{0:T(1024)S(1)}, f32[1280]{0:T(1024)}, u32[]{:S(2)}) copy-start(f32[1280]{0:T(1024)} %param.12) | copy-start | bytes 15364
  23.2 13.5 %copy-start.5 = (bf16[3,2,160,640]{3,2,1,0:T(8,128)(2,1)}, bf16[3,2,160,640]{3,2,1,0:T(8,128)(2,1)S(1)}, u32[]{:S(2)}) copy-start(bf16[3,2,160,640]{3,2,1,0:T(8,128)(2,1)S(1)} %pad_maximum_fusion.mine_ref) | copy-start | bytes 3686404
  31.5 5.3 %collective-permute-start.5 = (bf16[3,2,160,640]{3,2,1,0:T(8,128)(2,1)S(1)}, bf16[3,2,160,640]{3,2,1,0:T(8,128)(2,1)}, u32[]{:S(2)}, u32[]{:S(2)}) collective-permute-start(bf16[3,2,160,640]{3,2,1,0:T(8,128)(2,1)S(1)} %pad_maximum_fusion.mine_ref), channel_id=1, source_target_pairs={{0,2},{2,0},{4,6},{6,4},{8,10},{10,8},{12,14},{14,12},{16,18},{18,... | collective-permute-start | bytes 3686408 | tf_op jit(solution)/shard_map/ppermute | solution.py:42
  33.5 16.3 %collective-permute-start.8 = (bf16[1,160,640]{2,1,0:T(8,128)(2,1)S(1)}, bf16[1,160,640]{2,1,0:T(8,128)(2,1)S(1)}, u32[]{:S(2)}, u32[]{:S(2)}) collective-permute-start(bf16[1,160,640]{2,1,0:T(8,128)(2,1)S(1)} %constant_dynamic-slice_fusion), channel_id=1, source_target_pairs={{0,64},{64,128},{128,192},{192,0},{1,65},{65,129},{129,193},{193,1... | collective-permute-start | bytes 614408 | tf_op jit(solution)/shard_map/ppermute | solution.py:38
  33.6 16.3 %collective-permute-start.6 = (bf16[1,160,640]{2,1,0:T(8,128)(2,1)S(1)}, bf16[1,160,640]{2,1,0:T(8,128)(2,1)S(1)}, u32[]{:S(2)}, u32[]{:S(2)}) collective-permute-start(bf16[1,160,640]{2,1,0:T(8,128)(2,1)S(1)} %constant_dynamic-slice_fusion), channel_id=1, source_target_pairs={{0,192},{64,0},{128,64},{192,128},{1,193},{65,1},{129,65},{193,129... | collective-permute-start | bytes 614408 | tf_op jit(solution)/shard_map/ppermute | solution.py:38
  41.2 27.6 %all-to-all-start = ((bf16[8,160,256]{2,1,0:T(8,128)(2,1)}), bf16[8,160,256]{2,1,0:T(8,128)(2,1)}, u32[]{:S(2)}, u32[]{:S(2)}) async-start(bf16[8,160,256]{2,1,0:T(8,128)(2,1)} %project.2), calls=%async_computation | async-start | bytes 1310720 | tf_op jit(solution)/shard_map/all_to_all | solution.py:50
  49.7 6.2 %copy-start.15 = (bf16[640,320]{1,0:T(8,128)(2,1)S(1)}, bf16[640,320]{1,0:T(8,128)(2,1)}, u32[]{:S(2)}) copy-start(bf16[640,320]{1,0:T(8,128)(2,1)} %copy-done.14) | copy-start | bytes 1228804
  49.8 5.9 %collective-permute-start.9 = (bf16[1,80,640]{2,1,0:T(8,128)(2,1)S(1)}, bf16[1,80,640]{2,1,0:T(8,128)(2,1)S(1)}, u32[]{:S(2)}, u32[]{:S(2)}) collective-permute-start(bf16[1,80,640]{2,1,0:T(8,128)(2,1)S(1)} %slice.57), channel_id=1, source_target_pairs={{0,64},{64,128},{128,192},{192,0},{1,65},{65,129},{129,193},{193,1... | collective-permute-start | bytes 307208 | tf_op jit(solution)/shard_map/ppermute | solution.py:38
  49.9 5.8 %collective-permute-start.7 = (bf16[1,80,640]{2,1,0:T(8,128)(2,1)S(1)}, bf16[1,80,640]{2,1,0:T(8,128)(2,1)S(1)}, u32[]{:S(2)}, u32[]{:S(2)}) collective-permute-start(bf16[1,80,640]{2,1,0:T(8,128)(2,1)S(1)} %slice.56), channel_id=1, source_target_pairs={{0,192},{64,0},{128,64},{192,128},{1,193},{65,1},{129,65},{193,129... | collective-permute-start | bytes 307208 | tf_op jit(solution)/shard_map/ppermute | solution.py:38
  55.8 2.1 %copy-start.7 = (bf16[3,1,160,640]{3,2,1,0:T(8,128)(2,1)}, bf16[3,1,160,640]{3,2,1,0:T(8,128)(2,1)S(1)}, u32[]{:S(2)}) copy-start(bf16[3,1,160,640]{3,2,1,0:T(8,128)(2,1)S(1)} %pad_maximum_fusion.2.mine_ref) | copy-start | bytes 1843204
  55.8 2.1 %collective-permute-start.10 = (bf16[3,1,160,640]{3,2,1,0:T(8,128)(2,1)S(1)}, bf16[3,1,160,640]{3,2,1,0:T(8,128)(2,1)S(1)}, u32[]{:S(2)}, u32[]{:S(2)}) collective-permute-start(bf16[3,1,160,640]{3,2,1,0:T(8,128)(2,1)S(1)} %pad_maximum_fusion.2.mine_ref), channel_id=1, source_target_pairs={{0,2},{2,0},{4,6},{6,4},{8,10},{10,8},{12,14},{14,12},{16,18},{18,... | collective-permute-start | bytes 1843208 | tf_op jit(solution)/shard_map/ppermute | solution.py:42
  56.1 20.5 %copy-start = (bf16[2,640,320]{2,1,0:T(8,128)(2,1)}, bf16[2,640,320]{2,1,0:T(8,128)(2,1)S(1)}, u32[]{:S(2)}) copy-start(bf16[2,640,320]{2,1,0:T(8,128)(2,1)S(1)} %pad_maximum_fusion.1.own) | copy-start | bytes 2457604
  56.2 19.7 %copy-start.21 = (s32[1,8192]{1,0:T(1,128)S(1)}, s32[1,8192]{1,0:T(1,128)}, u32[]{:S(2)}) copy-start(s32[1,8192]{1,0:T(1,128)} %kframe_ref.1) | copy-start | bytes 98308
  58.0 0.8 copy-start.12
  68.8 18.6 %collective-permute-start.11 = (bf16[8,160,256]{2,1,0:T(8,128)(2,1)}, bf16[8,160,256]{2,1,0:T(8,128)(2,1)}, u32[]{:S(2)}, u32[]{:S(2)}) collective-permute-start(bf16[8,160,256]{2,1,0:T(8,128)(2,1)} %all-to-all-done.own), channel_id=1, source_target_pairs={{0,32},{2,34},{4,36},{6,38},{8,40},{10,42},{12,44},{14,46},{16,48}... | collective-permute-start | bytes 1966088 | tf_op jit(solution)/shard_map/ppermute | solution.py:42
  70.4 17.0 %all-to-all-start.1 = ((bf16[8,80,256]{2,1,0:T(8,128)(2,1)}), bf16[8,80,256]{2,1,0:T(8,128)(2,1)S(1)}, u32[]{:S(2)}, u32[]{:S(2)}) async-start(bf16[8,80,256]{2,1,0:T(8,128)(2,1)} %project.3), calls=%async_computation.1 | async-start | bytes 655360 | tf_op jit(solution)/shard_map/all_to_all | solution.py:50
  76.7 12.3 %copy-start.22 = (s32[1,8,1,256]{3,1,2,0:T(8,128)}, s32[1,8,1,256]{3,1,2,0:T(8,128)S(1)}, u32[]{:S(2)}) copy-start(s32[1,8,1,256]{3,1,2,0:T(8,128)S(1)} %copy.48) | copy-start | bytes 24580
  77.3 20.9 %collective-permute-start.14 = (bf16[2,640,320]{1,2,0:T(8,128)(2,1)S(1)}, bf16[2,640,320]{1,2,0:T(8,128)(2,1)S(1)}, u32[]{:S(2)}, u32[]{:S(2)}) collective-permute-start(bf16[2,640,320]{1,2,0:T(8,128)(2,1)S(1)} %copy.37), channel_id=1, source_target_pairs={{0,64},{64,128},{128,192},{192,0},{1,65},{65,129},{129,193},{193,1... | collective-permute-start | bytes 2457608 | tf_op jit(solution)/shard_map/ppermute | solution.py:38
  77.4 20.8 %collective-permute-start.13 = (bf16[2,640,320]{1,2,0:T(8,128)(2,1)S(1)}, bf16[2,640,320]{1,2,0:T(8,128)(2,1)S(1)}, u32[]{:S(2)}, u32[]{:S(2)}) collective-permute-start(bf16[2,640,320]{1,2,0:T(8,128)(2,1)S(1)} %copy.37), channel_id=1, source_target_pairs={{0,192},{64,0},{128,64},{192,128},{1,193},{65,1},{129,65},{193,129... | collective-permute-start | bytes 2457608 | tf_op jit(solution)/shard_map/ppermute | solution.py:38
  80.8 17.4 %collective-permute-start.12 = (bf16[8,160,256]{2,1,0:T(8,128)(2,1)}, bf16[8,160,256]{2,1,0:T(8,128)(2,1)}, u32[]{:S(2)}, u32[]{:S(2)}) collective-permute-start(bf16[8,160,256]{2,1,0:T(8,128)(2,1)} %all-to-all-done.own), channel_id=1, source_target_pairs={{0,2},{2,0},{4,6},{6,4},{8,10},{10,8},{12,14},{14,12},{16,18},{18,... | collective-permute-start | bytes 1966088 | tf_op jit(solution)/shard_map/ppermute | solution.py:42
  87.4 10.8 %copy-start.20 = (bf16[8,80,256]{2,1,0:T(8,128)(2,1)}, bf16[8,80,256]{2,1,0:T(8,128)(2,1)S(1)}, u32[]{:S(2)}) copy-start(bf16[8,80,256]{2,1,0:T(8,128)(2,1)S(1)} %all-to-all-done.1.q_ref) | copy-start | bytes 983044
  87.4 10.8 %collective-permute-start.15 = (bf16[8,160,256]{2,1,0:T(8,128)(2,1)}, bf16[8,160,256]{2,1,0:T(8,128)(2,1)}, u32[]{:S(2)}, u32[]{:S(2)}) collective-permute-start(bf16[8,160,256]{2,1,0:T(8,128)(2,1)} %collective-permute-done.11.far), channel_id=1, source_target_pairs={{0,2},{2,0},{4,6},{6,4},{8,10},{10,8},{12,14},{14,12},{16,18},{18,... | collective-permute-start | bytes 1966088 | tf_op jit(solution)/shard_map/ppermute | solution.py:42
  112.3 17.6 %all-to-all-start.2 = ((bf16[8,80,256]{2,1,0:T(8,128)(2,1)}), bf16[8,80,256]{2,1,0:T(8,128)(2,1)S(1)}, u32[]{:S(2)}, u32[]{:S(2)}) async-start(bf16[8,80,256]{2,1,0:T(8,128)(2,1)} %attention.1), calls=%async_computation.2 | async-start | bytes 655360 | tf_op jit(solution)/shard_map/all_to_all | solution.py:50
  120.2 7.7 %copy-start.1 = (bf16[2,640,320]{2,1,0:T(8,128)(2,1)}, bf16[2,640,320]{2,1,0:T(8,128)(2,1)S(1)}, u32[]{:S(2)}) copy-start(bf16[2,640,320]{2,1,0:T(8,128)(2,1)S(1)} %copy.42.right) | copy-start | bytes 2457604
  121.1 11.7 %copy-start.25 = (s32[1,64,4]{1,2,0:T(4,128)S(1)}, s32[1,64,4]{1,2,0:T(4,128)}, u32[]{:S(2)}) copy-start(s32[1,64,4]{1,2,0:T(4,128)} %param.11) | copy-start | bytes 3076
  121.1 11.8 %copy-start.24 = (f32[1280]{0:T(1024)S(1)}, f32[1280]{0:T(1024)}, u32[]{:S(2)}) copy-start(f32[1280]{0:T(1024)} %param.15) | copy-start | bytes 15364
  121.1 14.8 %collective-permute-start.17 = (bf16[2,320,320]{2,1,0:T(8,128)(2,1)}, bf16[2,320,320]{2,1,0:T(8,128)(2,1)}, u32[]{:S(2)}, u32[]{:S(2)}) collective-permute-start(bf16[2,320,320]{2,1,0:T(8,128)(2,1)} %slice.58), channel_id=1, source_target_pairs={{0,192},{64,0},{128,64},{192,128},{1,193},{65,1},{129,65},{193,129... | collective-permute-start | bytes 1228808 | tf_op jit(solution)/shard_map/ppermute | solution.py:38
  127.9 11.9 %copy-start.2 = (bf16[2,640,320]{2,1,0:T(8,128)(2,1)}, bf16[2,640,320]{2,1,0:T(8,128)(2,1)S(1)}, u32[]{:S(2)}) copy-start(bf16[2,640,320]{2,1,0:T(8,128)(2,1)S(1)} %copy.43.left) | copy-start | bytes 2457604
  128.0 11.8 %collective-permute-start.18 = (bf16[2,320,320]{2,1,0:T(8,128)(2,1)S(1)}, bf16[2,320,320]{2,1,0:T(8,128)(2,1)S(1)}, u32[]{:S(2)}, u32[]{:S(2)}) collective-permute-start(bf16[2,320,320]{2,1,0:T(8,128)(2,1)S(1)} %slice.59), channel_id=1, source_target_pairs={{0,64},{64,128},{128,192},{192,0},{1,65},{65,129},{129,193},{193,1... | collective-permute-start | bytes 1228808 | tf_op jit(solution)/shard_map/ppermute | solution.py:38
  129.9 9.9 %copy-start.10 = (bf16[8,80,256]{2,1,0:T(8,128)(2,1)}, bf16[8,80,256]{2,1,0:T(8,128)(2,1)S(1)}, u32[]{:S(2)}) copy-start(bf16[8,80,256]{2,1,0:T(8,128)(2,1)S(1)} %all-to-all-done.2.attn_ref) | copy-start | bytes 983044
  129.9 9.9 %collective-permute-start.16 = (bf16[8,80,256]{2,1,0:T(8,128)(2,1)S(1)}, bf16[8,80,256]{2,1,0:T(8,128)(2,1)S(1)}, u32[]{:S(2)}, u32[]{:S(2)}) collective-permute-start(bf16[8,80,256]{2,1,0:T(8,128)(2,1)S(1)} %all-to-all-done.2.attn_ref), channel_id=1, source_target_pairs={{0,1},{1,0},{2,3},{3,2},{4,5},{5,4},{6,7},{7,6},{8,9},{9,8},{10,11... | collective-permute-start | bytes 983048 | tf_op jit(solution)/shard_map/ppermute | solution.py:46
  139.8 0.9 copy-start.17
  146.6 16.3 %collective-permute-start.20 = (bf16[256,1280]{1,0:T(8,128)(2,1)}, bf16[256,1280]{1,0:T(8,128)(2,1)S(1)}, u32[]{:S(2)}, u32[]{:S(2)}) collective-permute-start(bf16[256,1280]{1,0:T(8,128)(2,1)} %output.1.own), channel_id=1, source_target_pairs={{0,64},{64,128},{128,192},{192,0},{1,65},{65,129},{129,193},{193,1... | collective-permute-start | bytes 1966088 | tf_op jit(solution)/shard_map/ppermute | solution.py:38
  150.3 14.9 %collective-permute-start.19 = (bf16[256,1280]{1,0:T(8,128)(2,1)}, bf16[256,1280]{1,0:T(8,128)(2,1)S(1)}, u32[]{:S(2)}, u32[]{:S(2)}) collective-permute-start(bf16[256,1280]{1,0:T(8,128)(2,1)} %output.1.own), channel_id=1, source_target_pairs={{0,192},{64,0},{128,64},{192,128},{1,193},{65,1},{129,65},{193,129... | collective-permute-start | bytes 1966088 | tf_op jit(solution)/shard_map/ppermute | solution.py:38
  162.9 9.3 %copy-start.8 = (bf16[256,1280]{1,0:T(8,128)(2,1)}, bf16[256,1280]{1,0:T(8,128)(2,1)S(1)}, u32[]{:S(2)}) copy-start(bf16[256,1280]{1,0:T(8,128)(2,1)S(1)} %collective-permute-done.20.left) | copy-start | bytes 1966084
  163.0 9.3 %collective-permute-start.22 = (bf16[128,1280]{1,0:T(8,128)(2,1)S(1)}, bf16[128,1280]{1,0:T(8,128)(2,1)S(1)}, u32[]{:S(2)}, u32[]{:S(2)}) collective-permute-start(bf16[128,1280]{1,0:T(8,128)(2,1)S(1)} %slice.61), channel_id=1, source_target_pairs={{0,64},{64,128},{128,192},{192,0},{1,65},{65,129},{129,193},{193,1... | collective-permute-start | bytes 983048 | tf_op jit(solution)/shard_map/ppermute | solution.py:38
  165.2 7.1 %copy-start.9 = (bf16[256,1280]{1,0:T(8,128)(2,1)}, bf16[256,1280]{1,0:T(8,128)(2,1)S(1)}, u32[]{:S(2)}) copy-start(bf16[256,1280]{1,0:T(8,128)(2,1)S(1)} %collective-permute-done.19.right) | copy-start | bytes 1966084
  165.2 7.2 %collective-permute-start.21 = (bf16[128,1280]{1,0:T(8,128)(2,1)S(1)}, bf16[128,1280]{1,0:T(8,128)(2,1)S(1)}, u32[]{:S(2)}, u32[]{:S(2)}) collective-permute-start(bf16[128,1280]{1,0:T(8,128)(2,1)S(1)} %slice.60), channel_id=1, source_target_pairs={{0,192},{64,0},{128,64},{192,128},{1,193},{65,1},{129,65},{193,129... | collective-permute-start | bytes 983048 | tf_op jit(solution)/shard_map/ppermute | solution.py:38
  (4 other events, 3.1 us)

commit v4 on v3

--- a/solution.py
+++ b/solution.py
@@ -201,55 +201,71 @@
     out_ref[...] = rms_norm(total, gain_ref[...]).astype(bf16)
 
 
-def merger_kernel(place_ref, own, right, left, opp_a, opp_b, up_ref, down_ref, out_ref, tokens):
-    me = place_ref[0]
-
-    def put(distance, source, first_half):
-        for part in range(source.shape[0] // 128):
-            slot = lax.rem(me + distance + 1, SECTIONS) * 2 + first_half + part
-            rows = pl.ds(pl.multiple_of(slot * 32, 32), 32)
+def merger_kernel(sizes, place_ref, *refs):
+    count = len(sizes)
+    sources, (up_ref, down_ref), outs, tokens = refs[:count], refs[count : count + 2], refs[count + 2 : -1], refs[-1]
+    tp = place_ref[3]
+    place = 0
+    for source, size in zip(sources, sizes):
+        for part in range(size // 128):
+            half = jnp.bitwise_xor(tp, place % 2)
+            rows = pl.ds(pl.multiple_of(place // 2 * 64 + half * 32, 32), 32)
             for j in range(4):
                 low = part * 128 + j * 32
                 tokens[j, rows, :] = source[low : low + 32, :]
-
-    put(0, own, 0)
-    put(1, right, 0)
-    put(3, left, 0)
-    put(2, opp_a, 0)
-    put(2, opp_b, 1)
-    hidden = jnp.zeros((256, 320), f32)
+            place += 1
+    hidden = jnp.zeros((place * 32, 320), f32)
     for j in range(4):
         hidden += jnp.dot(tokens[j], up_ref[j * 1280 : (j + 1) * 1280, :], preferred_element_type=f32)
     hidden = (0.5 * hidden * (1.0 + lax.erf(hidden * (0.5**0.5)))).astype(bf16)
     for k in range(7):
         columns = slice(k * 512, (k + 1) * 512)
-        out_ref[:, columns] = jnp.dot(hidden, down_ref[:, columns], preferred_element_type=f32).astype(bf16)
+        made = jnp.dot(hidden, down_ref[:, columns], preferred_element_type=f32).astype(bf16)
+        for n, out in enumerate(outs):
+            out[:, columns] = made[n * 32 : (n + 1) * 32]
+
+
+def merge(place, pieces, merger_up, merger_down, name):
+    sizes = [piece.shape[0] for piece in pieces]
+    total = sum(sizes) // 4
+    return call(
+        functools.partial(merger_kernel, sizes),
+        tuple(jax.ShapeDtypeStruct((32, 3584), bf16) for _ in range(total // 32)),
+        [SMEM] + [VMEM] * (len(pieces) + 2),
+        [pltpu.VMEM((4, total, 1280), bf16)],
+        flops=2 * 256 * 320 * (5120 + 3584),
+        moved=6000000,
+        name=name,
+    )(place, *pieces, merger_up, merger_down)
+
+
+def send(value, distance, flip):
+    route = [(s * 2 + t, (s + distance) % SECTIONS * 2 + (t ^ flip)) for s in range(SECTIONS) for t in range(2)]
+    return lax.ppermute(value, ("section", "tp"), route)
 
 
 def on_device(patches, frame_ids, groups, norm_gain, qkv_weight, out_weight, merge_gain, merger_up, merger_down):
-    me, blk = lax.axis_index("section"), lax.axis_index("blk")
+    me, blk, tp = lax.axis_index("section"), lax.axis_index("blk"), lax.axis_index("tp")
     core, y = blk % 2, blk // 16
-    place = jnp.stack([me, core, y]).astype(jnp.int32)
+    place = jnp.stack([me, core, y, tp]).astype(jnp.int32)
     patch = patches[0]
     normed = rms_norm(patch.astype(f32), norm_gain).astype(bf16)
 
     kv_own, q_own = qkv_weight[1:3], qkv_weight[0:1]
-    kv_mine, out_weight_t = lax.optimization_barrier((fetch(kv_own, core), tp_swap(out_weight)))
-    kv_mine, q_own = lax.optimization_barrier((kv_mine, q_own))
+    kv_mine, q_own = lax.optimization_barrier((fetch(kv_own, core), q_own))
     kv = z_exchange(project(place, normed, kv_own, kv_mine, 1.0))
-    q = project(place, normed, q_own, fetch(q_own, core), HD ** (-0.5) * math.log2(math.e))
+    q_mine, out_weight_t = lax.optimization_barrier((fetch(q_own, core), tp_swap(out_weight)))
     out_own = jnp.stack([out_weight, out_weight_t])
-    q, out_own = lax.optimization_barrier((q, out_own))
     out_right, out_left = section_shift(out_own, -1), section_shift(out_own, 1)
+    q = project(place, normed, q_own, q_mine, HD ** (-0.5) * math.log2(math.e))
     kv, q = lax.optimization_barrier((kv, q))
     far = blk_swap(kv, 16)
     near = blk_swap(kv, 1)
     q = z_exchange(q)
-    far, q = lax.optimization_barrier((far, q))
+    far, q, out_right, out_left = lax.optimization_barrier((far, q, out_right, out_left))
     across = blk_swap(far, 1)
-
-    out_right, out_left, across = lax.optimization_barrier((out_right, out_left, across))
     out_a, out_b = section_shift(out_right[:, :320], -1), section_shift(out_left[:, 320:], 1)
+
     attn = z_exchange(attention(place, frame_ids[0], q, (kv, near, far, across), y, core))
     attn_t = tp_swap(attn)
     order = groups[0].reshape(2, 32, 4).transpose(0, 2, 1).reshape(256, 1)
@@ -263,18 +279,18 @@
         name="output",
     )(place, order, merge_gain[None, :], patch, attn, attn_t, out_own, out_right, out_left, out_a, out_b)
 
-    right, left, opp_a, opp_b = ring_halves(own)
-    partial = call(
-        merger_kernel,
-        jax.ShapeDtypeStruct((256, 3584), bf16),
-        [SMEM] + [VMEM] * 7,
-        [pltpu.VMEM((4, 256, 1280), bf16)],
-        flops=2 * 256 * 320 * (5120 + 3584),
-        moved=9000000,
-        name="merger",
-    )(place, own, right, left, opp_a, opp_b, merger_up, merger_down)
-    parts = lax.all_to_all(partial.reshape(8, 32, 3584), ("section", "tp"), 0, 0, tiled=True)
-    return jnp.sum(parts.astype(f32), axis=0).astype(bf16)[None]
+    right, left = section_shift(own, -1), section_shift(own, 1)
+    own_same, own_other = merge(place, [own], merger_up, merger_down, "merge_own")
+    right, left, own_same, own_other = lax.optimization_barrier((right, left, own_same, own_other))
+    opp_a, opp_b = section_shift(right[:128], -1), section_shift(left[128:], 1)
+    sums = [send(own_same, 1, 0), send(own_other, 1, 1)]
+    right_same, right_other, left_same, left_other = merge(
+        place, [right, left], merger_up, merger_down, "merge_next"
+    )
+    sums += [send(right_same, 2, 0), send(right_other, 2, 1), left_same, send(left_other, 0, 1)]
+    opp_same, opp_other = merge(place, [opp_a, opp_b], merger_up, merger_down, "merge_opposite")
+    sums += [send(opp_same, 3, 0), send(opp_other, 3, 1)]
+    return sum(part.astype(f32) for part in sums).astype(bf16)[None]
 
 
 def solution(mesh):

time: 210 us -> 198 us (0.943); the launches traced: 206 us -> 197 us
  blocking collectives: 24 us -> 0 us
  starting transfers between devices: 59.6 us -> 72.1 us
  Pallas kernels: 35.2 us -> 43.7 us
  waiting for transfers between devices: 62 us -> 55.9 us
    all_to_all x1 -> x0, blocking collectives: 24 us -> none  [on_device(): lax.all_to_all(partial.reshape(8, 32, 3584), ('section', 'tp'), 0, 0, til...]
    ppermute x0 -> x7, starting transfers between devices: none -> 13.7 us  [send(): return lax.ppermute(value, ('section', 'tp'), route)]
    all_to_all x3, waiting for transfers between devices: 15.1 us -> 4.3 us  [z_exchange(): lax.all_to_all(value, 'blk', 0, 0, axis_index_groups=Z_GROUPS, tiled=True)]
    pallas_call x1 -> x3, Pallas kernels: 7.62 us -> 16.6 us  [merge(): call(functools.partial(merger_kernel, sizes), tuple((jax.ShapeDtypeStruct...]
    ppermute x0 -> x7, waiting for transfers between devices: none -> 8.66 us  [send(): return lax.ppermute(value, ('section', 'tp'), route)]
    ppermute x2, waiting for transfers between devices: 7.42 us -> 4.86 us  [tp_swap(): return lax.ppermute(value, 'tp', [(0, 1), (1, 0)])]
    unnamed x56 -> x60, local copies, waits for them, and re-layouts: 10.6 us -> 10.1 us
  transfers between devices with their start and end apart: 26 -> 33, of which waited for: 12 -> 16; matrix products, arithmetic and copies ran while one was open for 9% -> 9% of each run, Pallas kernels for 4% -> 12%
where the time goes in v4:
time: 198 us; the launch traced here: 197 us
  starting transfers between devices  72.1 us (36%)
  waiting for transfers between devices  55.9 us (28%)
  Pallas kernels  43.7 us (22%)
  local copies, waits for them, and re-layouts  19.2 us (10%)
  other arithmetic  5.1 us (3%)
    ppermute x16, waiting for transfers between devices, section_shift(): return lax.ppermute(value, 'section', route)  38 us
    ppermute x16, starting transfers between devices, section_shift(): return lax.ppermute(value, 'section', route)  29.1 us
    all_to_all x3, starting transfers between devices, z_exchange(): lax.all_to_all(value, 'blk', 0, 0, axis_index_groups=Z_GROUPS, tiled=True)  20.9 us
    pallas_call x3, Pallas kernels, merge(): call(functools.partial(merger_kernel, sizes), tuple((jax.ShapeDtypeStruct...  16.6 us
    ppermute x7, starting transfers between devices, send(): return lax.ppermute(value, ('section', 'tp'), route)  13.7 us
    pallas_call x1, Pallas kernels, attention(): call(attention_kernel, jax.ShapeDtypeStruct((ZN, HD, 256), bf16), [SMEM,...  13.6 us
    unnamed x60, local copies, waits for them, and re-layouts  10.1 us
    ppermute x7, waiting for transfers between devices, send(): return lax.ppermute(value, ('section', 'tp'), route)  8.66 us
  transfers between devices with their start and end apart: 33, of which 16 were waited for; matrix products, arithmetic and copies ran while one was open for 9% of the time, Pallas kernels for 12%

profile of v4, /device:TPU:32, one launch (start us, length us, event | category | flops | bytes accessed | tf_op | source)
XLA Modules:
  0.0 196.6 jit_solution(13623762781789545214)
XLA Ops:
  0.0 1.2 slice.38.own_ref
  1.3 1.6 collective-permute-start.2
  2.9 1.7 collective-permute-start
  4.6 9.2 %collective-permute-done.2 = bf16[2,160,640]{2,1,0:T(8,128)(2,1)S(1)} collective-permute-done((bf16[2,160,640]{2,1,0:T(8,128)(2,1)S(1)}, bf16[2,160,640]{2,1,0:T(8,128)(2,1)S(1)}, u32[]{:S(2)}, u32[]{:S(2)}) %collective-permute-start.2) | collective-permute-done | bytes 409632 | tf_op jit(solution)/shard_map/ppermute | solution.py:38
  14.2 3.0 %collective-permute-start.1 = (bf16[2,80,640]{2,1,0:T(8,128)(2,1)S(1)}, bf16[2,80,640]{2,1,0:T(8,128)(2,1)S(1)}, u32[]{:S(2)}, u32[]{:S(2)}) collective-permute-start(bf16[2,80,640]{2,1,0:T(8,128)(2,1)S(1)} %slice.54), channel_id=1, source_target_pairs={{0,192},{64,0},{128,64},{192,128},{1,193},{65,1},{129,65},{193,129... | collective-permute-start | bytes 614408 | tf_op jit(solution)/shard_map/ppermute | solution.py:38
  17.2 1.0 slice.41.own_ref
  18.3 2.8 %collective-permute-done.3 = bf16[2,80,640]{2,1,0:T(8,128)(2,1)S(1)} collective-permute-done((bf16[2,80,640]{2,1,0:T(8,128)(2,1)S(1)}, bf16[2,80,640]{2,1,0:T(8,128)(2,1)S(1)}, u32[]{:S(2)}, u32[]{:S(2)}) %collective-permute-start.3) | collective-permute-done | bytes 204832 | tf_op jit(solution)/shard_map/ppermute | solution.py:38
  22.4 1.1 fusion.2.normed_ref
  24.1 2.8 %collective-permute-start.5 = (bf16[1,160,640]{2,1,0:T(8,128)(2,1)S(1)}, bf16[1,160,640]{2,1,0:T(8,128)(2,1)S(1)}, u32[]{:S(2)}, u32[]{:S(2)}) collective-permute-start(bf16[1,160,640]{2,1,0:T(8,128)(2,1)S(1)} %constant_dynamic-slice_fusion), channel_id=1, source_target_pairs={{0,192},{64,0},{128,64},{192,128},{1,193},{65,1},{129,65},{193,129... | collective-permute-start | bytes 614408 | tf_op jit(solution)/shard_map/ppermute | solution.py:38
  26.8 1.1 copy-done.11
  27.9 4.4 %project.2 = bf16[8,160,256]{2,1,0:T(8,128)(2,1)} custom-call(s32[4]{0:T(128)} %pad_add_fusion.1.place_ref, bf16[256,1280]{1,0:T(8,128)(2,1)} %fusion.2.normed_ref, bf16[2,320,640]{2,1,0:T(8,128)(2,1)} %copy-done.4, bf16[3,2,160,640]{3,2,1,0:T(8,128)(2,1)} %copy-done.5, bf16[3,2,160,640]{3,2,1,0:T(8,128)(2,1)} %copy-done.11), custom_call_target="tpu_custom_call" | custom-call | flops 838860800 | bytes 3276800 | tf_op jit(solution)/shard_map/project/pallas_call | solution.py:90
  32.3 8.7 %all-to-all-start = ((bf16[8,160,256]{2,1,0:T(8,128)(2,1)}), bf16[8,160,256]{2,1,0:T(8,128)(2,1)}, u32[]{:S(2)}, u32[]{:S(2)}) async-start(bf16[8,160,256]{2,1,0:T(8,128)(2,1)} %project.2), calls=%async_computation | async-start | bytes 1310720 | tf_op jit(solution)/shard_map/all_to_all | solution.py:50
  41.3 3.3 %collective-permute-start.9 = (bf16[640,320]{1,0:T(8,128)(2,1)S(1)}, bf16[640,320]{1,0:T(8,128)(2,1)S(1)}, u32[]{:S(2)}, u32[]{:S(2)}) collective-permute-start(bf16[640,320]{1,0:T(8,128)(2,1)S(1)} %copy.41), channel_id=1, source_target_pairs={{0,1},{1,0},{2,3},{3,2},{4,5},{5,4},{6,7},{7,6},{8,9},{9,8},{10,11... | collective-permute-start | bytes 1228808 | tf_op jit(solution)/shard_map/ppermute | solution.py:46
  44.7 3.3 %collective-permute-start.6 = (bf16[1,80,640]{2,1,0:T(8,128)(2,1)S(1)}, bf16[1,80,640]{2,1,0:T(8,128)(2,1)S(1)}, u32[]{:S(2)}, u32[]{:S(2)}) collective-permute-start(bf16[1,80,640]{2,1,0:T(8,128)(2,1)S(1)} %slice.56), channel_id=1, source_target_pairs={{0,192},{64,0},{128,64},{192,128},{1,193},{65,1},{129,65},{193,129... | collective-permute-start | bytes 307208 | tf_op jit(solution)/shard_map/ppermute | solution.py:38
  48.0 2.5 %collective-permute-done.8 = bf16[1,80,640]{2,1,0:T(8,128)(2,1)S(1)} collective-permute-done((bf16[1,80,640]{2,1,0:T(8,128)(2,1)S(1)}, bf16[1,80,640]{2,1,0:T(8,128)(2,1)S(1)}, u32[]{:S(2)}, u32[]{:S(2)}) %collective-permute-start.8) | collective-permute-done | bytes 102432 | tf_op jit(solution)/shard_map/ppermute | solution.py:38
  50.6 4.9 %collective-permute-done.9 = bf16[640,320]{1,0:T(8,128)(2,1)S(1)} collective-permute-done((bf16[640,320]{1,0:T(8,128)(2,1)S(1)}, bf16[640,320]{1,0:T(8,128)(2,1)S(1)}, u32[]{:S(2)}, u32[]{:S(2)}) %collective-permute-start.9) | collective-permute-done | bytes 409632 | tf_op jit(solution)/shard_map/ppermute | solution.py:46
  55.7 1.3 copy.43
  57.0 1.7 collective-permute-start.12
  59.1 3.2 %project.3 = bf16[8,80,256]{2,1,0:T(8,128)(2,1)} custom-call(s32[4]{0:T(128)} %pad_add_fusion.1.place_ref, bf16[256,1280]{1,0:T(8,128)(2,1)} %fusion.2.normed_ref, bf16[1,320,640]{2,1,0:T(8,128)(2,1)} %copy-done.6, bf16[3,1,160,640]{3,2,1,0:T(8,128)(2,1)} %copy-done.7, bf16[3,1,160,640]{3,2,1,0:T(8,128)(2,1)} %collective-permute-done.10.other_ref), custom_call_target="tpu_custom_call" | custom-call | flops 419430400 | bytes 1638400 | tf_op jit(solution)/shard_map/project/pallas_call | solution.py:90
  62.3 1.7 collective-permute-start.11
  63.9 7.2 %all-to-all-start.1 = ((bf16[8,80,256]{2,1,0:T(8,128)(2,1)}), bf16[8,80,256]{2,1,0:T(8,128)(2,1)S(1)}, u32[]{:S(2)}, u32[]{:S(2)}) async-start(bf16[8,80,256]{2,1,0:T(8,128)(2,1)} %project.3), calls=%async_computation.1 | async-start | bytes 655360 | tf_op jit(solution)/shard_map/all_to_all | solution.py:50
  72.8 5.1 %collective-permute-done.12 = bf16[2,640,320]{1,2,0:T(8,128)(2,1)S(1)} collective-permute-done((bf16[2,640,320]{1,2,0:T(8,128)(2,1)}, bf16[2,640,320]{1,2,0:T(8,128)(2,1)S(1)}, u32[]{:S(2)}, u32[]{:S(2)}) %collective-permute-start.12) | collective-permute-done | bytes 819232 | tf_op jit(solution)/shard_map/ppermute | solution.py:38
  77.9 2.7 %collective-permute-done.13 = bf16[2,640,320]{1,2,0:T(8,128)(2,1)} collective-permute-done((bf16[2,640,320]{1,2,0:T(8,128)(2,1)}, bf16[2,640,320]{1,2,0:T(8,128)(2,1)}, u32[]{:S(2)}, u32[]{:S(2)}) %collective-permute-start.13) | collective-permute-done | bytes 819232 | tf_op jit(solution)/shard_map/ppermute | solution.py:38
  80.6 2.2 %all-to-all-done.1.q_ref = bf16[8,80,256]{2,1,0:T(8,128)(2,1)S(1)} async-done(((bf16[8,80,256]{2,1,0:T(8,128)(2,1)}), bf16[8,80,256]{2,1,0:T(8,128)(2,1)S(1)}, u32[]{:S(2)}, u32[]{:S(2)}) %all-to-all-start.1) | async-done | bytes 327712 | tf_op jit(solution)/shard_map/all_to_all | solution.py:50
  85.9 13.6 %attention.1 = bf16[8,80,256]{2,1,0:T(8,128)(2,1)} custom-call(s32[2,8]{1,0:T(2,128)} %pad_add_fusion.bounds_ref, s32[4]{0:T(128)} %pad_add_fusion.1.place_ref, s32[8,256]{1,0:T(8,128)} %bitcast.53, s32[1,8192]{1,0:T(1,128)} %kframe_ref.1, bf16[8,80,256]{2,1,0:T(8,128)(2,1)} %copy-done.17, bf16[8,160,256]{2,1,0:T(8,128)(2,1)} %all-to-all-done.own, ...), custom_call_target="tpu_custom_call" | custom-call | flops 8589934592 | bytes 2621440 | tf_op jit(solution)/shard_map/attention/pallas_call | solution.py:170
  99.6 5.0 %all-to-all-start.2 = ((bf16[8,80,256]{2,1,0:T(8,128)(2,1)}), bf16[8,80,256]{2,1,0:T(8,128)(2,1)S(1)}, u32[]{:S(2)}, u32[]{:S(2)}) async-start(bf16[8,80,256]{2,1,0:T(8,128)(2,1)} %attention.1), calls=%async_computation.2 | async-start | bytes 655360 | tf_op jit(solution)/shard_map/all_to_all | solution.py:50
  105.2 1.9 copy.49.left
  107.2 8.1 %collective-permute-start.17 = (bf16[2,320,320]{2,1,0:T(8,128)(2,1)S(1)}, bf16[2,320,320]{2,1,0:T(8,128)(2,1)S(1)}, u32[]{:S(2)}, u32[]{:S(2)}) collective-permute-start(bf16[2,320,320]{2,1,0:T(8,128)(2,1)S(1)} %slice.58), channel_id=1, source_target_pairs={{0,192},{64,0},{128,64},{192,128},{1,193},{65,1},{129,65},{193,129... | collective-permute-start | bytes 1228808 | tf_op jit(solution)/shard_map/ppermute | solution.py:38
  115.5 2.1 %all-to-all-done.2.attn_ref = bf16[8,80,256]{2,1,0:T(8,128)(2,1)S(1)} async-done(((bf16[8,80,256]{2,1,0:T(8,128)(2,1)}), bf16[8,80,256]{2,1,0:T(8,128)(2,1)S(1)}, u32[]{:S(2)}, u32[]{:S(2)}) %all-to-all-start.2) | async-done | bytes 327712 | tf_op jit(solution)/shard_map/all_to_all | solution.py:50
  117.5 3.3 %collective-permute-start.16 = (bf16[8,80,256]{2,1,0:T(8,128)(2,1)S(1)}, bf16[8,80,256]{2,1,0:T(8,128)(2,1)}, u32[]{:S(2)}, u32[]{:S(2)}) collective-permute-start(bf16[8,80,256]{2,1,0:T(8,128)(2,1)S(1)} %all-to-all-done.2.attn_ref), channel_id=1, source_target_pairs={{0,1},{1,0},{2,3},{3,2},{4,5},{5,4},{6,7},{7,6},{8,9},{9,8},{10,11... | collective-permute-start | bytes 983048 | tf_op jit(solution)/shard_map/ppermute | solution.py:46
  122.3 3.9 %collective-permute-done.17.opp_a = bf16[2,320,320]{2,1,0:T(8,128)(2,1)S(1)} collective-permute-done((bf16[2,320,320]{2,1,0:T(8,128)(2,1)S(1)}, bf16[2,320,320]{2,1,0:T(8,128)(2,1)S(1)}, u32[]{:S(2)}, u32[]{:S(2)}) %collective-permute-start.17) | collective-permute-done | bytes 409632 | tf_op jit(solution)/shard_map/ppermute | solution.py:38
  126.2 4.1 %collective-permute-done.18.opp_b = bf16[2,320,320]{2,1,0:T(8,128)(2,1)S(1)} collective-permute-done((bf16[2,320,320]{2,1,0:T(8,128)(2,1)S(1)}, bf16[2,320,320]{2,1,0:T(8,128)(2,1)S(1)}, u32[]{:S(2)}, u32[]{:S(2)}) %collective-permute-start.18) | collective-permute-done | bytes 409632 | tf_op jit(solution)/shard_map/ppermute | solution.py:38
  131.2 5.9 %output.1.refs_0_ = bf16[256,1280]{1,0:T(8,128)(2,1)} custom-call(s32[4]{0:T(128)} %pad_add_fusion.1.place_ref, s32[256,1]{1,0:T(8,128)} %reshape.138.order_ref, f32[1,1280]{1,0:T(1,128)} %broadcast_in_dim.4.gain_ref, bf16[256,1280]{1,0:T(8,128)(2,1)} %bitcast.44, bf16[8,80,256]{2,1,0:T(8,128)(2,1)} %copy-done.10, ...), custom_call_target="tpu_custom_call" | custom-call | flops 1179648000 | bytes 5000000 | tf_op jit(solution)/shard_map/output/pallas_call | solution.py:272
  137.1 3.2 %collective-permute-start.19 = (bf16[256,1280]{1,0:T(8,128)(2,1)}, bf16[256,1280]{1,0:T(8,128)(2,1)S(1)}, u32[]{:S(2)}, u32[]{:S(2)}) collective-permute-start(bf16[256,1280]{1,0:T(8,128)(2,1)} %output.1.refs_0_), channel_id=1, source_target_pairs={{0,192},{64,0},{128,64},{192,128},{1,193},{65,1},{129,65},{193,129... | collective-permute-start | bytes 1966088 | tf_op jit(solution)/shard_map/ppermute | solution.py:38
  140.3 5.8 %copy.50.refs_1_.refs_2_ = bf16[5120,320]{1,0:T(8,128)(2,1)} copy(bf16[5120,320]{0,1:T(8,128)(2,1)} %param.16) | data formatting | bytes 6553600 | tf_op args[7]
  146.2 5.4 %merge_own.1 = (bf16[32,3584]{1,0:T(8,128)(2,1)}, bf16[32,3584]{1,0:T(8,128)(2,1)}) custom-call(s32[4]{0:T(128)} %pad_add_fusion.1.place_ref, bf16[256,1280]{1,0:T(8,128)(2,1)} %output.1.refs_0_, bf16[5120,320]{1,0:T(8,128)(2,1)} %copy.50.refs_1_.refs_2_, bf16[320,3584]{1,0:T(8,128)(2,1)} %refs_3_.3), custom_call_target="tpu_custom_call" | custom-call | flops 1426063360 | bytes 6000000 | tf_op jit(solution)/shard_map/merge_own/pallas_call | solution.py:231
  151.6 4.1 %collective-permute-done.19.refs_0_ = bf16[256,1280]{1,0:T(8,128)(2,1)S(1)} collective-permute-done((bf16[256,1280]{1,0:T(8,128)(2,1)}, bf16[256,1280]{1,0:T(8,128)(2,1)S(1)}, u32[]{:S(2)}, u32[]{:S(2)}) %collective-permute-start.19) | collective-permute-done | bytes 655392 | tf_op jit(solution)/shard_map/ppermute | solution.py:38
  155.6 3.6 %collective-permute-done.20.refs_1_ = bf16[256,1280]{1,0:T(8,128)(2,1)S(1)} collective-permute-done((bf16[256,1280]{1,0:T(8,128)(2,1)}, bf16[256,1280]{1,0:T(8,128)(2,1)S(1)}, u32[]{:S(2)}, u32[]{:S(2)}) %collective-permute-start.20) | collective-permute-done | bytes 655392 | tf_op jit(solution)/shard_map/ppermute | solution.py:38
  159.4 2.1 %collective-permute-start.27 = (bf16[128,1280]{1,0:T(8,128)(2,1)S(1)}, bf16[128,1280]{1,0:T(8,128)(2,1)S(1)}, u32[]{:S(2)}, u32[]{:S(2)}) collective-permute-start(bf16[128,1280]{1,0:T(8,128)(2,1)S(1)} %slice.47), channel_id=1, source_target_pairs={{0,64},{64,128},{128,192},{192,0},{1,65},{65,129},{129,193},{193,1... | collective-permute-start | bytes 983048 | tf_op jit(solution)/shard_map/ppermute | solution.py:38
  161.5 5.7 %merge_next.1 = (bf16[32,3584]{1,0:T(8,128)(2,1)}, bf16[32,3584]{1,0:T(8,128)(2,1)}, bf16[32,3584]{1,0:T(8,128)(2,1)}, bf16[32,3584]{1,0:T(8,128)(2,1)}) custom-call(s32[4]{0:T(128)} %pad_add_fusion.1.place_ref, bf16[256,1280]{1,0:T(8,128)(2,1)} %copy-done.8, bf16[256,1280]{1,0:T(8,128)(2,1)} %copy-done.9, bf16[5120,320]{1,0:T(8,128)(2,1)} %copy.50.refs_1_.refs_2_, ...), custom_call_target="tpu_custom_call" | custom-call | flops 1426063360 | bytes 6000000 | tf_op jit(solution)/shard_map/merge_next/pallas_call | solution.py:231
  167.2 2.8 %collective-permute-start.25 = (bf16[32,3584]{1,0:T(8,128)(2,1)}, bf16[32,3584]{1,0:T(8,128)(2,1)S(1)}, u32[]{:S(2)}, u32[]{:S(2)}) collective-permute-start(bf16[32,3584]{1,0:T(8,128)(2,1)} %get-tuple-element.46), channel_id=1, source_target_pairs={{0,1},{1,0},{64,65},{65,64},{128,129},{129,128},{192,193},{193,192... | collective-permute-start | bytes 688136 | tf_op jit(solution)/shard_map/ppermute | solution.py:244
  170.1 3.7 %collective-permute-start.23 = (bf16[32,3584]{1,0:T(8,128)(2,1)}, bf16[32,3584]{1,0:T(8,128)(2,1)S(1)}, u32[]{:S(2)}, u32[]{:S(2)}) collective-permute-start(bf16[32,3584]{1,0:T(8,128)(2,1)} %get-tuple-element.43), channel_id=1, source_target_pairs={{0,128},{1,129},{64,192},{65,193},{128,0},{129,1},{192,64},{193,65... | collective-permute-start | bytes 688136 | tf_op jit(solution)/shard_map/ppermute | solution.py:244
  173.7 2.4 %collective-permute-start.22 = (bf16[32,3584]{1,0:T(8,128)(2,1)S(1)}, bf16[32,3584]{1,0:T(8,128)(2,1)S(1)}, u32[]{:S(2)}, u32[]{:S(2)}) collective-permute-start(bf16[32,3584]{1,0:T(8,128)(2,1)S(1)} %copy-done.27), channel_id=1, source_target_pairs={{0,65},{1,64},{64,129},{65,128},{128,193},{129,192},{192,1},{193,0... | collective-permute-start | bytes 688136 | tf_op jit(solution)/shard_map/ppermute | solution.py:244
  176.9 5.4 %merge_opposite.1 = (bf16[32,3584]{1,0:T(8,128)(2,1)}, bf16[32,3584]{1,0:T(8,128)(2,1)}) custom-call(s32[4]{0:T(128)} %pad_add_fusion.1.place_ref, bf16[128,1280]{1,0:T(8,128)(2,1)} %copy-done.15, bf16[128,1280]{1,0:T(8,128)(2,1)} %copy-done.16, bf16[5120,320]{1,0:T(8,128)(2,1)} %copy.50.refs_1_.refs_2_, bf16[320,3584]{1,0:T(8,128)(2,1)} %refs_3_.3), custom_call_target="tpu_custom_call" | custom-call | flops 1426063360 | bytes 6000000 | tf_op jit(solution)/shard_map/merge_opposite/pallas_call | solution.py:231
  182.4 3.3 %collective-permute-start.29 = (bf16[32,3584]{1,0:T(8,128)(2,1)}, bf16[32,3584]{1,0:T(8,128)(2,1)S(1)}, u32[]{:S(2)}, u32[]{:S(2)}) collective-permute-start(bf16[32,3584]{1,0:T(8,128)(2,1)} %get-tuple-element.48), channel_id=1, source_target_pairs={{0,193},{1,192},{64,1},{65,0},{128,65},{129,64},{192,129},{193,128... | collective-permute-start | bytes 688136 | tf_op jit(solution)/shard_map/ppermute | solution.py:244
  185.6 1.4 collective-permute-start.28
  187.0 6.2 %collective-permute-done.22 = bf16[32,3584]{1,0:T(8,128)(2,1)S(1)} collective-permute-done((bf16[32,3584]{1,0:T(8,128)(2,1)S(1)}, bf16[32,3584]{1,0:T(8,128)(2,1)S(1)}, u32[]{:S(2)}, u32[]{:S(2)}) %collective-permute-start.22) | collective-permute-done | bytes 229408 | tf_op jit(solution)/shard_map/ppermute | solution.py:244
  193.2 1.2 collective-permute-done.21
  (126 shorter events, 14.2 us)
Async XLA Ops:
  1.2 19.9 %copy-start.4 = (bf16[2,320,640]{2,1,0:T(8,128)(2,1)}, bf16[2,320,640]{2,1,0:T(8,128)(2,1)S(1)}, u32[]{:S(2)}) copy-start(bf16[2,320,640]{2,1,0:T(8,128)(2,1)S(1)} %slice.38.own_ref) | copy-start | bytes 2457604
  1.3 12.5 %collective-permute-start.2 = (bf16[2,160,640]{2,1,0:T(8,128)(2,1)S(1)}, bf16[2,160,640]{2,1,0:T(8,128)(2,1)S(1)}, u32[]{:S(2)}, u32[]{:S(2)}) collective-permute-start(bf16[2,160,640]{2,1,0:T(8,128)(2,1)S(1)} %constant_dynamic-slice_fusion.1), channel_id=1, source_target_pairs={{0,64},{64,128},{128,192},{192,0},{1,65},{65,129},{129,193},{193,1... | collective-permute-start | bytes 1228808 | tf_op jit(solution)/shard_map/ppermute | solution.py:38
  2.9 11.3 %collective-permute-start = (bf16[2,160,640]{2,1,0:T(8,128)(2,1)S(1)}, bf16[2,160,640]{2,1,0:T(8,128)(2,1)S(1)}, u32[]{:S(2)}, u32[]{:S(2)}) collective-permute-start(bf16[2,160,640]{2,1,0:T(8,128)(2,1)S(1)} %constant_dynamic-slice_fusion.1), channel_id=1, source_target_pairs={{0,192},{64,0},{128,64},{192,128},{1,193},{65,1},{129,65},{193,129... | collective-permute-start | bytes 1228808 | tf_op jit(solution)/shard_map/ppermute | solution.py:38
  13.8 7.2 %collective-permute-start.3 = (bf16[2,80,640]{2,1,0:T(8,128)(2,1)S(1)}, bf16[2,80,640]{2,1,0:T(8,128)(2,1)S(1)}, u32[]{:S(2)}, u32[]{:S(2)}) collective-permute-start(bf16[2,80,640]{2,1,0:T(8,128)(2,1)S(1)} %slice.55), channel_id=1, source_target_pairs={{0,64},{64,128},{128,192},{192,0},{1,65},{65,129},{129,193},{193,1... | collective-permute-start | bytes 614408 | tf_op jit(solution)/shard_map/ppermute | solution.py:38
  14.2 6.9 %collective-permute-start.1 = (bf16[2,80,640]{2,1,0:T(8,128)(2,1)S(1)}, bf16[2,80,640]{2,1,0:T(8,128)(2,1)S(1)}, u32[]{:S(2)}, u32[]{:S(2)}) collective-permute-start(bf16[2,80,640]{2,1,0:T(8,128)(2,1)S(1)} %slice.54), channel_id=1, source_target_pairs={{0,192},{64,0},{128,64},{192,128},{1,193},{65,1},{129,65},{193,129... | collective-permute-start | bytes 614408 | tf_op jit(solution)/shard_map/ppermute | solution.py:38
  21.3 5.5 %copy-start.5 = (bf16[3,2,160,640]{3,2,1,0:T(8,128)(2,1)}, bf16[3,2,160,640]{3,2,1,0:T(8,128)(2,1)S(1)}, u32[]{:S(2)}) copy-start(bf16[3,2,160,640]{3,2,1,0:T(8,128)(2,1)S(1)} %pad_maximum_fusion.mine_ref) | copy-start | bytes 3686404
  21.3 5.5 %collective-permute-start.4 = (bf16[3,2,160,640]{3,2,1,0:T(8,128)(2,1)S(1)}, bf16[3,2,160,640]{3,2,1,0:T(8,128)(2,1)S(1)}, u32[]{:S(2)}, u32[]{:S(2)}) collective-permute-start(bf16[3,2,160,640]{3,2,1,0:T(8,128)(2,1)S(1)} %pad_maximum_fusion.mine_ref), channel_id=1, source_target_pairs={{0,2},{2,0},{4,6},{6,4},{8,10},{10,8},{12,14},{14,12},{16,18},{18,... | collective-permute-start | bytes 3686408 | tf_op jit(solution)/shard_map/ppermute | solution.py:42
  23.5 21.0 %collective-permute-start.7 = (bf16[1,160,640]{2,1,0:T(8,128)(2,1)S(1)}, bf16[1,160,640]{2,1,0:T(8,128)(2,1)S(1)}, u32[]{:S(2)}, u32[]{:S(2)}) collective-permute-start(bf16[1,160,640]{2,1,0:T(8,128)(2,1)S(1)} %constant_dynamic-slice_fusion), channel_id=1, source_target_pairs={{0,64},{64,128},{128,192},{192,0},{1,65},{65,129},{129,193},{193,1... | collective-permute-start | bytes 614408 | tf_op jit(solution)/shard_map/ppermute | solution.py:38
  24.1 20.6 %collective-permute-start.5 = (bf16[1,160,640]{2,1,0:T(8,128)(2,1)S(1)}, bf16[1,160,640]{2,1,0:T(8,128)(2,1)S(1)}, u32[]{:S(2)}, u32[]{:S(2)}) collective-permute-start(bf16[1,160,640]{2,1,0:T(8,128)(2,1)S(1)} %constant_dynamic-slice_fusion), channel_id=1, source_target_pairs={{0,192},{64,0},{128,64},{192,128},{1,193},{65,1},{129,65},{193,129... | collective-permute-start | bytes 614408 | tf_op jit(solution)/shard_map/ppermute | solution.py:38
  32.3 8.7 %copy-start.14 = (bf16[640,320]{0,1:T(8,128)(2,1)S(1)}, bf16[640,320]{0,1:T(8,128)(2,1)}, u32[]{:S(2)}) copy-start(bf16[640,320]{0,1:T(8,128)(2,1)} %param.14) | copy-start | bytes 1228804
  32.3 30.0 %all-to-all-start = ((bf16[8,160,256]{2,1,0:T(8,128)(2,1)}), bf16[8,160,256]{2,1,0:T(8,128)(2,1)}, u32[]{:S(2)}, u32[]{:S(2)}) async-start(bf16[8,160,256]{2,1,0:T(8,128)(2,1)} %project.2), calls=%async_computation | async-start | bytes 1310720 | tf_op jit(solution)/shard_map/all_to_all | solution.py:50
  41.3 14.2 %collective-permute-start.9 = (bf16[640,320]{1,0:T(8,128)(2,1)S(1)}, bf16[640,320]{1,0:T(8,128)(2,1)S(1)}, u32[]{:S(2)}, u32[]{:S(2)}) collective-permute-start(bf16[640,320]{1,0:T(8,128)(2,1)S(1)} %copy.41), channel_id=1, source_target_pairs={{0,1},{1,0},{2,3},{3,2},{4,5},{5,4},{6,7},{7,6},{8,9},{9,8},{10,11... | collective-permute-start | bytes 1228808 | tf_op jit(solution)/shard_map/ppermute | solution.py:46
  44.6 5.9 %collective-permute-start.8 = (bf16[1,80,640]{2,1,0:T(8,128)(2,1)S(1)}, bf16[1,80,640]{2,1,0:T(8,128)(2,1)S(1)}, u32[]{:S(2)}, u32[]{:S(2)}) collective-permute-start(bf16[1,80,640]{2,1,0:T(8,128)(2,1)S(1)} %slice.57), channel_id=1, source_target_pairs={{0,64},{64,128},{128,192},{192,0},{1,65},{65,129},{129,193},{193,1... | collective-permute-start | bytes 307208 | tf_op jit(solution)/shard_map/ppermute | solution.py:38
  44.7 5.8 %collective-permute-start.6 = (bf16[1,80,640]{2,1,0:T(8,128)(2,1)S(1)}, bf16[1,80,640]{2,1,0:T(8,128)(2,1)S(1)}, u32[]{:S(2)}, u32[]{:S(2)}) collective-permute-start(bf16[1,80,640]{2,1,0:T(8,128)(2,1)S(1)} %slice.56), channel_id=1, source_target_pairs={{0,192},{64,0},{128,64},{192,128},{1,193},{65,1},{129,65},{193,129... | collective-permute-start | bytes 307208 | tf_op jit(solution)/shard_map/ppermute | solution.py:38
  50.6 6.4 %copy-start.7 = (bf16[3,1,160,640]{3,2,1,0:T(8,128)(2,1)}, bf16[3,1,160,640]{3,2,1,0:T(8,128)(2,1)S(1)}, u32[]{:S(2)}) copy-start(bf16[3,1,160,640]{3,2,1,0:T(8,128)(2,1)S(1)} %pad_maximum_fusion.2.mine_ref) | copy-start | bytes 1843204
  55.5 3.6 %collective-permute-start.10 = (bf16[3,1,160,640]{3,2,1,0:T(8,128)(2,1)S(1)}, bf16[3,1,160,640]{3,2,1,0:T(8,128)(2,1)}, u32[]{:S(2)}, u32[]{:S(2)}) collective-permute-start(bf16[3,1,160,640]{3,2,1,0:T(8,128)(2,1)S(1)} %pad_maximum_fusion.2.mine_ref), channel_id=1, source_target_pairs={{0,2},{2,0},{4,6},{6,4},{8,10},{10,8},{12,14},{14,12},{16,18},{18,... | collective-permute-start | bytes 1843208 | tf_op jit(solution)/shard_map/ppermute | solution.py:42
  55.7 6.6 %copy-start = (bf16[2,640,320]{2,1,0:T(8,128)(2,1)}, bf16[2,640,320]{2,1,0:T(8,128)(2,1)S(1)}, u32[]{:S(2)}) copy-start(bf16[2,640,320]{2,1,0:T(8,128)(2,1)S(1)} %pad_maximum_fusion.1.own) | copy-start | bytes 2457604
  57.0 14.6 %copy-start.19 = (s32[1,8192]{1,0:T(1,128)S(1)}, s32[1,8192]{1,0:T(1,128)}, u32[]{:S(2)}) copy-start(s32[1,8192]{1,0:T(1,128)} %kframe_ref.1) | copy-start | bytes 98308
  57.0 20.9 %collective-permute-start.12 = (bf16[2,640,320]{1,2,0:T(8,128)(2,1)}, bf16[2,640,320]{1,2,0:T(8,128)(2,1)S(1)}, u32[]{:S(2)}, u32[]{:S(2)}) collective-permute-start(bf16[2,640,320]{1,2,0:T(8,128)(2,1)} %copy.43), channel_id=1, source_target_pairs={{0,192},{64,0},{128,64},{192,128},{1,193},{65,1},{129,65},{193,129... | collective-permute-start | bytes 2457608 | tf_op jit(solution)/shard_map/ppermute | solution.py:38
  58.7 21.9 %collective-permute-start.13 = (bf16[2,640,320]{1,2,0:T(8,128)(2,1)}, bf16[2,640,320]{1,2,0:T(8,128)(2,1)}, u32[]{:S(2)}, u32[]{:S(2)}) collective-permute-start(bf16[2,640,320]{1,2,0:T(8,128)(2,1)} %copy.43), channel_id=1, source_target_pairs={{0,64},{64,128},{128,192},{192,0},{1,65},{65,129},{129,193},{193,1... | collective-permute-start | bytes 2457608 | tf_op jit(solution)/shard_map/ppermute | solution.py:38
  62.3 20.5 %collective-permute-start.11 = (bf16[8,160,256]{2,1,0:T(8,128)(2,1)}, bf16[8,160,256]{2,1,0:T(8,128)(2,1)S(1)}, u32[]{:S(2)}, u32[]{:S(2)}) collective-permute-start(bf16[8,160,256]{2,1,0:T(8,128)(2,1)} %all-to-all-done.own), channel_id=1, source_target_pairs={{0,32},{2,34},{4,36},{6,38},{8,40},{10,42},{12,44},{14,46},{16,48}... | collective-permute-start | bytes 1966088 | tf_op jit(solution)/shard_map/ppermute | solution.py:42
  63.9 18.9 %all-to-all-start.1 = ((bf16[8,80,256]{2,1,0:T(8,128)(2,1)}), bf16[8,80,256]{2,1,0:T(8,128)(2,1)S(1)}, u32[]{:S(2)}, u32[]{:S(2)}) async-start(bf16[8,80,256]{2,1,0:T(8,128)(2,1)} %project.3), calls=%async_computation.1 | async-start | bytes 655360 | tf_op jit(solution)/shard_map/all_to_all | solution.py:50
  72.5 12.7 %copy-start.20 = (s32[1,8,1,256]{3,1,2,0:T(8,128)}, s32[1,8,1,256]{3,1,2,0:T(8,128)S(1)}, u32[]{:S(2)}) copy-start(s32[1,8,1,256]{3,1,2,0:T(8,128)S(1)} %copy.56) | copy-start | bytes 24580
  72.7 12.4 %collective-permute-start.14 = (bf16[8,160,256]{2,1,0:T(8,128)(2,1)}, bf16[8,160,256]{2,1,0:T(8,128)(2,1)S(1)}, u32[]{:S(2)}, u32[]{:S(2)}) collective-permute-start(bf16[8,160,256]{2,1,0:T(8,128)(2,1)} %all-to-all-done.own), channel_id=1, source_target_pairs={{0,2},{2,0},{4,6},{6,4},{8,10},{10,8},{12,14},{14,12},{16,18},{18,... | collective-permute-start | bytes 1966088 | tf_op jit(solution)/shard_map/ppermute | solution.py:42
  82.8 2.3 %collective-permute-start.15 = (bf16[8,160,256]{2,1,0:T(8,128)(2,1)S(1)}, bf16[8,160,256]{2,1,0:T(8,128)(2,1)}, u32[]{:S(2)}, u32[]{:S(2)}) collective-permute-start(bf16[8,160,256]{2,1,0:T(8,128)(2,1)S(1)} %collective-permute-done.11.far), channel_id=1, source_target_pairs={{0,2},{2,0},{4,6},{6,4},{8,10},{10,8},{12,14},{14,12},{16,18},{18,... | collective-permute-start | bytes 1966088 | tf_op jit(solution)/shard_map/ppermute | solution.py:42
  99.6 18.0 %all-to-all-start.2 = ((bf16[8,80,256]{2,1,0:T(8,128)(2,1)}), bf16[8,80,256]{2,1,0:T(8,128)(2,1)S(1)}, u32[]{:S(2)}, u32[]{:S(2)}) async-start(bf16[8,80,256]{2,1,0:T(8,128)(2,1)} %attention.1), calls=%async_computation.2 | async-start | bytes 655360 | tf_op jit(solution)/shard_map/all_to_all | solution.py:50
  107.1 23.3 %copy-start.2 = (bf16[2,640,320]{2,1,0:T(8,128)(2,1)}, bf16[2,640,320]{2,1,0:T(8,128)(2,1)S(1)}, u32[]{:S(2)}) copy-start(bf16[2,640,320]{2,1,0:T(8,128)(2,1)S(1)} %copy.49.left) | copy-start | bytes 2457604
  107.1 13.7 %copy-start.23 = (s32[1,64,4]{1,2,0:T(4,128)S(1)}, s32[1,64,4]{1,2,0:T(4,128)}, u32[]{:S(2)}) copy-start(s32[1,64,4]{1,2,0:T(4,128)} %param.11) | copy-start | bytes 3076
  107.1 14.6 %copy-start.22 = (f32[1280]{0:T(1024)S(1)}, f32[1280]{0:T(1024)}, u32[]{:S(2)}) copy-start(f32[1280]{0:T(1024)} %param.15) | copy-start | bytes 15364
  107.2 19.0 %collective-permute-start.17 = (bf16[2,320,320]{2,1,0:T(8,128)(2,1)S(1)}, bf16[2,320,320]{2,1,0:T(8,128)(2,1)S(1)}, u32[]{:S(2)}, u32[]{:S(2)}) collective-permute-start(bf16[2,320,320]{2,1,0:T(8,128)(2,1)S(1)} %slice.58), channel_id=1, source_target_pairs={{0,192},{64,0},{128,64},{192,128},{1,193},{65,1},{129,65},{193,129... | collective-permute-start | bytes 1228808 | tf_op jit(solution)/shard_map/ppermute | solution.py:38
  115.4 15.0 %collective-permute-start.18 = (bf16[2,320,320]{2,1,0:T(8,128)(2,1)S(1)}, bf16[2,320,320]{2,1,0:T(8,128)(2,1)S(1)}, u32[]{:S(2)}, u32[]{:S(2)}) collective-permute-start(bf16[2,320,320]{2,1,0:T(8,128)(2,1)S(1)} %slice.59), channel_id=1, source_target_pairs={{0,64},{64,128},{128,192},{192,0},{1,65},{65,129},{129,193},{193,1... | collective-permute-start | bytes 1228808 | tf_op jit(solution)/shard_map/ppermute | solution.py:38
  117.5 12.8 %copy-start.10 = (bf16[8,80,256]{2,1,0:T(8,128)(2,1)}, bf16[8,80,256]{2,1,0:T(8,128)(2,1)S(1)}, u32[]{:S(2)}) copy-start(bf16[8,80,256]{2,1,0:T(8,128)(2,1)S(1)} %all-to-all-done.2.attn_ref) | copy-start | bytes 983044
  117.5 12.8 %collective-permute-start.16 = (bf16[8,80,256]{2,1,0:T(8,128)(2,1)S(1)}, bf16[8,80,256]{2,1,0:T(8,128)(2,1)}, u32[]{:S(2)}, u32[]{:S(2)}) collective-permute-start(bf16[8,80,256]{2,1,0:T(8,128)(2,1)S(1)} %all-to-all-done.2.attn_ref), channel_id=1, source_target_pairs={{0,1},{1,0},{2,3},{3,2},{4,5},{5,4},{6,7},{7,6},{8,9},{9,8},{10,11... | collective-permute-start | bytes 983048 | tf_op jit(solution)/shard_map/ppermute | solution.py:46
  137.1 18.5 %collective-permute-start.19 = (bf16[256,1280]{1,0:T(8,128)(2,1)}, bf16[256,1280]{1,0:T(8,128)(2,1)S(1)}, u32[]{:S(2)}, u32[]{:S(2)}) collective-permute-start(bf16[256,1280]{1,0:T(8,128)(2,1)} %output.1.refs_0_), channel_id=1, source_target_pairs={{0,192},{64,0},{128,64},{192,128},{1,193},{65,1},{129,65},{193,129... | collective-permute-start | bytes 1966088 | tf_op jit(solution)/shard_map/ppermute | solution.py:38
  140.3 18.9 %collective-permute-start.20 = (bf16[256,1280]{1,0:T(8,128)(2,1)}, bf16[256,1280]{1,0:T(8,128)(2,1)S(1)}, u32[]{:S(2)}, u32[]{:S(2)}) collective-permute-start(bf16[256,1280]{1,0:T(8,128)(2,1)} %output.1.refs_0_), channel_id=1, source_target_pairs={{0,64},{64,128},{128,192},{192,0},{1,65},{65,129},{129,193},{193,1... | collective-permute-start | bytes 1966088 | tf_op jit(solution)/shard_map/ppermute | solution.py:38
  155.6 5.9 %copy-start.8 = (bf16[256,1280]{1,0:T(8,128)(2,1)}, bf16[256,1280]{1,0:T(8,128)(2,1)S(1)}, u32[]{:S(2)}) copy-start(bf16[256,1280]{1,0:T(8,128)(2,1)S(1)} %collective-permute-done.19.refs_0_) | copy-start | bytes 1966084
  159.3 14.5 %collective-permute-start.26 = (bf16[128,1280]{1,0:T(8,128)(2,1)S(1)}, bf16[128,1280]{1,0:T(8,128)(2,1)S(1)}, u32[]{:S(2)}, u32[]{:S(2)}) collective-permute-start(bf16[128,1280]{1,0:T(8,128)(2,1)S(1)} %slice.46), channel_id=1, source_target_pairs={{0,192},{64,0},{128,64},{192,128},{1,193},{65,1},{129,65},{193,129... | collective-permute-start | bytes 983048 | tf_op jit(solution)/shard_map/ppermute | solution.py:38
  159.4 14.4 %copy-start.27 = (bf16[32,3584]{1,0:T(8,128)(2,1)S(1)}, bf16[32,3584]{1,0:T(8,128)(2,1)}, u32[]{:S(2)}) copy-start(bf16[32,3584]{1,0:T(8,128)(2,1)} %get-tuple-element.40) | copy-start | bytes 688132
  159.4 16.8 %copy-start.26 = (bf16[32,3584]{1,0:T(8,128)(2,1)S(1)}, bf16[32,3584]{1,0:T(8,128)(2,1)}, u32[]{:S(2)}) copy-start(bf16[32,3584]{1,0:T(8,128)(2,1)} %get-tuple-element.39) | copy-start | bytes 688132
  159.4 16.8 %collective-permute-start.27 = (bf16[128,1280]{1,0:T(8,128)(2,1)S(1)}, bf16[128,1280]{1,0:T(8,128)(2,1)S(1)}, u32[]{:S(2)}, u32[]{:S(2)}) collective-permute-start(bf16[128,1280]{1,0:T(8,128)(2,1)S(1)} %slice.47), channel_id=1, source_target_pairs={{0,64},{64,128},{128,192},{192,0},{1,65},{65,129},{129,193},{193,1... | collective-permute-start | bytes 983048 | tf_op jit(solution)/shard_map/ppermute | solution.py:38
  167.2 15.1 %collective-permute-start.25 = (bf16[32,3584]{1,0:T(8,128)(2,1)}, bf16[32,3584]{1,0:T(8,128)(2,1)S(1)}, u32[]{:S(2)}, u32[]{:S(2)}) collective-permute-start(bf16[32,3584]{1,0:T(8,128)(2,1)} %get-tuple-element.46), channel_id=1, source_target_pairs={{0,1},{1,0},{64,65},{65,64},{128,129},{129,128},{192,193},{193,192... | collective-permute-start | bytes 688136 | tf_op jit(solution)/shard_map/ppermute | solution.py:244
  170.1 15.6 %collective-permute-start.24 = (bf16[32,3584]{1,0:T(8,128)(2,1)}, bf16[32,3584]{1,0:T(8,128)(2,1)S(1)}, u32[]{:S(2)}, u32[]{:S(2)}) collective-permute-start(bf16[32,3584]{1,0:T(8,128)(2,1)} %get-tuple-element.44), channel_id=1, source_target_pairs={{0,129},{1,128},{64,193},{65,192},{128,1},{129,0},{192,65},{193,64... | collective-permute-start | bytes 688136 | tf_op jit(solution)/shard_map/ppermute | solution.py:244
  170.1 25.6 %copy-start.18 = (bf16[32,3584]{1,0:T(8,128)(2,1)S(1)}, bf16[32,3584]{1,0:T(8,128)(2,1)}, u32[]{:S(2)}) copy-start(bf16[32,3584]{1,0:T(8,128)(2,1)} %get-tuple-element.45) | copy-start | bytes 688132
  170.1 16.9 %collective-permute-start.23 = (bf16[32,3584]{1,0:T(8,128)(2,1)}, bf16[32,3584]{1,0:T(8,128)(2,1)S(1)}, u32[]{:S(2)}, u32[]{:S(2)}) collective-permute-start(bf16[32,3584]{1,0:T(8,128)(2,1)} %get-tuple-element.43), channel_id=1, source_target_pairs={{0,128},{1,129},{64,192},{65,193},{128,0},{129,1},{192,64},{193,65... | collective-permute-start | bytes 688136 | tf_op jit(solution)/shard_map/ppermute | solution.py:244
  173.7 19.5 %collective-permute-start.22 = (bf16[32,3584]{1,0:T(8,128)(2,1)S(1)}, bf16[32,3584]{1,0:T(8,128)(2,1)S(1)}, u32[]{:S(2)}, u32[]{:S(2)}) collective-permute-start(bf16[32,3584]{1,0:T(8,128)(2,1)S(1)} %copy-done.27), channel_id=1, source_target_pairs={{0,65},{1,64},{64,129},{65,128},{128,193},{129,192},{192,1},{193,0... | collective-permute-start | bytes 688136 | tf_op jit(solution)/shard_map/ppermute | solution.py:244
  176.2 18.2 %collective-permute-start.21 = (bf16[32,3584]{1,0:T(8,128)(2,1)S(1)}, bf16[32,3584]{1,0:T(8,128)(2,1)S(1)}, u32[]{:S(2)}, u32[]{:S(2)}) collective-permute-start(bf16[32,3584]{1,0:T(8,128)(2,1)S(1)} %copy-done.26), channel_id=1, source_target_pairs={{0,64},{1,65},{64,128},{65,129},{128,192},{129,193},{192,0},{193,1... | collective-permute-start | bytes 688136 | tf_op jit(solution)/shard_map/ppermute | solution.py:244
  182.4 13.0 %collective-permute-start.29 = (bf16[32,3584]{1,0:T(8,128)(2,1)}, bf16[32,3584]{1,0:T(8,128)(2,1)S(1)}, u32[]{:S(2)}, u32[]{:S(2)}) collective-permute-start(bf16[32,3584]{1,0:T(8,128)(2,1)} %get-tuple-element.48), channel_id=1, source_target_pairs={{0,193},{1,192},{64,1},{65,0},{128,65},{129,64},{192,129},{193,128... | collective-permute-start | bytes 688136 | tf_op jit(solution)/shard_map/ppermute | solution.py:244
  185.6 10.0 %collective-permute-start.28 = (bf16[32,3584]{1,0:T(8,128)(2,1)}, bf16[32,3584]{1,0:T(8,128)(2,1)S(1)}, u32[]{:S(2)}, u32[]{:S(2)}) collective-permute-start(bf16[32,3584]{1,0:T(8,128)(2,1)} %get-tuple-element.47), channel_id=1, source_target_pairs={{0,192},{1,193},{64,0},{65,1},{128,64},{129,65},{192,128},{193,129... | collective-permute-start | bytes 688136 | tf_op jit(solution)/shard_map/ppermute | solution.py:244
  (13 other events, 26.7 us)

commit v5 on v4

--- a/solution.py
+++ b/solution.py
@@ -14,20 +14,20 @@
 SECTIONS = 4
 VMEM = pl.BlockSpec(memory_space=pltpu.VMEM)
 SMEM = pl.BlockSpec(memory_space=pltpu.SMEM)
-LIMIT = 56 * 1024 * 1024
+MIB = 1024 * 1024
 bf16, f32 = jnp.bfloat16, jnp.float32
 
 Z_GROUPS = [[y * 16 + z * 2 + c for z in range(ZN)] for y in range(2) for c in range(2)]
 
 
-def call(kernel, out_shape, specs, scratch=(), flops=0, moved=0, name=None):
+def call(kernel, out_shape, specs, scratch=(), flops=0, moved=0, name=None, grant=14):
     return pl.pallas_call(
         kernel,
         out_shape=out_shape,
         in_specs=specs,
         out_specs=jax.tree.map(lambda _: VMEM, out_shape),
         scratch_shapes=list(scratch),
-        compiler_params=pltpu.CompilerParams(vmem_limit_bytes=LIMIT),
+        compiler_params=pltpu.CompilerParams(vmem_limit_bytes=grant * MIB),
         cost_estimate=pl.CostEstimate(flops=flops, bytes_accessed=moved, transcendentals=0),
         name=name,
     )
@@ -52,15 +52,6 @@
 
 def rms_norm(value, gain):
     return value * lax.rsqrt(jnp.mean(value * value, axis=-1, keepdims=True) + 1e-06) * gain
-
-
-def ring_halves(own):
-    half = own.shape[-2] // 2
-    right = section_shift(own, -1)
-    left = section_shift(own, 1)
-    opposite_a = section_shift(right[..., :half, :], -1)
-    opposite_b = section_shift(left[..., half:, :], 1)
-    return right, left, opposite_a, opposite_b
 
 
 def project_kernel(scale, count, place_ref, normed_ref, own_ref, mine_ref, other_ref, out_ref, weight):
@@ -78,10 +69,11 @@
             out_ref[h, t * HD : (t + 1) * HD, :] = turned[h * HD : (h + 1) * HD, :]
 
 
-def fetch(own, core):
+def fetch(own, core, *beside):
     half = lax.dynamic_slice_in_dim(own, core * 160, 160, axis=1)
-    right, left, opp_a, opp_b = ring_halves(half)
-    return jnp.stack([right, jnp.concatenate([opp_a, opp_b], axis=1), left])
+    right, left, *beside = lax.optimization_barrier((section_shift(half, -1), section_shift(half, 1), *beside))
+    opp_a, opp_b = section_shift(right[:, :80], -1), section_shift(left[:, 80:], 1)
+    return jnp.stack([right, jnp.concatenate([opp_a, opp_b], axis=1), left]), *beside
 
 
 def project(place, normed, own, mine, scale):
@@ -252,10 +244,15 @@
     normed = rms_norm(patch.astype(f32), norm_gain).astype(bf16)
 
     kv_own, q_own = qkv_weight[1:3], qkv_weight[0:1]
-    kv_mine, q_own = lax.optimization_barrier((fetch(kv_own, core), q_own))
+    out_half = tp_swap(lax.dynamic_slice_in_dim(out_weight, core * 160, 160, axis=1))
+    kv_mine, out_half = fetch(kv_own, core, out_half)
+    kv_mine, q_own = lax.optimization_barrier((kv_mine, q_own))
     kv = z_exchange(project(place, normed, kv_own, kv_mine, 1.0))
-    q_mine, out_weight_t = lax.optimization_barrier((fetch(q_own, core), tp_swap(out_weight)))
-    out_own = jnp.stack([out_weight, out_weight_t])
+    out_rest = blk_swap(out_half, 1)
+    out_weight_t = jnp.where(
+        core == 0, jnp.concatenate([out_half, out_rest], axis=1), jnp.concatenate([out_rest, out_half], axis=1)
+    )
+    q_mine, out_own = lax.optimization_barrier((fetch(q_own, core)[0], jnp.stack([out_weight, out_weight_t])))
     out_right, out_left = section_shift(out_own, -1), section_shift(out_own, 1)
     q = project(place, normed, q_own, q_mine, HD ** (-0.5) * math.log2(math.e))
     kv, q = lax.optimization_barrier((kv, q))

time: 198 us -> 191 us (0.965); the launches traced: 197 us -> 187 us
  Pallas kernels: 43.7 us -> 36.9 us
  starting transfers between devices: 72.1 us -> 66.2 us
  local copies, waits for them, and re-layouts: 19.2 us -> 22.9 us
    ppermute x16, waiting for transfers between devices: 38 us -> 26.2 us  [section_shift(): return lax.ppermute(value, 'section', route)]
    pallas_call x3, Pallas kernels: 16.6 us -> 7.62 us  [merge(): call(functools.partial(merger_kernel, sizes), tuple((jax.ShapeDtypeStruct...]
    ppermute x16, starting transfers between devices: 29.1 us -> 22.6 us  [section_shift(): return lax.ppermute(value, 'section', route)]
    all_to_all x3, waiting for transfers between devices: 4.3 us -> 9.13 us  [z_exchange(): lax.all_to_all(value, 'blk', 0, 0, axis_index_groups=Z_GROUPS, tiled=True)]
    ppermute x2, waiting for transfers between devices: 4.86 us -> 9.52 us  [tp_swap(): return lax.ppermute(value, 'tp', [(0, 1), (1, 0)])]
    pallas_call x1, Pallas kernels: 13.6 us -> 17.9 us  [attention(): call(attention_kernel, jax.ShapeDtypeStruct((ZN, HD, 256), bf16), [SMEM,...]
    another operation x5, other arithmetic: 0.49 us -> 2.58 us  [the longest x4 2.39 us: fetch(): jnp.stack([right, jnp.concatenate([opp_a, opp_b], axis=1), left])]
    unnamed x60 -> x30, local copies, waits for them, and re-layouts: 10.1 us -> 10 us
  transfers between devices with their start and end apart: 33 -> 34, of which waited for: 16 -> 19; matrix products, arithmetic and copies ran while one was open for 9% -> 12% of each run, Pallas kernels for 12% -> 8%
where the time goes in v5:
time: 191 us; the launch traced here: 187 us
  starting transfers between devices  66.2 us (35%)
  waiting for transfers between devices  54.3 us (28%)
  Pallas kernels  36.9 us (19%)
  local copies, waits for them, and re-layouts  22.9 us (12%)
  other arithmetic  6.83 us (4%)
    ppermute x16, waiting for transfers between devices, section_shift(): return lax.ppermute(value, 'section', route)  26.2 us
    ppermute x16, starting transfers between devices, section_shift(): return lax.ppermute(value, 'section', route)  22.6 us
    all_to_all x3, starting transfers between devices, z_exchange(): lax.all_to_all(value, 'blk', 0, 0, axis_index_groups=Z_GROUPS, tiled=True)  20 us
    pallas_call x1, Pallas kernels, attention(): call(attention_kernel, jax.ShapeDtypeStruct((ZN, HD, 256), bf16), [SMEM,...  17.9 us
    ppermute x7, starting transfers between devices, send(): return lax.ppermute(value, ('section', 'tp'), route)  14.7 us
    unnamed x30, local copies, waits for them, and re-layouts  10 us
    ppermute x2, waiting for transfers between devices, tp_swap(): return lax.ppermute(value, 'tp', [(0, 1), (1, 0)])  9.52 us
    all_to_all x3, waiting for transfers between devices, z_exchange(): lax.all_to_all(value, 'blk', 0, 0, axis_index_groups=Z_GROUPS, tiled=True)  9.13 us
  transfers between devices with their start and end apart: 34, of which 19 were waited for; matrix products, arithmetic and copies ran while one was open for 12% of the time, Pallas kernels for 8%

profile of v5, /device:TPU:32, one launch (start us, length us, event | category | flops | bytes accessed | tf_op | source)
XLA Modules:
  0.0 187.5 jit_solution(3063079329017850188)
XLA Ops:
  0.0 1.3 slice.38.own_ref
  1.3 2.8 %collective-permute-start = (bf16[2,160,640]{2,1,0:T(8,128)(2,1)S(1)}, bf16[2,160,640]{2,1,0:T(8,128)(2,1)S(1)}, u32[]{:S(2)}, u32[]{:S(2)}) collective-permute-start(bf16[2,160,640]{2,1,0:T(8,128)(2,1)S(1)} %constant_dynamic-slice_fusion.2), channel_id=1, source_target_pairs={{0,192},{64,0},{128,64},{192,128},{1,193},{65,1},{129,65},{193,129... | collective-permute-start | bytes 1228808 | tf_op jit(solution)/shard_map/ppermute | solution.py:38
  4.6 3.3 %collective-permute-start.2 = (bf16[640,160]{1,0:T(8,128)(2,1)S(1)}, bf16[640,160]{1,0:T(8,128)(2,1)}, u32[]{:S(2)}, u32[]{:S(2)}) collective-permute-start(bf16[640,160]{1,0:T(8,128)(2,1)S(1)} %constant_dynamic-slice_fusion.1), channel_id=1, source_target_pairs={{0,1},{1,0},{2,3},{3,2},{4,5},{5,4},{6,7},{7,6},{8,9},{9,8},{10,11... | collective-permute-start | bytes 614408 | tf_op jit(solution)/shard_map/ppermute | solution.py:46
  7.9 7.6 %collective-permute-done.2 = bf16[640,160]{1,0:T(8,128)(2,1)} collective-permute-done((bf16[640,160]{1,0:T(8,128)(2,1)S(1)}, bf16[640,160]{1,0:T(8,128)(2,1)}, u32[]{:S(2)}, u32[]{:S(2)}) %collective-permute-start.2) | collective-permute-done | bytes 204832 | tf_op jit(solution)/shard_map/ppermute | solution.py:46
  16.5 3.3 %collective-permute-start.3 = (bf16[2,80,640]{2,1,0:T(8,128)(2,1)S(1)}, bf16[2,80,640]{2,1,0:T(8,128)(2,1)S(1)}, u32[]{:S(2)}, u32[]{:S(2)}) collective-permute-start(bf16[2,80,640]{2,1,0:T(8,128)(2,1)S(1)} %slice.39), channel_id=1, source_target_pairs={{0,192},{64,0},{128,64},{192,128},{1,193},{65,1},{129,65},{193,129... | collective-permute-start | bytes 614408 | tf_op jit(solution)/shard_map/ppermute | solution.py:38
  20.8 2.6 %collective-permute-done.4 = bf16[2,80,640]{2,1,0:T(8,128)(2,1)S(1)} collective-permute-done((bf16[2,80,640]{2,1,0:T(8,128)(2,1)S(1)}, bf16[2,80,640]{2,1,0:T(8,128)(2,1)S(1)}, u32[]{:S(2)}, u32[]{:S(2)}) %collective-permute-start.4) | collective-permute-done | bytes 204832 | tf_op jit(solution)/shard_map/ppermute | solution.py:38
  23.5 1.2 pad_maximum_fusion.mine_ref
  26.4 3.3 %collective-permute-start.6 = (bf16[1,160,640]{2,1,0:T(8,128)(2,1)}, bf16[1,160,640]{2,1,0:T(8,128)(2,1)S(1)}, u32[]{:S(2)}, u32[]{:S(2)}) collective-permute-start(bf16[1,160,640]{2,1,0:T(8,128)(2,1)} %constant_dynamic-slice_fusion), channel_id=1, source_target_pairs={{0,192},{64,0},{128,64},{192,128},{1,193},{65,1},{129,65},{193,129... | collective-permute-start | bytes 614408 | tf_op jit(solution)/shard_map/ppermute | solution.py:38
  29.8 4.0 %project.2 = bf16[8,160,256]{2,1,0:T(8,128)(2,1)} custom-call(s32[4]{0:T(128)S(1)} %pad_add_fusion.1.place_ref, bf16[256,1280]{1,0:T(8,128)(2,1)S(1)} %fusion.2.normed_ref, bf16[2,320,640]{2,1,0:T(8,128)(2,1)S(1)} %slice.38.own_ref, bf16[3,2,160,640]{3,2,1,0:T(8,128)(2,1)} %pad_maximum_fusion.mine_ref, bf16[3,2,160,640]{3,2,1,0:T(8,128)(2,1)} %collective-permute-done.5.other_ref), custom_call_target="tpu_custom_call" | custom-call | flops 838860800 | bytes 3276800 | tf_op jit(solution)/shard_map/project/pallas_call | solution.py:82
  33.8 8.7 %all-to-all-start = ((bf16[8,160,256]{2,1,0:T(8,128)(2,1)}), bf16[8,160,256]{2,1,0:T(8,128)(2,1)S(1)}, u32[]{:S(2)}, u32[]{:S(2)}) async-start(bf16[8,160,256]{2,1,0:T(8,128)(2,1)} %project.2), calls=%async_computation | async-start | bytes 1310720 | tf_op jit(solution)/shard_map/all_to_all | solution.py:50
  42.5 1.6 maximum_select_fusion
  45.3 3.3 %collective-permute-start.8 = (bf16[1,80,640]{2,1,0:T(8,128)(2,1)S(1)}, bf16[1,80,640]{2,1,0:T(8,128)(2,1)S(1)}, u32[]{:S(2)}, u32[]{:S(2)}) collective-permute-start(bf16[1,80,640]{2,1,0:T(8,128)(2,1)S(1)} %slice.42), channel_id=1, source_target_pairs={{0,192},{64,0},{128,64},{192,128},{1,193},{65,1},{129,65},{193,129... | collective-permute-start | bytes 307208 | tf_op jit(solution)/shard_map/ppermute | solution.py:38
  48.8 2.3 %collective-permute-done.9 = bf16[1,80,640]{2,1,0:T(8,128)(2,1)S(1)} collective-permute-done((bf16[1,80,640]{2,1,0:T(8,128)(2,1)S(1)}, bf16[1,80,640]{2,1,0:T(8,128)(2,1)S(1)}, u32[]{:S(2)}, u32[]{:S(2)}) %collective-permute-start.9) | collective-permute-done | bytes 102432 | tf_op jit(solution)/shard_map/ppermute | solution.py:38
  52.4 1.3 copy.43
  53.7 3.3 %collective-permute-start.13 = (bf16[2,640,320]{1,2,0:T(8,128)(2,1)}, bf16[2,640,320]{1,2,0:T(8,128)(2,1)}, u32[]{:S(2)}, u32[]{:S(2)}) collective-permute-start(bf16[2,640,320]{1,2,0:T(8,128)(2,1)} %copy.43), channel_id=1, source_target_pairs={{0,192},{64,0},{128,64},{192,128},{1,193},{65,1},{129,65},{193,129... | collective-permute-start | bytes 2457608 | tf_op jit(solution)/shard_map/ppermute | solution.py:38
  57.0 2.7 %project.3 = bf16[8,80,256]{2,1,0:T(8,128)(2,1)} custom-call(s32[4]{0:T(128)S(1)} %pad_add_fusion.1.place_ref, bf16[256,1280]{1,0:T(8,128)(2,1)S(1)} %fusion.2.normed_ref, bf16[1,320,640]{2,1,0:T(8,128)(2,1)S(1)} %slice.41.own_ref, bf16[3,1,160,640]{3,2,1,0:T(8,128)(2,1)S(1)} %pad_maximum_fusion.2.mine_ref, ...), custom_call_target="tpu_custom_call" | custom-call | flops 419430400 | bytes 1638400 | tf_op jit(solution)/shard_map/project/pallas_call | solution.py:82
  59.7 1.6 all-to-all-done.own
  61.3 1.6 collective-permute-start.12
  62.9 5.7 %all-to-all-start.1 = ((bf16[8,80,256]{2,1,0:T(8,128)(2,1)}), bf16[8,80,256]{2,1,0:T(8,128)(2,1)S(1)}, u32[]{:S(2)}, u32[]{:S(2)}) async-start(bf16[8,80,256]{2,1,0:T(8,128)(2,1)} %project.3), calls=%async_computation.1 | async-start | bytes 655360 | tf_op jit(solution)/shard_map/all_to_all | solution.py:50
  70.1 5.4 %collective-permute-done.13 = bf16[2,640,320]{1,2,0:T(8,128)(2,1)} collective-permute-done((bf16[2,640,320]{1,2,0:T(8,128)(2,1)}, bf16[2,640,320]{1,2,0:T(8,128)(2,1)}, u32[]{:S(2)}, u32[]{:S(2)}) %collective-permute-start.13) | collective-permute-done | bytes 819232 | tf_op jit(solution)/shard_map/ppermute | solution.py:38
  75.5 3.4 %collective-permute-done.14 = bf16[2,640,320]{1,2,0:T(8,128)(2,1)} collective-permute-done((bf16[2,640,320]{1,2,0:T(8,128)(2,1)}, bf16[2,640,320]{1,2,0:T(8,128)(2,1)}, u32[]{:S(2)}, u32[]{:S(2)}) %collective-permute-start.14) | collective-permute-done | bytes 819232 | tf_op jit(solution)/shard_map/ppermute | solution.py:38
  78.9 1.5 all-to-all-done.1.q_ref
  82.7 17.9 %attention.1 = bf16[8,80,256]{2,1,0:T(8,128)(2,1)} custom-call(s32[2,8]{1,0:T(2,128)S(1)} %pad_add_fusion.bounds_ref, s32[4]{0:T(128)S(1)} %pad_add_fusion.1.place_ref, s32[8,256]{1,0:T(8,128)S(1)} %bitcast.48, s32[1,8192]{1,0:T(1,128)S(1)} %copy-done.5, bf16[8,80,256]{2,1,0:T(8,128)(2,1)S(1)} %all-to-all-done.1.q_ref, ...), custom_call_target="tpu_custom_call" | custom-call | flops 8589934592 | bytes 2621440 | tf_op jit(solution)/shard_map/attention/pallas_call | solution.py:162
  100.6 5.7 %all-to-all-start.2 = ((bf16[8,80,256]{2,1,0:T(8,128)(2,1)}), bf16[8,80,256]{2,1,0:T(8,128)(2,1)S(1)}, u32[]{:S(2)}, u32[]{:S(2)}) async-start(bf16[8,80,256]{2,1,0:T(8,128)(2,1)} %attention.1), calls=%async_computation.2 | async-start | bytes 655360 | tf_op jit(solution)/shard_map/all_to_all | solution.py:50
  106.3 1.5 copy.48.right
  107.8 1.6 copy.49.left
  110.2 2.1 %collective-permute-start.18 = (bf16[2,320,320]{2,1,0:T(8,128)(2,1)}, bf16[2,320,320]{2,1,0:T(8,128)(2,1)}, u32[]{:S(2)}, u32[]{:S(2)}) collective-permute-start(bf16[2,320,320]{2,1,0:T(8,128)(2,1)} %slice.54), channel_id=1, source_target_pairs={{0,192},{64,0},{128,64},{192,128},{1,193},{65,1},{129,65},{193,129... | collective-permute-start | bytes 1228808 | tf_op jit(solution)/shard_map/ppermute | solution.py:38
  113.1 6.0 %all-to-all-done.2.attn_ref = bf16[8,80,256]{2,1,0:T(8,128)(2,1)S(1)} async-done(((bf16[8,80,256]{2,1,0:T(8,128)(2,1)}), bf16[8,80,256]{2,1,0:T(8,128)(2,1)S(1)}, u32[]{:S(2)}, u32[]{:S(2)}) %all-to-all-start.2) | async-done | bytes 327712 | tf_op jit(solution)/shard_map/all_to_all | solution.py:50
  119.2 3.2 %collective-permute-start.17 = (bf16[8,80,256]{2,1,0:T(8,128)(2,1)S(1)}, bf16[8,80,256]{2,1,0:T(8,128)(2,1)}, u32[]{:S(2)}, u32[]{:S(2)}) collective-permute-start(bf16[8,80,256]{2,1,0:T(8,128)(2,1)S(1)} %all-to-all-done.2.attn_ref), channel_id=1, source_target_pairs={{0,1},{1,0},{2,3},{3,2},{4,5},{5,4},{6,7},{7,6},{8,9},{9,8},{10,11... | collective-permute-start | bytes 983048 | tf_op jit(solution)/shard_map/ppermute | solution.py:46
  122.6 1.9 %collective-permute-done.18.opp_a = bf16[2,320,320]{2,1,0:T(8,128)(2,1)} collective-permute-done((bf16[2,320,320]{2,1,0:T(8,128)(2,1)}, bf16[2,320,320]{2,1,0:T(8,128)(2,1)}, u32[]{:S(2)}, u32[]{:S(2)}) %collective-permute-start.18) | collective-permute-done | bytes 409632 | tf_op jit(solution)/shard_map/ppermute | solution.py:38
  124.5 4.1 %collective-permute-done.19.opp_b = bf16[2,320,320]{2,1,0:T(8,128)(2,1)} collective-permute-done((bf16[2,320,320]{2,1,0:T(8,128)(2,1)}, bf16[2,320,320]{2,1,0:T(8,128)(2,1)}, u32[]{:S(2)}, u32[]{:S(2)}) %collective-permute-start.19) | collective-permute-done | bytes 409632 | tf_op jit(solution)/shard_map/ppermute | solution.py:38
  128.6 1.9 %collective-permute-done.17.attn_t_ref = bf16[8,80,256]{2,1,0:T(8,128)(2,1)} collective-permute-done((bf16[8,80,256]{2,1,0:T(8,128)(2,1)S(1)}, bf16[8,80,256]{2,1,0:T(8,128)(2,1)}, u32[]{:S(2)}, u32[]{:S(2)}) %collective-permute-start.17) | collective-permute-done | bytes 327712 | tf_op jit(solution)/shard_map/ppermute | solution.py:46
  131.6 4.7 %output.1.refs_0_ = bf16[256,1280]{1,0:T(8,128)(2,1)} custom-call(s32[4]{0:T(128)S(1)} %pad_add_fusion.1.place_ref, s32[256,1]{1,0:T(8,128)S(1)} %reshape.193.order_ref, f32[1,1280]{1,0:T(1,128)S(1)} %broadcast_in_dim.4.gain_ref, bf16[256,1280]{1,0:T(8,128)(2,1)S(1)} %bitcast.45, bf16[8,80,256]{2,1,0:T(8,128)(2,1)S(1)} %all-to-all-done.2.attn_ref, ...), custom_call_target="tpu_custom_call" | custom-call | flops 1179648000 | bytes 5000000 | tf_op jit(solution)/shard_map/output/pallas_call | solution.py:269
  136.4 2.0 %collective-permute-start.21 = (bf16[256,1280]{1,0:T(8,128)(2,1)}, bf16[256,1280]{1,0:T(8,128)(2,1)}, u32[]{:S(2)}, u32[]{:S(2)}) collective-permute-start(bf16[256,1280]{1,0:T(8,128)(2,1)} %output.1.refs_0_), channel_id=1, source_target_pairs={{0,64},{64,128},{128,192},{192,0},{1,65},{65,129},{129,193},{193,1... | collective-permute-start | bytes 1966088 | tf_op jit(solution)/shard_map/ppermute | solution.py:38
  138.4 6.0 %copy.50.refs_1_.refs_2_ = bf16[5120,320]{1,0:T(8,128)(2,1)} copy(bf16[5120,320]{0,1:T(8,128)(2,1)} %param.16) | data formatting | bytes 6553600 | tf_op args[7]
  144.4 2.1 %copy-done = bf16[5120,320]{1,0:T(8,128)(2,1)S(1)} copy-done((bf16[5120,320]{1,0:T(8,128)(2,1)S(1)}, bf16[5120,320]{1,0:T(8,128)(2,1)}, u32[]{:S(2)}) %copy-start) | copy-done | bytes 3276824
  146.5 2.8 %merge_own.1 = (bf16[32,3584]{1,0:T(8,128)(2,1)S(1)}, bf16[32,3584]{1,0:T(8,128)(2,1)S(1)}) custom-call(s32[4]{0:T(128)S(1)} %pad_add_fusion.1.place_ref, bf16[256,1280]{1,0:T(8,128)(2,1)} %output.1.refs_0_, bf16[5120,320]{1,0:T(8,128)(2,1)S(1)} %copy-done, bf16[320,3584]{1,0:T(8,128)(2,1)S(1)} %copy-done.2), custom_call_target="tpu_custom_call" | custom-call | flops 1426063360 | bytes 6000000 | tf_op jit(solution)/shard_map/merge_own/pallas_call | solution.py:223
  149.3 3.2 %collective-permute-done.20.refs_0_ = bf16[256,1280]{1,0:T(8,128)(2,1)S(1)} collective-permute-done((bf16[256,1280]{1,0:T(8,128)(2,1)}, bf16[256,1280]{1,0:T(8,128)(2,1)S(1)}, u32[]{:S(2)}, u32[]{:S(2)}) %collective-permute-start.20) | collective-permute-done | bytes 655392 | tf_op jit(solution)/shard_map/ppermute | solution.py:38
  152.5 2.4 %collective-permute-done.21.refs_1_ = bf16[256,1280]{1,0:T(8,128)(2,1)} collective-permute-done((bf16[256,1280]{1,0:T(8,128)(2,1)}, bf16[256,1280]{1,0:T(8,128)(2,1)}, u32[]{:S(2)}, u32[]{:S(2)}) %collective-permute-start.21) | collective-permute-done | bytes 655392 | tf_op jit(solution)/shard_map/ppermute | solution.py:38
  156.3 1.9 %collective-permute-start.28 = (bf16[128,1280]{1,0:T(8,128)(2,1)S(1)}, bf16[128,1280]{1,0:T(8,128)(2,1)S(1)}, u32[]{:S(2)}, u32[]{:S(2)}) collective-permute-start(bf16[128,1280]{1,0:T(8,128)(2,1)S(1)} %slice.47), channel_id=1, source_target_pairs={{0,64},{64,128},{128,192},{192,0},{1,65},{65,129},{129,193},{193,1... | collective-permute-start | bytes 983048 | tf_op jit(solution)/shard_map/ppermute | solution.py:38
  158.2 2.7 %merge_next.1 = (bf16[32,3584]{1,0:T(8,128)(2,1)S(1)}, bf16[32,3584]{1,0:T(8,128)(2,1)S(1)}, bf16[32,3584]{1,0:T(8,128)(2,1)S(1)}, bf16[32,3584]{1,0:T(8,128)(2,1)S(1)}) custom-call(s32[4]{0:T(128)S(1)} %pad_add_fusion.1.place_ref, bf16[256,1280]{1,0:T(8,128)(2,1)S(1)} %collective-permute-done.20.refs_0_, bf16[256,1280]{1,0:T(8,128)(2,1)} %collective-permute-done.21.refs_1_, ...), custom_call_target="tpu_custom_call" | custom-call | flops 1426063360 | bytes 6000000 | tf_op jit(solution)/shard_map/merge_next/pallas_call | solution.py:223
  160.8 3.0 %collective-permute-start.26 = (bf16[32,3584]{1,0:T(8,128)(2,1)S(1)}, bf16[32,3584]{1,0:T(8,128)(2,1)S(1)}, u32[]{:S(2)}, u32[]{:S(2)}) collective-permute-start(bf16[32,3584]{1,0:T(8,128)(2,1)S(1)} %get-tuple-element.56), channel_id=1, source_target_pairs={{0,1},{1,0},{64,65},{65,64},{128,129},{129,128},{192,193},{193,192... | collective-permute-start | bytes 688136 | tf_op jit(solution)/shard_map/ppermute | solution.py:236
  163.8 3.6 %collective-permute-start.24 = (bf16[32,3584]{1,0:T(8,128)(2,1)S(1)}, bf16[32,3584]{1,0:T(8,128)(2,1)S(1)}, u32[]{:S(2)}, u32[]{:S(2)}) collective-permute-start(bf16[32,3584]{1,0:T(8,128)(2,1)S(1)} %get-tuple-element.53), channel_id=1, source_target_pairs={{0,128},{1,129},{64,192},{65,193},{128,0},{129,1},{192,64},{193,65... | collective-permute-start | bytes 688136 | tf_op jit(solution)/shard_map/ppermute | solution.py:236
  167.4 2.4 %collective-permute-start.23 = (bf16[32,3584]{1,0:T(8,128)(2,1)S(1)}, bf16[32,3584]{1,0:T(8,128)(2,1)S(1)}, u32[]{:S(2)}, u32[]{:S(2)}) collective-permute-start(bf16[32,3584]{1,0:T(8,128)(2,1)S(1)} %get-tuple-element.50), channel_id=1, source_target_pairs={{0,65},{1,64},{64,129},{65,128},{128,193},{129,192},{192,1},{193,0... | collective-permute-start | bytes 688136 | tf_op jit(solution)/shard_map/ppermute | solution.py:236
  169.8 2.1 %merge_opposite.1 = (bf16[32,3584]{1,0:T(8,128)(2,1)S(1)}, bf16[32,3584]{1,0:T(8,128)(2,1)S(1)}) custom-call(s32[4]{0:T(128)S(1)} %pad_add_fusion.1.place_ref, bf16[128,1280]{1,0:T(8,128)(2,1)S(1)} %collective-permute-done.27.refs_0_, bf16[128,1280]{1,0:T(8,128)(2,1)S(1)} %collective-permute-done.28.refs_1_, bf16[5120,320]{1,0:T(8,128)(2,1)S(1)} %copy-done.1, ...), custom_call_target="tpu_custom_call" | custom-call | flops 1426063360 | bytes 6000000 | tf_op jit(solution)/shard_map/merge_opposite/pallas_call | solution.py:223
  172.1 5.8 %collective-permute-start.30 = (bf16[32,3584]{1,0:T(8,128)(2,1)S(1)}, bf16[32,3584]{1,0:T(8,128)(2,1)S(1)}, u32[]{:S(2)}, u32[]{:S(2)}) collective-permute-start(bf16[32,3584]{1,0:T(8,128)(2,1)S(1)} %get-tuple-element.58), channel_id=1, source_target_pairs={{0,193},{1,192},{64,1},{65,0},{128,65},{129,64},{192,129},{193,128... | collective-permute-start | bytes 688136 | tf_op jit(solution)/shard_map/ppermute | solution.py:236
  178.9 6.3 %collective-permute-done.23 = bf16[32,3584]{1,0:T(8,128)(2,1)S(1)} collective-permute-done((bf16[32,3584]{1,0:T(8,128)(2,1)S(1)}, bf16[32,3584]{1,0:T(8,128)(2,1)S(1)}, u32[]{:S(2)}, u32[]{:S(2)}) %collective-permute-start.23) | collective-permute-done | bytes 229408 | tf_op jit(solution)/shard_map/ppermute | solution.py:236
  185.3 1.2 collective-permute-done.22
  (100 shorter events, 17.0 us)
Async XLA Ops:
  0.0 4.2 %copy-start.9 = (bf16[640,320]{0,1:T(8,128)(2,1)S(1)}, bf16[640,320]{0,1:T(8,128)(2,1)}, u32[]{:S(2)}) copy-start(bf16[640,320]{0,1:T(8,128)(2,1)} %param.14) | copy-start | bytes 1228804
  1.3 14.2 %collective-permute-start = (bf16[2,160,640]{2,1,0:T(8,128)(2,1)S(1)}, bf16[2,160,640]{2,1,0:T(8,128)(2,1)S(1)}, u32[]{:S(2)}, u32[]{:S(2)}) collective-permute-start(bf16[2,160,640]{2,1,0:T(8,128)(2,1)S(1)} %constant_dynamic-slice_fusion.2), channel_id=1, source_target_pairs={{0,192},{64,0},{128,64},{192,128},{1,193},{65,1},{129,65},{193,129... | collective-permute-start | bytes 1228808 | tf_op jit(solution)/shard_map/ppermute | solution.py:38
  4.2 12.1 %collective-permute-start.1 = (bf16[2,160,640]{2,1,0:T(8,128)(2,1)S(1)}, bf16[2,160,640]{2,1,0:T(8,128)(2,1)S(1)}, u32[]{:S(2)}, u32[]{:S(2)}) collective-permute-start(bf16[2,160,640]{2,1,0:T(8,128)(2,1)S(1)} %constant_dynamic-slice_fusion.2), channel_id=1, source_target_pairs={{0,64},{64,128},{128,192},{192,0},{1,65},{65,129},{129,193},{193,1... | collective-permute-start | bytes 1228808 | tf_op jit(solution)/shard_map/ppermute | solution.py:38
  4.5 18.9 %copy-start.6 = (bf16[640,320]{1,0:T(8,128)(2,1)}, bf16[640,320]{1,0:T(8,128)(2,1)S(1)}, u32[]{:S(2)}) copy-start(bf16[640,320]{1,0:T(8,128)(2,1)S(1)} %copy.41) | copy-start | bytes 1228804
  4.6 10.9 %collective-permute-start.2 = (bf16[640,160]{1,0:T(8,128)(2,1)S(1)}, bf16[640,160]{1,0:T(8,128)(2,1)}, u32[]{:S(2)}, u32[]{:S(2)}) collective-permute-start(bf16[640,160]{1,0:T(8,128)(2,1)S(1)} %constant_dynamic-slice_fusion.1), channel_id=1, source_target_pairs={{0,1},{1,0},{2,3},{3,2},{4,5},{5,4},{6,7},{7,6},{8,9},{9,8},{10,11... | collective-permute-start | bytes 614408 | tf_op jit(solution)/shard_map/ppermute | solution.py:46
  16.3 7.0 %collective-permute-start.4 = (bf16[2,80,640]{2,1,0:T(8,128)(2,1)S(1)}, bf16[2,80,640]{2,1,0:T(8,128)(2,1)S(1)}, u32[]{:S(2)}, u32[]{:S(2)}) collective-permute-start(bf16[2,80,640]{2,1,0:T(8,128)(2,1)S(1)} %slice.40), channel_id=1, source_target_pairs={{0,64},{64,128},{128,192},{192,0},{1,65},{65,129},{129,193},{193,1... | collective-permute-start | bytes 614408 | tf_op jit(solution)/shard_map/ppermute | solution.py:38
  16.5 6.9 %collective-permute-start.3 = (bf16[2,80,640]{2,1,0:T(8,128)(2,1)S(1)}, bf16[2,80,640]{2,1,0:T(8,128)(2,1)S(1)}, u32[]{:S(2)}, u32[]{:S(2)}) collective-permute-start(bf16[2,80,640]{2,1,0:T(8,128)(2,1)S(1)} %slice.39), channel_id=1, source_target_pairs={{0,192},{64,0},{128,64},{192,128},{1,193},{65,1},{129,65},{193,129... | collective-permute-start | bytes 614408 | tf_op jit(solution)/shard_map/ppermute | solution.py:38
  23.4 1.3 copy-start.3
  23.4 1.5 copy-start.10
  24.7 5.2 %collective-permute-start.5 = (bf16[3,2,160,640]{3,2,1,0:T(8,128)(2,1)}, bf16[3,2,160,640]{3,2,1,0:T(8,128)(2,1)}, u32[]{:S(2)}, u32[]{:S(2)}) collective-permute-start(bf16[3,2,160,640]{3,2,1,0:T(8,128)(2,1)} %pad_maximum_fusion.mine_ref), channel_id=1, source_target_pairs={{0,2},{2,0},{4,6},{6,4},{8,10},{10,8},{12,14},{14,12},{16,18},{18,... | collective-permute-start | bytes 3686408 | tf_op jit(solution)/shard_map/ppermute | solution.py:42
  25.1 17.4 %collective-permute-start.10 = (bf16[640,160]{1,0:T(8,128)(2,1)}, bf16[640,160]{1,0:T(8,128)(2,1)}, u32[]{:S(2)}, u32[]{:S(2)}) collective-permute-start(bf16[640,160]{1,0:T(8,128)(2,1)} %collective-permute-done.2), channel_id=1, source_target_pairs={{0,2},{2,0},{4,6},{6,4},{8,10},{10,8},{12,14},{14,12},{16,18},{18,... | collective-permute-start | bytes 614408 | tf_op jit(solution)/shard_map/ppermute | solution.py:42
  26.4 17.7 %collective-permute-start.6 = (bf16[1,160,640]{2,1,0:T(8,128)(2,1)}, bf16[1,160,640]{2,1,0:T(8,128)(2,1)S(1)}, u32[]{:S(2)}, u32[]{:S(2)}) collective-permute-start(bf16[1,160,640]{2,1,0:T(8,128)(2,1)} %constant_dynamic-slice_fusion), channel_id=1, source_target_pairs={{0,192},{64,0},{128,64},{192,128},{1,193},{65,1},{129,65},{193,129... | collective-permute-start | bytes 614408 | tf_op jit(solution)/shard_map/ppermute | solution.py:38
  29.8 14.4 %collective-permute-start.7 = (bf16[1,160,640]{2,1,0:T(8,128)(2,1)}, bf16[1,160,640]{2,1,0:T(8,128)(2,1)}, u32[]{:S(2)}, u32[]{:S(2)}) collective-permute-start(bf16[1,160,640]{2,1,0:T(8,128)(2,1)} %constant_dynamic-slice_fusion), channel_id=1, source_target_pairs={{0,64},{64,128},{128,192},{192,0},{1,65},{65,129},{129,193},{193,1... | collective-permute-start | bytes 614408 | tf_op jit(solution)/shard_map/ppermute | solution.py:38
  33.8 14.8 %copy-start.7 = (bf16[640,320]{1,0:T(8,128)(2,1)S(1)}, bf16[640,320]{1,0:T(8,128)(2,1)}, u32[]{:S(2)}) copy-start(bf16[640,320]{1,0:T(8,128)(2,1)} %copy-done.6) | copy-start | bytes 1228804
  33.8 27.5 %all-to-all-start = ((bf16[8,160,256]{2,1,0:T(8,128)(2,1)}), bf16[8,160,256]{2,1,0:T(8,128)(2,1)S(1)}, u32[]{:S(2)}, u32[]{:S(2)}) async-start(bf16[8,160,256]{2,1,0:T(8,128)(2,1)} %project.2), calls=%async_computation | async-start | bytes 1310720 | tf_op jit(solution)/shard_map/all_to_all | solution.py:50
  44.2 7.0 %copy-start.8 = (bf16[1,160,640]{2,1,0:T(8,128)(2,1)}, bf16[1,160,640]{2,1,0:T(8,128)(2,1)S(1)}, u32[]{:S(2)}) copy-start(bf16[1,160,640]{2,1,0:T(8,128)(2,1)S(1)} %collective-permute-done.6) | copy-start | bytes 614404
  45.2 6.0 %collective-permute-start.9 = (bf16[1,80,640]{2,1,0:T(8,128)(2,1)S(1)}, bf16[1,80,640]{2,1,0:T(8,128)(2,1)S(1)}, u32[]{:S(2)}, u32[]{:S(2)}) collective-permute-start(bf16[1,80,640]{2,1,0:T(8,128)(2,1)S(1)} %slice.43), channel_id=1, source_target_pairs={{0,64},{64,128},{128,192},{192,0},{1,65},{65,129},{129,193},{193,1... | collective-permute-start | bytes 307208 | tf_op jit(solution)/shard_map/ppermute | solution.py:38
  45.3 5.8 %collective-permute-start.8 = (bf16[1,80,640]{2,1,0:T(8,128)(2,1)S(1)}, bf16[1,80,640]{2,1,0:T(8,128)(2,1)S(1)}, u32[]{:S(2)}, u32[]{:S(2)}) collective-permute-start(bf16[1,80,640]{2,1,0:T(8,128)(2,1)S(1)} %slice.42), channel_id=1, source_target_pairs={{0,192},{64,0},{128,64},{192,128},{1,193},{65,1},{129,65},{193,129... | collective-permute-start | bytes 307208 | tf_op jit(solution)/shard_map/ppermute | solution.py:38
  52.3 4.7 %collective-permute-start.11 = (bf16[3,1,160,640]{3,2,1,0:T(8,128)(2,1)S(1)}, bf16[3,1,160,640]{3,2,1,0:T(8,128)(2,1)}, u32[]{:S(2)}, u32[]{:S(2)}) collective-permute-start(bf16[3,1,160,640]{3,2,1,0:T(8,128)(2,1)S(1)} %pad_maximum_fusion.2.mine_ref), channel_id=1, source_target_pairs={{0,2},{2,0},{4,6},{6,4},{8,10},{10,8},{12,14},{14,12},{16,18},{18,... | collective-permute-start | bytes 1843208 | tf_op jit(solution)/shard_map/ppermute | solution.py:42
  53.7 15.4 %copy-start.5 = (s32[1,8192]{1,0:T(1,128)S(1)}, s32[1,8192]{1,0:T(1,128)}, u32[]{:S(2)}) copy-start(s32[1,8192]{1,0:T(1,128)} %kframe_ref.1) | copy-start | bytes 98308
  53.7 21.8 %collective-permute-start.13 = (bf16[2,640,320]{1,2,0:T(8,128)(2,1)}, bf16[2,640,320]{1,2,0:T(8,128)(2,1)}, u32[]{:S(2)}, u32[]{:S(2)}) collective-permute-start(bf16[2,640,320]{1,2,0:T(8,128)(2,1)} %copy.43), channel_id=1, source_target_pairs={{0,192},{64,0},{128,64},{192,128},{1,193},{65,1},{129,65},{193,129... | collective-permute-start | bytes 2457608 | tf_op jit(solution)/shard_map/ppermute | solution.py:38
  57.0 21.9 %collective-permute-start.14 = (bf16[2,640,320]{1,2,0:T(8,128)(2,1)}, bf16[2,640,320]{1,2,0:T(8,128)(2,1)}, u32[]{:S(2)}, u32[]{:S(2)}) collective-permute-start(bf16[2,640,320]{1,2,0:T(8,128)(2,1)} %copy.43), channel_id=1, source_target_pairs={{0,64},{64,128},{128,192},{192,0},{1,65},{65,129},{129,193},{193,1... | collective-permute-start | bytes 2457608 | tf_op jit(solution)/shard_map/ppermute | solution.py:38
  61.3 19.1 %collective-permute-start.12 = (bf16[8,160,256]{2,1,0:T(8,128)(2,1)S(1)}, bf16[8,160,256]{2,1,0:T(8,128)(2,1)S(1)}, u32[]{:S(2)}, u32[]{:S(2)}) collective-permute-start(bf16[8,160,256]{2,1,0:T(8,128)(2,1)S(1)} %all-to-all-done.own), channel_id=1, source_target_pairs={{0,32},{2,34},{4,36},{6,38},{8,40},{10,42},{12,44},{14,46},{16,48}... | collective-permute-start | bytes 1966088 | tf_op jit(solution)/shard_map/ppermute | solution.py:42
  62.9 17.6 %all-to-all-start.1 = ((bf16[8,80,256]{2,1,0:T(8,128)(2,1)}), bf16[8,80,256]{2,1,0:T(8,128)(2,1)S(1)}, u32[]{:S(2)}, u32[]{:S(2)}) async-start(bf16[8,80,256]{2,1,0:T(8,128)(2,1)} %project.3), calls=%async_computation.1 | async-start | bytes 655360 | tf_op jit(solution)/shard_map/all_to_all | solution.py:50
  70.0 12.0 %collective-permute-start.15 = (bf16[8,160,256]{2,1,0:T(8,128)(2,1)S(1)}, bf16[8,160,256]{2,1,0:T(8,128)(2,1)}, u32[]{:S(2)}, u32[]{:S(2)}) collective-permute-start(bf16[8,160,256]{2,1,0:T(8,128)(2,1)S(1)} %all-to-all-done.own), channel_id=1, source_target_pairs={{0,2},{2,0},{4,6},{6,4},{8,10},{10,8},{12,14},{14,12},{16,18},{18,... | collective-permute-start | bytes 1966088 | tf_op jit(solution)/shard_map/ppermute | solution.py:42
  80.4 2.2 %collective-permute-start.16 = (bf16[8,160,256]{2,1,0:T(8,128)(2,1)S(1)}, bf16[8,160,256]{2,1,0:T(8,128)(2,1)}, u32[]{:S(2)}, u32[]{:S(2)}) collective-permute-start(bf16[8,160,256]{2,1,0:T(8,128)(2,1)S(1)} %collective-permute-done.12.far), channel_id=1, source_target_pairs={{0,2},{2,0},{4,6},{6,4},{8,10},{10,8},{12,14},{14,12},{16,18},{18,... | collective-permute-start | bytes 1966088 | tf_op jit(solution)/shard_map/ppermute | solution.py:42
  100.6 18.6 %all-to-all-start.2 = ((bf16[8,80,256]{2,1,0:T(8,128)(2,1)}), bf16[8,80,256]{2,1,0:T(8,128)(2,1)S(1)}, u32[]{:S(2)}, u32[]{:S(2)}) async-start(bf16[8,80,256]{2,1,0:T(8,128)(2,1)} %attention.1), calls=%async_computation.2 | async-start | bytes 655360 | tf_op jit(solution)/shard_map/all_to_all | solution.py:50
  109.4 13.0 %copy-start.12 = (s32[1,64,4]{1,2,0:T(4,128)S(1)}, s32[1,64,4]{1,2,0:T(4,128)}, u32[]{:S(2)}) copy-start(s32[1,64,4]{1,2,0:T(4,128)} %param.11) | copy-start | bytes 3076
  109.4 13.2 %copy-start.11 = (f32[1280]{0:T(1024)S(1)}, f32[1280]{0:T(1024)}, u32[]{:S(2)}) copy-start(f32[1280]{0:T(1024)} %param.15) | copy-start | bytes 15364
  110.2 14.3 %collective-permute-start.18 = (bf16[2,320,320]{2,1,0:T(8,128)(2,1)}, bf16[2,320,320]{2,1,0:T(8,128)(2,1)}, u32[]{:S(2)}, u32[]{:S(2)}) collective-permute-start(bf16[2,320,320]{2,1,0:T(8,128)(2,1)} %slice.54), channel_id=1, source_target_pairs={{0,192},{64,0},{128,64},{192,128},{1,193},{65,1},{129,65},{193,129... | collective-permute-start | bytes 1228808 | tf_op jit(solution)/shard_map/ppermute | solution.py:38
  113.1 15.5 %collective-permute-start.19 = (bf16[2,320,320]{2,1,0:T(8,128)(2,1)}, bf16[2,320,320]{2,1,0:T(8,128)(2,1)}, u32[]{:S(2)}, u32[]{:S(2)}) collective-permute-start(bf16[2,320,320]{2,1,0:T(8,128)(2,1)} %slice.55), channel_id=1, source_target_pairs={{0,64},{64,128},{128,192},{192,0},{1,65},{65,129},{129,193},{193,1... | collective-permute-start | bytes 1228808 | tf_op jit(solution)/shard_map/ppermute | solution.py:38
  119.2 11.4 %collective-permute-start.17 = (bf16[8,80,256]{2,1,0:T(8,128)(2,1)S(1)}, bf16[8,80,256]{2,1,0:T(8,128)(2,1)}, u32[]{:S(2)}, u32[]{:S(2)}) collective-permute-start(bf16[8,80,256]{2,1,0:T(8,128)(2,1)S(1)} %all-to-all-done.2.attn_ref), channel_id=1, source_target_pairs={{0,1},{1,0},{2,3},{3,2},{4,5},{5,4},{6,7},{7,6},{8,9},{9,8},{10,11... | collective-permute-start | bytes 983048 | tf_op jit(solution)/shard_map/ppermute | solution.py:46
  130.6 1.1 copy-start.4
  136.4 16.2 %collective-permute-start.20 = (bf16[256,1280]{1,0:T(8,128)(2,1)}, bf16[256,1280]{1,0:T(8,128)(2,1)S(1)}, u32[]{:S(2)}, u32[]{:S(2)}) collective-permute-start(bf16[256,1280]{1,0:T(8,128)(2,1)} %output.1.refs_0_), channel_id=1, source_target_pairs={{0,192},{64,0},{128,64},{192,128},{1,193},{65,1},{129,65},{193,129... | collective-permute-start | bytes 1966088 | tf_op jit(solution)/shard_map/ppermute | solution.py:38
  136.4 18.6 %collective-permute-start.21 = (bf16[256,1280]{1,0:T(8,128)(2,1)}, bf16[256,1280]{1,0:T(8,128)(2,1)}, u32[]{:S(2)}, u32[]{:S(2)}) collective-permute-start(bf16[256,1280]{1,0:T(8,128)(2,1)} %output.1.refs_0_), channel_id=1, source_target_pairs={{0,64},{64,128},{128,192},{192,0},{1,65},{65,129},{129,193},{193,1... | collective-permute-start | bytes 1966088 | tf_op jit(solution)/shard_map/ppermute | solution.py:38
  138.4 6.0 %copy-start.2 = (bf16[320,3584]{1,0:T(8,128)(2,1)S(1)}, bf16[320,3584]{1,0:T(8,128)(2,1)}, u32[]{:S(2)}) copy-start(bf16[320,3584]{1,0:T(8,128)(2,1)} %refs_3_.3) | copy-start | bytes 6881284
  144.4 2.1 %copy-start = (bf16[5120,320]{1,0:T(8,128)(2,1)S(1)}, bf16[5120,320]{1,0:T(8,128)(2,1)}, u32[]{:S(2)}) copy-start(bf16[5120,320]{1,0:T(8,128)(2,1)} %copy.50.refs_1_.refs_2_) | copy-start | bytes 9830404
  146.5 11.7 %copy-start.1 = (bf16[5120,320]{1,0:T(8,128)(2,1)S(1)}, bf16[5120,320]{1,0:T(8,128)(2,1)}, u32[]{:S(2)}) copy-start(bf16[5120,320]{1,0:T(8,128)(2,1)} %copy.50.refs_1_.refs_2_) | copy-start | bytes 9830404
  155.0 12.4 %collective-permute-start.27 = (bf16[128,1280]{1,0:T(8,128)(2,1)S(1)}, bf16[128,1280]{1,0:T(8,128)(2,1)S(1)}, u32[]{:S(2)}, u32[]{:S(2)}) collective-permute-start(bf16[128,1280]{1,0:T(8,128)(2,1)S(1)} %slice.46), channel_id=1, source_target_pairs={{0,192},{64,0},{128,64},{192,128},{1,193},{65,1},{129,65},{193,129... | collective-permute-start | bytes 983048 | tf_op jit(solution)/shard_map/ppermute | solution.py:38
  156.3 13.5 %collective-permute-start.28 = (bf16[128,1280]{1,0:T(8,128)(2,1)S(1)}, bf16[128,1280]{1,0:T(8,128)(2,1)S(1)}, u32[]{:S(2)}, u32[]{:S(2)}) collective-permute-start(bf16[128,1280]{1,0:T(8,128)(2,1)S(1)} %slice.47), channel_id=1, source_target_pairs={{0,64},{64,128},{128,192},{192,0},{1,65},{65,129},{129,193},{193,1... | collective-permute-start | bytes 983048 | tf_op jit(solution)/shard_map/ppermute | solution.py:38
  160.8 11.2 %collective-permute-start.26 = (bf16[32,3584]{1,0:T(8,128)(2,1)S(1)}, bf16[32,3584]{1,0:T(8,128)(2,1)S(1)}, u32[]{:S(2)}, u32[]{:S(2)}) collective-permute-start(bf16[32,3584]{1,0:T(8,128)(2,1)S(1)} %get-tuple-element.56), channel_id=1, source_target_pairs={{0,1},{1,0},{64,65},{65,64},{128,129},{129,128},{192,193},{193,192... | collective-permute-start | bytes 688136 | tf_op jit(solution)/shard_map/ppermute | solution.py:236
  163.8 14.0 %collective-permute-start.25 = (bf16[32,3584]{1,0:T(8,128)(2,1)S(1)}, bf16[32,3584]{1,0:T(8,128)(2,1)S(1)}, u32[]{:S(2)}, u32[]{:S(2)}) collective-permute-start(bf16[32,3584]{1,0:T(8,128)(2,1)S(1)} %get-tuple-element.54), channel_id=1, source_target_pairs={{0,129},{1,128},{64,193},{65,192},{128,1},{129,0},{192,65},{193,64... | collective-permute-start | bytes 688136 | tf_op jit(solution)/shard_map/ppermute | solution.py:236
  163.8 15.1 %collective-permute-start.24 = (bf16[32,3584]{1,0:T(8,128)(2,1)S(1)}, bf16[32,3584]{1,0:T(8,128)(2,1)S(1)}, u32[]{:S(2)}, u32[]{:S(2)}) collective-permute-start(bf16[32,3584]{1,0:T(8,128)(2,1)S(1)} %get-tuple-element.53), channel_id=1, source_target_pairs={{0,128},{1,129},{64,192},{65,193},{128,0},{129,1},{192,64},{193,65... | collective-permute-start | bytes 688136 | tf_op jit(solution)/shard_map/ppermute | solution.py:236
  167.4 17.9 %collective-permute-start.23 = (bf16[32,3584]{1,0:T(8,128)(2,1)S(1)}, bf16[32,3584]{1,0:T(8,128)(2,1)S(1)}, u32[]{:S(2)}, u32[]{:S(2)}) collective-permute-start(bf16[32,3584]{1,0:T(8,128)(2,1)S(1)} %get-tuple-element.50), channel_id=1, source_target_pairs={{0,65},{1,64},{64,129},{65,128},{128,193},{129,192},{192,1},{193,0... | collective-permute-start | bytes 688136 | tf_op jit(solution)/shard_map/ppermute | solution.py:236
  169.8 16.7 %collective-permute-start.22 = (bf16[32,3584]{1,0:T(8,128)(2,1)S(1)}, bf16[32,3584]{1,0:T(8,128)(2,1)S(1)}, u32[]{:S(2)}, u32[]{:S(2)}) collective-permute-start(bf16[32,3584]{1,0:T(8,128)(2,1)S(1)} %get-tuple-element.49), channel_id=1, source_target_pairs={{0,64},{1,65},{64,128},{65,129},{128,192},{129,193},{192,0},{193,1... | collective-permute-start | bytes 688136 | tf_op jit(solution)/shard_map/ppermute | solution.py:236
  172.1 14.5 %collective-permute-start.30 = (bf16[32,3584]{1,0:T(8,128)(2,1)S(1)}, bf16[32,3584]{1,0:T(8,128)(2,1)S(1)}, u32[]{:S(2)}, u32[]{:S(2)}) collective-permute-start(bf16[32,3584]{1,0:T(8,128)(2,1)S(1)} %get-tuple-element.58), channel_id=1, source_target_pairs={{0,193},{1,192},{64,1},{65,0},{128,65},{129,64},{192,129},{193,128... | collective-permute-start | bytes 688136 | tf_op jit(solution)/shard_map/ppermute | solution.py:236
  177.9 8.7 %collective-permute-start.29 = (bf16[32,3584]{1,0:T(8,128)(2,1)S(1)}, bf16[32,3584]{1,0:T(8,128)(2,1)S(1)}, u32[]{:S(2)}, u32[]{:S(2)}) collective-permute-start(bf16[32,3584]{1,0:T(8,128)(2,1)S(1)} %get-tuple-element.57), channel_id=1, source_target_pairs={{0,192},{1,193},{64,0},{65,1},{128,64},{129,65},{192,128},{193,129... | collective-permute-start | bytes 688136 | tf_op jit(solution)/shard_map/ppermute | solution.py:236

commit v6 on v5

--- a/solution.py
+++ b/solution.py
@@ -54,11 +54,11 @@
     return value * lax.rsqrt(jnp.mean(value * value, axis=-1, keepdims=True) + 1e-06) * gain
 
 
-def project_kernel(scale, count, place_ref, normed_ref, own_ref, mine_ref, other_ref, out_ref, weight):
+def project_kernel(scale, low, count, place_ref, normed_ref, own_ref, mine_ref, other_ref, out_ref, weight):
     me, core = place_ref[0], place_ref[1]
     row = lambda section, half: pl.ds(pl.multiple_of(section * 320 + half * 160, 16), 160)
     for t in range(count):
-        weight[t, pl.ds(pl.multiple_of(me * 320, 16), 320), :] = own_ref[t]
+        weight[t, pl.ds(pl.multiple_of(me * 320, 16), 320), :] = own_ref[low + t]
         for source, half in ((mine_ref, core), (other_ref, 1 - core)):
             for k in range(3):
                 section = lax.rem(me + k + 1, SECTIONS)
@@ -69,25 +69,25 @@
             out_ref[h, t * HD : (t + 1) * HD, :] = turned[h * HD : (h + 1) * HD, :]
 
 
-def fetch(own, core, *beside):
-    half = lax.dynamic_slice_in_dim(own, core * 160, 160, axis=1)
+def fetch(weight, low, count, core, *beside):
+    half = lax.dynamic_slice(weight, (low, core * 160, 0), (count, 160, weight.shape[2]))
     right, left, *beside = lax.optimization_barrier((section_shift(half, -1), section_shift(half, 1), *beside))
     opp_a, opp_b = section_shift(right[:, :80], -1), section_shift(left[:, 80:], 1)
     return jnp.stack([right, jnp.concatenate([opp_a, opp_b], axis=1), left]), *beside
 
 
-def project(place, normed, own, mine, scale):
-    count = own.shape[0]
+def project(place, normed, weight, low, mine, scale):
+    count = mine.shape[1]
     other = blk_swap(mine, 1)
     return call(
-        functools.partial(project_kernel, scale, count),
+        functools.partial(project_kernel, scale, low, count),
         jax.ShapeDtypeStruct((ZN, count * HD, 256), bf16),
         [SMEM] + [VMEM] * 4,
         [pltpu.VMEM((count, 1280, 640), bf16)],
         flops=2 * 256 * 1280 * 640 * count,
         moved=count * 2 * 1280 * 640,
         name="project",
-    )(place, normed, own, mine, other)
+    )(place, normed, weight, mine, other)
 
 
 def attention_kernel(bounds_ref, place_ref, qframe_ref, kframe_ref, q_ref, own, near, far, across, out_ref, keys, values, held):
@@ -243,27 +243,28 @@
     patch = patches[0]
     normed = rms_norm(patch.astype(f32), norm_gain).astype(bf16)
 
-    kv_own, q_own = qkv_weight[1:3], qkv_weight[0:1]
     out_half = tp_swap(lax.dynamic_slice_in_dim(out_weight, core * 160, 160, axis=1))
-    kv_mine, out_half = fetch(kv_own, core, out_half)
-    kv_mine, q_own = lax.optimization_barrier((kv_mine, q_own))
-    kv = z_exchange(project(place, normed, kv_own, kv_mine, 1.0))
+    kv_mine, out_half = fetch(qkv_weight, 1, 2, core, out_half)
+    kv_mine, later = lax.optimization_barrier((kv_mine, qkv_weight))
+    kv = z_exchange(project(place, normed, qkv_weight, 1, kv_mine, 1.0))
+    (q_mine,) = fetch(later, 0, 1, core)
+    q = project(place, normed, qkv_weight, 0, q_mine, HD ** (-0.5) * math.log2(math.e))
+    kv, q, out_half = lax.optimization_barrier((kv, q, out_half))
+    far = blk_swap(kv, 16)
+    near = blk_swap(kv, 1)
+    q = z_exchange(q)
     out_rest = blk_swap(out_half, 1)
     out_weight_t = jnp.where(
         core == 0, jnp.concatenate([out_half, out_rest], axis=1), jnp.concatenate([out_rest, out_half], axis=1)
     )
-    q_mine, out_own = lax.optimization_barrier((fetch(q_own, core)[0], jnp.stack([out_weight, out_weight_t])))
+    far, q, out_own = lax.optimization_barrier((far, q, jnp.stack([out_weight, out_weight_t])))
+    across = blk_swap(far, 1)
+
     out_right, out_left = section_shift(out_own, -1), section_shift(out_own, 1)
-    q = project(place, normed, q_own, q_mine, HD ** (-0.5) * math.log2(math.e))
-    kv, q = lax.optimization_barrier((kv, q))
-    far = blk_swap(kv, 16)
-    near = blk_swap(kv, 1)
-    q = z_exchange(q)
-    far, q, out_right, out_left = lax.optimization_barrier((far, q, out_right, out_left))
-    across = blk_swap(far, 1)
+    attn = attention(place, frame_ids[0], q, (kv, near, far, across), y, core)
+    attn, out_right, out_left = lax.optimization_barrier((attn, out_right, out_left))
+    attn = z_exchange(attn)
     out_a, out_b = section_shift(out_right[:, :320], -1), section_shift(out_left[:, 320:], 1)
-
-    attn = z_exchange(attention(place, frame_ids[0], q, (kv, near, far, across), y, core))
     attn_t = tp_swap(attn)
     order = groups[0].reshape(2, 32, 4).transpose(0, 2, 1).reshape(256, 1)
     own = call(

time: 191 us -> 193 us (1.010); the launches traced: 187 us -> 194 us
  waiting for transfers between devices: 54.3 us -> 60.7 us
  starting transfers between devices: 66.2 us -> 69.6 us
  other arithmetic: 6.83 us -> 4.58 us
    all_to_all x3, waiting for transfers between devices: 9.13 us -> 23.9 us  [z_exchange(): lax.all_to_all(value, 'blk', 0, 0, axis_index_groups=Z_GROUPS, tiled=True)]
    ppermute x16, waiting for transfers between devices: 26.2 us -> 13.9 us  [section_shift(): return lax.ppermute(value, 'section', route)]
    ppermute x16, starting transfers between devices: 22.6 us -> 25.9 us  [section_shift(): return lax.ppermute(value, 'section', route)]
    slice x2 -> x0, local copies, waits for them, and re-layouts: 2.3 us -> none  [on_device(): kv_own, q_own = (qkv_weight[1:3], qkv_weight[0:1])]
    ppermute x6, waiting for transfers between devices: 0.64 us -> 2.88 us  [blk_swap(): return lax.ppermute(value, 'blk', [(i, i ^ bit) for i in range(32)])]
    ppermute x7, starting transfers between devices: 14.7 us -> 16.8 us  [send(): return lax.ppermute(value, ('section', 'tp'), route)]
    unnamed x30 -> x28, local copies, waits for them, and re-layouts: 10 us -> 11.8 us
  transfers between devices with their start and end apart: 34 -> 34, of which waited for: 19 -> 15; matrix products, arithmetic and copies ran while one was open for 12% -> 10% of each run, Pallas kernels for 8% -> 17%
where the time goes in v6:
time: 193 us; the launch traced here: 194 us
  starting transfers between devices  69.6 us (36%)
  waiting for transfers between devices  60.7 us (31%)
  Pallas kernels  37 us (19%)
  local copies, waits for them, and re-layouts  21.4 us (11%)
  other arithmetic  4.58 us (2%)
    ppermute x16, starting transfers between devices, section_shift(): return lax.ppermute(value, 'section', route)  25.9 us
    all_to_all x3, waiting for transfers between devices, z_exchange(): lax.all_to_all(value, 'blk', 0, 0, axis_index_groups=Z_GROUPS, tiled=True)  23.9 us
    pallas_call x1, Pallas kernels, attention(): call(attention_kernel, jax.ShapeDtypeStruct((ZN, HD, 256), bf16), [SMEM,...  18.6 us
    all_to_all x3, starting transfers between devices, z_exchange(): lax.all_to_all(value, 'blk', 0, 0, axis_index_groups=Z_GROUPS, tiled=True)  18.2 us
    ppermute x7, starting transfers between devices, send(): return lax.ppermute(value, ('section', 'tp'), route)  16.8 us
    ppermute x16, waiting for transfers between devices, section_shift(): return lax.ppermute(value, 'section', route)  13.9 us
    unnamed x28, local copies, waits for them, and re-layouts  11.8 us
    ppermute x2, waiting for transfers between devices, tp_swap(): return lax.ppermute(value, 'tp', [(0, 1), (1, 0)])  11.4 us
  transfers between devices with their start and end apart: 34, of which 15 were waited for; matrix products, arithmetic and copies ran while one was open for 10% of the time, Pallas kernels for 17%

profile of v6, /device:TPU:32, one launch (start us, length us, event | category | flops | bytes accessed | tf_op | source)
XLA Modules:
  0.0 193.7 jit_solution(7234096796978530791)
XLA Ops:
  0.0 1.0 constant_dynamic-slice_fusion.2
  1.0 1.6 collective-permute-start.1
  2.6 1.7 collective-permute-start
  4.4 1.3 copy.41
  5.8 3.3 %collective-permute-start.2 = (bf16[640,160]{1,0:T(8,128)(2,1)S(1)}, bf16[640,160]{1,0:T(8,128)(2,1)S(1)}, u32[]{:S(2)}, u32[]{:S(2)}) collective-permute-start(bf16[640,160]{1,0:T(8,128)(2,1)S(1)} %constant_dynamic-slice_fusion.1), channel_id=1, source_target_pairs={{0,1},{1,0},{2,3},{3,2},{4,5},{5,4},{6,7},{7,6},{8,9},{9,8},{10,11... | collective-permute-start | bytes 614408 | tf_op jit(solution)/shard_map/ppermute | solution.py:46
  9.1 7.2 %collective-permute-done.2 = bf16[640,160]{1,0:T(8,128)(2,1)S(1)} collective-permute-done((bf16[640,160]{1,0:T(8,128)(2,1)S(1)}, bf16[640,160]{1,0:T(8,128)(2,1)S(1)}, u32[]{:S(2)}, u32[]{:S(2)}) %collective-permute-start.2) | collective-permute-done | bytes 204832 | tf_op jit(solution)/shard_map/ppermute | solution.py:46
  16.7 3.0 %collective-permute-start.3 = (bf16[2,80,640]{2,1,0:T(8,128)(2,1)S(1)}, bf16[2,80,640]{2,1,0:T(8,128)(2,1)S(1)}, u32[]{:S(2)}, u32[]{:S(2)}) collective-permute-start(bf16[2,80,640]{2,1,0:T(8,128)(2,1)S(1)} %slice.32), channel_id=1, source_target_pairs={{0,192},{64,0},{128,64},{192,128},{1,193},{65,1},{129,65},{193,129... | collective-permute-start | bytes 614408 | tf_op jit(solution)/shard_map/ppermute | solution.py:38
  19.7 3.7 %collective-permute-done.4 = bf16[2,80,640]{2,1,0:T(8,128)(2,1)S(1)} collective-permute-done((bf16[2,80,640]{2,1,0:T(8,128)(2,1)S(1)}, bf16[2,80,640]{2,1,0:T(8,128)(2,1)S(1)}, u32[]{:S(2)}, u32[]{:S(2)}) %collective-permute-start.4) | collective-permute-done | bytes 204832 | tf_op jit(solution)/shard_map/ppermute | solution.py:38
  23.5 1.2 pad_maximum_fusion.mine_ref
  27.2 2.7 %collective-permute-start.6 = (bf16[1,160,640]{2,1,0:T(8,128)(2,1)}, bf16[1,160,640]{2,1,0:T(8,128)(2,1)S(1)}, u32[]{:S(2)}, u32[]{:S(2)}) collective-permute-start(bf16[1,160,640]{2,1,0:T(8,128)(2,1)} %constant_dynamic-slice_fusion), channel_id=1, source_target_pairs={{0,192},{64,0},{128,64},{192,128},{1,193},{65,1},{129,65},{193,129... | collective-permute-start | bytes 614408 | tf_op jit(solution)/shard_map/ppermute | solution.py:38
  29.9 4.0 %project.2 = bf16[8,160,256]{2,1,0:T(8,128)(2,1)} custom-call(s32[4]{0:T(128)S(1)} %pad_add_fusion.1.place_ref, bf16[256,1280]{1,0:T(8,128)(2,1)S(1)} %fusion.2.normed_ref, bf16[3,320,640]{2,1,0:T(8,128)(2,1)S(1)} %copy-done.3, bf16[3,2,160,640]{3,2,1,0:T(8,128)(2,1)} %pad_maximum_fusion.mine_ref, bf16[3,2,160,640]{3,2,1,0:T(8,128)(2,1)} %collective-permute-done.5.other_ref), custom_call_target="tpu_custom_call" | custom-call | flops 838860800 | bytes 3276800 | tf_op jit(solution)/shard_map/project/pallas_call | solution.py:82
  33.9 8.6 %all-to-all-start = ((bf16[8,160,256]{2,1,0:T(8,128)(2,1)}), bf16[8,160,256]{2,1,0:T(8,128)(2,1)S(1)}, u32[]{:S(2)}, u32[]{:S(2)}) async-start(bf16[8,160,256]{2,1,0:T(8,128)(2,1)} %project.2), calls=%async_computation | async-start | bytes 1310720 | tf_op jit(solution)/shard_map/all_to_all | solution.py:50
  42.6 3.2 %collective-permute-start.8 = (bf16[1,80,640]{2,1,0:T(8,128)(2,1)S(1)}, bf16[1,80,640]{2,1,0:T(8,128)(2,1)S(1)}, u32[]{:S(2)}, u32[]{:S(2)}) collective-permute-start(bf16[1,80,640]{2,1,0:T(8,128)(2,1)S(1)} %slice.34), channel_id=1, source_target_pairs={{0,192},{64,0},{128,64},{192,128},{1,193},{65,1},{129,65},{193,129... | collective-permute-start | bytes 307208 | tf_op jit(solution)/shard_map/ppermute | solution.py:38
  45.8 2.6 %collective-permute-done.9 = bf16[1,80,640]{2,1,0:T(8,128)(2,1)S(1)} collective-permute-done((bf16[1,80,640]{2,1,0:T(8,128)(2,1)S(1)}, bf16[1,80,640]{2,1,0:T(8,128)(2,1)S(1)}, u32[]{:S(2)}, u32[]{:S(2)}) %collective-permute-start.9) | collective-permute-done | bytes 102432 | tf_op jit(solution)/shard_map/ppermute | solution.py:38
  48.7 2.0 %collective-permute-done.10.other_ref = bf16[3,1,160,640]{3,2,1,0:T(8,128)(2,1)S(1)} collective-permute-done((bf16[3,1,160,640]{3,2,1,0:T(8,128)(2,1)S(1)}, bf16[3,1,160,640]{3,2,1,0:T(8,128)(2,1)S(1)}, u32[]{:S(2)}, u32[]{:S(2)}) %collective-permute-start.10) | collective-permute-done | bytes 614432 | tf_op jit(solution)/shard_map/ppermute | solution.py:42
  50.7 2.2 %project.3 = bf16[8,80,256]{2,1,0:T(8,128)(2,1)} custom-call(s32[4]{0:T(128)S(1)} %pad_add_fusion.1.place_ref, bf16[256,1280]{1,0:T(8,128)(2,1)S(1)} %fusion.2.normed_ref, bf16[3,320,640]{2,1,0:T(8,128)(2,1)S(1)} %copy-done.3, bf16[3,1,160,640]{3,2,1,0:T(8,128)(2,1)S(1)} %pad_maximum_fusion.2.mine_ref, ...), custom_call_target="tpu_custom_call" | custom-call | flops 419430400 | bytes 1638400 | tf_op jit(solution)/shard_map/project/pallas_call | solution.py:82
  52.9 8.1 %all-to-all-done.own = bf16[8,160,256]{2,1,0:T(8,128)(2,1)S(1)} async-done(((bf16[8,160,256]{2,1,0:T(8,128)(2,1)}), bf16[8,160,256]{2,1,0:T(8,128)(2,1)S(1)}, u32[]{:S(2)}, u32[]{:S(2)}) %all-to-all-start) | async-done | bytes 655392 | tf_op jit(solution)/shard_map/all_to_all | solution.py:50
  61.0 1.6 collective-permute-start.11
  63.8 4.8 %all-to-all-start.1 = ((bf16[8,80,256]{2,1,0:T(8,128)(2,1)}), bf16[8,80,256]{2,1,0:T(8,128)(2,1)S(1)}, u32[]{:S(2)}, u32[]{:S(2)}) async-start(bf16[8,80,256]{2,1,0:T(8,128)(2,1)} %project.3), calls=%async_computation.1 | async-start | bytes 655360 | tf_op jit(solution)/shard_map/all_to_all | solution.py:50
  71.2 9.5 %all-to-all-done.1.q_ref = bf16[8,80,256]{2,1,0:T(8,128)(2,1)S(1)} async-done(((bf16[8,80,256]{2,1,0:T(8,128)(2,1)}), bf16[8,80,256]{2,1,0:T(8,128)(2,1)S(1)}, u32[]{:S(2)}, u32[]{:S(2)}) %all-to-all-start.1) | async-done | bytes 327712 | tf_op jit(solution)/shard_map/all_to_all | solution.py:50
  82.2 1.3 copy.43
  83.5 3.2 %collective-permute-start.15 = (bf16[2,640,320]{1,2,0:T(8,128)(2,1)}, bf16[2,640,320]{1,2,0:T(8,128)(2,1)S(1)}, u32[]{:S(2)}, u32[]{:S(2)}) collective-permute-start(bf16[2,640,320]{1,2,0:T(8,128)(2,1)} %copy.43), channel_id=1, source_target_pairs={{0,192},{64,0},{128,64},{192,128},{1,193},{65,1},{129,65},{193,129... | collective-permute-start | bytes 2457608 | tf_op jit(solution)/shard_map/ppermute | solution.py:38
  86.8 18.6 %attention.1 = bf16[8,80,256]{2,1,0:T(8,128)(2,1)} custom-call(s32[2,8]{1,0:T(2,128)S(1)} %pad_add_fusion.bounds_ref, s32[4]{0:T(128)S(1)} %pad_add_fusion.1.place_ref, s32[8,256]{1,0:T(8,128)S(1)} %bitcast.48, s32[1,8192]{1,0:T(1,128)S(1)} %copy-done.6, bf16[8,80,256]{2,1,0:T(8,128)(2,1)S(1)} %all-to-all-done.1.q_ref, ...), custom_call_target="tpu_custom_call" | custom-call | flops 8589934592 | bytes 2621440 | tf_op jit(solution)/shard_map/attention/pallas_call | solution.py:162
  105.7 4.8 %all-to-all-start.2 = ((bf16[8,80,256]{2,1,0:T(8,128)(2,1)}), bf16[8,80,256]{2,1,0:T(8,128)(2,1)S(1)}, u32[]{:S(2)}, u32[]{:S(2)}) async-start(bf16[8,80,256]{2,1,0:T(8,128)(2,1)} %attention.1), calls=%async_computation.2 | async-start | bytes 655360 | tf_op jit(solution)/shard_map/all_to_all | solution.py:50
  112.0 2.8 %collective-permute-start.18 = (bf16[2,320,320]{2,1,0:T(8,128)(2,1)}, bf16[2,320,320]{2,1,0:T(8,128)(2,1)}, u32[]{:S(2)}, u32[]{:S(2)}) collective-permute-start(bf16[2,320,320]{2,1,0:T(8,128)(2,1)} %slice.46), channel_id=1, source_target_pairs={{0,192},{64,0},{128,64},{192,128},{1,193},{65,1},{129,65},{193,129... | collective-permute-start | bytes 1228808 | tf_op jit(solution)/shard_map/ppermute | solution.py:38
  114.8 1.5 copy.49.left
  117.2 6.3 %all-to-all-done.2.attn_ref = bf16[8,80,256]{2,1,0:T(8,128)(2,1)S(1)} async-done(((bf16[8,80,256]{2,1,0:T(8,128)(2,1)}), bf16[8,80,256]{2,1,0:T(8,128)(2,1)S(1)}, u32[]{:S(2)}, u32[]{:S(2)}) %all-to-all-start.2) | async-done | bytes 327712 | tf_op jit(solution)/shard_map/all_to_all | solution.py:50
  123.6 2.9 %collective-permute-start.17 = (bf16[8,80,256]{2,1,0:T(8,128)(2,1)S(1)}, bf16[8,80,256]{2,1,0:T(8,128)(2,1)}, u32[]{:S(2)}, u32[]{:S(2)}) collective-permute-start(bf16[8,80,256]{2,1,0:T(8,128)(2,1)S(1)} %all-to-all-done.2.attn_ref), channel_id=1, source_target_pairs={{0,1},{1,0},{2,3},{3,2},{4,5},{5,4},{6,7},{7,6},{8,9},{9,8},{10,11... | collective-permute-start | bytes 983048 | tf_op jit(solution)/shard_map/ppermute | solution.py:46
  126.7 4.0 %collective-permute-done.19.opp_b = bf16[2,320,320]{2,1,0:T(8,128)(2,1)} collective-permute-done((bf16[2,320,320]{2,1,0:T(8,128)(2,1)}, bf16[2,320,320]{2,1,0:T(8,128)(2,1)}, u32[]{:S(2)}, u32[]{:S(2)}) %collective-permute-start.19) | collective-permute-done | bytes 409632 | tf_op jit(solution)/shard_map/ppermute | solution.py:38
  130.7 4.2 %collective-permute-done.17.attn_t_ref = bf16[8,80,256]{2,1,0:T(8,128)(2,1)} collective-permute-done((bf16[8,80,256]{2,1,0:T(8,128)(2,1)S(1)}, bf16[8,80,256]{2,1,0:T(8,128)(2,1)}, u32[]{:S(2)}, u32[]{:S(2)}) %collective-permute-start.17) | collective-permute-done | bytes 327712 | tf_op jit(solution)/shard_map/ppermute | solution.py:46
  134.9 1.1 copy-done.5
  136.0 4.7 %output.1.refs_0_ = bf16[256,1280]{1,0:T(8,128)(2,1)} custom-call(s32[4]{0:T(128)S(1)} %pad_add_fusion.1.place_ref, s32[256,1]{1,0:T(8,128)S(1)} %reshape.193.order_ref, f32[1,1280]{1,0:T(1,128)S(1)} %broadcast_in_dim.4.gain_ref, bf16[256,1280]{1,0:T(8,128)(2,1)S(1)} %bitcast.45, bf16[8,80,256]{2,1,0:T(8,128)(2,1)S(1)} %all-to-all-done.2.attn_ref, ...), custom_call_target="tpu_custom_call" | custom-call | flops 1179648000 | bytes 5000000 | tf_op jit(solution)/shard_map/output/pallas_call | solution.py:270
  140.7 3.2 %collective-permute-start.20 = (bf16[256,1280]{1,0:T(8,128)(2,1)}, bf16[256,1280]{1,0:T(8,128)(2,1)}, u32[]{:S(2)}, u32[]{:S(2)}) collective-permute-start(bf16[256,1280]{1,0:T(8,128)(2,1)} %output.1.refs_0_), channel_id=1, source_target_pairs={{0,192},{64,0},{128,64},{192,128},{1,193},{65,1},{129,65},{193,129... | collective-permute-start | bytes 1966088 | tf_op jit(solution)/shard_map/ppermute | solution.py:38
  143.9 6.0 %copy.50.refs_1_.refs_2_ = bf16[5120,320]{1,0:T(8,128)(2,1)} copy(bf16[5120,320]{0,1:T(8,128)(2,1)} %param.16) | data formatting | bytes 6553600 | tf_op args[7]
  149.9 2.1 %copy-done = bf16[5120,320]{1,0:T(8,128)(2,1)S(1)} copy-done((bf16[5120,320]{1,0:T(8,128)(2,1)S(1)}, bf16[5120,320]{1,0:T(8,128)(2,1)}, u32[]{:S(2)}) %copy-start) | copy-done | bytes 3276824
  152.1 2.8 %merge_own.1 = (bf16[32,3584]{1,0:T(8,128)(2,1)S(1)}, bf16[32,3584]{1,0:T(8,128)(2,1)S(1)}) custom-call(s32[4]{0:T(128)S(1)} %pad_add_fusion.1.place_ref, bf16[256,1280]{1,0:T(8,128)(2,1)} %output.1.refs_0_, bf16[5120,320]{1,0:T(8,128)(2,1)S(1)} %copy-done, bf16[320,3584]{1,0:T(8,128)(2,1)S(1)} %copy-done.2), custom_call_target="tpu_custom_call" | custom-call | flops 1426063360 | bytes 6000000 | tf_op jit(solution)/shard_map/merge_own/pallas_call | solution.py:223
  154.9 3.1 %collective-permute-done.21.refs_1_ = bf16[256,1280]{1,0:T(8,128)(2,1)S(1)} collective-permute-done((bf16[256,1280]{1,0:T(8,128)(2,1)}, bf16[256,1280]{1,0:T(8,128)(2,1)S(1)}, u32[]{:S(2)}, u32[]{:S(2)}) %collective-permute-start.21) | collective-permute-done | bytes 655392 | tf_op jit(solution)/shard_map/ppermute | solution.py:38
  158.2 1.0 slice.38
  159.2 3.3 %collective-permute-start.27 = (bf16[128,1280]{1,0:T(8,128)(2,1)S(1)}, bf16[128,1280]{1,0:T(8,128)(2,1)S(1)}, u32[]{:S(2)}, u32[]{:S(2)}) collective-permute-start(bf16[128,1280]{1,0:T(8,128)(2,1)S(1)} %slice.38), channel_id=1, source_target_pairs={{0,192},{64,0},{128,64},{192,128},{1,193},{65,1},{129,65},{193,129... | collective-permute-start | bytes 983048 | tf_op jit(solution)/shard_map/ppermute | solution.py:38
  162.5 3.6 %collective-permute-start.23 = (bf16[32,3584]{1,0:T(8,128)(2,1)S(1)}, bf16[32,3584]{1,0:T(8,128)(2,1)S(1)}, u32[]{:S(2)}, u32[]{:S(2)}) collective-permute-start(bf16[32,3584]{1,0:T(8,128)(2,1)S(1)} %get-tuple-element.52), channel_id=1, source_target_pairs={{0,65},{1,64},{64,129},{65,128},{128,193},{129,192},{192,1},{193,0... | collective-permute-start | bytes 688136 | tf_op jit(solution)/shard_map/ppermute | solution.py:236
  166.1 2.6 %merge_next.1 = (bf16[32,3584]{1,0:T(8,128)(2,1)S(1)}, bf16[32,3584]{1,0:T(8,128)(2,1)S(1)}, bf16[32,3584]{1,0:T(8,128)(2,1)S(1)}, bf16[32,3584]{1,0:T(8,128)(2,1)S(1)}) custom-call(s32[4]{0:T(128)S(1)} %pad_add_fusion.1.place_ref, bf16[256,1280]{1,0:T(8,128)(2,1)} %collective-permute-done.20.refs_0_, bf16[256,1280]{1,0:T(8,128)(2,1)S(1)} %collective-permute-done.21.refs_1_, ...), custom_call_target="tpu_custom_call" | custom-call | flops 1426063360 | bytes 6000000 | tf_op jit(solution)/shard_map/merge_next/pallas_call | solution.py:223
  168.8 3.5 %collective-permute-start.24 = (bf16[32,3584]{1,0:T(8,128)(2,1)S(1)}, bf16[32,3584]{1,0:T(8,128)(2,1)S(1)}, u32[]{:S(2)}, u32[]{:S(2)}) collective-permute-start(bf16[32,3584]{1,0:T(8,128)(2,1)S(1)} %get-tuple-element.55), channel_id=1, source_target_pairs={{0,128},{1,129},{64,192},{65,193},{128,0},{129,1},{192,64},{193,65... | collective-permute-start | bytes 688136 | tf_op jit(solution)/shard_map/ppermute | solution.py:236
  173.2 2.2 %collective-permute-start.26 = (bf16[32,3584]{1,0:T(8,128)(2,1)S(1)}, bf16[32,3584]{1,0:T(8,128)(2,1)S(1)}, u32[]{:S(2)}, u32[]{:S(2)}) collective-permute-start(bf16[32,3584]{1,0:T(8,128)(2,1)S(1)} %get-tuple-element.58), channel_id=1, source_target_pairs={{0,1},{1,0},{64,65},{65,64},{128,129},{129,128},{192,193},{193,192... | collective-permute-start | bytes 688136 | tf_op jit(solution)/shard_map/ppermute | solution.py:236
  175.4 2.1 %merge_opposite.1 = (bf16[32,3584]{1,0:T(8,128)(2,1)S(1)}, bf16[32,3584]{1,0:T(8,128)(2,1)S(1)}) custom-call(s32[4]{0:T(128)S(1)} %pad_add_fusion.1.place_ref, bf16[128,1280]{1,0:T(8,128)(2,1)S(1)} %collective-permute-done.27.refs_0_, bf16[128,1280]{1,0:T(8,128)(2,1)S(1)} %collective-permute-done.28.refs_1_, bf16[5120,320]{1,0:T(8,128)(2,1)S(1)} %copy-done.1, ...), custom_call_target="tpu_custom_call" | custom-call | flops 1426063360 | bytes 6000000 | tf_op jit(solution)/shard_map/merge_opposite/pallas_call | solution.py:223
  177.5 6.6 %collective-permute-start.29 = (bf16[32,3584]{1,0:T(8,128)(2,1)S(1)}, bf16[32,3584]{1,0:T(8,128)(2,1)S(1)}, u32[]{:S(2)}, u32[]{:S(2)}) collective-permute-start(bf16[32,3584]{1,0:T(8,128)(2,1)S(1)} %get-tuple-element.59), channel_id=1, source_target_pairs={{0,192},{1,193},{64,0},{65,1},{128,64},{129,65},{192,128},{193,129... | collective-permute-start | bytes 688136 | tf_op jit(solution)/shard_map/ppermute | solution.py:236
  184.1 1.4 collective-permute-done.24
  185.5 5.0 %collective-permute-done.25 = bf16[32,3584]{1,0:T(8,128)(2,1)S(1)} collective-permute-done((bf16[32,3584]{1,0:T(8,128)(2,1)S(1)}, bf16[32,3584]{1,0:T(8,128)(2,1)S(1)}, u32[]{:S(2)}, u32[]{:S(2)}) %collective-permute-start.25) | collective-permute-done | bytes 229408 | tf_op jit(solution)/shard_map/ppermute | solution.py:236
  190.6 2.2 %collective-permute-done.30 = bf16[32,3584]{1,0:T(8,128)(2,1)S(1)} collective-permute-done((bf16[32,3584]{1,0:T(8,128)(2,1)S(1)}, bf16[32,3584]{1,0:T(8,128)(2,1)S(1)}, u32[]{:S(2)}, u32[]{:S(2)}) %collective-permute-start.30) | collective-permute-done | bytes 229408 | tf_op jit(solution)/shard_map/ppermute | solution.py:236
  (96 shorter events, 13.7 us)
Async XLA Ops:
  1.0 15.2 %collective-permute-start.1 = (bf16[2,160,640]{2,1,0:T(8,128)(2,1)S(1)}, bf16[2,160,640]{2,1,0:T(8,128)(2,1)S(1)}, u32[]{:S(2)}, u32[]{:S(2)}) collective-permute-start(bf16[2,160,640]{2,1,0:T(8,128)(2,1)S(1)} %constant_dynamic-slice_fusion.2), channel_id=1, source_target_pairs={{0,64},{64,128},{128,192},{192,0},{1,65},{65,129},{129,193},{193,1... | collective-permute-start | bytes 1228808 | tf_op jit(solution)/shard_map/ppermute | solution.py:38
  2.6 13.7 %collective-permute-start = (bf16[2,160,640]{2,1,0:T(8,128)(2,1)S(1)}, bf16[2,160,640]{2,1,0:T(8,128)(2,1)S(1)}, u32[]{:S(2)}, u32[]{:S(2)}) collective-permute-start(bf16[2,160,640]{2,1,0:T(8,128)(2,1)S(1)} %constant_dynamic-slice_fusion.2), channel_id=1, source_target_pairs={{0,192},{64,0},{128,64},{192,128},{1,193},{65,1},{129,65},{193,129... | collective-permute-start | bytes 1228808 | tf_op jit(solution)/shard_map/ppermute | solution.py:38
  5.6 17.8 %copy-start.7 = (bf16[640,320]{1,0:T(8,128)(2,1)}, bf16[640,320]{1,0:T(8,128)(2,1)S(1)}, u32[]{:S(2)}) copy-start(bf16[640,320]{1,0:T(8,128)(2,1)S(1)} %copy.41) | copy-start | bytes 1228804
  5.8 10.5 %collective-permute-start.2 = (bf16[640,160]{1,0:T(8,128)(2,1)S(1)}, bf16[640,160]{1,0:T(8,128)(2,1)S(1)}, u32[]{:S(2)}, u32[]{:S(2)}) collective-permute-start(bf16[640,160]{1,0:T(8,128)(2,1)S(1)} %constant_dynamic-slice_fusion.1), channel_id=1, source_target_pairs={{0,1},{1,0},{2,3},{3,2},{4,5},{5,4},{6,7},{7,6},{8,9},{9,8},{10,11... | collective-permute-start | bytes 614408 | tf_op jit(solution)/shard_map/ppermute | solution.py:46
  16.3 7.0 %collective-permute-start.4 = (bf16[2,80,640]{2,1,0:T(8,128)(2,1)S(1)}, bf16[2,80,640]{2,1,0:T(8,128)(2,1)S(1)}, u32[]{:S(2)}, u32[]{:S(2)}) collective-permute-start(bf16[2,80,640]{2,1,0:T(8,128)(2,1)S(1)} %slice.33), channel_id=1, source_target_pairs={{0,64},{64,128},{128,192},{192,0},{1,65},{65,129},{129,193},{193,1... | collective-permute-start | bytes 614408 | tf_op jit(solution)/shard_map/ppermute | solution.py:38
  16.7 6.7 %collective-permute-start.3 = (bf16[2,80,640]{2,1,0:T(8,128)(2,1)S(1)}, bf16[2,80,640]{2,1,0:T(8,128)(2,1)S(1)}, u32[]{:S(2)}, u32[]{:S(2)}) collective-permute-start(bf16[2,80,640]{2,1,0:T(8,128)(2,1)S(1)} %slice.32), channel_id=1, source_target_pairs={{0,192},{64,0},{128,64},{192,128},{1,193},{65,1},{129,65},{193,129... | collective-permute-start | bytes 614408 | tf_op jit(solution)/shard_map/ppermute | solution.py:38
  23.4 1.3 copy-start.4
  23.5 1.5 copy-start.9
  24.7 1.3 copy-start.3
  24.7 5.2 %collective-permute-start.5 = (bf16[3,2,160,640]{3,2,1,0:T(8,128)(2,1)}, bf16[3,2,160,640]{3,2,1,0:T(8,128)(2,1)}, u32[]{:S(2)}, u32[]{:S(2)}) collective-permute-start(bf16[3,2,160,640]{3,2,1,0:T(8,128)(2,1)} %pad_maximum_fusion.mine_ref), channel_id=1, source_target_pairs={{0,2},{2,0},{4,6},{6,4},{8,10},{10,8},{12,14},{14,12},{16,18},{18,... | collective-permute-start | bytes 3686408 | tf_op jit(solution)/shard_map/ppermute | solution.py:42
  26.7 15.8 %collective-permute-start.7 = (bf16[1,160,640]{2,1,0:T(8,128)(2,1)}, bf16[1,160,640]{2,1,0:T(8,128)(2,1)S(1)}, u32[]{:S(2)}, u32[]{:S(2)}) collective-permute-start(bf16[1,160,640]{2,1,0:T(8,128)(2,1)} %constant_dynamic-slice_fusion), channel_id=1, source_target_pairs={{0,64},{64,128},{128,192},{192,0},{1,65},{65,129},{129,193},{193,1... | collective-permute-start | bytes 614408 | tf_op jit(solution)/shard_map/ppermute | solution.py:38
  27.2 15.2 %collective-permute-start.6 = (bf16[1,160,640]{2,1,0:T(8,128)(2,1)}, bf16[1,160,640]{2,1,0:T(8,128)(2,1)S(1)}, u32[]{:S(2)}, u32[]{:S(2)}) collective-permute-start(bf16[1,160,640]{2,1,0:T(8,128)(2,1)} %constant_dynamic-slice_fusion), channel_id=1, source_target_pairs={{0,192},{64,0},{128,64},{192,128},{1,193},{65,1},{129,65},{193,129... | collective-permute-start | bytes 614408 | tf_op jit(solution)/shard_map/ppermute | solution.py:38
  33.9 27.1 %all-to-all-start = ((bf16[8,160,256]{2,1,0:T(8,128)(2,1)}), bf16[8,160,256]{2,1,0:T(8,128)(2,1)S(1)}, u32[]{:S(2)}, u32[]{:S(2)}) async-start(bf16[8,160,256]{2,1,0:T(8,128)(2,1)} %project.2), calls=%async_computation | async-start | bytes 1310720 | tf_op jit(solution)/shard_map/all_to_all | solution.py:50
  42.5 5.9 %collective-permute-start.9 = (bf16[1,80,640]{2,1,0:T(8,128)(2,1)S(1)}, bf16[1,80,640]{2,1,0:T(8,128)(2,1)S(1)}, u32[]{:S(2)}, u32[]{:S(2)}) collective-permute-start(bf16[1,80,640]{2,1,0:T(8,128)(2,1)S(1)} %slice.35), channel_id=1, source_target_pairs={{0,64},{64,128},{128,192},{192,0},{1,65},{65,129},{129,193},{193,1... | collective-permute-start | bytes 307208 | tf_op jit(solution)/shard_map/ppermute | solution.py:38
  42.6 5.9 %collective-permute-start.8 = (bf16[1,80,640]{2,1,0:T(8,128)(2,1)S(1)}, bf16[1,80,640]{2,1,0:T(8,128)(2,1)S(1)}, u32[]{:S(2)}, u32[]{:S(2)}) collective-permute-start(bf16[1,80,640]{2,1,0:T(8,128)(2,1)S(1)} %slice.34), channel_id=1, source_target_pairs={{0,192},{64,0},{128,64},{192,128},{1,193},{65,1},{129,65},{193,129... | collective-permute-start | bytes 307208 | tf_op jit(solution)/shard_map/ppermute | solution.py:38
  48.6 14.5 %copy-start.6 = (s32[1,8192]{1,0:T(1,128)S(1)}, s32[1,8192]{1,0:T(1,128)}, u32[]{:S(2)}) copy-start(s32[1,8192]{1,0:T(1,128)} %kframe_ref.1) | copy-start | bytes 98308
  48.6 2.1 %collective-permute-start.10 = (bf16[3,1,160,640]{3,2,1,0:T(8,128)(2,1)S(1)}, bf16[3,1,160,640]{3,2,1,0:T(8,128)(2,1)S(1)}, u32[]{:S(2)}, u32[]{:S(2)}) collective-permute-start(bf16[3,1,160,640]{3,2,1,0:T(8,128)(2,1)S(1)} %pad_maximum_fusion.2.mine_ref), channel_id=1, source_target_pairs={{0,2},{2,0},{4,6},{6,4},{8,10},{10,8},{12,14},{14,12},{16,18},{18,... | collective-permute-start | bytes 1843208 | tf_op jit(solution)/shard_map/ppermute | solution.py:42
  52.9 18.1 %copy-start.8 = (bf16[640,320]{1,0:T(8,128)(2,1)S(1)}, bf16[640,320]{1,0:T(8,128)(2,1)}, u32[]{:S(2)}) copy-start(bf16[640,320]{1,0:T(8,128)(2,1)} %copy-done.7) | copy-start | bytes 1228804
  61.0 19.7 %collective-permute-start.11 = (bf16[8,160,256]{2,1,0:T(8,128)(2,1)S(1)}, bf16[8,160,256]{2,1,0:T(8,128)(2,1)S(1)}, u32[]{:S(2)}, u32[]{:S(2)}) collective-permute-start(bf16[8,160,256]{2,1,0:T(8,128)(2,1)S(1)} %all-to-all-done.own), channel_id=1, source_target_pairs={{0,32},{2,34},{4,36},{6,38},{8,40},{10,42},{12,44},{14,46},{16,48}... | collective-permute-start | bytes 1966088 | tf_op jit(solution)/shard_map/ppermute | solution.py:42
  63.8 16.8 %all-to-all-start.1 = ((bf16[8,80,256]{2,1,0:T(8,128)(2,1)}), bf16[8,80,256]{2,1,0:T(8,128)(2,1)S(1)}, u32[]{:S(2)}, u32[]{:S(2)}) async-start(bf16[8,80,256]{2,1,0:T(8,128)(2,1)} %project.3), calls=%async_computation.1 | async-start | bytes 655360 | tf_op jit(solution)/shard_map/all_to_all | solution.py:50
  68.6 1.9 collective-permute-start.12
  69.1 17.6 %collective-permute-start.13 = (bf16[8,160,256]{2,1,0:T(8,128)(2,1)S(1)}, bf16[8,160,256]{2,1,0:T(8,128)(2,1)}, u32[]{:S(2)}, u32[]{:S(2)}) collective-permute-start(bf16[8,160,256]{2,1,0:T(8,128)(2,1)S(1)} %all-to-all-done.own), channel_id=1, source_target_pairs={{0,2},{2,0},{4,6},{6,4},{8,10},{10,8},{12,14},{14,12},{16,18},{18,... | collective-permute-start | bytes 1966088 | tf_op jit(solution)/shard_map/ppermute | solution.py:42
  80.6 6.1 %collective-permute-start.14 = (bf16[8,160,256]{2,1,0:T(8,128)(2,1)S(1)}, bf16[8,160,256]{2,1,0:T(8,128)(2,1)}, u32[]{:S(2)}, u32[]{:S(2)}) collective-permute-start(bf16[8,160,256]{2,1,0:T(8,128)(2,1)S(1)} %collective-permute-done.11.far), channel_id=1, source_target_pairs={{0,2},{2,0},{4,6},{6,4},{8,10},{10,8},{12,14},{14,12},{16,18},{18,... | collective-permute-start | bytes 1966088 | tf_op jit(solution)/shard_map/ppermute | solution.py:42
  83.5 22.2 %collective-permute-start.16 = (bf16[2,640,320]{1,2,0:T(8,128)(2,1)}, bf16[2,640,320]{1,2,0:T(8,128)(2,1)}, u32[]{:S(2)}, u32[]{:S(2)}) collective-permute-start(bf16[2,640,320]{1,2,0:T(8,128)(2,1)} %copy.43), channel_id=1, source_target_pairs={{0,64},{64,128},{128,192},{192,0},{1,65},{65,129},{129,193},{193,1... | collective-permute-start | bytes 2457608 | tf_op jit(solution)/shard_map/ppermute | solution.py:38
  83.5 22.2 %collective-permute-start.15 = (bf16[2,640,320]{1,2,0:T(8,128)(2,1)}, bf16[2,640,320]{1,2,0:T(8,128)(2,1)S(1)}, u32[]{:S(2)}, u32[]{:S(2)}) collective-permute-start(bf16[2,640,320]{1,2,0:T(8,128)(2,1)} %copy.43), channel_id=1, source_target_pairs={{0,192},{64,0},{128,64},{192,128},{1,193},{65,1},{129,65},{193,129... | collective-permute-start | bytes 2457608 | tf_op jit(solution)/shard_map/ppermute | solution.py:38
  105.7 17.9 %all-to-all-start.2 = ((bf16[8,80,256]{2,1,0:T(8,128)(2,1)}), bf16[8,80,256]{2,1,0:T(8,128)(2,1)S(1)}, u32[]{:S(2)}, u32[]{:S(2)}) async-start(bf16[8,80,256]{2,1,0:T(8,128)(2,1)} %attention.1), calls=%async_computation.2 | async-start | bytes 655360 | tf_op jit(solution)/shard_map/all_to_all | solution.py:50
  112.0 14.5 %copy-start.11 = (s32[1,64,4]{1,2,0:T(4,128)S(1)}, s32[1,64,4]{1,2,0:T(4,128)}, u32[]{:S(2)}) copy-start(s32[1,64,4]{1,2,0:T(4,128)} %param.11) | copy-start | bytes 3076
  112.0 14.6 %copy-start.10 = (f32[1280]{0:T(1024)S(1)}, f32[1280]{0:T(1024)}, u32[]{:S(2)}) copy-start(f32[1280]{0:T(1024)} %param.15) | copy-start | bytes 15364
  112.0 14.7 %collective-permute-start.18 = (bf16[2,320,320]{2,1,0:T(8,128)(2,1)}, bf16[2,320,320]{2,1,0:T(8,128)(2,1)}, u32[]{:S(2)}, u32[]{:S(2)}) collective-permute-start(bf16[2,320,320]{2,1,0:T(8,128)(2,1)} %slice.46), channel_id=1, source_target_pairs={{0,192},{64,0},{128,64},{192,128},{1,193},{65,1},{129,65},{193,129... | collective-permute-start | bytes 1228808 | tf_op jit(solution)/shard_map/ppermute | solution.py:38
  117.2 13.5 %collective-permute-start.19 = (bf16[2,320,320]{2,1,0:T(8,128)(2,1)}, bf16[2,320,320]{2,1,0:T(8,128)(2,1)}, u32[]{:S(2)}, u32[]{:S(2)}) collective-permute-start(bf16[2,320,320]{2,1,0:T(8,128)(2,1)} %slice.47), channel_id=1, source_target_pairs={{0,64},{64,128},{128,192},{192,0},{1,65},{65,129},{129,193},{193,1... | collective-permute-start | bytes 1228808 | tf_op jit(solution)/shard_map/ppermute | solution.py:38
  123.6 11.3 %collective-permute-start.17 = (bf16[8,80,256]{2,1,0:T(8,128)(2,1)S(1)}, bf16[8,80,256]{2,1,0:T(8,128)(2,1)}, u32[]{:S(2)}, u32[]{:S(2)}) collective-permute-start(bf16[8,80,256]{2,1,0:T(8,128)(2,1)S(1)} %all-to-all-done.2.attn_ref), channel_id=1, source_target_pairs={{0,1},{1,0},{2,3},{3,2},{4,5},{5,4},{6,7},{7,6},{8,9},{9,8},{10,11... | collective-permute-start | bytes 983048 | tf_op jit(solution)/shard_map/ppermute | solution.py:46
  134.9 1.1 copy-start.5
  140.7 17.3 %collective-permute-start.21 = (bf16[256,1280]{1,0:T(8,128)(2,1)}, bf16[256,1280]{1,0:T(8,128)(2,1)S(1)}, u32[]{:S(2)}, u32[]{:S(2)}) collective-permute-start(bf16[256,1280]{1,0:T(8,128)(2,1)} %output.1.refs_0_), channel_id=1, source_target_pairs={{0,64},{64,128},{128,192},{192,0},{1,65},{65,129},{129,193},{193,1... | collective-permute-start | bytes 1966088 | tf_op jit(solution)/shard_map/ppermute | solution.py:38
  140.7 17.3 %collective-permute-start.20 = (bf16[256,1280]{1,0:T(8,128)(2,1)}, bf16[256,1280]{1,0:T(8,128)(2,1)}, u32[]{:S(2)}, u32[]{:S(2)}) collective-permute-start(bf16[256,1280]{1,0:T(8,128)(2,1)} %output.1.refs_0_), channel_id=1, source_target_pairs={{0,192},{64,0},{128,64},{192,128},{1,193},{65,1},{129,65},{193,129... | collective-permute-start | bytes 1966088 | tf_op jit(solution)/shard_map/ppermute | solution.py:38
  143.9 6.0 %copy-start.2 = (bf16[320,3584]{1,0:T(8,128)(2,1)S(1)}, bf16[320,3584]{1,0:T(8,128)(2,1)}, u32[]{:S(2)}) copy-start(bf16[320,3584]{1,0:T(8,128)(2,1)} %refs_3_.3) | copy-start | bytes 6881284
  149.9 2.1 %copy-start = (bf16[5120,320]{1,0:T(8,128)(2,1)S(1)}, bf16[5120,320]{1,0:T(8,128)(2,1)}, u32[]{:S(2)}) copy-start(bf16[5120,320]{1,0:T(8,128)(2,1)} %copy.50.refs_1_.refs_2_) | copy-start | bytes 9830404
  152.1 14.1 %copy-start.1 = (bf16[5120,320]{1,0:T(8,128)(2,1)S(1)}, bf16[5120,320]{1,0:T(8,128)(2,1)}, u32[]{:S(2)}) copy-start(bf16[5120,320]{1,0:T(8,128)(2,1)} %copy.50.refs_1_.refs_2_) | copy-start | bytes 9830404
  158.1 14.2 %collective-permute-start.28 = (bf16[128,1280]{1,0:T(8,128)(2,1)S(1)}, bf16[128,1280]{1,0:T(8,128)(2,1)S(1)}, u32[]{:S(2)}, u32[]{:S(2)}) collective-permute-start(bf16[128,1280]{1,0:T(8,128)(2,1)S(1)} %slice.39), channel_id=1, source_target_pairs={{0,64},{64,128},{128,192},{192,0},{1,65},{65,129},{129,193},{193,1... | collective-permute-start | bytes 983048 | tf_op jit(solution)/shard_map/ppermute | solution.py:38
  159.2 14.0 %collective-permute-start.27 = (bf16[128,1280]{1,0:T(8,128)(2,1)S(1)}, bf16[128,1280]{1,0:T(8,128)(2,1)S(1)}, u32[]{:S(2)}, u32[]{:S(2)}) collective-permute-start(bf16[128,1280]{1,0:T(8,128)(2,1)S(1)} %slice.38), channel_id=1, source_target_pairs={{0,192},{64,0},{128,64},{192,128},{1,193},{65,1},{129,65},{193,129... | collective-permute-start | bytes 983048 | tf_op jit(solution)/shard_map/ppermute | solution.py:38
  162.5 15.0 %collective-permute-start.22 = (bf16[32,3584]{1,0:T(8,128)(2,1)S(1)}, bf16[32,3584]{1,0:T(8,128)(2,1)S(1)}, u32[]{:S(2)}, u32[]{:S(2)}) collective-permute-start(bf16[32,3584]{1,0:T(8,128)(2,1)S(1)} %get-tuple-element.51), channel_id=1, source_target_pairs={{0,64},{1,65},{64,128},{65,129},{128,192},{129,193},{192,0},{193,1... | collective-permute-start | bytes 688136 | tf_op jit(solution)/shard_map/ppermute | solution.py:236
  162.5 21.6 %collective-permute-start.23 = (bf16[32,3584]{1,0:T(8,128)(2,1)S(1)}, bf16[32,3584]{1,0:T(8,128)(2,1)S(1)}, u32[]{:S(2)}, u32[]{:S(2)}) collective-permute-start(bf16[32,3584]{1,0:T(8,128)(2,1)S(1)} %get-tuple-element.52), channel_id=1, source_target_pairs={{0,65},{1,64},{64,129},{65,128},{128,193},{129,192},{192,1},{193,0... | collective-permute-start | bytes 688136 | tf_op jit(solution)/shard_map/ppermute | solution.py:236
  168.8 16.8 %collective-permute-start.24 = (bf16[32,3584]{1,0:T(8,128)(2,1)S(1)}, bf16[32,3584]{1,0:T(8,128)(2,1)S(1)}, u32[]{:S(2)}, u32[]{:S(2)}) collective-permute-start(bf16[32,3584]{1,0:T(8,128)(2,1)S(1)} %get-tuple-element.55), channel_id=1, source_target_pairs={{0,128},{1,129},{64,192},{65,193},{128,0},{129,1},{192,64},{193,65... | collective-permute-start | bytes 688136 | tf_op jit(solution)/shard_map/ppermute | solution.py:236
  172.2 18.3 %collective-permute-start.25 = (bf16[32,3584]{1,0:T(8,128)(2,1)S(1)}, bf16[32,3584]{1,0:T(8,128)(2,1)S(1)}, u32[]{:S(2)}, u32[]{:S(2)}) collective-permute-start(bf16[32,3584]{1,0:T(8,128)(2,1)S(1)} %get-tuple-element.56), channel_id=1, source_target_pairs={{0,129},{1,128},{64,193},{65,192},{128,1},{129,0},{192,65},{193,64... | collective-permute-start | bytes 688136 | tf_op jit(solution)/shard_map/ppermute | solution.py:236
  173.2 17.4 %collective-permute-start.26 = (bf16[32,3584]{1,0:T(8,128)(2,1)S(1)}, bf16[32,3584]{1,0:T(8,128)(2,1)S(1)}, u32[]{:S(2)}, u32[]{:S(2)}) collective-permute-start(bf16[32,3584]{1,0:T(8,128)(2,1)S(1)} %get-tuple-element.58), channel_id=1, source_target_pairs={{0,1},{1,0},{64,65},{65,64},{128,129},{129,128},{192,193},{193,192... | collective-permute-start | bytes 688136 | tf_op jit(solution)/shard_map/ppermute | solution.py:236
  177.5 13.1 %collective-permute-start.29 = (bf16[32,3584]{1,0:T(8,128)(2,1)S(1)}, bf16[32,3584]{1,0:T(8,128)(2,1)S(1)}, u32[]{:S(2)}, u32[]{:S(2)}) collective-permute-start(bf16[32,3584]{1,0:T(8,128)(2,1)S(1)} %get-tuple-element.59), channel_id=1, source_target_pairs={{0,192},{1,193},{64,0},{65,1},{128,64},{129,65},{192,128},{193,129... | collective-permute-start | bytes 688136 | tf_op jit(solution)/shard_map/ppermute | solution.py:236
  184.1 8.7 %collective-permute-start.30 = (bf16[32,3584]{1,0:T(8,128)(2,1)S(1)}, bf16[32,3584]{1,0:T(8,128)(2,1)S(1)}, u32[]{:S(2)}, u32[]{:S(2)}) collective-permute-start(bf16[32,3584]{1,0:T(8,128)(2,1)S(1)} %get-tuple-element.60), channel_id=1, source_target_pairs={{0,193},{1,192},{64,1},{65,0},{128,65},{129,64},{192,129},{193,128... | collective-permute-start | bytes 688136 | tf_op jit(solution)/shard_map/ppermute | solution.py:236

commit v7 on v6

--- a/solution.py
+++ b/solution.py
@@ -231,6 +231,10 @@
     )(place, *pieces, merger_up, merger_down)
 
 
+def add(one, two):
+    return (one.astype(f32) + two.astype(f32)).astype(bf16)
+
+
 def send(value, distance, flip):
     route = [(s * 2 + t, (s + distance) % SECTIONS * 2 + (t ^ flip)) for s in range(SECTIONS) for t in range(2)]
     return lax.ppermute(value, ("section", "tp"), route)
@@ -247,24 +251,23 @@
     kv_mine, out_half = fetch(qkv_weight, 1, 2, core, out_half)
     kv_mine, later = lax.optimization_barrier((kv_mine, qkv_weight))
     kv = z_exchange(project(place, normed, qkv_weight, 1, kv_mine, 1.0))
-    (q_mine,) = fetch(later, 0, 1, core)
-    q = project(place, normed, qkv_weight, 0, q_mine, HD ** (-0.5) * math.log2(math.e))
-    kv, q, out_half = lax.optimization_barrier((kv, q, out_half))
-    far = blk_swap(kv, 16)
-    near = blk_swap(kv, 1)
-    q = z_exchange(q)
     out_rest = blk_swap(out_half, 1)
     out_weight_t = jnp.where(
         core == 0, jnp.concatenate([out_half, out_rest], axis=1), jnp.concatenate([out_rest, out_half], axis=1)
     )
-    far, q, out_own = lax.optimization_barrier((far, q, jnp.stack([out_weight, out_weight_t])))
+    (q_mine,) = fetch(later, 0, 1, core)
+    q_mine, out_own = lax.optimization_barrier((q_mine, jnp.stack([out_weight, out_weight_t])))
+    out_right, out_left = section_shift(out_own, -1), section_shift(out_own, 1)
+    q = project(place, normed, qkv_weight, 0, q_mine, HD ** (-0.5) * math.log2(math.e))
+    kv, q = lax.optimization_barrier((kv, q))
+    far = blk_swap(kv, 16)
+    near = blk_swap(kv, 1)
+    q = z_exchange(q)
+    far, q, out_right, out_left = lax.optimization_barrier((far, q, out_right, out_left))
     across = blk_swap(far, 1)
-
-    out_right, out_left = section_shift(out_own, -1), section_shift(out_own, 1)
-    attn = attention(place, frame_ids[0], q, (kv, near, far, across), y, core)
-    attn, out_right, out_left = lax.optimization_barrier((attn, out_right, out_left))
-    attn = z_exchange(attn)
     out_a, out_b = section_shift(out_right[:, :320], -1), section_shift(out_left[:, 320:], 1)
+
+    attn = z_exchange(attention(place, frame_ids[0], q, (kv, near, far, across), y, core))
     attn_t = tp_swap(attn)
     order = groups[0].reshape(2, 32, 4).transpose(0, 2, 1).reshape(256, 1)
     own = call(
@@ -281,13 +284,16 @@
     own_same, own_other = merge(place, [own], merger_up, merger_down, "merge_own")
     right, left, own_same, own_other = lax.optimization_barrier((right, left, own_same, own_other))
     opp_a, opp_b = section_shift(right[:128], -1), section_shift(left[128:], 1)
-    sums = [send(own_same, 1, 0), send(own_other, 1, 1)]
+    mine = add(own_same, tp_swap(own_other))
     right_same, right_other, left_same, left_other = merge(
         place, [right, left], merger_up, merger_down, "merge_next"
     )
-    sums += [send(right_same, 2, 0), send(right_other, 2, 1), left_same, send(left_other, 0, 1)]
+    opp_a, opp_b, right_other = lax.optimization_barrier((opp_a, opp_b, right_other))
+    theirs = add(right_same, tp_swap(right_other))
     opp_same, opp_other = merge(place, [opp_a, opp_b], merger_up, merger_down, "merge_opposite")
-    sums += [send(opp_same, 3, 0), send(opp_other, 3, 1)]
+    opp_same, opp_other, left_other, mine = lax.optimization_barrier((opp_same, opp_other, left_other, mine))
+    sums = [send(opp_same, 3, 0), send(opp_other, 3, 1), section_shift(theirs, 2), section_shift(mine, 1)]
+    sums += [left_same, tp_swap(left_other)]
     return sum(part.astype(f32) for part in sums).astype(bf16)[None]
 
 

time: 193 us -> 188 us (0.974)
  waiting for transfers between devices: 60.7 us -> 55 us
  starting transfers between devices: 69.6 us -> 66 us
    ppermute x7 -> x2, starting transfers between devices: 16.8 us -> 3.78 us  [send(): return lax.ppermute(value, ('section', 'tp'), route)]
    ppermute x16 -> x18, waiting for transfers between devices: 13.9 us -> 25.6 us  [section_shift(): return lax.ppermute(value, 'section', route)]
    all_to_all x3, waiting for transfers between devices: 23.9 us -> 13.2 us  [z_exchange(): lax.all_to_all(value, 'blk', 0, 0, axis_index_groups=Z_GROUPS, tiled=True)]
    ppermute x2 -> x5, starting transfers between devices: 6.18 us -> 14.3 us  [tp_swap(): return lax.ppermute(value, 'tp', [(0, 1), (1, 0)])]
    ppermute x2 -> x5, waiting for transfers between devices: 11.4 us -> 7.27 us  [tp_swap(): return lax.ppermute(value, 'tp', [(0, 1), (1, 0)])]
    ppermute x6, waiting for transfers between devices: 2.88 us -> 0.51 us  [blk_swap(): return lax.ppermute(value, 'blk', [(i, i ^ bit) for i in range(32)])]
    ppermute x16 -> x18, starting transfers between devices: 25.9 us -> 27.8 us  [section_shift(): return lax.ppermute(value, 'section', route)]
    unnamed x28 -> x38, local copies, waits for them, and re-layouts: 11.8 us -> 13.2 us
  transfers between devices with their start and end apart: 34 -> 34, of which waited for: 15 -> 15; matrix products, arithmetic and copies ran while one was open for 10% -> 10% of each run, Pallas kernels for 17% -> 7%
where the time goes in v7:
time: 188 us; the launch traced here: 187 us
  starting transfers between devices  66 us (35%)
  waiting for transfers between devices  55 us (29%)
  Pallas kernels  36.5 us (19%)
  local copies, waits for them, and re-layouts  23.2 us (12%)
  other arithmetic  5.7 us (3%)
    ppermute x18, starting transfers between devices, section_shift(): return lax.ppermute(value, 'section', route)  27.8 us
    ppermute x18, waiting for transfers between devices, section_shift(): return lax.ppermute(value, 'section', route)  25.6 us
    pallas_call x1, Pallas kernels, attention(): call(attention_kernel, jax.ShapeDtypeStruct((ZN, HD, 256), bf16), [SMEM,...  18.4 us
    all_to_all x3, starting transfers between devices, z_exchange(): lax.all_to_all(value, 'blk', 0, 0, axis_index_groups=Z_GROUPS, tiled=True)  18.1 us
    ppermute x5, starting transfers between devices, tp_swap(): return lax.ppermute(value, 'tp', [(0, 1), (1, 0)])  14.3 us
    unnamed x38, local copies, waits for them, and re-layouts  13.2 us
    all_to_all x3, waiting for transfers between devices, z_exchange(): lax.all_to_all(value, 'blk', 0, 0, axis_index_groups=Z_GROUPS, tiled=True)  13.2 us
    ppermute x2, waiting for transfers between devices, send(): return lax.ppermute(value, ('section', 'tp'), route)  8.44 us
  transfers between devices with their start and end apart: 34, of which 15 were waited for; matrix products, arithmetic and copies ran while one was open for 10% of the time, Pallas kernels for 7%

profile of v7, /device:TPU:32, one launch (start us, length us, event | category | flops | bytes accessed | tf_op | source)
XLA Modules:
  0.0 186.8 jit_solution(4599034077276190420)
XLA Ops:
  1.0 1.6 collective-permute-start.1
  2.6 1.7 collective-permute-start
  4.4 1.3 copy.41
  5.8 3.3 %collective-permute-start.2 = (bf16[640,160]{1,0:T(8,128)(2,1)S(1)}, bf16[640,160]{1,0:T(8,128)(2,1)S(1)}, u32[]{:S(2)}, u32[]{:S(2)}) collective-permute-start(bf16[640,160]{1,0:T(8,128)(2,1)S(1)} %constant_dynamic-slice_fusion.1), channel_id=1, source_target_pairs={{0,1},{1,0},{2,3},{3,2},{4,5},{5,4},{6,7},{7,6},{8,9},{9,8},{10,11... | collective-permute-start | bytes 614408 | tf_op jit(solution)/shard_map/ppermute | solution.py:46
  9.1 7.2 %collective-permute-done.2 = bf16[640,160]{1,0:T(8,128)(2,1)S(1)} collective-permute-done((bf16[640,160]{1,0:T(8,128)(2,1)S(1)}, bf16[640,160]{1,0:T(8,128)(2,1)S(1)}, u32[]{:S(2)}, u32[]{:S(2)}) %collective-permute-start.2) | collective-permute-done | bytes 204832 | tf_op jit(solution)/shard_map/ppermute | solution.py:46
  17.4 3.0 %collective-permute-start.3 = (bf16[2,80,640]{2,1,0:T(8,128)(2,1)S(1)}, bf16[2,80,640]{2,1,0:T(8,128)(2,1)S(1)}, u32[]{:S(2)}, u32[]{:S(2)}) collective-permute-start(bf16[2,80,640]{2,1,0:T(8,128)(2,1)S(1)} %slice.32), channel_id=1, source_target_pairs={{0,192},{64,0},{128,64},{192,128},{1,193},{65,1},{129,65},{193,129... | collective-permute-start | bytes 614408 | tf_op jit(solution)/shard_map/ppermute | solution.py:38
  20.4 3.7 %collective-permute-done.4 = bf16[2,80,640]{2,1,0:T(8,128)(2,1)S(1)} collective-permute-done((bf16[2,80,640]{2,1,0:T(8,128)(2,1)S(1)}, bf16[2,80,640]{2,1,0:T(8,128)(2,1)S(1)}, u32[]{:S(2)}, u32[]{:S(2)}) %collective-permute-start.4) | collective-permute-done | bytes 204832 | tf_op jit(solution)/shard_map/ppermute | solution.py:38
  24.2 1.2 pad_maximum_fusion.mine_ref
  27.4 2.8 %collective-permute-start.6 = (bf16[1,160,640]{2,1,0:T(8,128)(2,1)S(1)}, bf16[1,160,640]{2,1,0:T(8,128)(2,1)S(1)}, u32[]{:S(2)}, u32[]{:S(2)}) collective-permute-start(bf16[1,160,640]{2,1,0:T(8,128)(2,1)S(1)} %constant_dynamic-slice_fusion), channel_id=1, source_target_pairs={{0,192},{64,0},{128,64},{192,128},{1,193},{65,1},{129,65},{193,129... | collective-permute-start | bytes 614408 | tf_op jit(solution)/shard_map/ppermute | solution.py:38
  30.3 3.9 %project.2 = bf16[8,160,256]{2,1,0:T(8,128)(2,1)} custom-call(s32[4]{0:T(128)S(1)} %pad_add_fusion.1.place_ref, bf16[256,1280]{1,0:T(8,128)(2,1)S(1)} %fusion.2.normed_ref, bf16[3,320,640]{2,1,0:T(8,128)(2,1)S(1)} %copy-done.3, bf16[3,2,160,640]{3,2,1,0:T(8,128)(2,1)} %pad_maximum_fusion.mine_ref, bf16[3,2,160,640]{3,2,1,0:T(8,128)(2,1)} %collective-permute-done.5.other_ref), custom_call_target="tpu_custom_call" | custom-call | flops 838860800 | bytes 3276800 | tf_op jit(solution)/shard_map/project/pallas_call | solution.py:82
  34.2 8.6 %all-to-all-start = ((bf16[8,160,256]{2,1,0:T(8,128)(2,1)}), bf16[8,160,256]{2,1,0:T(8,128)(2,1)}, u32[]{:S(2)}, u32[]{:S(2)}) async-start(bf16[8,160,256]{2,1,0:T(8,128)(2,1)} %project.2), calls=%async_computation | async-start | bytes 1310720 | tf_op jit(solution)/shard_map/all_to_all | solution.py:50
  42.8 1.5 maximum_select_fusion
  44.4 3.2 %collective-permute-start.8 = (bf16[1,80,640]{2,1,0:T(8,128)(2,1)S(1)}, bf16[1,80,640]{2,1,0:T(8,128)(2,1)S(1)}, u32[]{:S(2)}, u32[]{:S(2)}) collective-permute-start(bf16[1,80,640]{2,1,0:T(8,128)(2,1)S(1)} %slice.34), channel_id=1, source_target_pairs={{0,192},{64,0},{128,64},{192,128},{1,193},{65,1},{129,65},{193,129... | collective-permute-start | bytes 307208 | tf_op jit(solution)/shard_map/ppermute | solution.py:38
  47.9 2.4 %collective-permute-done.9 = bf16[1,80,640]{2,1,0:T(8,128)(2,1)S(1)} collective-permute-done((bf16[1,80,640]{2,1,0:T(8,128)(2,1)S(1)}, bf16[1,80,640]{2,1,0:T(8,128)(2,1)S(1)}, u32[]{:S(2)}, u32[]{:S(2)}) %collective-permute-start.9) | collective-permute-done | bytes 102432 | tf_op jit(solution)/shard_map/ppermute | solution.py:38
  50.5 1.3 copy.43
  51.9 3.1 %collective-permute-start.13 = (bf16[2,640,320]{1,2,0:T(8,128)(2,1)}, bf16[2,640,320]{1,2,0:T(8,128)(2,1)}, u32[]{:S(2)}, u32[]{:S(2)}) collective-permute-start(bf16[2,640,320]{1,2,0:T(8,128)(2,1)} %copy.43), channel_id=1, source_target_pairs={{0,192},{64,0},{128,64},{192,128},{1,193},{65,1},{129,65},{193,129... | collective-permute-start | bytes 2457608 | tf_op jit(solution)/shard_map/ppermute | solution.py:38
  55.1 2.0 %project.3 = bf16[8,80,256]{2,1,0:T(8,128)(2,1)S(1)} custom-call(s32[4]{0:T(128)S(1)} %pad_add_fusion.1.place_ref, bf16[256,1280]{1,0:T(8,128)(2,1)S(1)} %fusion.2.normed_ref, bf16[3,320,640]{2,1,0:T(8,128)(2,1)S(1)} %copy-done.3, bf16[3,1,160,640]{3,2,1,0:T(8,128)(2,1)S(1)} %pad_maximum_fusion.2.mine_ref, ...), custom_call_target="tpu_custom_call" | custom-call | flops 419430400 | bytes 1638400 | tf_op jit(solution)/shard_map/project/pallas_call | solution.py:82
  57.8 3.9 %all-to-all-done.own = bf16[8,160,256]{2,1,0:T(8,128)(2,1)} async-done(((bf16[8,160,256]{2,1,0:T(8,128)(2,1)}), bf16[8,160,256]{2,1,0:T(8,128)(2,1)}, u32[]{:S(2)}, u32[]{:S(2)}) %all-to-all-start) | async-done | bytes 655392 | tf_op jit(solution)/shard_map/all_to_all | solution.py:50
  61.7 1.6 collective-permute-start.12
  63.3 4.8 %all-to-all-start.1 = ((bf16[8,80,256]{2,1,0:T(8,128)(2,1)}), bf16[8,80,256]{2,1,0:T(8,128)(2,1)S(1)}, u32[]{:S(2)}, u32[]{:S(2)}) async-start(bf16[8,80,256]{2,1,0:T(8,128)(2,1)} %copy-done.6), calls=%async_computation.1 | async-start | bytes 655360 | tf_op jit(solution)/shard_map/all_to_all | solution.py:50
  69.7 4.6 %collective-permute-done.14 = bf16[2,640,320]{1,2,0:T(8,128)(2,1)} collective-permute-done((bf16[2,640,320]{1,2,0:T(8,128)(2,1)}, bf16[2,640,320]{1,2,0:T(8,128)(2,1)}, u32[]{:S(2)}, u32[]{:S(2)}) %collective-permute-start.14) | collective-permute-done | bytes 819232 | tf_op jit(solution)/shard_map/ppermute | solution.py:38
  74.3 5.8 %all-to-all-done.1.q_ref = bf16[8,80,256]{2,1,0:T(8,128)(2,1)S(1)} async-done(((bf16[8,80,256]{2,1,0:T(8,128)(2,1)}), bf16[8,80,256]{2,1,0:T(8,128)(2,1)S(1)}, u32[]{:S(2)}, u32[]{:S(2)}) %all-to-all-start.1) | async-done | bytes 327712 | tf_op jit(solution)/shard_map/all_to_all | solution.py:50
  82.2 18.4 %attention.1 = bf16[8,80,256]{2,1,0:T(8,128)(2,1)} custom-call(s32[2,8]{1,0:T(2,128)S(1)} %pad_add_fusion.bounds_ref, s32[4]{0:T(128)S(1)} %pad_add_fusion.1.place_ref, s32[8,256]{1,0:T(8,128)S(1)} %bitcast.48, s32[1,8192]{1,0:T(1,128)S(1)} %copy-done.7, bf16[8,80,256]{2,1,0:T(8,128)(2,1)S(1)} %all-to-all-done.1.q_ref, ...), custom_call_target="tpu_custom_call" | custom-call | flops 8589934592 | bytes 2621440 | tf_op jit(solution)/shard_map/attention/pallas_call | solution.py:162
  100.6 4.8 %all-to-all-start.2 = ((bf16[8,80,256]{2,1,0:T(8,128)(2,1)}), bf16[8,80,256]{2,1,0:T(8,128)(2,1)S(1)}, u32[]{:S(2)}, u32[]{:S(2)}) async-start(bf16[8,80,256]{2,1,0:T(8,128)(2,1)} %attention.1), calls=%async_computation.2 | async-start | bytes 655360 | tf_op jit(solution)/shard_map/all_to_all | solution.py:50
  105.4 1.5 copy.48.right
  107.8 2.6 %collective-permute-start.18 = (bf16[2,320,320]{2,1,0:T(8,128)(2,1)}, bf16[2,320,320]{2,1,0:T(8,128)(2,1)}, u32[]{:S(2)}, u32[]{:S(2)}) collective-permute-start(bf16[2,320,320]{2,1,0:T(8,128)(2,1)} %slice.46), channel_id=1, source_target_pairs={{0,192},{64,0},{128,64},{192,128},{1,193},{65,1},{129,65},{193,129... | collective-permute-start | bytes 1228808 | tf_op jit(solution)/shard_map/ppermute | solution.py:38
  110.3 1.5 copy.49.left
  112.7 3.4 %all-to-all-done.2.attn_ref = bf16[8,80,256]{2,1,0:T(8,128)(2,1)S(1)} async-done(((bf16[8,80,256]{2,1,0:T(8,128)(2,1)}), bf16[8,80,256]{2,1,0:T(8,128)(2,1)S(1)}, u32[]{:S(2)}, u32[]{:S(2)}) %all-to-all-start.2) | async-done | bytes 327712 | tf_op jit(solution)/shard_map/all_to_all | solution.py:50
  116.2 2.8 %collective-permute-start.17 = (bf16[8,80,256]{2,1,0:T(8,128)(2,1)S(1)}, bf16[8,80,256]{2,1,0:T(8,128)(2,1)}, u32[]{:S(2)}, u32[]{:S(2)}) collective-permute-start(bf16[8,80,256]{2,1,0:T(8,128)(2,1)S(1)} %all-to-all-done.2.attn_ref), channel_id=1, source_target_pairs={{0,1},{1,0},{2,3},{3,2},{4,5},{5,4},{6,7},{7,6},{8,9},{9,8},{10,11... | collective-permute-start | bytes 983048 | tf_op jit(solution)/shard_map/ppermute | solution.py:46
  119.2 2.6 %collective-permute-done.18.opp_a = bf16[2,320,320]{2,1,0:T(8,128)(2,1)} collective-permute-done((bf16[2,320,320]{2,1,0:T(8,128)(2,1)}, bf16[2,320,320]{2,1,0:T(8,128)(2,1)}, u32[]{:S(2)}, u32[]{:S(2)}) %collective-permute-start.18) | collective-permute-done | bytes 409632 | tf_op jit(solution)/shard_map/ppermute | solution.py:38
  121.8 5.1 %collective-permute-done.19.opp_b = bf16[2,320,320]{2,1,0:T(8,128)(2,1)} collective-permute-done((bf16[2,320,320]{2,1,0:T(8,128)(2,1)}, bf16[2,320,320]{2,1,0:T(8,128)(2,1)}, u32[]{:S(2)}, u32[]{:S(2)}) %collective-permute-start.19) | collective-permute-done | bytes 409632 | tf_op jit(solution)/shard_map/ppermute | solution.py:38
  127.0 1.1 copy-done.5
  128.1 4.7 %output.1.refs_0_ = bf16[256,1280]{1,0:T(8,128)(2,1)} custom-call(s32[4]{0:T(128)S(1)} %pad_add_fusion.1.place_ref, s32[256,1]{1,0:T(8,128)S(1)} %reshape.193.order_ref, f32[1,1280]{1,0:T(1,128)S(1)} %broadcast_in_dim.4.gain_ref, bf16[256,1280]{1,0:T(8,128)(2,1)S(1)} %bitcast.45, bf16[8,80,256]{2,1,0:T(8,128)(2,1)S(1)} %all-to-all-done.2.attn_ref, ...), custom_call_target="tpu_custom_call" | custom-call | flops 1179648000 | bytes 5000000 | tf_op jit(solution)/shard_map/output/pallas_call | solution.py:273
  132.8 3.2 %collective-permute-start.20 = (bf16[256,1280]{1,0:T(8,128)(2,1)}, bf16[256,1280]{1,0:T(8,128)(2,1)}, u32[]{:S(2)}, u32[]{:S(2)}) collective-permute-start(bf16[256,1280]{1,0:T(8,128)(2,1)} %output.1.refs_0_), channel_id=1, source_target_pairs={{0,192},{64,0},{128,64},{192,128},{1,193},{65,1},{129,65},{193,129... | collective-permute-start | bytes 1966088 | tf_op jit(solution)/shard_map/ppermute | solution.py:38
  136.0 5.9 %copy.50.refs_1_.refs_2_ = bf16[5120,320]{1,0:T(8,128)(2,1)} copy(bf16[5120,320]{0,1:T(8,128)(2,1)} %param.16) | data formatting | bytes 6553600 | tf_op args[7]
  142.0 2.1 %copy-done = bf16[5120,320]{1,0:T(8,128)(2,1)S(1)} copy-done((bf16[5120,320]{1,0:T(8,128)(2,1)S(1)}, bf16[5120,320]{1,0:T(8,128)(2,1)}, u32[]{:S(2)}) %copy-start) | copy-done | bytes 3276824
  144.1 2.8 %merge_own.1 = (bf16[32,3584]{1,0:T(8,128)(2,1)S(1)}, bf16[32,3584]{1,0:T(8,128)(2,1)S(1)}) custom-call(s32[4]{0:T(128)S(1)} %pad_add_fusion.1.place_ref, bf16[256,1280]{1,0:T(8,128)(2,1)} %output.1.refs_0_, bf16[5120,320]{1,0:T(8,128)(2,1)S(1)} %copy-done, bf16[320,3584]{1,0:T(8,128)(2,1)S(1)} %copy-done.2), custom_call_target="tpu_custom_call" | custom-call | flops 1426063360 | bytes 6000000 | tf_op jit(solution)/shard_map/merge_own/pallas_call | solution.py:223
  146.9 4.7 %collective-permute-done.21.refs_1_ = bf16[256,1280]{1,0:T(8,128)(2,1)S(1)} collective-permute-done((bf16[256,1280]{1,0:T(8,128)(2,1)}, bf16[256,1280]{1,0:T(8,128)(2,1)S(1)}, u32[]{:S(2)}, u32[]{:S(2)}) %collective-permute-start.21) | collective-permute-done | bytes 655392 | tf_op jit(solution)/shard_map/ppermute | solution.py:38
  152.7 3.5 %collective-permute-start.22 = (bf16[128,1280]{1,0:T(8,128)(2,1)S(1)}, bf16[128,1280]{1,0:T(8,128)(2,1)S(1)}, u32[]{:S(2)}, u32[]{:S(2)}) collective-permute-start(bf16[128,1280]{1,0:T(8,128)(2,1)S(1)} %slice.38), channel_id=1, source_target_pairs={{0,192},{64,0},{128,64},{192,128},{1,193},{65,1},{129,65},{193,129... | collective-permute-start | bytes 983048 | tf_op jit(solution)/shard_map/ppermute | solution.py:38
  156.3 2.8 %collective-permute-start.24 = (bf16[32,3584]{1,0:T(8,128)(2,1)S(1)}, bf16[32,3584]{1,0:T(8,128)(2,1)S(1)}, u32[]{:S(2)}, u32[]{:S(2)}) collective-permute-start(bf16[32,3584]{1,0:T(8,128)(2,1)S(1)} %get-tuple-element.65), channel_id=1, source_target_pairs={{0,1},{1,0},{2,3},{3,2},{4,5},{5,4},{6,7},{7,6},{8,9},{9,8},{10,11... | collective-permute-start | bytes 688136 | tf_op jit(solution)/shard_map/ppermute | solution.py:46
  159.1 2.6 %merge_next.1 = (bf16[32,3584]{1,0:T(8,128)(2,1)S(1)}, bf16[32,3584]{1,0:T(8,128)(2,1)S(1)}, bf16[32,3584]{1,0:T(8,128)(2,1)S(1)}, bf16[32,3584]{1,0:T(8,128)(2,1)S(1)}) custom-call(s32[4]{0:T(128)S(1)} %pad_add_fusion.1.place_ref, bf16[256,1280]{1,0:T(8,128)(2,1)} %collective-permute-done.20.refs_0_, bf16[256,1280]{1,0:T(8,128)(2,1)S(1)} %collective-permute-done.21.refs_1_, ...), custom_call_target="tpu_custom_call" | custom-call | flops 1426063360 | bytes 6000000 | tf_op jit(solution)/shard_map/merge_next/pallas_call | solution.py:223
  161.7 2.4 %collective-permute-done.23.refs_1_ = bf16[128,1280]{1,0:T(8,128)(2,1)S(1)} collective-permute-done((bf16[128,1280]{1,0:T(8,128)(2,1)S(1)}, bf16[128,1280]{1,0:T(8,128)(2,1)S(1)}, u32[]{:S(2)}, u32[]{:S(2)}) %collective-permute-start.23) | collective-permute-done | bytes 327712 | tf_op jit(solution)/shard_map/ppermute | solution.py:38
  164.1 2.7 %collective-permute-start.27 = (bf16[32,3584]{1,0:T(8,128)(2,1)S(1)}, bf16[32,3584]{1,0:T(8,128)(2,1)S(1)}, u32[]{:S(2)}, u32[]{:S(2)}) collective-permute-start(bf16[32,3584]{1,0:T(8,128)(2,1)S(1)} %get-tuple-element.69), channel_id=1, source_target_pairs={{0,1},{1,0},{2,3},{3,2},{4,5},{5,4},{6,7},{7,6},{8,9},{9,8},{10,11... | collective-permute-start | bytes 688136 | tf_op jit(solution)/shard_map/ppermute | solution.py:46
  166.9 2.1 %merge_opposite.1 = (bf16[32,3584]{1,0:T(8,128)(2,1)S(1)}, bf16[32,3584]{1,0:T(8,128)(2,1)S(1)}) custom-call(s32[4]{0:T(128)S(1)} %pad_add_fusion.1.place_ref, bf16[128,1280]{1,0:T(8,128)(2,1)S(1)} %collective-permute-done.22.refs_0_, bf16[128,1280]{1,0:T(8,128)(2,1)S(1)} %collective-permute-done.23.refs_1_, bf16[5120,320]{1,0:T(8,128)(2,1)S(1)} %copy-done.1, ...), custom_call_target="tpu_custom_call" | custom-call | flops 1426063360 | bytes 6000000 | tf_op jit(solution)/shard_map/merge_opposite/pallas_call | solution.py:223
  169.0 3.1 %collective-permute-start.25 = (bf16[32,3584]{1,0:T(8,128)(2,1)S(1)}, bf16[32,3584]{1,0:T(8,128)(2,1)S(1)}, u32[]{:S(2)}, u32[]{:S(2)}) collective-permute-start(bf16[32,3584]{1,0:T(8,128)(2,1)S(1)} %get-tuple-element.66), channel_id=1, source_target_pairs={{0,192},{1,193},{64,0},{65,1},{128,64},{129,65},{192,128},{193,129... | collective-permute-start | bytes 688136 | tf_op jit(solution)/shard_map/ppermute | solution.py:240
  172.8 1.6 collective-permute-start.29
  174.4 2.7 %collective-permute-start.30 = (bf16[32,3584]{1,0:T(8,128)(2,1)S(1)}, bf16[32,3584]{1,0:T(8,128)(2,1)S(1)}, u32[]{:S(2)}, u32[]{:S(2)}) collective-permute-start(bf16[32,3584]{1,0:T(8,128)(2,1)S(1)} %get-tuple-element.72), channel_id=1, source_target_pairs={{0,1},{1,0},{2,3},{3,2},{4,5},{5,4},{6,7},{7,6},{8,9},{9,8},{10,11... | collective-permute-start | bytes 688136 | tf_op jit(solution)/shard_map/ppermute | solution.py:46
  178.1 7.8 %collective-permute-done.26 = bf16[32,3584]{1,0:T(8,128)(2,1)S(1)} collective-permute-done((bf16[32,3584]{1,0:T(8,128)(2,1)S(1)}, bf16[32,3584]{1,0:T(8,128)(2,1)S(1)}, u32[]{:S(2)}, u32[]{:S(2)}) %collective-permute-start.26) | collective-permute-done | bytes 229408 | tf_op jit(solution)/shard_map/ppermute | solution.py:240
  (108 shorter events, 15.1 us)
Async XLA Ops:
  1.0 15.2 %collective-permute-start.1 = (bf16[2,160,640]{2,1,0:T(8,128)(2,1)S(1)}, bf16[2,160,640]{2,1,0:T(8,128)(2,1)S(1)}, u32[]{:S(2)}, u32[]{:S(2)}) collective-permute-start(bf16[2,160,640]{2,1,0:T(8,128)(2,1)S(1)} %constant_dynamic-slice_fusion.2), channel_id=1, source_target_pairs={{0,64},{64,128},{128,192},{192,0},{1,65},{65,129},{129,193},{193,1... | collective-permute-start | bytes 1228808 | tf_op jit(solution)/shard_map/ppermute | solution.py:38
  2.6 14.4 %collective-permute-start = (bf16[2,160,640]{2,1,0:T(8,128)(2,1)S(1)}, bf16[2,160,640]{2,1,0:T(8,128)(2,1)S(1)}, u32[]{:S(2)}, u32[]{:S(2)}) collective-permute-start(bf16[2,160,640]{2,1,0:T(8,128)(2,1)S(1)} %constant_dynamic-slice_fusion.2), channel_id=1, source_target_pairs={{0,192},{64,0},{128,64},{192,128},{1,193},{65,1},{129,65},{193,129... | collective-permute-start | bytes 1228808 | tf_op jit(solution)/shard_map/ppermute | solution.py:38
  5.8 10.5 %collective-permute-start.2 = (bf16[640,160]{1,0:T(8,128)(2,1)S(1)}, bf16[640,160]{1,0:T(8,128)(2,1)S(1)}, u32[]{:S(2)}, u32[]{:S(2)}) collective-permute-start(bf16[640,160]{1,0:T(8,128)(2,1)S(1)} %constant_dynamic-slice_fusion.1), channel_id=1, source_target_pairs={{0,1},{1,0},{2,3},{3,2},{4,5},{5,4},{6,7},{7,6},{8,9},{9,8},{10,11... | collective-permute-start | bytes 614408 | tf_op jit(solution)/shard_map/ppermute | solution.py:46
  17.0 7.0 %collective-permute-start.4 = (bf16[2,80,640]{2,1,0:T(8,128)(2,1)S(1)}, bf16[2,80,640]{2,1,0:T(8,128)(2,1)S(1)}, u32[]{:S(2)}, u32[]{:S(2)}) collective-permute-start(bf16[2,80,640]{2,1,0:T(8,128)(2,1)S(1)} %slice.33), channel_id=1, source_target_pairs={{0,64},{64,128},{128,192},{192,0},{1,65},{65,129},{129,193},{193,1... | collective-permute-start | bytes 614408 | tf_op jit(solution)/shard_map/ppermute | solution.py:38
  17.4 6.7 %collective-permute-start.3 = (bf16[2,80,640]{2,1,0:T(8,128)(2,1)S(1)}, bf16[2,80,640]{2,1,0:T(8,128)(2,1)S(1)}, u32[]{:S(2)}, u32[]{:S(2)}) collective-permute-start(bf16[2,80,640]{2,1,0:T(8,128)(2,1)S(1)} %slice.32), channel_id=1, source_target_pairs={{0,192},{64,0},{128,64},{192,128},{1,193},{65,1},{129,65},{193,129... | collective-permute-start | bytes 614408 | tf_op jit(solution)/shard_map/ppermute | solution.py:38
  24.1 1.3 copy-start.4
  24.2 1.5 copy-start.14
  25.4 1.4 copy-start.3
  25.4 4.9 %collective-permute-start.5 = (bf16[3,2,160,640]{3,2,1,0:T(8,128)(2,1)}, bf16[3,2,160,640]{3,2,1,0:T(8,128)(2,1)}, u32[]{:S(2)}, u32[]{:S(2)}) collective-permute-start(bf16[3,2,160,640]{3,2,1,0:T(8,128)(2,1)} %pad_maximum_fusion.mine_ref), channel_id=1, source_target_pairs={{0,2},{2,0},{4,6},{6,4},{8,10},{10,8},{12,14},{14,12},{16,18},{18,... | collective-permute-start | bytes 3686408 | tf_op jit(solution)/shard_map/ppermute | solution.py:42
  26.4 16.4 %collective-permute-start.10 = (bf16[640,160]{1,0:T(8,128)(2,1)S(1)}, bf16[640,160]{1,0:T(8,128)(2,1)}, u32[]{:S(2)}, u32[]{:S(2)}) collective-permute-start(bf16[640,160]{1,0:T(8,128)(2,1)S(1)} %copy-done.13), channel_id=1, source_target_pairs={{0,2},{2,0},{4,6},{6,4},{8,10},{10,8},{12,14},{14,12},{16,18},{18,... | collective-permute-start | bytes 614408 | tf_op jit(solution)/shard_map/ppermute | solution.py:42
  26.8 17.5 %collective-permute-start.7 = (bf16[1,160,640]{2,1,0:T(8,128)(2,1)S(1)}, bf16[1,160,640]{2,1,0:T(8,128)(2,1)S(1)}, u32[]{:S(2)}, u32[]{:S(2)}) collective-permute-start(bf16[1,160,640]{2,1,0:T(8,128)(2,1)S(1)} %constant_dynamic-slice_fusion), channel_id=1, source_target_pairs={{0,64},{64,128},{128,192},{192,0},{1,65},{65,129},{129,193},{193,1... | collective-permute-start | bytes 614408 | tf_op jit(solution)/shard_map/ppermute | solution.py:38
  27.4 16.9 %collective-permute-start.6 = (bf16[1,160,640]{2,1,0:T(8,128)(2,1)S(1)}, bf16[1,160,640]{2,1,0:T(8,128)(2,1)S(1)}, u32[]{:S(2)}, u32[]{:S(2)}) collective-permute-start(bf16[1,160,640]{2,1,0:T(8,128)(2,1)S(1)} %constant_dynamic-slice_fusion), channel_id=1, source_target_pairs={{0,192},{64,0},{128,64},{192,128},{1,193},{65,1},{129,65},{193,129... | collective-permute-start | bytes 614408 | tf_op jit(solution)/shard_map/ppermute | solution.py:38
  34.2 27.5 %all-to-all-start = ((bf16[8,160,256]{2,1,0:T(8,128)(2,1)}), bf16[8,160,256]{2,1,0:T(8,128)(2,1)}, u32[]{:S(2)}, u32[]{:S(2)}) async-start(bf16[8,160,256]{2,1,0:T(8,128)(2,1)} %project.2), calls=%async_computation | async-start | bytes 1310720 | tf_op jit(solution)/shard_map/all_to_all | solution.py:50
  44.3 3.4 %copy-start.8 = (bf16[1,160,640]{2,1,0:T(8,128)(2,1)}, bf16[1,160,640]{2,1,0:T(8,128)(2,1)S(1)}, u32[]{:S(2)}) copy-start(bf16[1,160,640]{2,1,0:T(8,128)(2,1)S(1)} %collective-permute-done.7) | copy-start | bytes 614404
  44.3 3.4 %copy-start.10 = (bf16[1,160,640]{2,1,0:T(8,128)(2,1)}, bf16[1,160,640]{2,1,0:T(8,128)(2,1)S(1)}, u32[]{:S(2)}) copy-start(bf16[1,160,640]{2,1,0:T(8,128)(2,1)S(1)} %collective-permute-done.6) | copy-start | bytes 614404
  44.4 5.9 %collective-permute-start.9 = (bf16[1,80,640]{2,1,0:T(8,128)(2,1)S(1)}, bf16[1,80,640]{2,1,0:T(8,128)(2,1)S(1)}, u32[]{:S(2)}, u32[]{:S(2)}) collective-permute-start(bf16[1,80,640]{2,1,0:T(8,128)(2,1)S(1)} %slice.35), channel_id=1, source_target_pairs={{0,64},{64,128},{128,192},{192,0},{1,65},{65,129},{129,193},{193,1... | collective-permute-start | bytes 307208 | tf_op jit(solution)/shard_map/ppermute | solution.py:38
  44.4 5.9 %collective-permute-start.8 = (bf16[1,80,640]{2,1,0:T(8,128)(2,1)S(1)}, bf16[1,80,640]{2,1,0:T(8,128)(2,1)S(1)}, u32[]{:S(2)}, u32[]{:S(2)}) collective-permute-start(bf16[1,80,640]{2,1,0:T(8,128)(2,1)S(1)} %slice.34), channel_id=1, source_target_pairs={{0,192},{64,0},{128,64},{192,128},{1,193},{65,1},{129,65},{193,129... | collective-permute-start | bytes 307208 | tf_op jit(solution)/shard_map/ppermute | solution.py:38
  47.7 2.7 %copy-start.9 = (bf16[1,160,640]{2,1,0:T(8,128)(2,1)S(1)}, bf16[1,160,640]{2,1,0:T(8,128)(2,1)}, u32[]{:S(2)}) copy-start(bf16[1,160,640]{2,1,0:T(8,128)(2,1)} %copy-done.8) | copy-start | bytes 614404
  47.7 2.7 %copy-start.11 = (bf16[1,160,640]{2,1,0:T(8,128)(2,1)S(1)}, bf16[1,160,640]{2,1,0:T(8,128)(2,1)}, u32[]{:S(2)}) copy-start(bf16[1,160,640]{2,1,0:T(8,128)(2,1)} %copy-done.10) | copy-start | bytes 614404
  50.4 4.6 %collective-permute-start.11 = (bf16[3,1,160,640]{3,2,1,0:T(8,128)(2,1)S(1)}, bf16[3,1,160,640]{3,2,1,0:T(8,128)(2,1)}, u32[]{:S(2)}, u32[]{:S(2)}) collective-permute-start(bf16[3,1,160,640]{3,2,1,0:T(8,128)(2,1)S(1)} %pad_maximum_fusion.2.mine_ref), channel_id=1, source_target_pairs={{0,2},{2,0},{4,6},{6,4},{8,10},{10,8},{12,14},{14,12},{16,18},{18,... | collective-permute-start | bytes 1843208 | tf_op jit(solution)/shard_map/ppermute | solution.py:42
  51.8 16.8 %copy-start.7 = (s32[1,8192]{1,0:T(1,128)S(1)}, s32[1,8192]{1,0:T(1,128)}, u32[]{:S(2)}) copy-start(s32[1,8192]{1,0:T(1,128)} %kframe_ref.1) | copy-start | bytes 98308
  51.8 22.4 %collective-permute-start.14 = (bf16[2,640,320]{1,2,0:T(8,128)(2,1)}, bf16[2,640,320]{1,2,0:T(8,128)(2,1)}, u32[]{:S(2)}, u32[]{:S(2)}) collective-permute-start(bf16[2,640,320]{1,2,0:T(8,128)(2,1)} %copy.43), channel_id=1, source_target_pairs={{0,64},{64,128},{128,192},{192,0},{1,65},{65,129},{129,193},{193,1... | collective-permute-start | bytes 2457608 | tf_op jit(solution)/shard_map/ppermute | solution.py:38
  51.9 22.3 %collective-permute-start.13 = (bf16[2,640,320]{1,2,0:T(8,128)(2,1)}, bf16[2,640,320]{1,2,0:T(8,128)(2,1)}, u32[]{:S(2)}, u32[]{:S(2)}) collective-permute-start(bf16[2,640,320]{1,2,0:T(8,128)(2,1)} %copy.43), channel_id=1, source_target_pairs={{0,192},{64,0},{128,64},{192,128},{1,193},{65,1},{129,65},{193,129... | collective-permute-start | bytes 2457608 | tf_op jit(solution)/shard_map/ppermute | solution.py:38
  61.7 18.4 %collective-permute-start.12 = (bf16[8,160,256]{2,1,0:T(8,128)(2,1)}, bf16[8,160,256]{2,1,0:T(8,128)(2,1)S(1)}, u32[]{:S(2)}, u32[]{:S(2)}) collective-permute-start(bf16[8,160,256]{2,1,0:T(8,128)(2,1)} %all-to-all-done.own), channel_id=1, source_target_pairs={{0,32},{2,34},{4,36},{6,38},{8,40},{10,42},{12,44},{14,46},{16,48}... | collective-permute-start | bytes 1966088 | tf_op jit(solution)/shard_map/ppermute | solution.py:42
  63.3 16.8 %all-to-all-start.1 = ((bf16[8,80,256]{2,1,0:T(8,128)(2,1)}), bf16[8,80,256]{2,1,0:T(8,128)(2,1)S(1)}, u32[]{:S(2)}, u32[]{:S(2)}) async-start(bf16[8,80,256]{2,1,0:T(8,128)(2,1)} %copy-done.6), calls=%async_computation.1 | async-start | bytes 655360 | tf_op jit(solution)/shard_map/all_to_all | solution.py:50
  69.6 12.1 %collective-permute-start.15 = (bf16[8,160,256]{2,1,0:T(8,128)(2,1)}, bf16[8,160,256]{2,1,0:T(8,128)(2,1)S(1)}, u32[]{:S(2)}, u32[]{:S(2)}) collective-permute-start(bf16[8,160,256]{2,1,0:T(8,128)(2,1)} %all-to-all-done.own), channel_id=1, source_target_pairs={{0,2},{2,0},{4,6},{6,4},{8,10},{10,8},{12,14},{14,12},{16,18},{18,... | collective-permute-start | bytes 1966088 | tf_op jit(solution)/shard_map/ppermute | solution.py:42
  80.1 2.1 %collective-permute-start.16 = (bf16[8,160,256]{2,1,0:T(8,128)(2,1)S(1)}, bf16[8,160,256]{2,1,0:T(8,128)(2,1)S(1)}, u32[]{:S(2)}, u32[]{:S(2)}) collective-permute-start(bf16[8,160,256]{2,1,0:T(8,128)(2,1)S(1)} %collective-permute-done.12.far), channel_id=1, source_target_pairs={{0,2},{2,0},{4,6},{6,4},{8,10},{10,8},{12,14},{14,12},{16,18},{18,... | collective-permute-start | bytes 1966088 | tf_op jit(solution)/shard_map/ppermute | solution.py:42
  100.6 15.6 %all-to-all-start.2 = ((bf16[8,80,256]{2,1,0:T(8,128)(2,1)}), bf16[8,80,256]{2,1,0:T(8,128)(2,1)S(1)}, u32[]{:S(2)}, u32[]{:S(2)}) async-start(bf16[8,80,256]{2,1,0:T(8,128)(2,1)} %attention.1), calls=%async_computation.2 | async-start | bytes 655360 | tf_op jit(solution)/shard_map/all_to_all | solution.py:50
  107.8 11.2 %copy-start.16 = (s32[1,64,4]{1,2,0:T(4,128)S(1)}, s32[1,64,4]{1,2,0:T(4,128)}, u32[]{:S(2)}) copy-start(s32[1,64,4]{1,2,0:T(4,128)} %param.11) | copy-start | bytes 3076
  107.8 11.3 %copy-start.15 = (f32[1280]{0:T(1024)S(1)}, f32[1280]{0:T(1024)}, u32[]{:S(2)}) copy-start(f32[1280]{0:T(1024)} %param.15) | copy-start | bytes 15364
  107.8 14.1 %collective-permute-start.18 = (bf16[2,320,320]{2,1,0:T(8,128)(2,1)}, bf16[2,320,320]{2,1,0:T(8,128)(2,1)}, u32[]{:S(2)}, u32[]{:S(2)}) collective-permute-start(bf16[2,320,320]{2,1,0:T(8,128)(2,1)} %slice.46), channel_id=1, source_target_pairs={{0,192},{64,0},{128,64},{192,128},{1,193},{65,1},{129,65},{193,129... | collective-permute-start | bytes 1228808 | tf_op jit(solution)/shard_map/ppermute | solution.py:38
  112.7 14.2 %collective-permute-start.19 = (bf16[2,320,320]{2,1,0:T(8,128)(2,1)}, bf16[2,320,320]{2,1,0:T(8,128)(2,1)}, u32[]{:S(2)}, u32[]{:S(2)}) collective-permute-start(bf16[2,320,320]{2,1,0:T(8,128)(2,1)} %slice.47), channel_id=1, source_target_pairs={{0,64},{64,128},{128,192},{192,0},{1,65},{65,129},{129,193},{193,1... | collective-permute-start | bytes 1228808 | tf_op jit(solution)/shard_map/ppermute | solution.py:38
  116.2 10.8 %collective-permute-start.17 = (bf16[8,80,256]{2,1,0:T(8,128)(2,1)S(1)}, bf16[8,80,256]{2,1,0:T(8,128)(2,1)}, u32[]{:S(2)}, u32[]{:S(2)}) collective-permute-start(bf16[8,80,256]{2,1,0:T(8,128)(2,1)S(1)} %all-to-all-done.2.attn_ref), channel_id=1, source_target_pairs={{0,1},{1,0},{2,3},{3,2},{4,5},{5,4},{6,7},{7,6},{8,9},{9,8},{10,11... | collective-permute-start | bytes 983048 | tf_op jit(solution)/shard_map/ppermute | solution.py:46
  127.0 1.1 copy-start.5
  132.8 18.8 %collective-permute-start.21 = (bf16[256,1280]{1,0:T(8,128)(2,1)}, bf16[256,1280]{1,0:T(8,128)(2,1)S(1)}, u32[]{:S(2)}, u32[]{:S(2)}) collective-permute-start(bf16[256,1280]{1,0:T(8,128)(2,1)} %output.1.refs_0_), channel_id=1, source_target_pairs={{0,64},{64,128},{128,192},{192,0},{1,65},{65,129},{129,193},{193,1... | collective-permute-start | bytes 1966088 | tf_op jit(solution)/shard_map/ppermute | solution.py:38
  132.8 18.8 %collective-permute-start.20 = (bf16[256,1280]{1,0:T(8,128)(2,1)}, bf16[256,1280]{1,0:T(8,128)(2,1)}, u32[]{:S(2)}, u32[]{:S(2)}) collective-permute-start(bf16[256,1280]{1,0:T(8,128)(2,1)} %output.1.refs_0_), channel_id=1, source_target_pairs={{0,192},{64,0},{128,64},{192,128},{1,193},{65,1},{129,65},{193,129... | collective-permute-start | bytes 1966088 | tf_op jit(solution)/shard_map/ppermute | solution.py:38
  136.0 5.9 %copy-start.2 = (bf16[320,3584]{1,0:T(8,128)(2,1)S(1)}, bf16[320,3584]{1,0:T(8,128)(2,1)}, u32[]{:S(2)}) copy-start(bf16[320,3584]{1,0:T(8,128)(2,1)} %refs_3_.3) | copy-start | bytes 6881284
  142.0 2.1 %copy-start = (bf16[5120,320]{1,0:T(8,128)(2,1)S(1)}, bf16[5120,320]{1,0:T(8,128)(2,1)}, u32[]{:S(2)}) copy-start(bf16[5120,320]{1,0:T(8,128)(2,1)} %copy.50.refs_1_.refs_2_) | copy-start | bytes 9830404
  144.1 15.0 %copy-start.1 = (bf16[5120,320]{1,0:T(8,128)(2,1)S(1)}, bf16[5120,320]{1,0:T(8,128)(2,1)}, u32[]{:S(2)}) copy-start(bf16[5120,320]{1,0:T(8,128)(2,1)} %copy.50.refs_1_.refs_2_) | copy-start | bytes 9830404
  152.7 11.4 %collective-permute-start.23 = (bf16[128,1280]{1,0:T(8,128)(2,1)S(1)}, bf16[128,1280]{1,0:T(8,128)(2,1)S(1)}, u32[]{:S(2)}, u32[]{:S(2)}) collective-permute-start(bf16[128,1280]{1,0:T(8,128)(2,1)S(1)} %slice.39), channel_id=1, source_target_pairs={{0,64},{64,128},{128,192},{192,0},{1,65},{65,129},{129,193},{193,1... | collective-permute-start | bytes 983048 | tf_op jit(solution)/shard_map/ppermute | solution.py:38
  152.7 11.4 %collective-permute-start.22 = (bf16[128,1280]{1,0:T(8,128)(2,1)S(1)}, bf16[128,1280]{1,0:T(8,128)(2,1)S(1)}, u32[]{:S(2)}, u32[]{:S(2)}) collective-permute-start(bf16[128,1280]{1,0:T(8,128)(2,1)S(1)} %slice.38), channel_id=1, source_target_pairs={{0,192},{64,0},{128,64},{192,128},{1,193},{65,1},{129,65},{193,129... | collective-permute-start | bytes 983048 | tf_op jit(solution)/shard_map/ppermute | solution.py:38
  156.3 10.6 %collective-permute-start.24 = (bf16[32,3584]{1,0:T(8,128)(2,1)S(1)}, bf16[32,3584]{1,0:T(8,128)(2,1)S(1)}, u32[]{:S(2)}, u32[]{:S(2)}) collective-permute-start(bf16[32,3584]{1,0:T(8,128)(2,1)S(1)} %get-tuple-element.65), channel_id=1, source_target_pairs={{0,1},{1,0},{2,3},{3,2},{4,5},{5,4},{6,7},{7,6},{8,9},{9,8},{10,11... | collective-permute-start | bytes 688136 | tf_op jit(solution)/shard_map/ppermute | solution.py:46
  164.1 13.1 %collective-permute-start.27 = (bf16[32,3584]{1,0:T(8,128)(2,1)S(1)}, bf16[32,3584]{1,0:T(8,128)(2,1)S(1)}, u32[]{:S(2)}, u32[]{:S(2)}) collective-permute-start(bf16[32,3584]{1,0:T(8,128)(2,1)S(1)} %get-tuple-element.69), channel_id=1, source_target_pairs={{0,1},{1,0},{2,3},{3,2},{4,5},{5,4},{6,7},{7,6},{8,9},{9,8},{10,11... | collective-permute-start | bytes 688136 | tf_op jit(solution)/shard_map/ppermute | solution.py:46
  169.0 9.0 %collective-permute-start.25 = (bf16[32,3584]{1,0:T(8,128)(2,1)S(1)}, bf16[32,3584]{1,0:T(8,128)(2,1)S(1)}, u32[]{:S(2)}, u32[]{:S(2)}) collective-permute-start(bf16[32,3584]{1,0:T(8,128)(2,1)S(1)} %get-tuple-element.66), channel_id=1, source_target_pairs={{0,192},{1,193},{64,0},{65,1},{128,64},{129,65},{192,128},{193,129... | collective-permute-start | bytes 688136 | tf_op jit(solution)/shard_map/ppermute | solution.py:240
  172.2 13.7 %collective-permute-start.26 = (bf16[32,3584]{1,0:T(8,128)(2,1)S(1)}, bf16[32,3584]{1,0:T(8,128)(2,1)S(1)}, u32[]{:S(2)}, u32[]{:S(2)}) collective-permute-start(bf16[32,3584]{1,0:T(8,128)(2,1)S(1)} %get-tuple-element.67), channel_id=1, source_target_pairs={{0,193},{1,192},{64,1},{65,0},{128,65},{129,64},{192,129},{193,128... | collective-permute-start | bytes 688136 | tf_op jit(solution)/shard_map/ppermute | solution.py:240
  172.8 13.1 %collective-permute-start.29 = (bf16[32,3584]{1,0:T(8,128)(2,1)S(1)}, bf16[32,3584]{1,0:T(8,128)(2,1)S(1)}, u32[]{:S(2)}, u32[]{:S(2)}) collective-permute-start(bf16[32,3584]{1,0:T(8,128)(2,1)S(1)} %add_convert_fusion.2), channel_id=1, source_target_pairs={{0,64},{64,128},{128,192},{192,0},{1,65},{65,129},{129,193},{193,1... | collective-permute-start | bytes 688136 | tf_op jit(solution)/shard_map/ppermute | solution.py:38
  174.4 11.5 %collective-permute-start.30 = (bf16[32,3584]{1,0:T(8,128)(2,1)S(1)}, bf16[32,3584]{1,0:T(8,128)(2,1)S(1)}, u32[]{:S(2)}, u32[]{:S(2)}) collective-permute-start(bf16[32,3584]{1,0:T(8,128)(2,1)S(1)} %get-tuple-element.72), channel_id=1, source_target_pairs={{0,1},{1,0},{2,3},{3,2},{4,5},{5,4},{6,7},{7,6},{8,9},{9,8},{10,11... | collective-permute-start | bytes 688136 | tf_op jit(solution)/shard_map/ppermute | solution.py:46
  177.2 8.7 %collective-permute-start.28 = (bf16[32,3584]{1,0:T(8,128)(2,1)S(1)}, bf16[32,3584]{1,0:T(8,128)(2,1)S(1)}, u32[]{:S(2)}, u32[]{:S(2)}) collective-permute-start(bf16[32,3584]{1,0:T(8,128)(2,1)S(1)} %add_convert_fusion.1), channel_id=1, source_target_pairs={{0,128},{64,192},{128,0},{192,64},{1,129},{65,193},{129,1},{193,65... | collective-permute-start | bytes 688136 | tf_op jit(solution)/shard_map/ppermute | solution.py:38
  (3 other events, 2.4 us)
